TPU v7x, 32 devices: a whole 2x2x4 slice. The times are simulated.
32 devices in a mesh: section: 2 (over y), fsdp: 4 (over z), replica: 4 (over x, core).
Axes of the slice: x: 2, y: 2, z: 4, core: 2. Of those that a mesh axis runs over, the one named last changes fastest.
Arguments:
- tokens: bfloat16 [2, 4, 512, 1536], P(None, 'replica', 'fsdp'), may hold values from -6 to 6
- cotangent: bfloat16 [2, 4, 512, 1536], P(None, 'replica', 'fsdp'), may hold values from -6 to 6
- seq_lengths: int32 [2, 4, 4], P(None, 'replica'), may hold values from 1 to 509, as said below
- routes: int32 [2, 2, 4, 512, 4], P('section', None, 'replica', 'fsdp'), may hold values from 0 to 7, all different within a row; in each aligned block of 128 rows (0 to 127, 128 to 255, ..., all dimensions but the last counted through in order) at most 64 rows name the same one
- gains: bfloat16 [2, 2, 1536], P('section', None, 'fsdp'), may hold values from 0.5 to 1.5
- w_query: bfloat16 [2, 1536, 1536], P('section', 'fsdp'), may hold values from -0.15625 to 0.15625
- w_key: bfloat16 [2, 1536, 256], P('section', 'fsdp'), may hold values from -0.15625 to 0.15625
- w_value: bfloat16 [2, 1536, 256], P('section', 'fsdp'), may hold values from -0.15625 to 0.15625
- w_out: bfloat16 [2, 1536, 1536], P('section', 'fsdp'), may hold values from -1.25 to 1.25
- w_router: bfloat16 [2, 1536, 8], P('section', 'fsdp'), may hold values from -0.078125 to 0.078125
- w_gate: bfloat16 [2, 8, 1536, 768], P('section', 'fsdp'), may hold values from -0.15625 to 0.15625
- w_up: bfloat16 [2, 8, 1536, 768], P('section', 'fsdp'), may hold values from -0.15625 to 0.15625
- w_down: bfloat16 [2, 8, 768, 1536], P('section', 'fsdp'), may hold values from -0.21875 to 0.21875
Outputs:
- layer_outputs: bfloat16 [2, 2, 4, 512, 1536], P('section', None, 'replica', 'fsdp')
- input_grads: bfloat16 [2, 2, 4, 512, 1536], P('section', None, 'replica', 'fsdp')
- grad_gains: float32 [2, 2, 1536], P('section', None, 'fsdp')
- grad_query: float32 [2, 1536, 1536], P('section', 'fsdp')
- grad_key: float32 [2, 1536, 256], P('section', 'fsdp')
- grad_value: float32 [2, 1536, 256], P('section', 'fsdp')
- grad_out: float32 [2, 1536, 1536], P('section', 'fsdp')
- grad_router: float32 [2, 1536, 8], P('section', 'fsdp')
- grad_gate: float32 [2, 8, 1536, 768], P('section', 'fsdp')
- grad_up: float32 [2, 8, 1536, 768], P('section', 'fsdp')
- grad_down: float32 [2, 8, 768, 1536], P('section', 'fsdp')
Inputs may be any that keep to these rules, and one draw needn't show every extreme that they name: `routes`: each row names 4 different experts; in each aligned block of 128 rows every expert is named by exactly 64 rows. `seq_lengths`: the 4 lengths of a pack are positive and sum to 512; the second sequence of each pack begins among its first 128 tokens and ends among its last 128.
All inputs are finite; a program needn't handle non-finite values.
Results may differ from a plain program's by a relative error of at most 0.028.
Values may be sent and summed in bfloat16 or wider, within the bound.
No kernel may reach another device: no remote copies, remote signals or barrier semaphores. Data moves between devices by JAX's collectives and lax.ppermute only.
A program may use at most 256 MiB of HBM per device.

v0:
```python
import jax
import jax.numpy as jnp
from jax import lax
from jax.sharding import PartitionSpec as P

HEAD = 128
ROPE_BASE = 1000000.0
EPS = 1e-06
MASKED = -1e30
F32 = jnp.float32
BF16 = jnp.bfloat16
S_AX, F_AX, R_AX = "section", "fsdp", "replica"
HIGHEST = lax.Precision.HIGHEST


def mm(a, b):
    return jnp.dot(a, b, preferred_element_type=F32)


def mm_nt(a, b):
    return lax.dot_general(a, b, (((1,), (1,)), ((), ())), preferred_element_type=F32)


def mm_tn(a, b):
    return lax.dot_general(a, b, (((0,), (0,)), ((), ())), preferred_element_type=F32)


def ein(spec, a, b):
    return jnp.einsum(spec, a, b, preferred_element_type=F32)


def rel_gather(value):
    folds = lax.axis_size(F_AX)
    parts = [value]
    for k in range(1, folds):
        parts.append(lax.ppermute(value, F_AX, [(i, (i + k) % folds) for i in range(folds)]))
    return parts


def rel_scatter(parts):
    folds = lax.axis_size(F_AX)
    total = parts[0].astype(F32)
    for k in range(1, folds):
        got = lax.ppermute(parts[k], F_AX, [(i, (i - k) % folds) for i in range(folds)])
        total = total + got.astype(F32)
    return total


def swap_section(value):
    return lax.ppermute(value, S_AX, [(0, 1), (1, 0)])


def swap_core(value):
    count = lax.axis_size(R_AX)
    return lax.ppermute(value, R_AX, [(i, i ^ 1) for i in range(count)])


def all_chips(value):
    count = lax.axis_size(R_AX) // 2
    mine = lax.axis_index(R_AX) // 2
    buffer = jnp.zeros((count,) + value.shape, value.dtype)
    buffer = lax.dynamic_update_index_in_dim(buffer, value, mine, 0)
    for k in range(1, count):
        pairs = [(2 * i + c, 2 * ((i + k) % count) + c) for i in range(count) for c in range(2)]
        got = lax.ppermute(value, R_AX, pairs)
        buffer = lax.dynamic_update_index_in_dim(buffer, got, (mine - k) % count, 0)
    return buffer


def rope_turn(values, cos, sin):
    half = HEAD // 2
    turned = jnp.concatenate([-values[..., half:], values[..., :half]], axis=-1)
    return values * cos + turned * sin


def rope_back(grads, cos, sin):
    half = HEAD // 2
    scaled = grads * sin
    turned = jnp.concatenate([scaled[..., half:], -scaled[..., :half]], axis=-1)
    return grads * cos + turned


def layout(lengths, position):
    bounds = jnp.cumsum(lengths)
    passed = (position[:, None] >= bounds[None, :]).astype(jnp.int32)
    segment = jnp.sum(passed, axis=1)
    start = jnp.sum(passed * lengths[None, :], axis=1)
    return segment, (position - start).astype(F32)


def gated(gate, up):
    return jax.nn.gelu(gate) * up


def attention_in(hidden, gain, w_qkv, common, kv_width):
    cos, sin = common["cos"], common["sin"]
    rows, width = hidden.shape
    q_width = w_qkv.shape[1] - 2 * kv_width
    scale = lax.rsqrt(jnp.mean(hidden * hidden, axis=1, keepdims=True) + EPS)
    normed = hidden * scale
    attn_in = (normed * gain.astype(F32)).astype(BF16)
    lin = mm(attn_in, w_qkv)
    turned = rope_turn(
        lin[:, : q_width + kv_width].reshape(rows, -1, HEAD), cos, sin
    ).astype(BF16).reshape(rows, -1)
    query = turned[:, :q_width]
    kv = jnp.concatenate([turned[:, q_width:], lin[:, q_width + kv_width :].astype(BF16)], axis=1)
    return dict(scale=scale, normed=normed, attn_in=attn_in, query=query, kv=kv)


def grouped_heads(value, groups):
    rows = value.shape[0]
    return value.reshape(rows, groups, -1, HEAD)


def attend(query, kv_all, allowed, groups):
    keys = kv_all[:, : groups * HEAD].reshape(-1, groups, HEAD)
    values = kv_all[:, groups * HEAD :].reshape(-1, groups, HEAD)
    raw = ein("tgha,sga->ghts", grouped_heads(query, groups), keys) * HEAD ** (-0.5)
    scores = jnp.where(allowed[None, None], raw, MASKED)
    top = jnp.max(scores, axis=3, keepdims=True)
    expo = jnp.exp(scores - top)
    probs = expo / jnp.sum(expo, axis=3, keepdims=True)
    mixed = ein("ghts,sga->tgha", probs.astype(BF16), values)
    return mixed.reshape(query.shape), probs


def attend_back(grad_mixed, mixed, probs, query, kv_all, groups):
    rows = query.shape[0]
    keys = kv_all[:, : groups * HEAD].reshape(-1, groups, HEAD)
    values = kv_all[:, groups * HEAD :].reshape(-1, groups, HEAD)
    grad_grouped = grouped_heads(grad_mixed, groups)
    delta = jnp.sum(
        grad_grouped.astype(F32) * grouped_heads(mixed, groups), axis=3
    )
    delta = jnp.transpose(delta, (1, 2, 0))[..., None]
    grad_probs = ein("tgha,sga->ghts", grad_grouped, values)
    grad_scores = (probs * (grad_probs - delta)).astype(BF16)
    score_scale = HEAD ** (-0.5)
    grad_query = (ein("ghts,sga->tgha", grad_scores, keys) * score_scale).reshape(rows, -1, HEAD)
    grad_key = ein("ghts,tgha->sga", grad_scores, grouped_heads(query, groups)) * score_scale
    grad_value = ein("ghts,tgha->sga", probs.astype(BF16), grad_grouped)
    count = kv_all.shape[0]
    grad_kv = jnp.concatenate(
        [grad_key.reshape(count, -1), grad_value.reshape(count, -1)], axis=1
    ).astype(BF16)
    return grad_query, grad_kv


def route_tables(routes_all, first_expert, local, capacity):
    experts = first_expert + jnp.arange(local, dtype=jnp.int32)
    named = jnp.any(routes_all[:, None] == experts[None, :, None, None], axis=3)
    rank = jnp.cumsum(named.astype(jnp.int32), axis=2) - 1
    slot = jnp.where(named, rank, -1)
    return (slot[:, :, None, :] == jnp.arange(capacity, dtype=jnp.int32)[None, None, :, None])


def pick_gates(moe_in, router, routes_now):
    logits = mm(moe_in, router)
    experts = jnp.arange(router.shape[1], dtype=jnp.int32)
    choose = (routes_now[:, :, None] == experts[None, None, :]).astype(F32)
    mix = jax.nn.softmax(jnp.sum(choose * logits[:, None, :], axis=2), axis=1)
    return choose, mix


def moe_forward(moe_in, router, routes_all, pick, first_expert, experts_w):
    gate_w, up_w, down_w = experts_w
    folds, local, capacity, rows = pick.shape
    width = moe_in.shape[1]
    blocks = jnp.stack(rel_gather(moe_in))
    low = pick.astype(BF16)
    flat = blocks.reshape(folds * rows, width)
    top = routes_all.shape[2]
    choose, mix = pick_gates(flat, router, routes_all.reshape(folds * rows, top))
    dense = jnp.sum(choose * mix[:, :, None], axis=1)
    mine = lax.dynamic_slice_in_dim(dense, first_expert, local, 1).reshape(folds, rows, local)
    gate_rows = jnp.sum(
        pick.astype(F32) * jnp.transpose(mine, (0, 2, 1))[:, :, None, :], axis=3
    )
    gate_rows = jnp.transpose(gate_rows, (1, 0, 2)).reshape(local, folds * capacity, 1)
    picked = ein("flct,ftd->lfcd", low, blocks).astype(BF16).reshape(local, folds * capacity, width)
    gate_pre = ein("lnd,ldf->lnf", picked, gate_w)
    up_pre = ein("lnd,ldf->lnf", picked, up_w)
    inner = gated(gate_pre, up_pre).astype(BF16)
    produced = ein("lnf,lfd->lnd", inner, down_w).astype(BF16)
    weighted = (produced.astype(F32) * gate_rows).astype(BF16)
    partial = ein(
        "flct,lfcd->ftd", low, weighted.reshape(local, folds, capacity, width)
    ).astype(BF16)
    summed = rel_scatter([partial[k] for k in range(folds)])
    kept = dict(
        picked=picked, gate_pre=gate_pre, up_pre=up_pre, produced=produced, gate_rows=gate_rows, low=low
    )
    return summed, kept


def moe_backward(grad_low, kept, experts_w, first_expert, expert_count):
    gate_w, up_w, down_w = experts_w
    low = kept["low"]
    folds, local, capacity, rows = low.shape
    width = grad_low.shape[1]
    blocks = jnp.stack(rel_gather(grad_low))
    picked = ein("flct,ftd->lfcd", low, blocks).reshape(local, folds * capacity, width)
    dots = jnp.sum(picked * kept["produced"].astype(F32), axis=2)
    grad_expert = (kept["gate_rows"] * picked).astype(BF16)
    grad_inner = ein("lnd,lfd->lnf", grad_expert, down_w)
    _, back = jax.vjp(gated, kept["gate_pre"], kept["up_pre"])
    grad_gate, grad_up = back(grad_inner)
    grad_gate, grad_up = grad_gate.astype(BF16), grad_up.astype(BF16)
    grad_rows = (
        ein("lnf,ldf->lnd", grad_gate, gate_w) + ein("lnf,ldf->lnd", grad_up, up_w)
    ).astype(BF16)
    partial = ein(
        "flct,lfcd->ftd", low, grad_rows.reshape(local, folds, capacity, width)
    ).astype(BF16)
    dots = dots.reshape(local, folds, capacity)
    dot_cols = jnp.einsum("flct,lfc->ftl", low.astype(F32), dots, precision=HIGHEST)
    pad = jnp.zeros((folds, rows, HEAD // 2), F32)
    dot_cols = lax.dynamic_update_slice(pad, dot_cols, (0, 0, first_expert))
    high = dot_cols.astype(BF16)
    rest = (dot_cols - high.astype(F32)).astype(BF16)
    packed = jnp.concatenate([partial, high, rest], axis=2)
    summed = rel_scatter([packed[k] for k in range(folds)])
    grad_dots = summed[:, width : width + HEAD // 2] + summed[:, width + HEAD // 2 :]
    return summed[:, :width], grad_dots[:, :expert_count], grad_expert


def layer_forward(layer_in, weights, experts_w, common, routes, pick):
    gains, w_qkv, w_out, router = weights
    groups = common["groups"]
    hidden = layer_in.astype(F32)
    kept = attention_in(hidden, gains[0], w_qkv, common, groups * HEAD)
    kv_all = jnp.concatenate(rel_gather(kept["kv"]), axis=0)
    mixed, probs = attend(kept["query"], kv_all, common["allowed"], groups)
    mixed_low = mixed.astype(BF16)
    residual = hidden + mm(mixed_low, w_out)
    scale_two = lax.rsqrt(jnp.mean(residual * residual, axis=1, keepdims=True) + EPS)
    normed_two = residual * scale_two
    moe_in = (normed_two * gains[1].astype(F32)).astype(BF16)
    choose, mix = pick_gates(moe_in, router, routes[0])
    summed, moe_kept = moe_forward(moe_in, router, routes, pick, common["first"], experts_w)
    out = (residual + summed).astype(BF16)
    kept.update(
        kv_all=kv_all, mixed=mixed, probs=probs, mixed_low=mixed_low, scale_two=scale_two,
        normed_two=normed_two, moe_in=moe_in, choose=choose, mix=mix, moe=moe_kept,
    )
    return out, kept


def layer_backward(grad_low, kept, weights, experts_w, common):
    gains, w_qkv, w_out, router = weights
    groups = common["groups"]
    grad_out = grad_low.astype(F32)
    rows = grad_out.shape[0]
    grad_moe_in, dots, grad_expert = moe_backward(
        grad_low, kept["moe"], experts_w, common["first"], router.shape[1]
    )
    mix, choose = kept["mix"], kept["choose"]
    grad_mix = jnp.sum(choose * dots[:, None, :], axis=2)
    grad_chosen = mix * (grad_mix - jnp.sum(mix * grad_mix, axis=1, keepdims=True))
    grad_logits = jnp.sum(choose * grad_chosen[:, :, None], axis=1)
    moe_in = kept["moe_in"]
    grad_router = jnp.dot(moe_in.astype(F32).T, grad_logits, precision=HIGHEST)
    grad_moe_in = grad_moe_in + jnp.dot(grad_logits, router.astype(F32).T, precision=HIGHEST)
    normed_two = kept["normed_two"]
    grad_norm = grad_moe_in * gains[1].astype(F32)
    grad_gain_two = jnp.sum(grad_moe_in * normed_two, axis=0)
    grad_mid = grad_out + kept["scale_two"] * (
        grad_norm - normed_two * jnp.mean(grad_norm * normed_two, axis=1, keepdims=True)
    )
    grad_attn = grad_mid.astype(BF16)
    grad_w_out = mm_tn(kept["mixed_low"], grad_attn)
    grad_mixed = mm_nt(grad_attn, w_out).astype(BF16)
    grad_query, grad_kv = attend_back(
        grad_mixed, kept["mixed"], kept["probs"], kept["query"], kept["kv_all"], groups
    )
    own = rel_scatter([grad_kv[k * rows : (k + 1) * rows] for k in range(lax.axis_size(F_AX))])
    cos, sin = common["cos"], common["sin"]
    kv_width = groups * HEAD
    grad_lin = jnp.concatenate(
        [
            rope_back(grad_query, cos, sin).reshape(rows, -1),
            rope_back(own[:, :kv_width].reshape(rows, -1, HEAD), cos, sin).reshape(rows, -1),
            own[:, kv_width:],
        ],
        axis=1,
    ).astype(BF16)
    grad_w_qkv = mm_tn(kept["attn_in"], grad_lin)
    grad_attn_in = mm_nt(grad_lin, w_qkv)
    normed = kept["normed"]
    grad_norm = grad_attn_in * gains[0].astype(F32)
    grad_gain_one = jnp.sum(grad_attn_in * normed, axis=0)
    grad_in = grad_mid + kept["scale"] * (
        grad_norm - normed * jnp.mean(grad_norm * normed, axis=1, keepdims=True)
    )
    small = jnp.concatenate(
        [grad_router, grad_gain_one[:, None], grad_gain_two[:, None]], axis=1
    )
    small = jnp.pad(small, ((0, 0), (0, HEAD - small.shape[1])))
    attn_grads = jnp.concatenate([grad_w_qkv, grad_w_out, small], axis=1).astype(BF16)
    return grad_in.astype(BF16), attn_grads, grad_expert


def expert_grads(rows_in, grad_rows, gate_w, up_w, down_w):
    gate_pre = mm(rows_in, gate_w)
    up_pre = mm(rows_in, up_w)
    inner, back = jax.vjp(gated, gate_pre, up_pre)
    grad_gate, grad_up = back(mm_nt(grad_rows, down_w))
    grad_gate, grad_up = grad_gate.astype(BF16), grad_up.astype(BF16)
    return (
        mm_tn(rows_in, grad_gate).astype(BF16),
        mm_tn(rows_in, grad_up).astype(BF16),
        mm_tn(inner.astype(BF16), grad_rows).astype(BF16),
    )


def body(
    tokens, cotangent, seq_lengths, routes, gains, w_query, w_key, w_value, w_out, w_router, w_gate, w_up, w_down
):
    section = lax.axis_index(S_AX)
    is_first = section == 0
    fold_id = lax.axis_index(F_AX)
    replica = lax.axis_index(R_AX)
    core = replica % 2
    folds, replicas = lax.axis_size(F_AX), lax.axis_size(R_AX)
    rows = tokens.shape[2]
    top = routes.shape[4]
    local = w_gate.shape[1]
    expert_count = w_router.shape[2]
    kv_width = w_key.shape[2]
    q_width = w_query.shape[2]
    capacity = rows * top // expert_count

    def own_batch(value):
        return lax.dynamic_index_in_dim(value, section, 0, keepdims=False)

    small = jnp.concatenate([w_router[0], gains[0].T], axis=1)
    small = jnp.pad(small, ((0, 0), (0, HEAD - small.shape[1])))
    first_part = jnp.concatenate([w_query[0], w_key[0], w_value[0], small], axis=1)
    share = first_part.shape[0] // replicas

    def spread(value):
        piece = lax.dynamic_slice_in_dim(value, replica * share, share, 0)
        full = lax.all_gather(piece, (S_AX, F_AX, R_AX), axis=0, tiled=True)
        return full.reshape(2, -1, value.shape[1])

    full_first = spread(first_part)
    full_out = spread(w_out[0])
    split = q_width + 2 * kv_width
    weights = []
    for layer in range(2):
        tail = full_first[layer, :, split:]
        weights.append(
            (
                tail[:, expert_count : expert_count + 2].T,
                full_first[layer, :, :split],
                full_out[layer],
                tail[:, :expert_count],
            )
        )

    def spread_expert(value):
        flat = value.reshape(replicas, -1, value.shape[-1])
        piece = lax.dynamic_index_in_dim(flat, replica, 0, keepdims=False)
        full = lax.all_gather(piece, (S_AX, R_AX), axis=0, tiled=True)
        return full.reshape((2,) + value.shape[1:])

    both_experts = [spread_expert(part) for part in (w_gate, w_up, w_down)]
    experts_w = [tuple(part[layer] for part in both_experts) for layer in range(2)]

    every = lax.all_gather(routes[0, :, 0].reshape(2, rows * top), (S_AX, F_AX), axis=0)
    every = every.reshape(2, folds, 2, rows, top)
    mine = lax.dynamic_index_in_dim(every, section, 2, keepdims=False)
    order = (fold_id - jnp.arange(folds)) % folds
    mine = jnp.take(mine, order, axis=1)
    first = fold_id * local
    picks = [route_tables(mine[layer], first, local, capacity) for layer in range(2)]

    lengths = own_batch(seq_lengths[:, 0])
    position = fold_id * rows + jnp.arange(rows, dtype=jnp.int32)
    key_pos = (order[:, None] * rows + jnp.arange(rows)[None, :]).reshape(-1).astype(jnp.int32)
    segment, offset = layout(lengths, position)
    key_seg, _ = layout(lengths, key_pos)
    freq = ROPE_BASE ** (-2.0 * jnp.arange(HEAD // 2, dtype=F32) / HEAD)
    angles = offset[:, None] * freq
    angles = jnp.concatenate([angles, angles], axis=1)[:, None, :]
    common = dict(
        cos=jnp.cos(angles), sin=jnp.sin(angles), groups=kv_width // HEAD, first=first,
        allowed=(segment[:, None] == key_seg[None, :]) & (key_pos[None, :] <= position[:, None]),
    )

    value = own_batch(tokens[:, 0])
    outs, kept = [], []
    for layer in range(2):
        value, state = layer_forward(
            value, weights[layer], experts_w[layer], common, mine[layer], picks[layer]
        )
        outs.append(value)
        kept.append(state)
    grad = own_batch(cotangent[:, 0])
    grads, attn_grads, expert_rows = [None, None], [None, None], [None, None]
    for layer in (1, 0):
        grad, attn_grads[layer], expert_rows[layer] = layer_backward(
            grad, kept[layer], weights[layer], experts_w[layer], common
        )
        grads[layer] = grad

    def own_layer(pair):
        return jnp.where(is_first, pair[0], pair[1])

    def other_layer(pair):
        return jnp.where(is_first, pair[1], pair[0])

    def by_section(keep, got):
        return jnp.stack([jnp.where(is_first, keep, got), jnp.where(is_first, got, keep)])

    def both_batches(pair):
        return by_section(own_layer(pair), swap_section(other_layer(pair)))

    half = local // 2

    def exchange(pair):
        chip = []
        for value in pair:
            keep = lax.dynamic_slice_in_dim(value, core * half, half, 0)
            give = lax.dynamic_slice_in_dim(value, (1 - core) * half, half, 0)
            got = swap_core(give)
            chip.append(
                jnp.concatenate(
                    [jnp.where(core == 0, keep, got), jnp.where(core == 0, got, keep)], axis=1
                )
            )
        batches = both_batches(chip)
        whole = all_chips(batches)
        return jnp.moveaxis(whole, 2, 0).reshape(half, -1, whole.shape[-1])

    x_rows = exchange([state["moe"]["picked"] for state in kept])
    g_rows = exchange(expert_rows)
    mine_w = [lax.dynamic_slice_in_dim(part[0], core * half, half, 0) for part in (w_gate, w_up, w_down)]
    made = [
        expert_grads(x_rows[i], g_rows[i], mine_w[0][i], mine_w[1][i], mine_w[2][i]) for i in range(half)
    ]
    expert_out = []
    for slot in range(3):
        keep = jnp.stack([one[slot] for one in made])
        got = swap_core(keep)
        both = jnp.concatenate(
            [jnp.where(core == 0, keep, got), jnp.where(core == 0, got, keep)], axis=0
        )
        expert_out.append(both.astype(F32)[None])

    shards = []
    for layer in range(2):
        piece = lax.psum_scatter(
            attn_grads[layer], (F_AX, S_AX, R_AX), scatter_dimension=0, tiled=True
        )
        shards.append(lax.all_gather(piece, (S_AX, R_AX), axis=0, tiled=True))
    shard = own_layer(shards).astype(F32)
    out_at = split + q_width
    small = shard[:, shard.shape[1] - HEAD :]
    layer_outputs = both_batches(outs)
    input_grads = both_batches(grads)
    return (
        layer_outputs[None, :, None],
        input_grads[None, :, None],
        small[:, expert_count : expert_count + 2].T[None],
        shard[None, :, :q_width],
        shard[None, :, q_width : q_width + kv_width],
        shard[None, :, q_width + kv_width : split],
        shard[None, :, split : shard.shape[1] - HEAD],
        small[None, :, :expert_count],
        expert_out[0],
        expert_out[1],
        expert_out[2],
    )


def solution(mesh):
    acts = P(None, R_AX, F_AX, None)
    rows = P(S_AX, F_AX, None)
    expert = P(S_AX, F_AX, None, None)
    stacked = P(S_AX, None, R_AX, F_AX, None)
    gain = P(S_AX, None, F_AX)
    return jax.shard_map(
        body,
        mesh=mesh,
        in_specs=(acts, acts, P(None, R_AX, None), stacked, gain)
        + (rows,) * 5
        + (expert,) * 3,
        out_specs=(stacked, stacked, gain) + (rows,) * 5 + (expert,) * 3,
        check_vma=False,
    )
```

profile of v0, /device:TPU:0, one launch (start us, length us, event | category | flops | bytes accessed | tf_op | source)
XLA Modules:
  0.0 1184.2 jit_solution(3947499780404765128)
XLA Ops:
  17.7 5.0 collective-permute-start.21
  24.1 48.1 %all_gather.26 = s32[8,2,512]{2,1,0:T(2,128)S(1)} all-gather(s32[1,2,512]{2,1,0:T(2,128)S(1)} %all_gather_reshape_squeeze.3), channel_id=1, replica_groups=mesh['section'=2,'fsdp'=4,'replica'=4] {'section','fsdp'}, dimensions={0}, use_global_device_ids=true | all-gather | bytes 36864 | tf_op jit(solution)/shard_map/all_gather | solution.py:371
  79.0 8.8 fusion.316
  87.8 45.8 %all-gather.24.cloned.1.call-done = bf16[1,3072,1536]{2,1,0:T(8,128)(2,1)} async-done(((bf16[1,384,1536]{2,1,0:T(8,128)(2,1)}), bf16[1,3072,1536]{2,1,0:T(8,128)(2,1)}) %all-gather.24.cloned.1.call-update) | async-done | bytes 9437200 | tf_op jit(solution)/shard_map/all_gather | solution.py:365
  133.6 8.1 fusion.317
  141.7 94.9 %all-gather.12.cloned.1.call-done = bf16[3072,2176]{1,0:T(8,128)(2,1)} async-done(((bf16[96,2176]{1,0:T(8,128)(2,1)}), bf16[3072,2176]{1,0:T(8,128)(2,1)}) %all-gather.12.cloned.1.call-update) | async-done | bytes 13369360 | tf_op jit(solution)/shard_map/all_gather | solution.py:344
  250.2 45.2 %all-gather.20.cloned.1.call-done = bf16[1,6144,768]{2,1,0:T(8,128)(2,1)} async-done(((bf16[1,768,768]{2,1,0:T(8,128)(2,1)}), bf16[1,6144,768]{2,1,0:T(8,128)(2,1)}) %all-gather.20.cloned.1.call-update) | async-done | bytes 9437200 | tf_op jit(solution)/shard_map/all_gather | solution.py:365
  295.4 8.1 fusion.315
  313.6 66.6 %all-gather.18.cloned.1.call-done = bf16[1,3072,1536]{2,1,0:T(8,128)(2,1)} async-done(((bf16[1,96,1536]{2,1,0:T(8,128)(2,1)}), bf16[1,3072,1536]{2,1,0:T(8,128)(2,1)}) %all-gather.18.cloned.1.call-update) | async-done | bytes 9437200 | tf_op jit(solution)/shard_map/all_gather | solution.py:344
  387.9 7.2 collective-permute-done.5
  395.1 26.0 %collective-permute-done.4 = bf16[128,1536]{1,0:T(8,128)(2,1)S(1)} collective-permute-done((bf16[128,1536]{1,0:T(8,128)(2,1)S(1)}, bf16[128,1536]{1,0:T(8,128)(2,1)S(1)}, u32[]{:S(2)}, u32[]{:S(2)}) %collective-permute-start.4) | collective-permute-done | bytes 393248 | tf_op jit(solution)/shard_map/ppermute | solution.py:36
  445.1 8.3 collective-permute-done.8
  453.4 14.9 %collective-permute-start.19 = (bf16[128,1536]{1,0:T(8,128)(2,1)}, bf16[128,1536]{1,0:T(8,128)(2,1)}, u32[]{:S(2)}, u32[]{:S(2)}) collective-permute-start(bf16[128,1536]{1,0:T(8,128)(2,1)} %get-tuple-element.182), channel_id=1, source_target_pairs={{0,4},{4,8},{8,12},{12,0},{1,5},{5,9},{9,13},{13,1},{2,6},{6,10},{... | collective-permute-start | bytes 1179656 | tf_op jit(solution)/shard_map/ppermute | solution.py:36
  482.1 9.4 collective-permute-start.11
  491.5 7.3 collective-permute-start.10
  502.7 7.2 collective-permute-done.10
  523.1 9.4 collective-permute-done.14
  532.4 21.0 %collective-permute-done.13 = bf16[128,1536]{1,0:T(8,128)(2,1)S(1)} collective-permute-done((bf16[128,1536]{1,0:T(8,128)(2,1)S(1)}, bf16[128,1536]{1,0:T(8,128)(2,1)S(1)}, u32[]{:S(2)}, u32[]{:S(2)}) %collective-permute-start.13) | collective-permute-done | bytes 393248 | tf_op jit(solution)/shard_map/ppermute | solution.py:36
  590.4 5.9 collective-permute-done.24
  596.3 15.0 %collective-permute-done.23 = bf16[128,1664]{1,0:T(8,128)(2,1)S(1)} collective-permute-done((bf16[128,1664]{1,0:T(8,128)(2,1)S(1)}, bf16[128,1664]{1,0:T(8,128)(2,1)S(1)}, u32[]{:S(2)}, u32[]{:S(2)}) %collective-permute-start.23) | collective-permute-done | bytes 426016 | tf_op jit(solution)/shard_map/ppermute | solution.py:44
  616.3 4.7 fusion.47
  631.5 11.6 collective-permute-start.27
  654.7 5.9 fusion.137
  660.7 4.6 convolution_convert_fusion
  665.5 9.6 fusion.5
  681.6 7.6 collective-permute-done.30
  689.2 26.5 %collective-permute-done.29 = bf16[128,1536]{1,0:T(8,128)(2,1)S(1)} collective-permute-done((bf16[128,1536]{1,0:T(8,128)(2,1)S(1)}, bf16[128,1536]{1,0:T(8,128)(2,1)S(1)}, u32[]{:S(2)}, u32[]{:S(2)}) %collective-permute-start.29) | collective-permute-done | bytes 393248 | tf_op jit(solution)/shard_map/ppermute | solution.py:36
  744.5 18.1 %collective-permute-done.33 = bf16[128,1664]{1,0:T(8,128)(2,1)S(1)} collective-permute-done((bf16[128,1664]{1,0:T(8,128)(2,1)S(1)}, bf16[128,1664]{1,0:T(8,128)(2,1)S(1)}, u32[]{:S(2)}, u32[]{:S(2)}) %collective-permute-start.33) | collective-permute-done | bytes 426016 | tf_op jit(solution)/shard_map/ppermute | solution.py:44
  762.6 26.6 %collective-permute-done.32 = bf16[128,1664]{1,0:T(8,128)(2,1)S(1)} collective-permute-done((bf16[128,1664]{1,0:T(8,128)(2,1)S(1)}, bf16[128,1664]{1,0:T(8,128)(2,1)S(1)}, u32[]{:S(2)}, u32[]{:S(2)}) %collective-permute-start.32) | collective-permute-done | bytes 426016 | tf_op jit(solution)/shard_map/ppermute | solution.py:44
  792.5 4.8 fusion.48
  802.8 10.3 collective-permute-start.36
  821.2 9.2 collective-permute-done.35
  830.6 6.0 fusion.127
  840.8 4.9 fusion.4
  849.6 7.5 collective-permute-start.17
  860.5 6.3 collective-permute-done.17
  866.8 15.9 %collective-permute-done.16 = bf16[128,1536]{1,0:T(8,128)(2,1)S(1)} collective-permute-done((bf16[128,1536]{1,0:T(8,128)(2,1)S(1)}, bf16[128,1536]{1,0:T(8,128)(2,1)S(1)}, u32[]{:S(2)}, u32[]{:S(2)}) %collective-permute-start.16) | collective-permute-done | bytes 393248 | tf_op jit(solution)/shard_map/ppermute | solution.py:44
  890.0 49.4 %collective-permute-done.40 = bf16[1,512,1536]{2,1,0:T(8,128)(2,1)S(1)} collective-permute-done((bf16[1,512,1536]{2,1,0:T(8,128)(2,1)S(1)}, bf16[1,512,1536]{2,1,0:T(8,128)(2,1)S(1)}, u32[]{:S(2)}, u32[]{:S(2)}) %collective-permute-start.40) | collective-permute-done | bytes 1572896 | tf_op jit(solution)/shard_map/ppermute | solution.py:50
  949.7 48.5 %collective-permute-done.44 = bf16[1,512,1536]{2,1,0:T(8,128)(2,1)S(1)} collective-permute-done((bf16[1,512,1536]{2,1,0:T(8,128)(2,1)S(1)}, bf16[1,512,1536]{2,1,0:T(8,128)(2,1)S(1)}, u32[]{:S(2)}, u32[]{:S(2)}) %collective-permute-start.44) | collective-permute-done | bytes 1572896 | tf_op jit(solution)/shard_map/ppermute | solution.py:50
  1006.0 23.4 %collective-permute-done.41 = bf16[2,1,512,1536]{3,2,1,0:T(8,128)(2,1)S(1)} collective-permute-done((bf16[2,1,512,1536]{3,2,1,0:T(8,128)(2,1)S(1)}, bf16[2,1,512,1536]{3,2,1,0:T(8,128)(2,1)S(1)}, u32[]{:S(2)}, u32[]{:S(2)}) %collective-permute-start.41) | collective-permute-done | bytes 3145760 | tf_op jit(solution)/shard_map/ppermute | solution.py:65
  1029.8 6.9 fusion.51
  1036.7 6.9 fusion.53
  1043.6 50.1 %collective-permute-done.45 = bf16[2,1,512,1536]{3,2,1,0:T(8,128)(2,1)S(1)} collective-permute-done((bf16[2,1,512,1536]{3,2,1,0:T(8,128)(2,1)S(1)}, bf16[2,1,512,1536]{3,2,1,0:T(8,128)(2,1)S(1)}, u32[]{:S(2)}, u32[]{:S(2)}) %collective-permute-start.45) | collective-permute-done | bytes 3145760 | tf_op jit(solution)/shard_map/ppermute | solution.py:65
  1096.0 8.1 fusion.55
  1104.1 12.9 %fusion.32 = bf16[1,1536,768]{2,1,0:T(8,128)(2,1)} fusion(bf16[2048,1536]{1,0:T(8,128)(2,1)S(1)} %bitcast.566, f32[2048,768]{1,0:T(8,128)} %fusion.51, f32[2048,768]{1,0:T(8,128)S(1)} %fusion.55, f32[2048,768]{1,0:T(8,128)} %fusion.53), kind=kOutput, calls=%fused_computation.78 | convolution fusion | flops 4866048000 | bytes 27525120 | tf_op jit(solution)/shard_map/dot_general | solution.py:25
  1116.9 7.1 fusion.35
  1124.6 10.4 fusion.42
  1153.2 16.6 %all-gather.14.cloned.1.call-done = bf16[384,3712]{1,0:T(8,128)(2,1)} async-done(((bf16[48,3712]{1,0:T(8,128)(2,1)}), bf16[384,3712]{1,0:T(8,128)(2,1)}) %all-gather.14.cloned.1.call-update) | async-done | bytes 2850832 | tf_op jit(solution)/shard_map/all_gather | solution.py:457
  (594 shorter events, 284.5 us)
Async XLA Ops:
  7.2 71.8 %all-gather.22.cloned.1.call-start = ((), (), s32[]{:S(2)}) async-start(), calls=%async_computation.9 | async-start | bytes 10616832 | tf_op jit(solution)/shard_map/all_gather | solution.py:365
  9.8 123.8 %all-gather.24.cloned.1.call-start = ((), (), s32[]{:S(2)}) async-start(), calls=%async_computation.10 | async-start | bytes 10616832 | tf_op jit(solution)/shard_map/all_gather | solution.py:365
  12.3 224.4 %all-gather.12.cloned.1.call-start = ((), (), s32[]{:S(2)}) async-start(), calls=%async_computation.2 | async-start | bytes 13787136 | tf_op jit(solution)/shard_map/all_gather | solution.py:344
  13.4 282.0 %all-gather.20.cloned.1.call-start = ((), (), s32[]{:S(2)}) async-start(), calls=%async_computation.8 | async-start | bytes 10616832 | tf_op jit(solution)/shard_map/all_gather | solution.py:365
  15.9 364.3 %all-gather.18.cloned.1.call-start = ((), (), s32[]{:S(2)}) async-start(), calls=%async_computation.7 | async-start | bytes 9732096 | tf_op jit(solution)/shard_map/all_gather | solution.py:344
  16.7 1079.0 %reduce-scatter.5.cloned.1.call-start = ((), (), s32[]{:S(2)}) async-start(), calls=%async_computation.5 | async-start | bytes 11759616 | tf_op jit(solution)/shard_map/reduce_scatter | solution.py:454
  17.7 481.1 %collective-permute-start.21 = (bf16[128,1536]{1,0:T(8,128)(2,1)}, bf16[128,1536]{1,0:T(8,128)(2,1)}, u32[]{:S(2)}, u32[]{:S(2)}) collective-permute-start(bf16[128,1536]{1,0:T(8,128)(2,1)} %get-tuple-element.182), channel_id=1, source_target_pairs={{0,12},{4,0},{8,4},{12,8},{1,13},{5,1},{9,5},{13,9},{2,14},{6,2},{... | collective-permute-start | bytes 1179656 | tf_op jit(solution)/shard_map/ppermute | solution.py:36
  22.8 476.0 %collective-permute-start.20 = (bf16[128,1536]{1,0:T(8,128)(2,1)}, bf16[128,1536]{1,0:T(8,128)(2,1)}, u32[]{:S(2)}, u32[]{:S(2)}) collective-permute-start(bf16[128,1536]{1,0:T(8,128)(2,1)} %get-tuple-element.182), channel_id=1, source_target_pairs={{0,8},{4,12},{8,0},{12,4},{1,9},{5,13},{9,1},{13,5},{2,10},{6,14},... | collective-permute-start | bytes 1179656 | tf_op jit(solution)/shard_map/ppermute | solution.py:36
  246.6 58.1 %collective-permute-start.2 = (bf16[128,512]{1,0:T(8,128)(2,1)S(1)}, bf16[128,512]{1,0:T(8,128)(2,1)S(1)}, u32[]{:S(2)}, u32[]{:S(2)}) collective-permute-start(bf16[128,512]{1,0:T(8,128)(2,1)S(1)} %pad_maximum_fusion.20), channel_id=1, source_target_pairs={{0,12},{4,0},{8,4},{12,8},{1,13},{5,1},{9,5},{13,9},{2,14},{6,2},{... | collective-permute-start | bytes 393224 | tf_op jit(solution)/shard_map/ppermute | solution.py:36
  248.1 56.6 %collective-permute-start.1 = (bf16[128,512]{1,0:T(8,128)(2,1)S(1)}, bf16[128,512]{1,0:T(8,128)(2,1)S(1)}, u32[]{:S(2)}, u32[]{:S(2)}) collective-permute-start(bf16[128,512]{1,0:T(8,128)(2,1)S(1)} %pad_maximum_fusion.20), channel_id=1, source_target_pairs={{0,8},{4,12},{8,0},{12,4},{1,9},{5,13},{9,1},{13,5},{2,10},{6,14},... | collective-permute-start | bytes 393224 | tf_op jit(solution)/shard_map/ppermute | solution.py:36
  248.8 55.9 %collective-permute-start = (bf16[128,512]{1,0:T(8,128)(2,1)S(1)}, bf16[128,512]{1,0:T(8,128)(2,1)S(1)}, u32[]{:S(2)}, u32[]{:S(2)}) collective-permute-start(bf16[128,512]{1,0:T(8,128)(2,1)S(1)} %pad_maximum_fusion.20), channel_id=1, source_target_pairs={{0,4},{4,8},{8,12},{12,0},{1,5},{5,9},{9,13},{13,1},{2,6},{6,10},{... | collective-permute-start | bytes 393224 | tf_op jit(solution)/shard_map/ppermute | solution.py:36
  385.5 35.6 %collective-permute-start.4 = (bf16[128,1536]{1,0:T(8,128)(2,1)S(1)}, bf16[128,1536]{1,0:T(8,128)(2,1)S(1)}, u32[]{:S(2)}, u32[]{:S(2)}) collective-permute-start(bf16[128,1536]{1,0:T(8,128)(2,1)S(1)} %multiply_convert_fusion.17), channel_id=1, source_target_pairs={{0,8},{4,12},{8,0},{12,4},{1,9},{5,13},{9,1},{13,5},{2,10},{6,14},... | collective-permute-start | bytes 1179656 | tf_op jit(solution)/shard_map/ppermute | solution.py:36
  386.6 34.5 %collective-permute-start.3 = (bf16[128,1536]{1,0:T(8,128)(2,1)S(1)}, bf16[128,1536]{1,0:T(8,128)(2,1)S(1)}, u32[]{:S(2)}, u32[]{:S(2)}) collective-permute-start(bf16[128,1536]{1,0:T(8,128)(2,1)S(1)} %multiply_convert_fusion.17), channel_id=1, source_target_pairs={{0,4},{4,8},{8,12},{12,0},{1,5},{5,9},{9,13},{13,1},{2,6},{6,10},{... | collective-permute-start | bytes 1179656 | tf_op jit(solution)/shard_map/ppermute | solution.py:36
  439.5 30.8 %collective-permute-start.7 = (bf16[128,1536]{1,0:T(8,128)(2,1)S(1)}, bf16[128,1536]{1,0:T(8,128)(2,1)S(1)}, u32[]{:S(2)}, u32[]{:S(2)}) collective-permute-start(bf16[128,1536]{1,0:T(8,128)(2,1)S(1)} %get-tuple-element.164), channel_id=1, source_target_pairs={{0,8},{4,12},{8,0},{12,4},{1,9},{5,13},{9,1},{13,5},{2,10},{6,14},... | collective-permute-start | bytes 1179656 | tf_op jit(solution)/shard_map/ppermute | solution.py:44
  441.5 28.8 %collective-permute-start.6 = (bf16[128,1536]{1,0:T(8,128)(2,1)S(1)}, bf16[128,1536]{1,0:T(8,128)(2,1)S(1)}, u32[]{:S(2)}, u32[]{:S(2)}) collective-permute-start(bf16[128,1536]{1,0:T(8,128)(2,1)S(1)} %get-tuple-element.162), channel_id=1, source_target_pairs={{0,12},{4,0},{8,4},{12,8},{1,13},{5,1},{9,5},{13,9},{2,14},{6,2},{... | collective-permute-start | bytes 1179656 | tf_op jit(solution)/shard_map/ppermute | solution.py:44
  453.4 45.4 %collective-permute-start.19 = (bf16[128,1536]{1,0:T(8,128)(2,1)}, bf16[128,1536]{1,0:T(8,128)(2,1)}, u32[]{:S(2)}, u32[]{:S(2)}) collective-permute-start(bf16[128,1536]{1,0:T(8,128)(2,1)} %get-tuple-element.182), channel_id=1, source_target_pairs={{0,4},{4,8},{8,12},{12,0},{1,5},{5,9},{9,13},{13,1},{2,6},{6,10},{... | collective-permute-start | bytes 1179656 | tf_op jit(solution)/shard_map/ppermute | solution.py:36
  482.1 20.6 %collective-permute-start.11 = (bf16[128,512]{1,0:T(8,128)(2,1)S(1)}, bf16[128,512]{1,0:T(8,128)(2,1)S(1)}, u32[]{:S(2)}, u32[]{:S(2)}) collective-permute-start(bf16[128,512]{1,0:T(8,128)(2,1)S(1)} %pad_maximum_fusion.21), channel_id=1, source_target_pairs={{0,12},{4,0},{8,4},{12,8},{1,13},{5,1},{9,5},{13,9},{2,14},{6,2},{... | collective-permute-start | bytes 393224 | tf_op jit(solution)/shard_map/ppermute | solution.py:36
  491.5 18.5 %collective-permute-start.10 = (bf16[128,512]{1,0:T(8,128)(2,1)S(1)}, bf16[128,512]{1,0:T(8,128)(2,1)S(1)}, u32[]{:S(2)}, u32[]{:S(2)}) collective-permute-start(bf16[128,512]{1,0:T(8,128)(2,1)S(1)} %pad_maximum_fusion.21), channel_id=1, source_target_pairs={{0,8},{4,12},{8,0},{12,4},{1,9},{5,13},{9,1},{13,5},{2,10},{6,14},... | collective-permute-start | bytes 393224 | tf_op jit(solution)/shard_map/ppermute | solution.py:36
  520.5 32.9 %collective-permute-start.13 = (bf16[128,1536]{1,0:T(8,128)(2,1)S(1)}, bf16[128,1536]{1,0:T(8,128)(2,1)S(1)}, u32[]{:S(2)}, u32[]{:S(2)}) collective-permute-start(bf16[128,1536]{1,0:T(8,128)(2,1)S(1)} %multiply_convert_fusion.16), channel_id=1, source_target_pairs={{0,8},{4,12},{8,0},{12,4},{1,9},{5,13},{9,1},{13,5},{2,10},{6,14},... | collective-permute-start | bytes 1179656 | tf_op jit(solution)/shard_map/ppermute | solution.py:36
  521.0 32.4 %collective-permute-start.12 = (bf16[128,1536]{1,0:T(8,128)(2,1)S(1)}, bf16[128,1536]{1,0:T(8,128)(2,1)S(1)}, u32[]{:S(2)}, u32[]{:S(2)}) collective-permute-start(bf16[128,1536]{1,0:T(8,128)(2,1)S(1)} %multiply_convert_fusion.16), channel_id=1, source_target_pairs={{0,4},{4,8},{8,12},{12,0},{1,5},{5,9},{9,13},{13,1},{2,6},{6,10},{... | collective-permute-start | bytes 1179656 | tf_op jit(solution)/shard_map/ppermute | solution.py:36
  584.5 26.8 %collective-permute-start.23 = (bf16[128,1664]{1,0:T(8,128)(2,1)S(1)}, bf16[128,1664]{1,0:T(8,128)(2,1)S(1)}, u32[]{:S(2)}, u32[]{:S(2)}) collective-permute-start(bf16[128,1664]{1,0:T(8,128)(2,1)S(1)} %get-tuple-element.157), channel_id=1, source_target_pairs={{0,8},{4,12},{8,0},{12,4},{1,9},{5,13},{9,1},{13,5},{2,10},{6,14},... | collective-permute-start | bytes 1277960 | tf_op jit(solution)/shard_map/ppermute | solution.py:44
  586.5 25.5 %collective-permute-start.22 = (bf16[128,1664]{1,0:T(8,128)(2,1)S(1)}, bf16[128,1664]{1,0:T(8,128)(2,1)S(1)}, u32[]{:S(2)}, u32[]{:S(2)}) collective-permute-start(bf16[128,1664]{1,0:T(8,128)(2,1)S(1)} %get-tuple-element.155), channel_id=1, source_target_pairs={{0,12},{4,0},{8,4},{12,8},{1,13},{5,1},{9,5},{13,9},{2,14},{6,2},{... | collective-permute-start | bytes 1277960 | tf_op jit(solution)/shard_map/ppermute | solution.py:44
  631.5 19.0 %collective-permute-start.27 = (bf16[128,512]{0,1:T(8,128)(2,1)S(1)}, bf16[128,512]{0,1:T(8,128)(2,1)S(1)}, u32[]{:S(2)}, u32[]{:S(2)}) collective-permute-start(bf16[128,512]{0,1:T(8,128)(2,1)S(1)} %get-tuple-element.187), channel_id=1, source_target_pairs={{0,4},{4,8},{8,12},{12,0},{1,5},{5,9},{9,13},{13,1},{2,6},{6,10},{... | collective-permute-start | bytes 393224 | tf_op jit(solution)/shard_map/ppermute | solution.py:44
  675.2 449.4 %reduce-scatter.3.cloned.1.call-start = ((), (), s32[]{:S(2)}) async-start(), calls=%async_computation.3 | async-start | bytes 11759616 | tf_op jit(solution)/shard_map/reduce_scatter | solution.py:454
  679.3 36.3 %collective-permute-start.29 = (bf16[128,1536]{1,0:T(8,128)(2,1)S(1)}, bf16[128,1536]{1,0:T(8,128)(2,1)S(1)}, u32[]{:S(2)}, u32[]{:S(2)}) collective-permute-start(bf16[128,1536]{1,0:T(8,128)(2,1)S(1)} %fusion.136), channel_id=1, source_target_pairs={{0,8},{4,12},{8,0},{12,4},{1,9},{5,13},{9,1},{13,5},{2,10},{6,14},... | collective-permute-start | bytes 1179656 | tf_op jit(solution)/shard_map/ppermute | solution.py:36
  681.3 34.3 %collective-permute-start.28 = (bf16[128,1536]{1,0:T(8,128)(2,1)S(1)}, bf16[128,1536]{1,0:T(8,128)(2,1)}, u32[]{:S(2)}, u32[]{:S(2)}) collective-permute-start(bf16[128,1536]{1,0:T(8,128)(2,1)S(1)} %fusion.136), channel_id=1, source_target_pairs={{0,4},{4,8},{8,12},{12,0},{1,5},{5,9},{9,13},{13,1},{2,6},{6,10},{... | collective-permute-start | bytes 1179656 | tf_op jit(solution)/shard_map/ppermute | solution.py:36
  738.7 23.9 %collective-permute-start.33 = (bf16[128,1664]{1,0:T(8,128)(2,1)S(1)}, bf16[128,1664]{1,0:T(8,128)(2,1)S(1)}, u32[]{:S(2)}, u32[]{:S(2)}) collective-permute-start(bf16[128,1664]{1,0:T(8,128)(2,1)S(1)} %get-tuple-element.153), channel_id=1, source_target_pairs={{0,4},{4,8},{8,12},{12,0},{1,5},{5,9},{9,13},{13,1},{2,6},{6,10},{... | collective-permute-start | bytes 1277960 | tf_op jit(solution)/shard_map/ppermute | solution.py:44
  738.8 50.4 %collective-permute-start.32 = (bf16[128,1664]{1,0:T(8,128)(2,1)S(1)}, bf16[128,1664]{1,0:T(8,128)(2,1)S(1)}, u32[]{:S(2)}, u32[]{:S(2)}) collective-permute-start(bf16[128,1664]{1,0:T(8,128)(2,1)S(1)} %get-tuple-element.154), channel_id=1, source_target_pairs={{0,8},{4,12},{8,0},{12,4},{1,9},{5,13},{9,1},{13,5},{2,10},{6,14},... | collective-permute-start | bytes 1277960 | tf_op jit(solution)/shard_map/ppermute | solution.py:44
  739.5 49.7 %collective-permute-start.31 = (bf16[128,1664]{1,0:T(8,128)(2,1)S(1)}, bf16[128,1664]{1,0:T(8,128)(2,1)S(1)}, u32[]{:S(2)}, u32[]{:S(2)}) collective-permute-start(bf16[128,1664]{1,0:T(8,128)(2,1)S(1)} %get-tuple-element.152), channel_id=1, source_target_pairs={{0,12},{4,0},{8,4},{12,8},{1,13},{5,1},{9,5},{13,9},{2,14},{6,2},{... | collective-permute-start | bytes 1277960 | tf_op jit(solution)/shard_map/ppermute | solution.py:44
  744.5 101.3 %collective-permute-start.38 = (bf16[1,256,1536]{2,1,0:T(8,128)(2,1)}, bf16[1,256,1536]{2,1,0:T(8,128)(2,1)}, u32[]{:S(2)}, u32[]{:S(2)}) collective-permute-start(bf16[1,256,1536]{2,1,0:T(8,128)(2,1)} %constant_dynamic-slice_fusion.3), channel_id=1, source_target_pairs={{0,1},{1,0},{2,3},{3,2},{4,5},{5,4},{6,7},{7,6},{8,9},{9,8},{10,11... | collective-permute-start | bytes 2359304 | tf_op jit(solution)/shard_map/ppermute | solution.py:55
  802.8 18.4 %collective-permute-start.36 = (bf16[128,512]{0,1:T(8,128)(2,1)S(1)}, bf16[128,512]{0,1:T(8,128)(2,1)S(1)}, u32[]{:S(2)}, u32[]{:S(2)}) collective-permute-start(bf16[128,512]{0,1:T(8,128)(2,1)S(1)} %get-tuple-element.184), channel_id=1, source_target_pairs={{0,4},{4,8},{8,12},{12,0},{1,5},{5,9},{9,13},{13,1},{2,6},{6,10},{... | collective-permute-start | bytes 393224 | tf_op jit(solution)/shard_map/ppermute | solution.py:44
  813.1 17.2 %collective-permute-start.35 = (bf16[128,512]{0,1:T(8,128)(2,1)S(1)}, bf16[128,512]{0,1:T(8,128)(2,1)S(1)}, u32[]{:S(2)}, u32[]{:S(2)}) collective-permute-start(bf16[128,512]{0,1:T(8,128)(2,1)S(1)} %get-tuple-element.185), channel_id=1, source_target_pairs={{0,8},{4,12},{8,0},{12,4},{1,9},{5,13},{9,1},{13,5},{2,10},{6,14},... | collective-permute-start | bytes 393224 | tf_op jit(solution)/shard_map/ppermute | solution.py:44
  813.9 16.5 %collective-permute-start.34 = (bf16[128,512]{0,1:T(8,128)(2,1)S(1)}, bf16[128,512]{0,1:T(8,128)(2,1)S(1)}, u32[]{:S(2)}, u32[]{:S(2)}) collective-permute-start(bf16[128,512]{0,1:T(8,128)(2,1)S(1)} %get-tuple-element.183), channel_id=1, source_target_pairs={{0,12},{4,0},{8,4},{12,8},{1,13},{5,1},{9,5},{13,9},{2,14},{6,2},{... | collective-permute-start | bytes 393224 | tf_op jit(solution)/shard_map/ppermute | solution.py:44
  845.8 307.4 %all-gather.16.cloned.1.call-start = ((), (), s32[]{:S(2)}) async-start(), calls=%async_computation.6 | async-start | bytes 3207168 | tf_op jit(solution)/shard_map/all_gather | solution.py:457
  849.6 17.2 %collective-permute-start.17 = (bf16[128,1536]{1,0:T(8,128)(2,1)S(1)}, bf16[128,1536]{1,0:T(8,128)(2,1)S(1)}, u32[]{:S(2)}, u32[]{:S(2)}) collective-permute-start(bf16[128,1536]{1,0:T(8,128)(2,1)S(1)} %get-tuple-element.160), channel_id=1, source_target_pairs={{0,4},{4,8},{8,12},{12,0},{1,5},{5,9},{9,13},{13,1},{2,6},{6,10},{... | collective-permute-start | bytes 1179656 | tf_op jit(solution)/shard_map/ppermute | solution.py:44
  857.2 25.6 %collective-permute-start.16 = (bf16[128,1536]{1,0:T(8,128)(2,1)S(1)}, bf16[128,1536]{1,0:T(8,128)(2,1)S(1)}, u32[]{:S(2)}, u32[]{:S(2)}) collective-permute-start(bf16[128,1536]{1,0:T(8,128)(2,1)S(1)} %get-tuple-element.161), channel_id=1, source_target_pairs={{0,8},{4,12},{8,0},{12,4},{1,9},{5,13},{9,1},{13,5},{2,10},{6,14},... | collective-permute-start | bytes 1179656 | tf_op jit(solution)/shard_map/ppermute | solution.py:44
  857.4 25.4 %collective-permute-start.15 = (bf16[128,1536]{1,0:T(8,128)(2,1)S(1)}, bf16[128,1536]{1,0:T(8,128)(2,1)S(1)}, u32[]{:S(2)}, u32[]{:S(2)}) collective-permute-start(bf16[128,1536]{1,0:T(8,128)(2,1)S(1)} %get-tuple-element.159), channel_id=1, source_target_pairs={{0,12},{4,0},{8,4},{12,8},{1,13},{5,1},{9,5},{13,9},{2,14},{6,2},{... | collective-permute-start | bytes 1179656 | tf_op jit(solution)/shard_map/ppermute | solution.py:44
  859.8 25.7 %collective-permute-start.39 = (bf16[1,256,1536]{2,1,0:T(8,128)(2,1)S(1)}, bf16[1,256,1536]{2,1,0:T(8,128)(2,1)S(1)}, u32[]{:S(2)}, u32[]{:S(2)}) collective-permute-start(bf16[1,256,1536]{2,1,0:T(8,128)(2,1)S(1)} %constant_dynamic-slice_fusion.2), channel_id=1, source_target_pairs={{0,1},{1,0},{2,3},{3,2},{4,5},{5,4},{6,7},{7,6},{8,9},{9,8},{10,11... | collective-permute-start | bytes 2359304 | tf_op jit(solution)/shard_map/ppermute | solution.py:55
  860.0 27.3 %collective-permute-start.43 = (bf16[1,256,1536]{2,1,0:T(8,128)(2,1)S(1)}, bf16[1,256,1536]{2,1,0:T(8,128)(2,1)S(1)}, u32[]{:S(2)}, u32[]{:S(2)}) collective-permute-start(bf16[1,256,1536]{2,1,0:T(8,128)(2,1)S(1)} %constant_dynamic-slice_fusion), channel_id=1, source_target_pairs={{0,1},{1,0},{2,3},{3,2},{4,5},{5,4},{6,7},{7,6},{8,9},{9,8},{10,11... | collective-permute-start | bytes 2359304 | tf_op jit(solution)/shard_map/ppermute | solution.py:55
  883.1 61.5 %collective-permute-start.18 = (bf16[128,1536]{1,0:T(8,128)(2,1)S(1)}, bf16[128,1536]{1,0:T(8,128)(2,1)S(1)}, u32[]{:S(2)}, u32[]{:S(2)}) collective-permute-start(bf16[128,1536]{1,0:T(8,128)(2,1)S(1)} %get-tuple-element.114), channel_id=1, source_target_pairs={{0,16},{16,0},{1,17},{17,1},{2,18},{18,2},{3,19},{19,3},{4,20},{20... | collective-permute-start | bytes 1179656 | tf_op jit(solution)/shard_map/ppermute | solution.py:50
  886.1 53.2 %collective-permute-start.40 = (bf16[1,512,1536]{2,1,0:T(8,128)(2,1)S(1)}, bf16[1,512,1536]{2,1,0:T(8,128)(2,1)S(1)}, u32[]{:S(2)}, u32[]{:S(2)}) collective-permute-start(bf16[1,512,1536]{2,1,0:T(8,128)(2,1)S(1)} %broadcast_select_fusion.2), channel_id=1, source_target_pairs={{0,16},{16,0},{1,17},{17,1},{2,18},{18,2},{3,19},{19,3},{4,20},{20... | collective-permute-start | bytes 4718600 | tf_op jit(solution)/shard_map/ppermute | solution.py:50
  888.3 59.5 %collective-permute-start.37 = (bf16[128,1536]{1,0:T(8,128)(2,1)S(1)}, bf16[128,1536]{1,0:T(8,128)(2,1)S(1)}, u32[]{:S(2)}, u32[]{:S(2)}) collective-permute-start(bf16[128,1536]{1,0:T(8,128)(2,1)S(1)} %get-tuple-element.108), channel_id=1, source_target_pairs={{0,16},{16,0},{1,17},{17,1},{2,18},{18,2},{3,19},{19,3},{4,20},{20... | collective-permute-start | bytes 1179656 | tf_op jit(solution)/shard_map/ppermute | solution.py:50
  940.5 88.9 %collective-permute-start.41 = (bf16[2,1,512,1536]{3,2,1,0:T(8,128)(2,1)S(1)}, bf16[2,1,512,1536]{3,2,1,0:T(8,128)(2,1)S(1)}, u32[]{:S(2)}, u32[]{:S(2)}) collective-permute-start(bf16[2,1,512,1536]{3,2,1,0:T(8,128)(2,1)S(1)} %pad_maximum_fusion), channel_id=1, source_target_pairs={{0,2},{1,3},{2,0},{3,1},{4,6},{5,7},{6,4},{7,5},{8,10},{9,11},{10,... | collective-permute-start | bytes 9437192 | tf_op jit(solution)/shard_map/ppermute | solution.py:65
  942.5 55.7 %collective-permute-start.44 = (bf16[1,512,1536]{2,1,0:T(8,128)(2,1)S(1)}, bf16[1,512,1536]{2,1,0:T(8,128)(2,1)S(1)}, u32[]{:S(2)}, u32[]{:S(2)}) collective-permute-start(bf16[1,512,1536]{2,1,0:T(8,128)(2,1)S(1)} %broadcast_select_fusion), channel_id=1, source_target_pairs={{0,16},{16,0},{1,17},{17,1},{2,18},{18,2},{3,19},{19,3},{4,20},{20... | collective-permute-start | bytes 4718600 | tf_op jit(solution)/shard_map/ppermute | solution.py:50
  999.2 94.6 %collective-permute-start.45 = (bf16[2,1,512,1536]{3,2,1,0:T(8,128)(2,1)S(1)}, bf16[2,1,512,1536]{3,2,1,0:T(8,128)(2,1)S(1)}, u32[]{:S(2)}, u32[]{:S(2)}) collective-permute-start(bf16[2,1,512,1536]{3,2,1,0:T(8,128)(2,1)S(1)} %pad_maximum_fusion.1), channel_id=1, source_target_pairs={{0,2},{1,3},{2,0},{3,1},{4,6},{5,7},{6,4},{7,5},{8,10},{9,11},{10,... | collective-permute-start | bytes 9437192 | tf_op jit(solution)/shard_map/ppermute | solution.py:65
  1095.7 74.0 %all-gather.14.cloned.1.call-start = ((), (), s32[]{:S(2)}) async-start(), calls=%async_computation.4 | async-start | bytes 3207168 | tf_op jit(solution)/shard_map/all_gather | solution.py:457
  1116.9 18.2 %collective-permute-start.46 = (bf16[1,1536,768]{2,1,0:T(8,128)(2,1)}, bf16[1,1536,768]{2,1,0:T(8,128)(2,1)}, u32[]{:S(2)}, u32[]{:S(2)}) collective-permute-start(bf16[1,1536,768]{2,1,0:T(8,128)(2,1)} %fusion.32), channel_id=1, source_target_pairs={{0,1},{1,0},{2,3},{3,2},{4,5},{5,4},{6,7},{7,6},{8,9},{9,8},{10,11... | collective-permute-start | bytes 7077896 | tf_op jit(solution)/shard_map/ppermute | solution.py:55
  1124.1 18.1 %collective-permute-start.47 = (bf16[1,1536,768]{2,1,0:T(8,128)(2,1)}, bf16[1,1536,768]{2,1,0:T(8,128)(2,1)S(1)}, u32[]{:S(2)}, u32[]{:S(2)}) collective-permute-start(bf16[1,1536,768]{2,1,0:T(8,128)(2,1)} %fusion.35), channel_id=1, source_target_pairs={{0,1},{1,0},{2,3},{3,2},{4,5},{5,4},{6,7},{7,6},{8,9},{9,8},{10,11... | collective-permute-start | bytes 7077896 | tf_op jit(solution)/shard_map/ppermute | solution.py:55
  (110 other events, 1450.7 us)
Sparse Core Ops, SparseCore 0:
  10.5 61.7 all-gather.21
  74.7 58.8 all-gather.23
  137.1 99.5 all-gather.11
  238.4 56.9 all-gather.19
  298.1 81.9 all-gather.17
  675.3 182.3 reduce-scatter.4
  863.7 174.5 reduce-scatter.2
  1095.8 38.7 all-gather.15
  1136.5 33.2 all-gather.13
where the time goes:
time: 1190 us; the launch traced here: 1180 us
  waiting for transfers between devices  663 us (56%)
  matrix products  177 us (15%)
  starting transfers between devices  116 us (10%)
  local copies, waits for them, and re-layouts  91 us (8%)
  other arithmetic  70.9 us (6%)
  blocking collectives  48.1 us (4%)
  between operations  16.9 us (1%)
    all_gather x2, waiting for transfers between devices, spread(): full = lax.all_gather(piece, (S_AX, F_AX, R_AX), axis=0, tiled=True)  162 us
    ppermute x18, waiting for transfers between devices, rel_scatter(): lax.ppermute(parts[k], F_AX, [(i, (i - k) % folds) for i in range(folds)])  115 us
    ppermute x18, waiting for transfers between devices, rel_gather(): lax.ppermute(value, F_AX, [(i, (i + k) % folds) for i in range(folds)])  105 us
    ppermute x4, waiting for transfers between devices, swap_section(): return lax.ppermute(value, S_AX, [(0, 1), (1, 0)])  100 us
    all_gather x3, waiting for transfers between devices, spread_expert(): full = lax.all_gather(piece, (S_AX, R_AX), axis=0, tiled=True)  91 us
    ppermute x2, waiting for transfers between devices, all_chips(): got = lax.ppermute(value, R_AX, pairs)  73.5 us
    dot_general x30, matrix products, ein(): return jnp.einsum(spec, a, b, preferred_element_type=F32)  59.8 us
    ppermute x18, starting transfers between devices, rel_scatter(): lax.ppermute(parts[k], F_AX, [(i, (i - k) % folds) for i in range(folds)])  54.4 us
  transfers between devices with their start and end apart: 58, of which 31 were waited for; matrix products, arithmetic and copies ran while one was open for 20% of the time, Pallas kernels for 0%

commit v1 on v0

v1 whole, which is shorter than its diff:
```python
import functools

import jax
import jax.numpy as jnp
from jax import lax
from jax.experimental import pallas as pl
from jax.experimental.pallas import tpu as pltpu
from jax.sharding import PartitionSpec as P

HEAD = 128
ROPE_BASE = 1000000.0
EPS = 1e-06
MASKED = -1e30
F32 = jnp.float32
BF16 = jnp.bfloat16
S_AX, F_AX, R_AX = "section", "fsdp", "replica"
HIGHEST = lax.Precision.HIGHEST
LANES = 128
GELU_C = 0.7978845608028654
GELU_A = 0.044715


def dot(a, b):
    return lax.dot_general(a, b, (((1,), (0,)), ((), ())), preferred_element_type=F32)


def dot_nt(a, b):
    return lax.dot_general(a, b, (((1,), (1,)), ((), ())), preferred_element_type=F32)


def dot_tn(a, b):
    return lax.dot_general(a, b, (((0,), (0,)), ((), ())), preferred_element_type=F32)


def gelu_parts(x):
    t = jnp.tanh(GELU_C * (x + GELU_A * x * x * x))
    value = 0.5 * x * (1.0 + t)
    slope = 0.5 * (1.0 + t) + 0.5 * x * (1.0 - t * t) * GELU_C * (1.0 + 3.0 * GELU_A * x * x)
    return value, slope


def lane_is(shape, number):
    return lax.broadcasted_iota(jnp.int32, shape, 1) == number


def masked_mix(logits, mask):
    kept = jnp.where(mask > 0.0, logits, -1e30)
    expo = jnp.exp(kept - jnp.max(kept, axis=1, keepdims=True)) * mask
    return expo / jnp.sum(expo, axis=1, keepdims=True)


def one_hot(slots_ref, block, step, capacity):
    rows = slots_ref.shape[2]
    place = lax.broadcasted_iota(jnp.int32, (capacity, rows), 0)
    return place == slots_ref[block, step : step + 1, :]


def weight_copies(scalars, own, pieces, buffers, sems):
    own_g, own_u, own_d = own
    parts = len(pieces[0][0])
    ff = own_g.shape[2] // parts
    is_own, flip = scalars[0], scalars[1]
    waits = {}
    for step in range(len(pieces[0])):
        for part in range(parts):
            expert = step ^ flip
            cols = pl.ds(part * ff, ff)
            sources = (own_g.at[expert, :, cols], own_u.at[expert, :, cols], own_d.at[expert, cols, :])
            for kind in range(3):
                target = buffers[kind].at[step, part]
                sem = sems.at[kind, step, part]

                @pl.when(is_own == 1)
                def _(source=sources[kind], target=target, sem=sem):
                    pltpu.make_async_copy(source, target, sem).start()

                @pl.when(is_own == 0)
                def _(source=pieces[kind][step][part], target=target, sem=sem):
                    pltpu.make_async_copy(source, target, sem).start()

                waits[kind, step, part] = pltpu.make_async_copy(
                    pieces[kind][step][part], target, sem
                )
    return waits


def split_refs(refs, counts):
    out, at = [], 0
    for count in counts:
        out.append(refs[at : at + count])
        at += count
    return out


def moe_fwd_kernel(folds, local, parts, capacity, *refs):
    (scalars, slots, mask, router), blocks, own, flat, outs, partials, scratch = split_refs(
        refs, (4, folds, 3, 3 * local * parts, 5, folds, 4)
    )
    scalars_ref = scalars
    picked_ref, gate_ref, up_ref, made_ref, grows_ref = outs
    buf_g, buf_u, buf_d, sems = scratch
    pieces = [
        [[flat[(kind * local + step) * parts + part] for part in range(parts)] for step in range(local)]
        for kind in range(3)
    ]
    waits = weight_copies(scalars_ref, own, pieces, (buf_g, buf_u, buf_d), sems)
    rows = blocks[0].shape[0]
    width = blocks[0].shape[1]
    ff = buf_g.shape[3]
    for k in range(folds):
        mix = masked_mix(dot(blocks[k][...], router[...]), mask[k])
        for step in range(local):
            pick = one_hot(slots, k, step, capacity)
            at = pl.ds(k * capacity, capacity)
            picked_ref[step, at, :] = dot(
                jnp.where(pick, 1.0, 0.0).astype(BF16), blocks[k][...]
            ).astype(BF16)
            grows_ref[step, at, :] = lax.dot_general(
                jnp.where(pick, 1.0, 0.0), mix, (((1,), (0,)), ((), ())),
                precision=HIGHEST, preferred_element_type=F32,
            )
    for step in range(local):
        for part in range(parts):
            for kind in range(3):
                waits[kind, step, part].wait()
            cols = pl.ds(part * ff, ff)
            x = picked_ref[step]
            gate = dot(x, buf_g[step, part])
            up = dot(x, buf_u[step, part])
            gate_ref[step, :, cols] = gate
            up_ref[step, :, cols] = up
            inner = (gelu_parts(gate)[0] * up).astype(BF16)
            term = dot(inner, buf_d[step, part])
            made = term if part == 0 else made + term
        made_ref[step] = made.astype(BF16)
    for k in range(folds):
        at = pl.ds(k * capacity, capacity)
        picks, weighted = [], []
        for step in range(local):
            gates = grows_ref[step, at, :]
            own_lane = lane_is(gates.shape, scalars_ref[2 + step])
            factor = jnp.sum(jnp.where(own_lane, gates, 0.0), axis=1, keepdims=True)
            picks.append(jnp.where(one_hot(slots, k, step, capacity), 1.0, 0.0).astype(BF16))
            weighted.append((made_ref[step, at, :].astype(F32) * factor).astype(BF16))
        partials[k][...] = dot_tn(
            jnp.concatenate(picks, axis=0), jnp.concatenate(weighted, axis=0)
        ).astype(BF16)


def moe_bwd_kernel(folds, local, parts, capacity, *refs):
    (scalars, slots, gate_ref, up_ref, made_ref, grows_ref), blocks, own, flat, (ge_ref,), partials, scratch = split_refs(
        refs, (6, folds, 3, 3 * local * parts, 1, folds, 6)
    )
    buf_g, buf_u, buf_d, sems, dx_ref, dots_ref = scratch
    pieces = [
        [[flat[(kind * local + step) * parts + part] for part in range(parts)] for step in range(local)]
        for kind in range(3)
    ]
    waits = weight_copies(scalars, own, pieces, (buf_g, buf_u, buf_d), sems)
    ff = buf_g.shape[3]
    for step in range(local):
        for k in range(folds):
            at = pl.ds(k * capacity, capacity)
            pick = jnp.where(one_hot(slots, k, step, capacity), 1.0, 0.0).astype(BF16)
            dout = dot(pick, blocks[k][...])
            gates = grows_ref[step, at, :]
            own_lane = lane_is(gates.shape, scalars[2 + step])
            factor = jnp.sum(jnp.where(own_lane, gates, 0.0), axis=1, keepdims=True)
            value = jnp.sum(dout * made_ref[step, at, :].astype(F32), axis=1, keepdims=True)
            lane = lax.broadcasted_iota(jnp.int32, gates.shape, 1)
            number = scalars[2 + step]
            dots_ref[step, at, :] = jnp.where(
                (lane == number) | (lane == number + LANES // 2), value, 0.0
            )
            ge_ref[step, at, :] = (dout * factor).astype(BF16)
    for step in range(local):
        ge = ge_ref[step]
        for part in range(parts):
            for kind in range(3):
                waits[kind, step, part].wait()
            cols = pl.ds(part * ff, ff)
            grad_inner = dot_nt(ge, buf_d[step, part])
            gate = gate_ref[step, :, cols]
            up = up_ref[step, :, cols]
            value, slope = gelu_parts(gate)
            grad_gate = (grad_inner * up * slope).astype(BF16)
            grad_up = (grad_inner * value).astype(BF16)
            term = dot_nt(grad_gate, buf_g[step, part]) + dot_nt(grad_up, buf_u[step, part])
            total = term if part == 0 else total + term
        dx_ref[step] = total.astype(BF16)
    for k in range(folds):
        at = pl.ds(k * capacity, capacity)
        hot = [one_hot(slots, k, step, capacity) for step in range(local)]
        picks = jnp.concatenate([jnp.where(one, 1.0, 0.0) for one in hot], axis=0)
        width = ge_ref.shape[2]
        partials[k][:, :width] = dot_tn(
            picks.astype(BF16), jnp.concatenate([dx_ref[step, at, :] for step in range(local)], axis=0)
        ).astype(BF16)
        dots = lax.dot_general(
            picks, jnp.concatenate([dots_ref[step, at, :] for step in range(local)], axis=0),
            (((0,), (0,)), ((), ())), precision=HIGHEST, preferred_element_type=F32,
        )
        high = dots.astype(BF16).astype(F32)
        lane = lax.broadcasted_iota(jnp.int32, dots.shape, 1)
        partials[k][:, width:] = jnp.where(lane < LANES // 2, high, dots - high).astype(BF16)


def vmem(count):
    return [pl.BlockSpec(memory_space=pltpu.VMEM)] * count


def anywhere(count):
    return [pl.BlockSpec(memory_space=pl.ANY)] * count


def weight_scratch(own, local, parts):
    width, ff = own[0].shape[1], own[0].shape[2] // parts
    return [
        pltpu.VMEM((local, parts, width, ff), BF16),
        pltpu.VMEM((local, parts, width, ff), BF16),
        pltpu.VMEM((local, parts, ff, width), BF16),
        pltpu.SemaphoreType.DMA((3, local, parts)),
    ]


def cost(rows, width, ff, products):
    return pl.CostEstimate(
        flops=2 * rows * width * ff * products, bytes_accessed=2 * 3 * width * ff * 2 + 8 * rows * width,
        transcendentals=rows * ff,
    )


def moe_fwd_call(scalars, slots, mask, router, blocks, own, flat, folds, local, rows, parts, width, ff, capacity):
    picked_rows = folds * capacity
    shapes = [
        jax.ShapeDtypeStruct((local, picked_rows, width), BF16),
        jax.ShapeDtypeStruct((local, picked_rows, ff), F32),
        jax.ShapeDtypeStruct((local, picked_rows, ff), F32),
        jax.ShapeDtypeStruct((local, picked_rows, width), BF16),
        jax.ShapeDtypeStruct((local, picked_rows, LANES), F32),
    ] + [jax.ShapeDtypeStruct((rows, width), BF16)] * folds
    out = pl.pallas_call(
        functools.partial(moe_fwd_kernel, folds, local, parts, capacity),
        out_shape=shapes,
        in_specs=[pl.BlockSpec(memory_space=pltpu.SMEM)]
        + vmem(3 + folds) + anywhere(3 + len(flat)),
        out_specs=vmem(len(shapes)),
        scratch_shapes=weight_scratch(own, local, parts),
        cost_estimate=cost(local * picked_rows, width, ff, 3),
        compiler_params=pltpu.CompilerParams(vmem_limit_bytes=56 << 20),
    )(scalars, slots, mask, router, *blocks, *own, *flat)
    return out[:5], out[5:]


def moe_bwd_call(scalars, slots, kept, blocks, own, flat, folds, local, rows, parts, width, ff, capacity):
    _, gate_pre, up_pre, made, gate_rows = kept
    picked_rows = folds * capacity
    shapes = [jax.ShapeDtypeStruct((local, picked_rows, width), BF16)] + [
        jax.ShapeDtypeStruct((rows, width + LANES), BF16)
    ] * folds
    out = pl.pallas_call(
        functools.partial(moe_bwd_kernel, folds, local, parts, capacity),
        out_shape=shapes,
        in_specs=[pl.BlockSpec(memory_space=pltpu.SMEM)]
        + vmem(5 + folds) + anywhere(3 + len(flat)),
        out_specs=vmem(len(shapes)),
        scratch_shapes=weight_scratch(own, local, parts)
        + [pltpu.VMEM((local, picked_rows, width), BF16), pltpu.VMEM((local, picked_rows, LANES), F32)],
        cost_estimate=cost(local * picked_rows, width, ff, 3),
        compiler_params=pltpu.CompilerParams(vmem_limit_bytes=56 << 20),
    )(scalars, slots, gate_pre, up_pre, made, gate_rows, *blocks, *own, *flat)
    return out[0], out[1:]


def mm(a, b):
    return jnp.dot(a, b, preferred_element_type=F32)


def mm_nt(a, b):
    return lax.dot_general(a, b, (((1,), (1,)), ((), ())), preferred_element_type=F32)


def mm_tn(a, b):
    return lax.dot_general(a, b, (((0,), (0,)), ((), ())), preferred_element_type=F32)


def ein(spec, a, b):
    return jnp.einsum(spec, a, b, preferred_element_type=F32)


def rel_gather(value):
    folds = lax.axis_size(F_AX)
    parts = [value]
    for k in range(1, folds):
        parts.append(lax.ppermute(value, F_AX, [(i, (i + k) % folds) for i in range(folds)]))
    return parts


def rel_scatter(parts):
    folds = lax.axis_size(F_AX)
    total = parts[0].astype(F32)
    for k in range(1, folds):
        got = lax.ppermute(parts[k], F_AX, [(i, (i - k) % folds) for i in range(folds)])
        total = total + got.astype(F32)
    return total


def swap_section(value):
    return lax.ppermute(value, S_AX, [(0, 1), (1, 0)])


def swap_core(value):
    count = lax.axis_size(R_AX)
    return lax.ppermute(value, R_AX, [(i, i ^ 1) for i in range(count)])


def rope_turn(values, cos, sin):
    half = HEAD // 2
    turned = jnp.concatenate([-values[..., half:], values[..., :half]], axis=-1)
    return values * cos + turned * sin


def rope_back(grads, cos, sin):
    half = HEAD // 2
    scaled = grads * sin
    turned = jnp.concatenate([scaled[..., half:], -scaled[..., :half]], axis=-1)
    return grads * cos + turned


def layout(lengths, position):
    bounds = jnp.cumsum(lengths)
    passed = (position[:, None] >= bounds[None, :]).astype(jnp.int32)
    segment = jnp.sum(passed, axis=1)
    start = jnp.sum(passed * lengths[None, :], axis=1)
    return segment, (position - start).astype(F32)


def gated(gate, up):
    return jax.nn.gelu(gate) * up


def attention_in(hidden, gain, w_qkv, common, kv_width):
    cos, sin = common["cos"], common["sin"]
    rows, width = hidden.shape
    q_width = w_qkv.shape[1] - 2 * kv_width
    scale = lax.rsqrt(jnp.mean(hidden * hidden, axis=1, keepdims=True) + EPS)
    normed = hidden * scale
    attn_in = (normed * gain.astype(F32)).astype(BF16)
    lin = mm(attn_in, w_qkv)
    turned = rope_turn(
        lin[:, : q_width + kv_width].reshape(rows, -1, HEAD), cos, sin
    ).astype(BF16).reshape(rows, -1)
    query = turned[:, :q_width]
    kv = jnp.concatenate([turned[:, q_width:], lin[:, q_width + kv_width :].astype(BF16)], axis=1)
    return dict(scale=scale, normed=normed, attn_in=attn_in, query=query, kv=kv)


def grouped_heads(value, groups):
    rows = value.shape[0]
    return value.reshape(rows, groups, -1, HEAD)


def attend(query, kv_all, allowed, groups):
    keys = kv_all[:, : groups * HEAD].reshape(-1, groups, HEAD)
    values = kv_all[:, groups * HEAD :].reshape(-1, groups, HEAD)
    raw = ein("tgha,sga->ghts", grouped_heads(query, groups), keys) * HEAD ** (-0.5)
    scores = jnp.where(allowed[None, None], raw, MASKED)
    top = jnp.max(scores, axis=3, keepdims=True)
    expo = jnp.exp(scores - top)
    probs = expo / jnp.sum(expo, axis=3, keepdims=True)
    mixed = ein("ghts,sga->tgha", probs.astype(BF16), values)
    return mixed.reshape(query.shape), probs


def attend_back(grad_mixed, mixed, probs, query, kv_all, groups):
    rows = query.shape[0]
    keys = kv_all[:, : groups * HEAD].reshape(-1, groups, HEAD)
    values = kv_all[:, groups * HEAD :].reshape(-1, groups, HEAD)
    grad_grouped = grouped_heads(grad_mixed, groups)
    delta = jnp.sum(
        grad_grouped.astype(F32) * grouped_heads(mixed, groups), axis=3
    )
    delta = jnp.transpose(delta, (1, 2, 0))[..., None]
    grad_probs = ein("tgha,sga->ghts", grad_grouped, values)
    grad_scores = (probs * (grad_probs - delta)).astype(BF16)
    score_scale = HEAD ** (-0.5)
    grad_query = (ein("ghts,sga->tgha", grad_scores, keys) * score_scale).reshape(rows, -1, HEAD)
    grad_key = ein("ghts,tgha->sga", grad_scores, grouped_heads(query, groups)) * score_scale
    grad_value = ein("ghts,tgha->sga", probs.astype(BF16), grad_grouped)
    count = kv_all.shape[0]
    grad_kv = jnp.concatenate(
        [grad_key.reshape(count, -1), grad_value.reshape(count, -1)], axis=1
    ).astype(BF16)
    return grad_query, grad_kv


def moe_forward(moe_in, router, mask, slots, scalars, experts_w, size):
    outs, partials = moe_fwd_call(
        scalars, slots, mask, router, rel_gather(moe_in), *experts_w, **size
    )
    return rel_scatter(partials), outs


def moe_backward(grad_low, kept, slots, scalars, experts_w, size, tie, send_rows):
    blocks, tied = lax.optimization_barrier((rel_gather(grad_low), tie))
    grad_expert, partials = moe_bwd_call(scalars, slots, kept, blocks, *experts_w, **size)
    sent = send_rows(grad_expert)
    summed = rel_scatter(partials)
    width = grad_low.shape[1]
    tail = summed[:, width:]
    half = LANES // 2
    dots = tail[:, :half] + tail[:, half:]
    return summed[:, :width], jnp.pad(dots, ((0, 0), (0, half))), sent, tied


def layer_forward(layer_in, weights, experts_w, common, mask, slots, scalars):
    gains, w_qkv, w_out, router = weights
    groups = common["groups"]
    hidden = layer_in.astype(F32)
    kept = attention_in(hidden, gains[0], w_qkv, common, groups * HEAD)
    kv_all = jnp.concatenate(rel_gather(kept["kv"]), axis=0)
    mixed, probs = attend(kept["query"], kv_all, common["allowed"], groups)
    mixed_low = mixed.astype(BF16)
    residual = hidden + mm(mixed_low, w_out)
    scale_two = lax.rsqrt(jnp.mean(residual * residual, axis=1, keepdims=True) + EPS)
    normed_two = residual * scale_two
    moe_in = (normed_two * gains[1].astype(F32)).astype(BF16)
    mix = masked_mix(mm(moe_in, router), mask[0])
    summed, moe_kept = moe_forward(moe_in, router, mask, slots, scalars, experts_w, common["size"])
    out = (residual + summed).astype(BF16)
    kept.update(
        kv_all=kv_all, mixed=mixed, probs=probs, mixed_low=mixed_low, scale_two=scale_two,
        normed_two=normed_two, moe_in=moe_in, mix=mix, moe=moe_kept,
    )
    return out, kept


def layer_backward(grad_low, kept, weights, experts_w, common, slots, scalars, tie, late_tie, send_rows):
    gains, w_qkv, w_out, router = weights
    groups = common["groups"]
    grad_out = grad_low.astype(F32)
    rows = grad_out.shape[0]
    grad_moe_in, dots, sent, tied = moe_backward(
        grad_low, kept["moe"], slots, scalars, experts_w, common["size"], tie, send_rows
    )
    mix = kept["mix"]
    grad_logits = mix * (dots - jnp.sum(mix * dots, axis=1, keepdims=True))
    moe_in = kept["moe_in"]
    count = common["experts"]
    grad_router = lax.dot_general(
        grad_logits[:, :count], moe_in.astype(F32), (((0,), (0,)), ((), ())), precision=HIGHEST
    )
    grad_moe_in = grad_moe_in + jnp.dot(grad_logits, router.astype(F32).T, precision=HIGHEST)
    normed_two = kept["normed_two"]
    grad_norm = grad_moe_in * gains[1].astype(F32)
    grad_gain_two = jnp.sum(grad_moe_in * normed_two, axis=0)
    grad_mid = grad_out + kept["scale_two"] * (
        grad_norm - normed_two * jnp.mean(grad_norm * normed_two, axis=1, keepdims=True)
    )
    grad_attn = grad_mid.astype(BF16)
    grad_mixed = mm_nt(grad_attn, w_out).astype(BF16)
    grad_query, grad_kv = attend_back(
        grad_mixed, kept["mixed"], kept["probs"], kept["query"], kept["kv_all"], groups
    )
    grad_kv, late_tied, sent = lax.optimization_barrier((grad_kv, late_tie, sent))
    own = rel_scatter([grad_kv[k * rows : (k + 1) * rows] for k in range(lax.axis_size(F_AX))])
    cos, sin = common["cos"], common["sin"]
    kv_width = groups * HEAD
    grad_lin = jnp.concatenate(
        [
            rope_back(grad_query, cos, sin).reshape(rows, -1),
            rope_back(own[:, :kv_width].reshape(rows, -1, HEAD), cos, sin).reshape(rows, -1),
            own[:, kv_width:],
        ],
        axis=1,
    ).astype(BF16)
    grad_attn_in = mm_nt(grad_lin, w_qkv)
    normed = kept["normed"]
    grad_norm = grad_attn_in * gains[0].astype(F32)
    grad_in = grad_mid + kept["scale"] * (
        grad_norm - normed * jnp.mean(grad_norm * normed, axis=1, keepdims=True)
    )
    small = jnp.concatenate([grad_router, grad_gain_two[None]], axis=0)
    return grad_in.astype(BF16), grad_attn, grad_lin, small.astype(BF16), sent, tied, late_tied


def expert_grads(rows_in, grad_rows, gate_w, up_w, down_w):
    gate_pre = mm(rows_in, gate_w)
    up_pre = mm(rows_in, up_w)
    inner, back = jax.vjp(gated, gate_pre, up_pre)
    grad_gate, grad_up = back(mm_nt(grad_rows, down_w))
    grad_gate, grad_up = grad_gate.astype(BF16), grad_up.astype(BF16)
    return (
        mm_tn(rows_in, grad_gate).astype(BF16),
        mm_tn(rows_in, grad_up).astype(BF16),
        mm_tn(inner.astype(BF16), grad_rows).astype(BF16),
    )


def body(
    tokens, cotangent, seq_lengths, routes, gains, w_query, w_key, w_value, w_out, w_router, w_gate, w_up, w_down
):
    section = lax.axis_index(S_AX)
    is_first = section == 0
    fold_id = lax.axis_index(F_AX)
    replica = lax.axis_index(R_AX)
    core = replica % 2
    folds, replicas = lax.axis_size(F_AX), lax.axis_size(R_AX)
    rows = tokens.shape[2]
    top = routes.shape[4]
    local = w_gate.shape[1]
    expert_count = w_router.shape[2]
    kv_width = w_key.shape[2]
    q_width = w_query.shape[2]
    capacity = rows * top // expert_count

    def own_batch(value):
        return lax.dynamic_index_in_dim(value, section, 0, keepdims=False)

    def swap_xor(value, bit):
        return lax.ppermute(value, R_AX, [(i, i ^ bit) for i in range(replicas)])

    flat_routes = routes[0, :, 0].reshape(2, rows * top)
    give = lax.dynamic_index_in_dim(flat_routes, 1 - section, 0, keepdims=False)
    keep = own_batch(flat_routes)
    got = swap_section(give)
    pair = jnp.stack([jnp.where(is_first, keep, got), jnp.where(is_first, got, keep)])
    mine = jnp.stack(rel_gather(pair), axis=1).reshape(2, folds, rows, top)
    first = fold_id * local
    flip = (replica // 2) % 2
    lanes = jnp.arange(LANES, dtype=jnp.int32)
    masks = jnp.any(mine[..., None] == lanes, axis=3)
    numbers = first + (jnp.arange(local, dtype=jnp.int32) ^ flip)
    named = jnp.any(mine[:, :, None] == numbers[None, None, :, None, None], axis=4)
    before = (jnp.arange(rows)[:, None] < jnp.arange(rows)[None, :]).astype(BF16)
    rank = ein("lfet,tu->lfeu", named.astype(BF16), before).astype(jnp.int32)
    slots_all = jnp.where(named, rank, -1)
    masks = masks.astype(F32)
    scalars = [
        jnp.concatenate([jnp.stack([(section == layer).astype(jnp.int32), flip]), numbers]).astype(jnp.int32)
        for layer in range(2)
    ]

    small = jnp.concatenate([w_router[0], gains[0].T], axis=1)
    small = jnp.pad(small, ((0, 0), (0, HEAD - small.shape[1])))
    shard = jnp.concatenate([w_query[0], w_key[0], w_value[0], small, w_out[0]], axis=1)
    share = shard.shape[0] // (2 * replicas)
    keep = lax.dynamic_slice_in_dim(shard, (section * replicas + replica) * share, share, 0)
    give = lax.dynamic_slice_in_dim(shard, ((1 - section) * replicas + replica) * share, share, 0)
    got = swap_section(give)
    split = q_width + 2 * kv_width
    weights = []
    for layer in range(2):
        piece = jnp.where(section == layer, keep, got)
        axes = (F_AX, S_AX, R_AX)
        head = lax.all_gather(piece[:, : split + LANES], axes, axis=0, tiled=True)
        out_w = lax.all_gather(piece[:, split + LANES :], axes, axis=0, tiled=True)
        tail = head[:, split:]
        weights.append((tail[:, expert_count : expert_count + 2].T, head[:, :split], out_w, tail))

    part_ff = w_gate.shape[3] // 2
    at = core * part_ff
    flat = []
    for part, axis in ((w_gate, 1), (w_up, 1), (w_down, 0)):
        chosen = lax.dynamic_index_in_dim(part[0], flip, 0, keepdims=False)
        piece = lax.dynamic_slice_in_dim(chosen, at, part_ff, axis)
        same = swap_section(piece)
        cross = swap_xor(same, 2)
        flat += [same, swap_core(same), cross, swap_core(cross)]
    experts_w = ((w_gate[0], w_up[0], w_down[0]), flat)
    size = dict(
        folds=folds, local=local, rows=rows, parts=2, width=tokens.shape[3], ff=w_gate.shape[3],
        capacity=capacity,
    )

    lengths = own_batch(seq_lengths[:, 0])
    position = fold_id * rows + jnp.arange(rows, dtype=jnp.int32)
    order = (fold_id - jnp.arange(folds)) % folds
    key_pos = (order[:, None] * rows + jnp.arange(rows)[None, :]).reshape(-1).astype(jnp.int32)
    segment, offset = layout(lengths, position)
    key_seg, _ = layout(lengths, key_pos)
    freq = ROPE_BASE ** (-2.0 * jnp.arange(HEAD // 2, dtype=F32) / HEAD)
    angles = offset[:, None] * freq
    angles = jnp.concatenate([angles, angles], axis=1)[:, None, :]
    common = dict(
        cos=jnp.cos(angles), sin=jnp.sin(angles), groups=kv_width // HEAD, size=size,
        experts=expert_count,
        allowed=(segment[:, None] == key_seg[None, :]) & (key_pos[None, :] <= position[:, None]),
    )

    value = own_batch(tokens[:, 0])
    outs, kept = [], []
    for layer in range(2):
        value, state = layer_forward(
            value, weights[layer], experts_w, common, masks[layer], slots_all[layer], scalars[layer]
        )
        outs.append(value)
        kept.append(state)

    def own_layer(pair):
        return jnp.where(is_first, pair[0], pair[1])

    def other_layer(pair):
        return jnp.where(is_first, pair[1], pair[0])

    def by_section(keep, got):
        return jnp.stack([jnp.where(is_first, keep, got), jnp.where(is_first, got, keep)])

    def both_batches(pair):
        return by_section(own_layer(pair), swap_section(other_layer(pair)))

    half = local // 2

    def chip_rows(pair):
        chip = []
        for value in pair:
            keep = lax.dynamic_slice_in_dim(value, (core ^ flip) * half, half, 0)
            give = lax.dynamic_slice_in_dim(value, (1 - (core ^ flip)) * half, half, 0)
            got = swap_core(give)
            chip.append(
                jnp.concatenate(
                    [jnp.where(core == 0, keep, got), jnp.where(core == 0, got, keep)], axis=1
                )
            )
        return chip

    chips = replicas // 2

    def all_x(value):
        return [swap_xor(value, bit) for bit in range(2, replicas, 2)]

    def by_order(value, others):
        whole = jnp.zeros((chips,) + value.shape, value.dtype)
        for at, part in enumerate([value] + others):
            whole = lax.dynamic_update_index_in_dim(whole, part, (replica // 2) ^ at, 0)
        return whole

    same_core = [[2 * i + c for i in range(chips)] for c in range(2)]

    def flat_rows(whole):
        return jnp.moveaxis(whole, 2, 0).reshape(half, -1, whole.shape[-1])

    x_rows = both_batches(chip_rows([state["moe"][0] for state in kept]))
    def both_rows(pair):
        return jnp.concatenate([own_layer(pair), swap_section(other_layer(pair))], axis=0)

    def own_columns(value):
        width = value.shape[1] // replicas
        whole = jnp.zeros((replicas, value.shape[0], width), value.dtype)
        for bit in range(replicas):
            piece = lax.dynamic_slice_in_dim(value, (replica ^ bit) * width, width, 1)
            got = piece if bit == 0 else swap_xor(piece, bit)
            whole = lax.dynamic_update_index_in_dim(whole, got, replica ^ bit, 0)
        return whole

    def weight_gradient(left, right, extra):
        total = mm_tn(left, right).astype(BF16)
        step = total.shape[0] // folds
        blocks = []
        for k in range(folds):
            goal = (fold_id - k) % folds
            block = lax.dynamic_slice_in_dim(total, goal * step, step, 0)
            if extra is not None:
                more = lax.dynamic_index_in_dim(extra, goal, 0, keepdims=False)
                block = jnp.concatenate([block, more], axis=0)
            blocks.append(block)
        mine = rel_scatter(blocks).astype(BF16)
        height, width = mine.shape
        whole = jnp.zeros((replicas, height, width), BF16)
        for bit in range(0, replicas, 2):
            same = mine if bit == 0 else swap_xor(mine, bit)
            for other, part in enumerate((same, swap_core(same))):
                whole = lax.dynamic_update_index_in_dim(whole, part, replica ^ (bit + other), 0)
        return whole

    left_rows = both_rows(
        [jnp.concatenate([state["attn_in"], state["mixed_low"]], axis=1) for state in kept]
    )
    grad = own_batch(cotangent[:, 0])
    grads, grad_attn, grad_lin = [None, None], [None, None], [None, None]
    smalls, expert_rows = [None, None], [None, None]
    tie = ()
    held = []

    def send_first(value):
        held.append(chip_rows([value])[0])
        return ()

    def send_both(value):
        chip = (chip_rows([value])[0], held[0])
        mine = own_layer(chip)
        return by_order(mine, all_x(mine)), swap_section(other_layer(chip))

    for layer in (1, 0):
        late_tie = (x_rows, left_rows) if layer == 1 else ()
        (grad, grad_attn[layer], grad_lin[layer], smalls[layer], expert_rows[layer], tied, late_tied) = layer_backward(
            grad, kept[layer], weights[layer], experts_w, common, slots_all[layer], scalars[layer], tie, late_tie,
            send_first if layer == 1 else send_both,
        )
        if layer == 1:
            x_rows, left_rows = late_tied
            x_rows = lax.all_gather(x_rows, R_AX, axis=0, axis_index_groups=same_core)
            left_rows = lax.all_gather(left_rows, R_AX, axis=0, tiled=True)
            tie = (x_rows, left_rows)
        else:
            x_rows, left_rows = tied
        grads[layer] = grad
    x_rows = flat_rows(x_rows)
    model = tokens.shape[3]
    piece = model // (folds * replicas)
    count = smalls[0].shape[0]
    tall = -(-count // 16) * 16
    with_small = []
    for layer in range(2):
        value = smalls[layer].reshape(count, folds, replicas, piece)
        value = jnp.transpose(value, (0, 2, 1, 3)).reshape(count, model)
        with_small.append(jnp.concatenate([grad_attn[layer], jnp.pad(value, ((0, tall - count), (0, 0)))], axis=0))
    right = own_columns(both_rows(with_small))
    right = right.reshape(replicas, 2, rows + tall, right.shape[2])
    extra = jnp.sum(right[:, :, rows:].astype(F32), axis=(0, 1)).reshape(tall, folds, piece)
    extra = jnp.pad(
        jnp.transpose(extra, (1, 0, 2)), ((0, 0), (0, 0), (0, right.shape[3] - piece))
    ).astype(BF16)
    out_shard = weight_gradient(
        left_rows[:, model:], right[:, :, :rows].reshape(-1, right.shape[3]), extra
    )
    def side_by_side(value):
        return jnp.concatenate([value[j].astype(F32) for j in range(replicas)], axis=1)

    small = side_by_side(out_shard[:, gains.shape[2] :, :piece])
    out_shard = side_by_side(out_shard[:, : gains.shape[2]])
    right = own_columns(both_rows(grad_lin))
    shard = weight_gradient(left_rows[:, :model], right.reshape(-1, right.shape[2]), None)
    shard = side_by_side(shard)
    own_w = jnp.concatenate([w_query[0], w_key[0], w_value[0]], axis=1).astype(F32)
    gain_one = jnp.sum(shard * own_w, axis=1) / gains[0, 0].astype(F32)
    mine, got = expert_rows[0]
    got = by_order(got, all_x(got))
    batches = [jnp.where(is_first, mine, got), jnp.where(is_first, got, mine)]
    g_rows = flat_rows(jnp.stack(batches, axis=1))
    mine_w = [lax.dynamic_slice_in_dim(part[0], core * half, half, 0) for part in (w_gate, w_up, w_down)]
    made = [
        expert_grads(x_rows[i], g_rows[i], mine_w[0][i], mine_w[1][i], mine_w[2][i]) for i in range(half)
    ]
    expert_out = []
    for slot in range(3):
        keep = jnp.stack([one[slot] for one in made])
        got = swap_core(keep)
        both = jnp.concatenate(
            [jnp.where(core == 0, keep, got), jnp.where(core == 0, got, keep)], axis=0
        )
        expert_out.append(both.astype(F32)[None])

    layer_outputs = both_batches(outs)
    input_grads = both_batches(grads)
    return (
        layer_outputs[None, :, None],
        input_grads[None, :, None],
        jnp.stack([gain_one, small[expert_count]])[None],
        shard[None, :, :q_width],
        shard[None, :, q_width : q_width + kv_width],
        shard[None, :, q_width + kv_width : split],
        out_shard[None],
        small[:expert_count].T[None],
        expert_out[0],
        expert_out[1],
        expert_out[2],
    )


def solution(mesh):
    acts = P(None, R_AX, F_AX, None)
    rows = P(S_AX, F_AX, None)
    expert = P(S_AX, F_AX, None, None)
    stacked = P(S_AX, None, R_AX, F_AX, None)
    gain = P(S_AX, None, F_AX)
    return jax.shard_map(
        body,
        mesh=mesh,
        in_specs=(acts, acts, P(None, R_AX, None), stacked, gain)
        + (rows,) * 5
        + (expert,) * 3,
        out_specs=(stacked, stacked, gain) + (rows,) * 5 + (expert,) * 3,
        check_vma=False,
    )
```

time: 1190 us -> 1040 us (0.87)
  waiting for transfers between devices: 663 us -> 507 us
  matrix products: 177 us -> 123 us
  Pallas kernels: 0 us -> 49.9 us
  blocking collectives: 48.1 us -> 0 us
  starting transfers between devices: 116 us -> 155 us
  other arithmetic: 70.9 us -> 85 us
    all_gather x7 -> x6, waiting for transfers between devices: 269 us -> 86.2 us  [the longest x2 55 us: body(): head = lax.all_gather(piece[:, :split + LANES], axes, axis=0, tiled=True)]
    pallas_call x0 -> x4, Pallas kernels: none -> 49.9 us  [the longest x2 26.3 us: moe_bwd_call(): pl.pallas_call(functools.partial(moe_bwd_kernel, folds, local, parts, cap...]
    all_gather x1 -> x0, blocking collectives: 48.1 us -> none  [body(): lax.all_gather(routes[0, :, 0].reshape(2, rows * top), (S_AX, F_AX), axis=0)]
    ppermute x4 -> x12, waiting for transfers between devices: 100 us -> 53.4 us  [swap_section(): return lax.ppermute(value, S_AX, [(0, 1), (1, 0)])]
    dot_general x30 -> x11, matrix products: 59.8 us -> 15.3 us  [ein(): return jnp.einsum(spec, a, b, preferred_element_type=F32)]
    ppermute x18 -> x21, waiting for transfers between devices: 105 us -> 132 us  [rel_gather(): lax.ppermute(value, F_AX, [(i, (i + k) % folds) for i in range(folds)])]
    ppermute x2 -> x13, waiting for transfers between devices: 73.5 us -> 99.4 us  [swap_xor(): return lax.ppermute(value, R_AX, [(i, i ^ bit) for i in range(replicas)])]
    ppermute x18 -> x24, starting transfers between devices: 54.4 us -> 77.5 us  [rel_scatter(): lax.ppermute(parts[k], F_AX, [(i, (i - k) % folds) for i in range(folds)])]
  transfers between devices with their start and end apart: 58 -> 93, of which waited for: 31 -> 44; matrix products, arithmetic and copies ran while one was open for 20% -> 25% of each run, Pallas kernels for 0% -> 4%
where the time goes in v1:
time: 1040 us; the launch traced here: 1030 us
  waiting for transfers between devices  507 us (49%)
  starting transfers between devices  155 us (15%)
  matrix products  123 us (12%)
  local copies, waits for them, and re-layouts  89.1 us (9%)
  other arithmetic  85 us (8%)
  Pallas kernels  49.9 us (5%)
  between operations  17.4 us (2%)
    ppermute x21, waiting for transfers between devices, rel_gather(): lax.ppermute(value, F_AX, [(i, (i + k) % folds) for i in range(folds)])  132 us
    ppermute x24, waiting for transfers between devices, rel_scatter(): lax.ppermute(parts[k], F_AX, [(i, (i - k) % folds) for i in range(folds)])  127 us
    ppermute x13, waiting for transfers between devices, swap_xor(): return lax.ppermute(value, R_AX, [(i, i ^ bit) for i in range(replicas)])  99.4 us
    ppermute x24, starting transfers between devices, rel_scatter(): lax.ppermute(parts[k], F_AX, [(i, (i - k) % folds) for i in range(folds)])  77.5 us
    all_gather x2, waiting for transfers between devices, body(): head = lax.all_gather(piece[:, :split + LANES], axes, axis=0, tiled=True)  55 us
    ppermute x12, waiting for transfers between devices, swap_section(): return lax.ppermute(value, S_AX, [(0, 1), (1, 0)])  53.4 us
    ppermute x21, starting transfers between devices, rel_gather(): lax.ppermute(value, F_AX, [(i, (i + k) % folds) for i in range(folds)])  45.4 us
    dot_general x5, matrix products, mm_tn(): lax.dot_general(a, b, (((0,), (0,)), ((), ())), preferred_element_type=F32)  40.7 us
  transfers between devices with their start and end apart: 93, of which 44 were waited for; matrix products, arithmetic and copies ran while one was open for 25% of the time, Pallas kernels for 4%

profile of v1, /device:TPU:0, one launch (start us, length us, event | category | flops | bytes accessed | tf_op | source)
XLA Modules:
  0.0 1026.0 jit_solution(2237297918349148621)
XLA Ops:
  19.6 8.3 collective-permute-done
  64.8 55.0 %all-gather.8.cloned.1.call-done = bf16[1536,2176]{1,0:T(8,128)(2,1)} async-done(((bf16[48,2176]{1,0:T(8,128)(2,1)}), bf16[1536,2176]{1,0:T(8,128)(2,1)}) %all-gather.8.cloned.1.call-update) | async-done | bytes 6684688 | tf_op jit(solution)/shard_map/all_gather | solution.py:556
  148.0 11.1 %collective-permute-done.2 = bf16[128,512]{1,0:T(8,128)(2,1)} collective-permute-done((bf16[128,512]{1,0:T(8,128)(2,1)}, bf16[128,512]{1,0:T(8,128)(2,1)}, u32[]{:S(2)}, u32[]{:S(2)}) %collective-permute-start.2) | collective-permute-done | bytes 131104 | tf_op jit(solution)/shard_map/ppermute | solution.py:295
  176.2 21.4 %collective-permute-done.37.refs_8_ = bf16[128,1536]{1,0:T(8,128)(2,1)} collective-permute-done((bf16[128,1536]{1,0:T(8,128)(2,1)S(1)}, bf16[128,1536]{1,0:T(8,128)(2,1)}, u32[]{:S(2)}, u32[]{:S(2)}) %collective-permute-start.37) | collective-permute-done | bytes 393248 | tf_op jit(solution)/shard_map/ppermute | solution.py:295
  202.3 6.5 collective-permute-done.38.refs_9_
  214.4 8.8 collective-permute-done.17.refs_17_.refs_19_
  223.2 30.9 %collective-permute-done.21.refs_21_.refs_23_ = bf16[384,1536]{1,0:T(8,128)(2,1)} collective-permute-done((bf16[384,1536]{1,0:T(8,128)(2,1)}, bf16[384,1536]{1,0:T(8,128)(2,1)}, u32[]{:S(2)}, u32[]{:S(2)}) %collective-permute-start.21) | collective-permute-done | bytes 1179680 | tf_op jit(solution)/shard_map/ppermute | solution.py:521
  262.1 14.4 %collective-permute-done.8.refs_5_ = bf16[128,1536]{1,0:T(8,128)(2,1)S(1)} collective-permute-done((bf16[128,1536]{1,0:T(8,128)(2,1)S(1)}, bf16[128,1536]{1,0:T(8,128)(2,1)S(1)}, u32[]{:S(2)}, u32[]{:S(2)}) %collective-permute-start.8) | collective-permute-done | bytes 393248 | tf_op jit(solution)/shard_map/ppermute | solution.py:295
  276.5 22.4 %collective-permute-done.9.refs_6_ = bf16[128,1536]{1,0:T(8,128)(2,1)S(1)} collective-permute-done((bf16[128,1536]{1,0:T(8,128)(2,1)S(1)}, bf16[128,1536]{1,0:T(8,128)(2,1)S(1)}, u32[]{:S(2)}, u32[]{:S(2)}) %collective-permute-start.9) | collective-permute-done | bytes 393248 | tf_op jit(solution)/shard_map/ppermute | solution.py:295
  299.8 11.8 %shard_map.212 = (bf16[2,256,1536]{2,1,0:T(8,128)(2,1)}, f32[2,256,768]{2,1,0:T(8,128)}, f32[2,256,768]{2,1,0:T(8,128)}, bf16[2,256,1536]{2,1,0:T(8,128)(2,1)}, ...) custom-call(s32[4]{0:T(128)} %get-tuple-element.290.refs_0_, ...), custom_call_target="tpu_custom_call" | custom-call | flops 3623878656 | bytes 20447232 | tf_op jit(solution)/shard_map/pallas_call | solution.py:242
  311.6 8.8 collective-permute-start.25
  331.7 18.7 %collective-permute-done.24 = bf16[128,1536]{1,0:T(8,128)(2,1)S(1)} collective-permute-done((bf16[128,1536]{1,0:T(8,128)(2,1)}, bf16[128,1536]{1,0:T(8,128)(2,1)S(1)}, u32[]{:S(2)}, u32[]{:S(2)}) %collective-permute-start.24) | collective-permute-done | bytes 393248 | tf_op jit(solution)/shard_map/ppermute | solution.py:303
  361.0 14.2 %collective-permute-start.28 = (bf16[128,512]{1,0:T(8,128)(2,1)S(1)}, bf16[128,512]{1,0:T(8,128)(2,1)S(1)}, u32[]{:S(2)}, u32[]{:S(2)}) collective-permute-start(bf16[128,512]{1,0:T(8,128)(2,1)S(1)} %pad_maximum_fusion.21), channel_id=1, source_target_pairs={{0,12},{4,0},{8,4},{12,8},{1,13},{5,1},{9,5},{13,9},{2,14},{6,2},{... | collective-permute-start | bytes 393224 | tf_op jit(solution)/shard_map/ppermute | solution.py:295
  381.5 14.0 %collective-permute-done.27 = bf16[128,512]{1,0:T(8,128)(2,1)S(1)} collective-permute-done((bf16[128,512]{1,0:T(8,128)(2,1)S(1)}, bf16[128,512]{1,0:T(8,128)(2,1)S(1)}, u32[]{:S(2)}, u32[]{:S(2)}) %collective-permute-start.27) | collective-permute-done | bytes 131104 | tf_op jit(solution)/shard_map/ppermute | solution.py:295
  423.4 14.6 %collective-permute-done.30.refs_6_ = bf16[128,1536]{1,0:T(8,128)(2,1)} collective-permute-done((bf16[128,1536]{1,0:T(8,128)(2,1)}, bf16[128,1536]{1,0:T(8,128)(2,1)}, u32[]{:S(2)}, u32[]{:S(2)}) %collective-permute-start.30) | collective-permute-done | bytes 393248 | tf_op jit(solution)/shard_map/ppermute | solution.py:295
  438.0 11.8 %shard_map.213 = (bf16[2,256,1536]{2,1,0:T(8,128)(2,1)}, f32[2,256,768]{2,1,0:T(8,128)}, f32[2,256,768]{2,1,0:T(8,128)}, bf16[2,256,1536]{2,1,0:T(8,128)(2,1)}, ...) custom-call(s32[4]{0:T(128)} %get-tuple-element.289.refs_0_, ...), custom_call_target="tpu_custom_call" | custom-call | flops 3623878656 | bytes 20447232 | tf_op jit(solution)/shard_map/pallas_call | solution.py:242
  449.8 13.1 %shard_map.214 = (bf16[2,256,1536]{2,1,0:T(8,128)(2,1)}, bf16[128,1664]{1,0:T(8,128)(2,1)}, bf16[128,1664]{1,0:T(8,128)(2,1)}, bf16[128,1664]{1,0:T(8,128)(2,1)}, bf16[128,1664]{1,0:T(8,128)(2,1)}) custom-call(s32[4]{0:T(128)} %get-tuple-element.289.refs_0_, s32[4,2,128]{2,1,0:T(2,128)} %get-tuple-element.281.refs_1_, ...), custom_call_target="tpu_custom_call" | custom-call | flops 3623878656 | bytes 20447232 | tf_op jit(solution)/shard_map/pallas_call | solution.py:261
  462.9 8.1 collective-permute-start.41
  475.7 5.9 collective-permute-done.41
  481.6 16.2 %collective-permute-done.40 = bf16[128,1664]{1,0:T(8,128)(2,1)} collective-permute-done((bf16[128,1664]{1,0:T(8,128)(2,1)}, bf16[128,1664]{1,0:T(8,128)(2,1)}, u32[]{:S(2)}, u32[]{:S(2)}) %collective-permute-start.40) | collective-permute-done | bytes 426016 | tf_op jit(solution)/shard_map/ppermute | solution.py:303
  522.7 22.3 %collective-permute-done.44 = bf16[1,512,1536]{2,1,0:T(8,128)(2,1)} collective-permute-done((bf16[1,512,1536]{2,1,0:T(8,128)(2,1)}, bf16[1,512,1536]{2,1,0:T(8,128)(2,1)}, u32[]{:S(2)}, u32[]{:S(2)}) %collective-permute-start.44) | collective-permute-done | bytes 1572896 | tf_op jit(solution)/shard_map/ppermute | solution.py:309
  549.7 9.7 collective-permute-start.34
  562.9 8.4 collective-permute-done.34
  571.2 13.7 %collective-permute-done.33 = bf16[128,1536]{1,0:T(8,128)(2,1)} collective-permute-done((bf16[128,1536]{1,0:T(8,128)(2,1)}, bf16[128,1536]{1,0:T(8,128)(2,1)}, u32[]{:S(2)}, u32[]{:S(2)}) %collective-permute-start.33) | collective-permute-done | bytes 393248 | tf_op jit(solution)/shard_map/ppermute | solution.py:303
  599.9 9.0 collective-permute-start.48
  632.1 6.8 collective-permute-done.49.refs_7_
  638.9 15.1 %collective-permute-done.50.refs_8_ = bf16[128,1536]{1,0:T(8,128)(2,1)S(1)} collective-permute-done((bf16[128,1536]{1,0:T(8,128)(2,1)S(1)}, bf16[128,1536]{1,0:T(8,128)(2,1)S(1)}, u32[]{:S(2)}, u32[]{:S(2)}) %collective-permute-start.50) | collective-permute-done | bytes 393248 | tf_op jit(solution)/shard_map/ppermute | solution.py:295
  654.8 31.2 %all-gather.16.cloned.1.call-done = bf16[1024,3072]{1,0:T(8,128)(2,1)} async-done(((bf16[256,3072]{1,0:T(8,128)(2,1)}), bf16[1024,3072]{1,0:T(8,128)(2,1)}) %all-gather.16.cloned.1.call-update) | async-done | bytes 6291472 | tf_op jit(solution)/shard_map/all_gather | solution.py:703
  685.9 13.2 %shard_map.215 = (bf16[2,256,1536]{2,1,0:T(8,128)(2,1)}, bf16[128,1664]{1,0:T(8,128)(2,1)}, bf16[128,1664]{1,0:T(8,128)(2,1)}, bf16[128,1664]{1,0:T(8,128)(2,1)}, bf16[128,1664]{1,0:T(8,128)(2,1)}) custom-call(s32[4]{0:T(128)} %get-tuple-element.290.refs_0_, s32[4,2,128]{2,1,0:T(2,128)} %get-tuple-element.282.refs_1_, ...), custom_call_target="tpu_custom_call" | custom-call | flops 3623878656 | bytes 20447232 | tf_op jit(solution)/shard_map/pallas_call | solution.py:261
  705.0 9.7 fusion.46
  714.7 6.9 fusion.48
  722.6 9.0 collective-permute-done.53
  753.1 8.2 collective-permute-done.73
  763.6 6.2 collective-permute-done.75
  778.0 9.7 collective-permute-start.79
  796.3 12.8 %collective-permute-done.78 = bf16[400,384]{1,0:T(8,128)(2,1)S(1)} collective-permute-done((bf16[400,384]{1,0:T(8,128)(2,1)S(1)}, bf16[400,384]{1,0:T(8,128)(2,1)S(1)}, u32[]{:S(2)}, u32[]{:S(2)}) %collective-permute-start.78) | collective-permute-done | bytes 307232 | tf_op jit(solution)/shard_map/ppermute | solution.py:303
  814.4 5.2 collective-permute-done.81
  823.8 29.0 %collective-permute-done.57 = bf16[1,512,1536]{2,1,0:T(8,128)(2,1)S(1)} collective-permute-done((bf16[1,512,1536]{2,1,0:T(8,128)(2,1)S(1)}, bf16[1,512,1536]{2,1,0:T(8,128)(2,1)S(1)}, u32[]{:S(2)}, u32[]{:S(2)}) %collective-permute-start.57) | collective-permute-done | bytes 1572896 | tf_op jit(solution)/shard_map/ppermute | solution.py:521
  853.1 7.1 collective-permute-start.61
  875.0 10.0 collective-permute-done.63
  891.2 14.7 %collective-permute-done.65 = bf16[256,512]{0,1:T(8,128)(2,1)} collective-permute-done((bf16[256,512]{0,1:T(8,128)(2,1)}, bf16[256,512]{0,1:T(8,128)(2,1)}, u32[]{:S(2)}, u32[]{:S(2)}) %collective-permute-start.65) | collective-permute-done | bytes 262176 | tf_op jit(solution)/shard_map/ppermute | solution.py:521
  917.8 8.2 collective-permute-done.69
  926.0 17.4 %collective-permute-done.68 = bf16[384,512]{1,0:T(8,128)(2,1)S(1)} collective-permute-done((bf16[384,512]{1,0:T(8,128)(2,1)S(1)}, bf16[384,512]{1,0:T(8,128)(2,1)S(1)}, u32[]{:S(2)}, u32[]{:S(2)}) %collective-permute-start.68) | collective-permute-done | bytes 393248 | tf_op jit(solution)/shard_map/ppermute | solution.py:303
  949.4 7.1 fusion.50
  956.5 11.8 %fusion.30 = bf16[1,1536,768]{2,1,0:T(8,128)(2,1)S(1)} fusion(bf16[2048,1536]{1,0:T(8,128)(2,1)} %bitcast.545, f32[2048,768]{1,0:T(8,128)} %fusion.50, f32[2048,768]{1,0:T(8,128)} %fusion.46), kind=kOutput, calls=%fused_computation.49 | convolution fusion | flops 4848746496 | bytes 21233664 | tf_op jit(solution)/shard_map/dot_general | solution.py:284
  968.4 13.2 %fusion.27 = bf16[1,1536,768]{2,1,0:T(8,128)(2,1)S(1)} fusion(bf16[2048,1536]{1,0:T(8,128)(2,1)S(1)} %bitcast.549, f32[2048,768]{1,0:T(8,128)} %fusion.46, f32[2048,768]{1,0:T(8,128)} %fusion.50, f32[2048,768]{1,0:T(8,128)} %fusion.48), kind=kOutput, calls=%fused_computation.48 | convolution fusion | flops 4866048000 | bytes 27525120 | tf_op jit(solution)/shard_map/dot_general | solution.py:284
  982.1 8.3 fusion.34
  991.4 7.5 collective-permute-done.72
  (769 shorter events, 361.2 us)
Async XLA Ops:
  7.2 112.6 %all-gather.8.cloned.1.call-start = ((), (), s32[]{:S(2)}) async-start(), calls=%async_computation | async-start | bytes 6893568 | tf_op jit(solution)/shard_map/all_gather | solution.py:556
  29.8 181.0 %all-gather.10.cloned.1.call-start = ((), (), s32[]{:S(2)}) async-start(), calls=%async_computation.1 | async-start | bytes 4866048 | tf_op jit(solution)/shard_map/all_gather | solution.py:557
  30.6 292.4 %all-gather.12.cloned.1.call-start = ((), (), s32[]{:S(2)}) async-start(), calls=%async_computation.2 | async-start | bytes 6893568 | tf_op jit(solution)/shard_map/all_gather | solution.py:556
  31.4 371.8 %all-gather.14.cloned.1.call-start = ((), (), s32[]{:S(2)}) async-start(), calls=%async_computation.3 | async-start | bytes 4866048 | tf_op jit(solution)/shard_map/all_gather | solution.py:557
  36.4 106.4 %collective-permute-start.11 = (bf16[1536,384]{1,0:T(8,128)(2,1)}, bf16[1536,384]{1,0:T(8,128)(2,1)S(1)}, u32[]{:S(2)}, u32[]{:S(2)}) collective-permute-start(bf16[1536,384]{1,0:T(8,128)(2,1)} %dynamic-slice_bitcast_fusion.2), channel_id=1, source_target_pairs={{0,16},{16,0},{1,17},{17,1},{2,18},{18,2},{3,19},{19,3},{4,20},{20... | collective-permute-start | bytes 3538952 | tf_op jit(solution)/shard_map/ppermute | solution.py:309
  39.6 130.5 %collective-permute-start.15 = (bf16[1536,384]{1,0:T(8,128)(2,1)}, bf16[1536,384]{1,0:T(8,128)(2,1)S(1)}, u32[]{:S(2)}, u32[]{:S(2)}) collective-permute-start(bf16[1536,384]{1,0:T(8,128)(2,1)} %dynamic-slice_bitcast_fusion.1), channel_id=1, source_target_pairs={{0,16},{16,0},{1,17},{17,1},{2,18},{18,2},{3,19},{19,3},{4,20},{20... | collective-permute-start | bytes 3538952 | tf_op jit(solution)/shard_map/ppermute | solution.py:309
  59.3 111.5 %collective-permute-start.19 = (bf16[384,1536]{1,0:T(8,128)(2,1)}, bf16[384,1536]{1,0:T(8,128)(2,1)}, u32[]{:S(2)}, u32[]{:S(2)}) collective-permute-start(bf16[384,1536]{1,0:T(8,128)(2,1)} %dynamic-slice_bitcast_fusion), channel_id=1, source_target_pairs={{0,16},{16,0},{1,17},{17,1},{2,18},{18,2},{3,19},{19,3},{4,20},{20... | collective-permute-start | bytes 3538952 | tf_op jit(solution)/shard_map/ppermute | solution.py:309
  60.7 105.4 %collective-permute-start.36 = (bf16[128,1536]{1,0:T(8,128)(2,1)S(1)}, bf16[128,1536]{1,0:T(8,128)(2,1)}, u32[]{:S(2)}, u32[]{:S(2)}) collective-permute-start(bf16[128,1536]{1,0:T(8,128)(2,1)S(1)} %dynamic-slice_bitcast_fusion.3.refs_6_), channel_id=1, source_target_pairs={{0,4},{4,8},{8,12},{12,0},{1,5},{5,9},{9,13},{13,1},{2,6},{6,10},{... | collective-permute-start | bytes 1179656 | tf_op jit(solution)/shard_map/ppermute | solution.py:295
  142.6 512.1 %all-gather.18.cloned.1.call-start = ((), (), s32[]{:S(2)}) async-start(), calls=%async_computation.5 | async-start | bytes 9437184 | tf_op jit(solution)/shard_map/all_gather | solution.py:702
  159.1 49.7 %collective-permute-start.12 = (bf16[1536,384]{1,0:T(8,128)(2,1)S(1)}, bf16[1536,384]{1,0:T(8,128)(2,1)}, u32[]{:S(2)}, u32[]{:S(2)}) collective-permute-start(bf16[1536,384]{1,0:T(8,128)(2,1)S(1)} %collective-permute-done.11.refs_11_.refs_13_), channel_id=1, source_target_pairs={{0,1},{1,0},{2,3},{3,2},{4,5},{5,4},{6,7},{7,6},{8,9},{9,8},{10,11... | collective-permute-start | bytes 3538952 | tf_op jit(solution)/shard_map/ppermute | solution.py:314
  159.1 50.2 %collective-permute-start.13 = (bf16[1536,384]{1,0:T(8,128)(2,1)S(1)}, bf16[1536,384]{1,0:T(8,128)(2,1)}, u32[]{:S(2)}, u32[]{:S(2)}) collective-permute-start(bf16[1536,384]{1,0:T(8,128)(2,1)S(1)} %collective-permute-done.11.refs_11_.refs_13_), channel_id=1, source_target_pairs={{0,2},{1,3},{2,0},{3,1},{4,6},{5,7},{6,4},{7,5},{8,10},{9,11},{10,... | collective-permute-start | bytes 3538952 | tf_op jit(solution)/shard_map/ppermute | solution.py:521
  166.1 31.5 %collective-permute-start.37 = (bf16[128,1536]{1,0:T(8,128)(2,1)S(1)}, bf16[128,1536]{1,0:T(8,128)(2,1)}, u32[]{:S(2)}, u32[]{:S(2)}) collective-permute-start(bf16[128,1536]{1,0:T(8,128)(2,1)S(1)} %dynamic-slice_bitcast_fusion.3.refs_6_), channel_id=1, source_target_pairs={{0,8},{4,12},{8,0},{12,4},{1,9},{5,13},{9,1},{13,5},{2,10},{6,14},... | collective-permute-start | bytes 1179656 | tf_op jit(solution)/shard_map/ppermute | solution.py:295
  170.2 53.0 %collective-permute-start.17 = (bf16[1536,384]{1,0:T(8,128)(2,1)S(1)}, bf16[1536,384]{1,0:T(8,128)(2,1)}, u32[]{:S(2)}, u32[]{:S(2)}) collective-permute-start(bf16[1536,384]{1,0:T(8,128)(2,1)S(1)} %collective-permute-done.15.refs_15_.refs_17_), channel_id=1, source_target_pairs={{0,2},{1,3},{2,0},{3,1},{4,6},{5,7},{6,4},{7,5},{8,10},{9,11},{10,... | collective-permute-start | bytes 3538952 | tf_op jit(solution)/shard_map/ppermute | solution.py:521
  170.8 83.2 %collective-permute-start.21 = (bf16[384,1536]{1,0:T(8,128)(2,1)}, bf16[384,1536]{1,0:T(8,128)(2,1)}, u32[]{:S(2)}, u32[]{:S(2)}) collective-permute-start(bf16[384,1536]{1,0:T(8,128)(2,1)} %collective-permute-done.19.refs_19_.refs_21_), channel_id=1, source_target_pairs={{0,2},{1,3},{2,0},{3,1},{4,6},{5,7},{6,4},{7,5},{8,10},{9,11},{10,... | collective-permute-start | bytes 3538952 | tf_op jit(solution)/shard_map/ppermute | solution.py:521
  208.8 45.4 %collective-permute-start.16 = (bf16[1536,384]{1,0:T(8,128)(2,1)S(1)}, bf16[1536,384]{1,0:T(8,128)(2,1)}, u32[]{:S(2)}, u32[]{:S(2)}) collective-permute-start(bf16[1536,384]{1,0:T(8,128)(2,1)S(1)} %collective-permute-done.15.refs_15_.refs_17_), channel_id=1, source_target_pairs={{0,1},{1,0},{2,3},{3,2},{4,5},{5,4},{6,7},{7,6},{8,9},{9,8},{10,11... | collective-permute-start | bytes 3538952 | tf_op jit(solution)/shard_map/ppermute | solution.py:314
  208.8 45.9 %collective-permute-start.20 = (bf16[384,1536]{1,0:T(8,128)(2,1)}, bf16[384,1536]{1,0:T(8,128)(2,1)}, u32[]{:S(2)}, u32[]{:S(2)}) collective-permute-start(bf16[384,1536]{1,0:T(8,128)(2,1)} %collective-permute-done.19.refs_19_.refs_21_), channel_id=1, source_target_pairs={{0,1},{1,0},{2,3},{3,2},{4,5},{5,4},{6,7},{7,6},{8,9},{9,8},{10,11... | collective-permute-start | bytes 3538952 | tf_op jit(solution)/shard_map/ppermute | solution.py:314
  209.3 47.0 %collective-permute-start.14 = (bf16[1536,384]{1,0:T(8,128)(2,1)}, bf16[1536,384]{1,0:T(8,128)(2,1)S(1)}, u32[]{:S(2)}, u32[]{:S(2)}) collective-permute-start(bf16[1536,384]{1,0:T(8,128)(2,1)} %collective-permute-done.13.refs_13_.refs_15_), channel_id=1, source_target_pairs={{0,1},{1,0},{2,3},{3,2},{4,5},{5,4},{6,7},{7,6},{8,9},{9,8},{10,11... | collective-permute-start | bytes 3538952 | tf_op jit(solution)/shard_map/ppermute | solution.py:314
  223.2 38.9 %collective-permute-start.18 = (bf16[1536,384]{1,0:T(8,128)(2,1)}, bf16[1536,384]{1,0:T(8,128)(2,1)S(1)}, u32[]{:S(2)}, u32[]{:S(2)}) collective-permute-start(bf16[1536,384]{1,0:T(8,128)(2,1)} %collective-permute-done.17.refs_17_.refs_19_), channel_id=1, source_target_pairs={{0,1},{1,0},{2,3},{3,2},{4,5},{5,4},{6,7},{7,6},{8,9},{9,8},{10,11... | collective-permute-start | bytes 3538952 | tf_op jit(solution)/shard_map/ppermute | solution.py:314
  254.7 44.2 %collective-permute-start.9 = (bf16[128,1536]{1,0:T(8,128)(2,1)S(1)}, bf16[128,1536]{1,0:T(8,128)(2,1)S(1)}, u32[]{:S(2)}, u32[]{:S(2)}) collective-permute-start(bf16[128,1536]{1,0:T(8,128)(2,1)S(1)} %multiply_convert_fusion.9.refs_4_), channel_id=1, source_target_pairs={{0,8},{4,12},{8,0},{12,4},{1,9},{5,13},{9,1},{13,5},{2,10},{6,14},... | collective-permute-start | bytes 1179656 | tf_op jit(solution)/shard_map/ppermute | solution.py:295
  256.3 42.6 %collective-permute-start.10 = (bf16[128,1536]{1,0:T(8,128)(2,1)S(1)}, bf16[128,1536]{1,0:T(8,128)(2,1)S(1)}, u32[]{:S(2)}, u32[]{:S(2)}) collective-permute-start(bf16[128,1536]{1,0:T(8,128)(2,1)S(1)} %multiply_convert_fusion.9.refs_4_), channel_id=1, source_target_pairs={{0,12},{4,0},{8,4},{12,8},{1,13},{5,1},{9,5},{13,9},{2,14},{6,2},{... | collective-permute-start | bytes 1179656 | tf_op jit(solution)/shard_map/ppermute | solution.py:295
  320.4 30.1 %collective-permute-start.24 = (bf16[128,1536]{1,0:T(8,128)(2,1)}, bf16[128,1536]{1,0:T(8,128)(2,1)S(1)}, u32[]{:S(2)}, u32[]{:S(2)}) collective-permute-start(bf16[128,1536]{1,0:T(8,128)(2,1)} %get-tuple-element.57), channel_id=1, source_target_pairs={{0,8},{4,12},{8,0},{12,4},{1,9},{5,13},{9,1},{13,5},{2,10},{6,14},... | collective-permute-start | bytes 1179656 | tf_op jit(solution)/shard_map/ppermute | solution.py:303
  321.7 28.8 %collective-permute-start.23 = (bf16[128,1536]{1,0:T(8,128)(2,1)}, bf16[128,1536]{1,0:T(8,128)(2,1)S(1)}, u32[]{:S(2)}, u32[]{:S(2)}) collective-permute-start(bf16[128,1536]{1,0:T(8,128)(2,1)} %get-tuple-element.56), channel_id=1, source_target_pairs={{0,12},{4,0},{8,4},{12,8},{1,13},{5,1},{9,5},{13,9},{2,14},{6,2},{... | collective-permute-start | bytes 1179656 | tf_op jit(solution)/shard_map/ppermute | solution.py:303
  376.8 44.3 %collective-permute-start.42 = (bf16[1,256,1536]{2,1,0:T(8,128)(2,1)}, bf16[1,256,1536]{2,1,0:T(8,128)(2,1)}, u32[]{:S(2)}, u32[]{:S(2)}) collective-permute-start(bf16[1,256,1536]{2,1,0:T(8,128)(2,1)} %constant_dynamic-slice_fusion.10), channel_id=1, source_target_pairs={{0,1},{1,0},{2,3},{3,2},{4,5},{5,4},{6,7},{7,6},{8,9},{9,8},{10,11... | collective-permute-start | bytes 2359304 | tf_op jit(solution)/shard_map/ppermute | solution.py:314
  407.9 30.1 %collective-permute-start.30 = (bf16[128,1536]{1,0:T(8,128)(2,1)}, bf16[128,1536]{1,0:T(8,128)(2,1)}, u32[]{:S(2)}, u32[]{:S(2)}) collective-permute-start(bf16[128,1536]{1,0:T(8,128)(2,1)} %multiply_convert_fusion.8.refs_4_), channel_id=1, source_target_pairs={{0,8},{4,12},{8,0},{12,4},{1,9},{5,13},{9,1},{13,5},{2,10},{6,14},... | collective-permute-start | bytes 1179656 | tf_op jit(solution)/shard_map/ppermute | solution.py:295
  408.2 29.8 %collective-permute-start.31 = (bf16[128,1536]{1,0:T(8,128)(2,1)}, bf16[128,1536]{1,0:T(8,128)(2,1)}, u32[]{:S(2)}, u32[]{:S(2)}) collective-permute-start(bf16[128,1536]{1,0:T(8,128)(2,1)} %multiply_convert_fusion.8.refs_4_), channel_id=1, source_target_pairs={{0,12},{4,0},{8,4},{12,8},{1,13},{5,1},{9,5},{13,9},{2,14},{6,2},{... | collective-permute-start | bytes 1179656 | tf_op jit(solution)/shard_map/ppermute | solution.py:295
  415.8 58.6 %collective-permute-start.45 = (bf16[128,3072]{1,0:T(8,128)(2,1)S(1)}, bf16[128,3072]{1,0:T(8,128)(2,1)S(1)}, u32[]{:S(2)}, u32[]{:S(2)}) collective-permute-start(bf16[128,3072]{1,0:T(8,128)(2,1)S(1)} %get-tuple-element.219), channel_id=1, source_target_pairs={{0,16},{16,0},{1,17},{17,1},{2,18},{18,2},{3,19},{19,3},{4,20},{20... | collective-permute-start | bytes 2359304 | tf_op jit(solution)/shard_map/ppermute | solution.py:309
  471.0 26.8 %collective-permute-start.40 = (bf16[128,1664]{1,0:T(8,128)(2,1)}, bf16[128,1664]{1,0:T(8,128)(2,1)}, u32[]{:S(2)}, u32[]{:S(2)}) collective-permute-start(bf16[128,1664]{1,0:T(8,128)(2,1)} %get-tuple-element.73), channel_id=1, source_target_pairs={{0,8},{4,12},{8,0},{12,4},{1,9},{5,13},{9,1},{13,5},{2,10},{6,14},... | collective-permute-start | bytes 1277960 | tf_op jit(solution)/shard_map/ppermute | solution.py:303
  471.0 27.0 %collective-permute-start.39 = (bf16[128,1664]{1,0:T(8,128)(2,1)}, bf16[128,1664]{1,0:T(8,128)(2,1)}, u32[]{:S(2)}, u32[]{:S(2)}) collective-permute-start(bf16[128,1664]{1,0:T(8,128)(2,1)} %get-tuple-element.72), channel_id=1, source_target_pairs={{0,12},{4,0},{8,4},{12,8},{1,13},{5,1},{9,5},{13,9},{2,14},{6,2},{... | collective-permute-start | bytes 1277960 | tf_op jit(solution)/shard_map/ppermute | solution.py:303
  474.4 31.0 %collective-permute-start.43 = (bf16[1,256,1536]{2,1,0:T(8,128)(2,1)}, bf16[1,256,1536]{2,1,0:T(8,128)(2,1)}, u32[]{:S(2)}, u32[]{:S(2)}) collective-permute-start(bf16[1,256,1536]{2,1,0:T(8,128)(2,1)} %constant_dynamic-slice_fusion.9), channel_id=1, source_target_pairs={{0,1},{1,0},{2,3},{3,2},{4,5},{5,4},{6,7},{7,6},{8,9},{9,8},{10,11... | collective-permute-start | bytes 2359304 | tf_op jit(solution)/shard_map/ppermute | solution.py:314
  508.6 36.3 %collective-permute-start.44 = (bf16[1,512,1536]{2,1,0:T(8,128)(2,1)}, bf16[1,512,1536]{2,1,0:T(8,128)(2,1)}, u32[]{:S(2)}, u32[]{:S(2)}) collective-permute-start(bf16[1,512,1536]{2,1,0:T(8,128)(2,1)} %broadcast_select_fusion.2), channel_id=1, source_target_pairs={{0,16},{16,0},{1,17},{17,1},{2,18},{18,2},{3,19},{19,3},{4,20},{20... | collective-permute-start | bytes 4718600 | tf_op jit(solution)/shard_map/ppermute | solution.py:309
  549.1 136.8 %all-gather.16.cloned.1.call-start = ((), (), s32[]{:S(2)}) async-start(), calls=%async_computation.4 | async-start | bytes 7864320 | tf_op jit(solution)/shard_map/all_gather | solution.py:703
  559.4 25.5 %collective-permute-start.33 = (bf16[128,1536]{1,0:T(8,128)(2,1)}, bf16[128,1536]{1,0:T(8,128)(2,1)}, u32[]{:S(2)}, u32[]{:S(2)}) collective-permute-start(bf16[128,1536]{1,0:T(8,128)(2,1)} %get-tuple-element.61), channel_id=1, source_target_pairs={{0,8},{4,12},{8,0},{12,4},{1,9},{5,13},{9,1},{13,5},{2,10},{6,14},... | collective-permute-start | bytes 1179656 | tf_op jit(solution)/shard_map/ppermute | solution.py:303
  561.3 23.6 %collective-permute-start.32 = (bf16[128,1536]{1,0:T(8,128)(2,1)}, bf16[128,1536]{1,0:T(8,128)(2,1)}, u32[]{:S(2)}, u32[]{:S(2)}) collective-permute-start(bf16[128,1536]{1,0:T(8,128)(2,1)} %get-tuple-element.60), channel_id=1, source_target_pairs={{0,12},{4,0},{8,4},{12,8},{1,13},{5,1},{9,5},{13,9},{2,14},{6,2},{... | collective-permute-start | bytes 1179656 | tf_op jit(solution)/shard_map/ppermute | solution.py:303
  562.9 67.1 %collective-permute-start.56 = (bf16[1,256,1536]{2,1,0:T(8,128)(2,1)}, bf16[1,256,1536]{2,1,0:T(8,128)(2,1)}, u32[]{:S(2)}, u32[]{:S(2)}) collective-permute-start(bf16[1,256,1536]{2,1,0:T(8,128)(2,1)} %constant_dynamic-slice_fusion.7), channel_id=1, source_target_pairs={{0,1},{1,0},{2,3},{3,2},{4,5},{5,4},{6,7},{7,6},{8,9},{9,8},{10,11... | collective-permute-start | bytes 2359304 | tf_op jit(solution)/shard_map/ppermute | solution.py:314
  627.5 26.5 %collective-permute-start.50 = (bf16[128,1536]{1,0:T(8,128)(2,1)S(1)}, bf16[128,1536]{1,0:T(8,128)(2,1)S(1)}, u32[]{:S(2)}, u32[]{:S(2)}) collective-permute-start(bf16[128,1536]{1,0:T(8,128)(2,1)S(1)} %fusion.93.refs_6_), channel_id=1, source_target_pairs={{0,8},{4,12},{8,0},{12,4},{1,9},{5,13},{9,1},{13,5},{2,10},{6,14},... | collective-permute-start | bytes 1179656 | tf_op jit(solution)/shard_map/ppermute | solution.py:295
  629.3 25.5 %collective-permute-start.51 = (bf16[128,1536]{1,0:T(8,128)(2,1)S(1)}, bf16[128,1536]{1,0:T(8,128)(2,1)}, u32[]{:S(2)}, u32[]{:S(2)}) collective-permute-start(bf16[128,1536]{1,0:T(8,128)(2,1)S(1)} %fusion.93.refs_6_), channel_id=1, source_target_pairs={{0,12},{4,0},{8,4},{12,8},{1,13},{5,1},{9,5},{13,9},{2,14},{6,2},{... | collective-permute-start | bytes 1179656 | tf_op jit(solution)/shard_map/ppermute | solution.py:295
  699.2 23.5 %collective-permute-start.54 = (bf16[128,1664]{1,0:T(8,128)(2,1)}, bf16[128,1664]{1,0:T(8,128)(2,1)S(1)}, u32[]{:S(2)}, u32[]{:S(2)}) collective-permute-start(bf16[128,1664]{1,0:T(8,128)(2,1)} %get-tuple-element.91), channel_id=1, source_target_pairs={{0,4},{4,8},{8,12},{12,0},{1,5},{5,9},{9,13},{13,1},{2,6},{6,10},{... | collective-permute-start | bytes 1277960 | tf_op jit(solution)/shard_map/ppermute | solution.py:303
  700.7 30.9 %collective-permute-start.53 = (bf16[128,1664]{1,0:T(8,128)(2,1)}, bf16[128,1664]{1,0:T(8,128)(2,1)S(1)}, u32[]{:S(2)}, u32[]{:S(2)}) collective-permute-start(bf16[128,1664]{1,0:T(8,128)(2,1)} %get-tuple-element.90), channel_id=1, source_target_pairs={{0,8},{4,12},{8,0},{12,4},{1,9},{5,13},{9,1},{13,5},{2,10},{6,14},... | collective-permute-start | bytes 1277960 | tf_op jit(solution)/shard_map/ppermute | solution.py:303
  703.1 28.5 %collective-permute-start.52 = (bf16[128,1664]{1,0:T(8,128)(2,1)}, bf16[128,1664]{1,0:T(8,128)(2,1)S(1)}, u32[]{:S(2)}, u32[]{:S(2)}) collective-permute-start(bf16[128,1664]{1,0:T(8,128)(2,1)} %get-tuple-element.89), channel_id=1, source_target_pairs={{0,12},{4,0},{8,4},{12,8},{1,13},{5,1},{9,5},{13,9},{2,14},{6,2},{... | collective-permute-start | bytes 1277960 | tf_op jit(solution)/shard_map/ppermute | solution.py:303
  722.6 67.9 %collective-permute-start.55 = (bf16[1,256,1536]{2,1,0:T(8,128)(2,1)}, bf16[1,256,1536]{2,1,0:T(8,128)(2,1)}, u32[]{:S(2)}, u32[]{:S(2)}) collective-permute-start(bf16[1,256,1536]{2,1,0:T(8,128)(2,1)} %constant_dynamic-slice_fusion.8), channel_id=1, source_target_pairs={{0,1},{1,0},{2,3},{3,2},{4,5},{5,4},{6,7},{7,6},{8,9},{9,8},{10,11... | collective-permute-start | bytes 2359304 | tf_op jit(solution)/shard_map/ppermute | solution.py:314
  810.6 42.2 %collective-permute-start.57 = (bf16[1,512,1536]{2,1,0:T(8,128)(2,1)S(1)}, bf16[1,512,1536]{2,1,0:T(8,128)(2,1)S(1)}, u32[]{:S(2)}, u32[]{:S(2)}) collective-permute-start(bf16[1,512,1536]{2,1,0:T(8,128)(2,1)S(1)} %get-tuple-element.202), channel_id=1, source_target_pairs={{0,2},{1,3},{2,0},{3,1},{4,6},{5,7},{6,4},{7,5},{8,10},{9,11},{10,... | collective-permute-start | bytes 4718600 | tf_op jit(solution)/shard_map/ppermute | solution.py:521
  812.2 40.8 %collective-permute-start.58 = (bf16[1,512,1536]{2,1,0:T(8,128)(2,1)S(1)}, bf16[1,512,1536]{2,1,0:T(8,128)(2,1)}, u32[]{:S(2)}, u32[]{:S(2)}) collective-permute-start(bf16[1,512,1536]{2,1,0:T(8,128)(2,1)S(1)} %get-tuple-element.201), channel_id=1, source_target_pairs={{0,16},{16,0},{1,17},{17,1},{2,18},{18,2},{3,19},{19,3},{4,20},{20... | collective-permute-start | bytes 4718600 | tf_op jit(solution)/shard_map/ppermute | solution.py:309
  862.6 82.7 %collective-permute-start.83 = (bf16[1,512,1536]{2,1,0:T(8,128)(2,1)}, bf16[1,512,1536]{2,1,0:T(8,128)(2,1)}, u32[]{:S(2)}, u32[]{:S(2)}) collective-permute-start(bf16[1,512,1536]{2,1,0:T(8,128)(2,1)} %collective-permute-done.58), channel_id=1, source_target_pairs={{0,2},{1,3},{2,0},{3,1},{4,6},{5,7},{6,4},{7,5},{8,10},{9,11},{10,... | collective-permute-start | bytes 4718600 | tf_op jit(solution)/shard_map/ppermute | solution.py:521
  888.3 28.5 %collective-permute-start.62 = (bf16[128,1536]{1,0:T(8,128)(2,1)S(1)}, bf16[128,1536]{1,0:T(8,128)(2,1)S(1)}, u32[]{:S(2)}, u32[]{:S(2)}) collective-permute-start(bf16[128,1536]{1,0:T(8,128)(2,1)S(1)} %get-tuple-element.179), channel_id=1, source_target_pairs={{0,16},{16,0},{1,17},{17,1},{2,18},{18,2},{3,19},{19,3},{4,20},{20... | collective-permute-start | bytes 1179656 | tf_op jit(solution)/shard_map/ppermute | solution.py:309
  913.8 29.5 %collective-permute-start.68 = (bf16[384,512]{1,0:T(8,128)(2,1)S(1)}, bf16[384,512]{1,0:T(8,128)(2,1)S(1)}, u32[]{:S(2)}, u32[]{:S(2)}) collective-permute-start(bf16[384,512]{1,0:T(8,128)(2,1)S(1)} %get-tuple-element.217), channel_id=1, source_target_pairs={{0,8},{4,12},{8,0},{12,4},{1,9},{5,13},{9,1},{13,5},{2,10},{6,14},... | collective-permute-start | bytes 1179656 | tf_op jit(solution)/shard_map/ppermute | solution.py:303
  915.0 28.4 %collective-permute-start.67 = (bf16[384,512]{1,0:T(8,128)(2,1)S(1)}, bf16[384,512]{1,0:T(8,128)(2,1)S(1)}, u32[]{:S(2)}, u32[]{:S(2)}) collective-permute-start(bf16[384,512]{1,0:T(8,128)(2,1)S(1)} %get-tuple-element.215), channel_id=1, source_target_pairs={{0,12},{4,0},{8,4},{12,8},{1,13},{5,1},{9,5},{13,9},{2,14},{6,2},{... | collective-permute-start | bytes 1179656 | tf_op jit(solution)/shard_map/ppermute | solution.py:303
  943.8 47.6 %collective-permute-start.70 = (bf16[384,512]{1,0:T(8,128)(2,1)S(1)}, bf16[384,512]{1,0:T(8,128)(2,1)S(1)}, u32[]{:S(2)}, u32[]{:S(2)}) collective-permute-start(bf16[384,512]{1,0:T(8,128)(2,1)S(1)} %get-tuple-element.176), channel_id=1, source_target_pairs={{0,1},{1,0},{2,3},{3,2},{4,5},{5,4},{6,7},{7,6},{8,9},{9,8},{10,11... | collective-permute-start | bytes 1179656 | tf_op jit(solution)/shard_map/ppermute | solution.py:314
  943.9 47.0 %collective-permute-start.71 = (bf16[384,512]{1,0:T(8,128)(2,1)S(1)}, bf16[384,512]{1,0:T(8,128)(2,1)S(1)}, u32[]{:S(2)}, u32[]{:S(2)}) collective-permute-start(bf16[384,512]{1,0:T(8,128)(2,1)S(1)} %get-tuple-element.176), channel_id=1, source_target_pairs={{0,2},{1,3},{2,0},{3,1},{4,6},{5,7},{6,4},{7,5},{8,10},{9,11},{10,... | collective-permute-start | bytes 1179656 | tf_op jit(solution)/shard_map/ppermute | solution.py:521
  (204 other events, 2939.9 us)
Sparse Core Ops, SparseCore 0:
  29.9 89.8 all-gather.7
  123.3 75.7 all-gather.9
  201.9 97.6 all-gather.11
  302.4 94.4 all-gather.13
  549.2 88.7 all-gather.17
  639.5 46.3 all-gather.15

commit v2 on v1

--- a/solution.py
+++ b/solution.py
@@ -53,6 +53,15 @@
     rows = slots_ref.shape[2]
     place = lax.broadcasted_iota(jnp.int32, (capacity, rows), 0)
     return place == slots_ref[block, step : step + 1, :]
+
+
+def route_mask(tile, at, top):
+    lane = lax.broadcasted_iota(jnp.int32, tile.shape, 1).astype(F32)
+    named = tile.astype(F32)
+    hit = lane == named[:, at : at + 1]
+    for k in range(1, top):
+        hit = hit | (lane == named[:, at + k : at + k + 1])
+    return jnp.where(hit, 1.0, 0.0)
 
 
 def weight_copies(scalars, own, pieces, buffers, sems):
@@ -92,12 +101,12 @@
     return out
 
 
-def moe_fwd_kernel(folds, local, parts, capacity, *refs):
-    (scalars, slots, mask, router), blocks, own, flat, outs, partials, scratch = split_refs(
-        refs, (4, folds, 3, 3 * local * parts, 5, folds, 4)
+def moe_fwd_kernel(folds, local, parts, capacity, routes_at, top, *refs):
+    (scalars, router), tiles, blocks, own, flat, outs, partials, scratch = split_refs(
+        refs, (2, folds, folds, 3, 3 * local * parts, 7, folds, 4)
     )
     scalars_ref = scalars
-    picked_ref, gate_ref, up_ref, made_ref, grows_ref = outs
+    picked_ref, gate_ref, up_ref, made_ref, grows_ref, slots, mix_ref = outs
     buf_g, buf_u, buf_d, sems = scratch
     pieces = [
         [[flat[(kind * local + step) * parts + part] for part in range(parts)] for step in range(local)]
@@ -107,8 +116,26 @@
     rows = blocks[0].shape[0]
     width = blocks[0].shape[1]
     ff = buf_g.shape[3]
+    square = (rows, rows)
+    earlier = jnp.where(
+        lax.broadcasted_iota(jnp.int32, square, 0) < lax.broadcasted_iota(jnp.int32, square, 1), 1.0, 0.0
+    ).astype(BF16)
+    same = jnp.where(
+        lax.broadcasted_iota(jnp.int32, square, 0) == lax.broadcasted_iota(jnp.int32, square, 1), 1.0, 0.0
+    ).astype(BF16)
     for k in range(folds):
-        mix = masked_mix(dot(blocks[k][...], router[...]), mask[k])
+        mask = route_mask(tiles[k][...], routes_at, top)
+        mix = masked_mix(dot(blocks[k][...], router[...]), mask)
+        if k == 0:
+            mix_ref[...] = mix
+        low = mask.astype(BF16)
+        rank = dot_tn(low, earlier)
+        named = dot_tn(low, same)
+        place = jnp.where(named > 0.5, rank, -1.0)
+        number = lax.broadcasted_iota(jnp.int32, place.shape, 0)
+        for step in range(local):
+            row = jnp.sum(jnp.where(number == scalars_ref[2 + step], place, 0.0), axis=0, keepdims=True)
+            slots[k, step : step + 1, :] = row.astype(jnp.int32)
         for step in range(local):
             pick = one_hot(slots, k, step, capacity)
             at = pl.ds(k * capacity, capacity)
@@ -230,7 +257,9 @@
     )
 
 
-def moe_fwd_call(scalars, slots, mask, router, blocks, own, flat, folds, local, rows, parts, width, ff, capacity):
+def moe_fwd_call(
+    scalars, tiles, routes_at, router, blocks, own, flat, folds, local, rows, parts, width, ff, capacity, top
+):
     picked_rows = folds * capacity
     shapes = [
         jax.ShapeDtypeStruct((local, picked_rows, width), BF16),
@@ -238,22 +267,24 @@
         jax.ShapeDtypeStruct((local, picked_rows, ff), F32),
         jax.ShapeDtypeStruct((local, picked_rows, width), BF16),
         jax.ShapeDtypeStruct((local, picked_rows, LANES), F32),
+        jax.ShapeDtypeStruct((folds, local, rows), jnp.int32),
+        jax.ShapeDtypeStruct((rows, LANES), F32),
     ] + [jax.ShapeDtypeStruct((rows, width), BF16)] * folds
     out = pl.pallas_call(
-        functools.partial(moe_fwd_kernel, folds, local, parts, capacity),
+        functools.partial(moe_fwd_kernel, folds, local, parts, capacity, routes_at, top),
         out_shape=shapes,
         in_specs=[pl.BlockSpec(memory_space=pltpu.SMEM)]
-        + vmem(3 + folds) + anywhere(3 + len(flat)),
+        + vmem(1 + 2 * folds) + anywhere(3 + len(flat)),
         out_specs=vmem(len(shapes)),
         scratch_shapes=weight_scratch(own, local, parts),
         cost_estimate=cost(local * picked_rows, width, ff, 3),
         compiler_params=pltpu.CompilerParams(vmem_limit_bytes=56 << 20),
-    )(scalars, slots, mask, router, *blocks, *own, *flat)
-    return out[:5], out[5:]
-
-
-def moe_bwd_call(scalars, slots, kept, blocks, own, flat, folds, local, rows, parts, width, ff, capacity):
-    _, gate_pre, up_pre, made, gate_rows = kept
+    )(scalars, router, *tiles, *blocks, *own, *flat)
+    return out[:7], out[7:]
+
+
+def moe_bwd_call(scalars, kept, blocks, own, flat, folds, local, rows, parts, width, ff, capacity, top):
+    _, gate_pre, up_pre, made, gate_rows, slots, _ = kept
     picked_rows = folds * capacity
     shapes = [jax.ShapeDtypeStruct((local, picked_rows, width), BF16)] + [
         jax.ShapeDtypeStruct((rows, width + LANES), BF16)
@@ -280,6 +311,13 @@
     return lax.dot_general(a, b, (((1,), (1,)), ((), ())), preferred_element_type=F32)
 
 
+def mm_shares(a, shares):
+    if shares.ndim == 2:
+        return mm_nt(a, shares)
+    width = shares.shape[2]
+    return sum(mm_nt(a[:, j * width : (j + 1) * width], shares[j]) for j in range(shares.shape[0]))
+
+
 def mm_tn(a, b):
     return lax.dot_general(a, b, (((0,), (0,)), ((), ())), preferred_element_type=F32)
 
@@ -305,6 +343,20 @@
     return total
 
 
+def send_back(parts):
+    folds = lax.axis_size(F_AX)
+    return [parts[0]] + [
+        lax.ppermute(parts[k], F_AX, [(i, (i - k) % folds) for i in range(folds)]) for k in range(1, folds)
+    ]
+
+
+def add_up(parts):
+    total = parts[0].astype(F32)
+    for part in parts[1:]:
+        total = total + part.astype(F32)
+    return total
+
+
 def swap_section(value):
     return lax.ppermute(value, S_AX, [(0, 1), (1, 0)])
 
@@ -339,20 +391,20 @@
     return jax.nn.gelu(gate) * up
 
 
-def attention_in(hidden, gain, w_qkv, common, kv_width):
-    cos, sin = common["cos"], common["sin"]
-    rows, width = hidden.shape
-    q_width = w_qkv.shape[1] - 2 * kv_width
+def attention_in(hidden, gain):
     scale = lax.rsqrt(jnp.mean(hidden * hidden, axis=1, keepdims=True) + EPS)
     normed = hidden * scale
-    attn_in = (normed * gain.astype(F32)).astype(BF16)
-    lin = mm(attn_in, w_qkv)
+    return scale, normed, (normed * gain.astype(F32)).astype(BF16)
+
+
+def turn_heads(lin, common, kv_width):
+    rows = lin.shape[0]
+    q_width = lin.shape[1] - 2 * kv_width
     turned = rope_turn(
-        lin[:, : q_width + kv_width].reshape(rows, -1, HEAD), cos, sin
+        lin[:, : q_width + kv_width].astype(F32).reshape(rows, -1, HEAD), common["cos"], common["sin"]
     ).astype(BF16).reshape(rows, -1)
-    query = turned[:, :q_width]
     kv = jnp.concatenate([turned[:, q_width:], lin[:, q_width + kv_width :].astype(BF16)], axis=1)
-    return dict(scale=scale, normed=normed, attn_in=attn_in, query=query, kv=kv)
+    return turned[:, :q_width], kv
 
 
 def grouped_heads(value, groups):
@@ -394,63 +446,79 @@
     return grad_query, grad_kv
 
 
-def moe_forward(moe_in, router, mask, slots, scalars, experts_w, size):
+def moe_forward(router, tiles, routes_at, scalars, experts_w, size, blocks):
     outs, partials = moe_fwd_call(
-        scalars, slots, mask, router, rel_gather(moe_in), *experts_w, **size
-    )
-    return rel_scatter(partials), outs
-
-
-def moe_backward(grad_low, kept, slots, scalars, experts_w, size, tie, send_rows):
-    blocks, tied = lax.optimization_barrier((rel_gather(grad_low), tie))
-    grad_expert, partials = moe_bwd_call(scalars, slots, kept, blocks, *experts_w, **size)
-    sent = send_rows(grad_expert)
-    summed = rel_scatter(partials)
-    width = grad_low.shape[1]
+        scalars, tiles, routes_at, router, blocks, *experts_w, **size
+    )
+    return partials, outs
+
+
+def moe_backward(blocks, kept, scalars, experts_w, size, tie, hooks):
+    blocks, tied = lax.optimization_barrier((blocks, tie))
+    grad_expert, partials = moe_bwd_call(scalars, kept, blocks, *experts_w, **size)
+    sent = hooks["rows"](grad_expert)
+    summed, sent = lax.optimization_barrier((rel_scatter(partials), sent))
+    width = blocks[0].shape[1]
     tail = summed[:, width:]
     half = LANES // 2
     dots = tail[:, :half] + tail[:, half:]
     return summed[:, :width], jnp.pad(dots, ((0, 0), (0, half))), sent, tied
 
 
-def layer_forward(layer_in, weights, experts_w, common, mask, slots, scalars):
+def layer_forward(layer_in, weights, experts_w, common, tiles, routes_at, scalars, tie, projected=None, out_product=None):
     gains, w_qkv, w_out, router = weights
     groups = common["groups"]
     hidden = layer_in.astype(F32)
-    kept = attention_in(hidden, gains[0], w_qkv, common, groups * HEAD)
-    kv_all = jnp.concatenate(rel_gather(kept["kv"]), axis=0)
-    mixed, probs = attend(kept["query"], kv_all, common["allowed"], groups)
+    scale, normed, attn_in = attention_in(hidden, gains[0])
+    lin = mm(attn_in, w_qkv) if projected is None else projected
+    lin, tied_lin = lax.optimization_barrier((lin, tie.get("lin", ())))
+    query, kv = turn_heads(lin, common, groups * HEAD)
+    kv_all, tied_kv = lax.optimization_barrier(
+        (jnp.concatenate(rel_gather(kv), axis=0), tie.get("kv", ()))
+    )
+    mixed, probs = attend(query, kv_all, common["allowed"], groups)
     mixed_low = mixed.astype(BF16)
-    residual = hidden + mm(mixed_low, w_out)
+    more = tie["mixed"](tied_lin, tied_kv, attn_in, mixed_low) if "mixed" in tie else ()
+    mixed_low, more = lax.optimization_barrier((mixed_low, more))
+    if out_product is None:
+        residual = hidden + mm(mixed_low, w_out)
+    else:
+        residual = hidden + out_product(mixed_low).astype(F32)
     scale_two = lax.rsqrt(jnp.mean(residual * residual, axis=1, keepdims=True) + EPS)
     normed_two = residual * scale_two
     moe_in = (normed_two * gains[1].astype(F32)).astype(BF16)
-    mix = masked_mix(mm(moe_in, router), mask[0])
-    summed, moe_kept = moe_forward(moe_in, router, mask, slots, scalars, experts_w, common["size"])
-    out = (residual + summed).astype(BF16)
-    kept.update(
+    if "moe" in tie:
+        moe_in, experts_w, more = tie["moe"](moe_in, experts_w, more)
+    blocks, tied = lax.optimization_barrier((rel_gather(moe_in), more))
+    parts, moe_kept = moe_forward(router, tiles, routes_at, scalars, experts_w, common["size"], blocks)
+    finish = lambda got: (residual + add_up(got)).astype(BF16)
+    out = finish(send_back(parts)) if "last" not in tie else (parts, finish)
+    kept = dict(
+        scale=scale, normed=normed, attn_in=attn_in, query=query, kv=kv,
         kv_all=kv_all, mixed=mixed, probs=probs, mixed_low=mixed_low, scale_two=scale_two,
-        normed_two=normed_two, moe_in=moe_in, mix=mix, moe=moe_kept,
-    )
-    return out, kept
-
-
-def layer_backward(grad_low, kept, weights, experts_w, common, slots, scalars, tie, late_tie, send_rows):
+        normed_two=normed_two, moe_in=moe_in, mix=moe_kept[6], moe=moe_kept,
+    )
+    return out, kept, experts_w, tied
+
+
+def layer_backward(grad_low, kept, weights, experts_w, common, scalars, tie, hooks):
     gains, w_qkv, w_out, router = weights
     groups = common["groups"]
     grad_out = grad_low.astype(F32)
     rows = grad_out.shape[0]
+    blocks = hooks["blocks"] if "blocks" in hooks else rel_gather(grad_low)
     grad_moe_in, dots, sent, tied = moe_backward(
-        grad_low, kept["moe"], slots, scalars, experts_w, common["size"], tie, send_rows
+        blocks, kept["moe"], scalars, experts_w, common["size"], tie, hooks
     )
     mix = kept["mix"]
     grad_logits = mix * (dots - jnp.sum(mix * dots, axis=1, keepdims=True))
     moe_in = kept["moe_in"]
     count = common["experts"]
-    grad_router = lax.dot_general(
-        grad_logits[:, :count], moe_in.astype(F32), (((0,), (0,)), ((), ())), precision=HIGHEST
-    )
-    grad_moe_in = grad_moe_in + jnp.dot(grad_logits, router.astype(F32).T, precision=HIGHEST)
+    high = grad_logits.astype(BF16)
+    rest = (grad_logits - high.astype(F32)).astype(BF16)
+    both = mm_tn(jnp.concatenate([high[:, :count], rest[:, :count]], axis=1), moe_in)
+    grad_router = both[:count] + both[count:]
+    grad_moe_in = grad_moe_in + mm_nt(high, router) + mm_nt(rest, router)
     normed_two = kept["normed_two"]
     grad_norm = grad_moe_in * gains[1].astype(F32)
     grad_gain_two = jnp.sum(grad_moe_in * normed_two, axis=0)
@@ -458,12 +526,16 @@
         grad_norm - normed_two * jnp.mean(grad_norm * normed_two, axis=1, keepdims=True)
     )
     grad_attn = grad_mid.astype(BF16)
-    grad_mixed = mm_nt(grad_attn, w_out).astype(BF16)
+    small = jnp.concatenate([grad_router, grad_gain_two[None]], axis=0).astype(BF16)
+    crossed = hooks["attn"](grad_attn, small, sent)
+    grad_mixed = mm_shares(grad_attn, w_out).astype(BF16)
     grad_query, grad_kv = attend_back(
         grad_mixed, kept["mixed"], kept["probs"], kept["query"], kept["kv_all"], groups
     )
-    grad_kv, late_tied, sent = lax.optimization_barrier((grad_kv, late_tie, sent))
+    grad_kv, crossed = lax.optimization_barrier((grad_kv, crossed))
+    later = hooks["later"](sent, crossed)
     own = rel_scatter([grad_kv[k * rows : (k + 1) * rows] for k in range(lax.axis_size(F_AX))])
+    own, later = lax.optimization_barrier((own, later))
     cos, sin = common["cos"], common["sin"]
     kv_width = groups * HEAD
     grad_lin = jnp.concatenate(
@@ -474,26 +546,23 @@
         ],
         axis=1,
     ).astype(BF16)
-    grad_attn_in = mm_nt(grad_lin, w_qkv)
+    grad_attn_in = mm_shares(grad_lin, w_qkv)
     normed = kept["normed"]
     grad_norm = grad_attn_in * gains[0].astype(F32)
     grad_in = grad_mid + kept["scale"] * (
         grad_norm - normed * jnp.mean(grad_norm * normed, axis=1, keepdims=True)
     )
-    small = jnp.concatenate([grad_router, grad_gain_two[None]], axis=0)
-    return grad_in.astype(BF16), grad_attn, grad_lin, small.astype(BF16), sent, tied, late_tied
-
-
-def expert_grads(rows_in, grad_rows, gate_w, up_w, down_w):
-    gate_pre = mm(rows_in, gate_w)
+    return grad_in.astype(BF16), grad_lin, later, tied
+
+
+def expert_middle(rows_in, grad_rows, gate_w, up_w, down_w):
+    value, slope = gelu_parts(mm(rows_in, gate_w))
     up_pre = mm(rows_in, up_w)
-    inner, back = jax.vjp(gated, gate_pre, up_pre)
-    grad_gate, grad_up = back(mm_nt(grad_rows, down_w))
-    grad_gate, grad_up = grad_gate.astype(BF16), grad_up.astype(BF16)
+    grad_inner = mm_nt(grad_rows, down_w)
     return (
-        mm_tn(rows_in, grad_gate).astype(BF16),
-        mm_tn(rows_in, grad_up).astype(BF16),
-        mm_tn(inner.astype(BF16), grad_rows).astype(BF16),
+        (value * up_pre).astype(BF16),
+        (grad_inner * up_pre * slope).astype(BF16),
+        (grad_inner * value).astype(BF16),
     )
 
 
@@ -505,6 +574,7 @@
     fold_id = lax.axis_index(F_AX)
     replica = lax.axis_index(R_AX)
     core = replica % 2
+    flip = (replica // 2) % 2
     folds, replicas = lax.axis_size(F_AX), lax.axis_size(R_AX)
     rows = tokens.shape[2]
     top = routes.shape[4]
@@ -520,57 +590,131 @@
     def swap_xor(value, bit):
         return lax.ppermute(value, R_AX, [(i, i ^ bit) for i in range(replicas)])
 
-    flat_routes = routes[0, :, 0].reshape(2, rows * top)
-    give = lax.dynamic_index_in_dim(flat_routes, 1 - section, 0, keepdims=False)
-    keep = own_batch(flat_routes)
-    got = swap_section(give)
-    pair = jnp.stack([jnp.where(is_first, keep, got), jnp.where(is_first, got, keep)])
-    mine = jnp.stack(rel_gather(pair), axis=1).reshape(2, folds, rows, top)
+    def own_layer(pair):
+        return jnp.where(is_first, pair[0], pair[1])
+
+    def other_layer(pair):
+        return jnp.where(is_first, pair[1], pair[0])
+
+    def by_section(keep, got):
+        return jnp.stack([jnp.where(is_first, keep, got), jnp.where(is_first, got, keep)])
+
+    def both_batches(pair):
+        return by_section(own_layer(pair), swap_section(other_layer(pair)))
+
+    split = q_width + 2 * kv_width
+    routes_at = HEAD // 4
+
+    def widened(pieces):
+        weights_part, routes_part = pieces
+        routes_part = jnp.pad(routes_part.astype(BF16), ((0, weights_part.shape[0] - rows), (0, 0)))
+        gap = jnp.zeros((weights_part.shape[0], routes_at - weights_part.shape[1]), BF16)
+        whole = jnp.concatenate([weights_part, gap, routes_part], axis=1)
+        return jnp.pad(whole, ((0, 0), (0, HEAD - whole.shape[1])))
+
+    small = jnp.concatenate([w_router[0], gains[0].T], axis=1)
+    my_routes = own_batch(routes[0, :, 0])
+    give_routes = lax.dynamic_index_in_dim(routes[0, :, 0], 1 - section, 0, keepdims=False)
+    joined = jnp.concatenate([w_query[0], w_key[0], w_value[0]], axis=1)
+    depth = joined.shape[0]
+
+    def column_share(value):
+        width = value.shape[1] // replicas
+        return lax.dynamic_slice_in_dim(value, replica * width, width, 1)
+
+    def stacked_parts(parts):
+        whole = jnp.zeros((folds,) + parts[0].shape, parts[0].dtype)
+        for k, part in enumerate(parts):
+            whole = lax.dynamic_update_index_in_dim(whole, part, (fold_id - k) % folds, 0)
+        return whole.reshape((-1,) + parts[0].shape[1:])
+
+    def stacked_rows(value):
+        return stacked_parts(rel_gather(value))
+
+    def of_first(value):
+        return jnp.where(is_first, value, swap_section(value))
+
+    def share_back(value):
+        whole = jnp.zeros(value.shape, value.dtype)
+        for bit in range(replicas):
+            got = value[bit] if bit == 0 else swap_xor(value[bit], bit)
+            whole = lax.dynamic_update_index_in_dim(whole, got, replica ^ bit, 0)
+        return jnp.concatenate([whole[j] for j in range(replicas)], axis=1)
+
+    def group_rows(value):
+        parts = []
+        for bit in range(0, replicas, 2):
+            same = value if bit == 0 else swap_xor(value, bit)
+            parts += [same, swap_core(same)]
+        return parts
+
+    my_tokens = own_batch(tokens[:, 0])
+    token_group = jnp.concatenate(group_rows(my_tokens), axis=0)
+    head_own = column_share(joined)
+    lin_width = head_own.shape[1]
+    head_swap = swap_section(jnp.concatenate([head_own, widened((small, give_routes))], axis=1))
+    got_routes = head_swap[:rows, lin_width + routes_at : lin_width + routes_at + top].astype(jnp.int32)
+    both_routes = jnp.where(
+        is_first,
+        jnp.concatenate([my_routes, got_routes], axis=1),
+        jnp.concatenate([got_routes, my_routes], axis=1),
+    )
+    tail_cols = jnp.where(is_first, small, head_swap[:, lin_width : lin_width + small.shape[1]])
+    head_got = jnp.concatenate(
+        [jnp.where(is_first, head_own, head_swap[:, :lin_width]), widened((tail_cols, both_routes))], axis=1
+    )
+    part_ff = w_gate.shape[3] // 2
+    pieces = []
+    for part, axis in ((w_gate, 1), (w_up, 1), (w_down, 0)):
+        chosen = lax.dynamic_index_in_dim(part[0], flip, 0, keepdims=False)
+        pieces.append(lax.dynamic_slice_in_dim(chosen, core * part_ff, part_ff, axis))
+    pieces, head_got = lax.optimization_barrier((pieces, head_got))
+    crossed_y = [swap_section(pieces[0]), None, None]
+    last_grad = own_batch(cotangent[:, 0])
+    head_got, last_blocks = lax.optimization_barrier((head_got, rel_gather(last_grad)))
+    head_parts, crossed_y[0] = lax.optimization_barrier((rel_gather(head_got), crossed_y[0]))
+    head_block = stacked_parts(head_parts)
+    tiles = [part[:rows, lin_width:] for part in head_parts]
+    crossed_y[1:] = [swap_section(value) for value in pieces[1:]]
     first = fold_id * local
-    flip = (replica // 2) % 2
-    lanes = jnp.arange(LANES, dtype=jnp.int32)
-    masks = jnp.any(mine[..., None] == lanes, axis=3)
     numbers = first + (jnp.arange(local, dtype=jnp.int32) ^ flip)
-    named = jnp.any(mine[:, :, None] == numbers[None, None, :, None, None], axis=4)
-    before = (jnp.arange(rows)[:, None] < jnp.arange(rows)[None, :]).astype(BF16)
-    rank = ein("lfet,tu->lfeu", named.astype(BF16), before).astype(jnp.int32)
-    slots_all = jnp.where(named, rank, -1)
-    masks = masks.astype(F32)
     scalars = [
         jnp.concatenate([jnp.stack([(section == layer).astype(jnp.int32), flip]), numbers]).astype(jnp.int32)
         for layer in range(2)
     ]
-
-    small = jnp.concatenate([w_router[0], gains[0].T], axis=1)
-    small = jnp.pad(small, ((0, 0), (0, HEAD - small.shape[1])))
-    shard = jnp.concatenate([w_query[0], w_key[0], w_value[0], small, w_out[0]], axis=1)
-    share = shard.shape[0] // (2 * replicas)
+    first_tail = head_block[:, lin_width:]
+    out_block = of_first(column_share(w_out[0]))
+    head_block, out_block = lax.optimization_barrier((head_block, out_block))
+    out_block = stacked_rows(out_block)
+    group_in = attention_in(token_group.astype(F32), first_tail[:, expert_count])[2]
+    first_lin = share_back(
+        mm(group_in, head_block[:, :lin_width]).astype(BF16).reshape(replicas, rows, lin_width)
+    )
+
+    def first_out(mixed_low):
+        group = jnp.concatenate(group_rows(mixed_low), axis=0)
+        made = mm(group, out_block).astype(BF16)
+        return share_back(made.reshape(replicas, rows, -1))
+
+    shard = jnp.concatenate([joined, jnp.pad(small, ((0, 0), (0, HEAD - small.shape[1]))), w_out[0]], axis=1)
+    share = depth // (2 * replicas)
     keep = lax.dynamic_slice_in_dim(shard, (section * replicas + replica) * share, share, 0)
     give = lax.dynamic_slice_in_dim(shard, ((1 - section) * replicas + replica) * share, share, 0)
+    give, _ = lax.optimization_barrier((give, head_got))
     got = swap_section(give)
-    split = q_width + 2 * kv_width
-    weights = []
-    for layer in range(2):
+
+    def whole_weights(layer, keep, got):
         piece = jnp.where(section == layer, keep, got)
-        axes = (F_AX, S_AX, R_AX)
-        head = lax.all_gather(piece[:, : split + LANES], axes, axis=0, tiled=True)
-        out_w = lax.all_gather(piece[:, split + LANES :], axes, axis=0, tiled=True)
-        tail = head[:, split:]
-        weights.append((tail[:, expert_count : expert_count + 2].T, head[:, :split], out_w, tail))
-
-    part_ff = w_gate.shape[3] // 2
-    at = core * part_ff
-    flat = []
-    for part, axis in ((w_gate, 1), (w_up, 1), (w_down, 0)):
-        chosen = lax.dynamic_index_in_dim(part[0], flip, 0, keepdims=False)
-        piece = lax.dynamic_slice_in_dim(chosen, at, part_ff, axis)
-        same = swap_section(piece)
-        cross = swap_xor(same, 2)
-        flat += [same, swap_core(same), cross, swap_core(cross)]
-    experts_w = ((w_gate[0], w_up[0], w_down[0]), flat)
+        full = lax.all_gather(piece, (F_AX, S_AX, R_AX), axis=0, tiled=True)
+        tail = full[:, split : split + LANES]
+        return tail[:, expert_count : expert_count + 2].T, full[:, :split], full[:, split + LANES :], tail
+
+    first_w = (
+        first_tail[:, expert_count : expert_count + 2].T, None, None, first_tail
+    )
     size = dict(
         folds=folds, local=local, rows=rows, parts=2, width=tokens.shape[3], ff=w_gate.shape[3],
-        capacity=capacity,
+        capacity=capacity, top=top,
     )
 
     lengths = own_batch(seq_lengths[:, 0])
@@ -588,26 +732,53 @@
         allowed=(segment[:, None] == key_seg[None, :]) & (key_pos[None, :] <= position[:, None]),
     )
 
-    value = own_batch(tokens[:, 0])
-    outs, kept = [], []
-    for layer in range(2):
-        value, state = layer_forward(
-            value, weights[layer], experts_w, common, masks[layer], slots_all[layer], scalars[layer]
+    def first_mixed(tied_lin, tied, attn_in, mixed_low):
+        gate_x, up_y = tied
+        held["second"] = whole_weights(1, *tied_lin)
+        return (crossed_y[0], up_y, crossed_y[2]), (gate_x,)
+
+    def first_moe(moe_in, own, more):
+        same, cross, moe_in = lax.optimization_barrier((*more, moe_in))
+        cross = [*cross, swap_xor(same[1], 2), swap_xor(same[2], 2)]
+        flat = []
+        for one, two in zip(same, cross):
+            flat += [one, swap_core(one), two, swap_core(two)]
+        return moe_in, (own, flat), ()
+
+    held = {}
+    first_value, first_kept, experts_w, _ = layer_forward(
+        my_tokens, first_w, (w_gate[0], w_up[0], w_down[0]), common, tiles, routes_at, scalars[0],
+        dict(lin=(keep, got), kv=(swap_xor(crossed_y[0], 2), crossed_y[1]), mixed=first_mixed, moe=first_moe),
+        first_lin, first_out,
+    )
+    head_share, out_share, _ = lax.optimization_barrier(
+        (head_block[:, :lin_width], out_block, first_kept["moe"][1])
+    )
+    weights_first = (
+        first_w[0], lax.all_gather(head_share, R_AX, axis=0), lax.all_gather(out_share, R_AX, axis=0), first_tail
+    )
+
+    second_w = held["second"]
+
+    def left_pair(attn_in, mixed_low):
+        pair = (
+            jnp.concatenate([first_kept["attn_in"], first_kept["mixed_low"]], axis=1),
+            jnp.concatenate([attn_in, mixed_low], axis=1),
         )
-        outs.append(value)
-        kept.append(state)
-
-    def own_layer(pair):
-        return jnp.where(is_first, pair[0], pair[1])
-
-    def other_layer(pair):
-        return jnp.where(is_first, pair[1], pair[0])
-
-    def by_section(keep, got):
-        return jnp.stack([jnp.where(is_first, keep, got), jnp.where(is_first, got, keep)])
-
-    def both_batches(pair):
-        return by_section(own_layer(pair), swap_section(other_layer(pair)))
+        return own_layer(pair), swap_section(other_layer(pair))
+
+    second_value, second_kept, _, tied = layer_forward(
+        first_value, second_w, experts_w, common, tiles, routes_at + top, scalars[1],
+        dict(
+            mixed=lambda one, two, attn_in, mixed_low: (attn_in, mixed_low),
+            moe=lambda moe_in, own, more: (moe_in, own, (left_pair(*more), weights_first)),
+            last=True,
+        ),
+    )
+    left_rows, weights_first = tied
+    second_parts, second_finish = second_value
+    left_rows = jnp.concatenate(left_rows, axis=0)
+    kept, weights = [first_kept, second_kept], [weights_first, second_w]
 
     half = local // 2
 
@@ -635,113 +806,117 @@
             whole = lax.dynamic_update_index_in_dim(whole, part, (replica // 2) ^ at, 0)
         return whole
 
-    same_core = [[2 * i + c for i in range(chips)] for c in range(2)]
-
     def flat_rows(whole):
-        return jnp.moveaxis(whole, 2, 0).reshape(half, -1, whole.shape[-1])
-
-    x_rows = both_batches(chip_rows([state["moe"][0] for state in kept]))
+        return jnp.moveaxis(whole, 1, 0).reshape(half, -1, whole.shape[-1])
+
+    x_chip = chip_rows([state["moe"][0] for state in kept])
+    x_mine, x_give = own_layer(x_chip), other_layer(x_chip)
     def both_rows(pair):
         return jnp.concatenate([own_layer(pair), swap_section(other_layer(pair))], axis=0)
 
     def own_columns(value):
         width = value.shape[1] // replicas
-        whole = jnp.zeros((replicas, value.shape[0], width), value.dtype)
+        parts = []
         for bit in range(replicas):
             piece = lax.dynamic_slice_in_dim(value, (replica ^ bit) * width, width, 1)
-            got = piece if bit == 0 else swap_xor(piece, bit)
-            whole = lax.dynamic_update_index_in_dim(whole, got, replica ^ bit, 0)
-        return whole
-
-    def weight_gradient(left, right, extra):
+            parts.append(piece if bit == 0 else swap_xor(piece, bit))
+        return jnp.stack(parts)
+
+    def fold_sum(left, right, extra, tie):
         total = mm_tn(left, right).astype(BF16)
-        step = total.shape[0] // folds
-        blocks = []
-        for k in range(folds):
-            goal = (fold_id - k) % folds
-            block = lax.dynamic_slice_in_dim(total, goal * step, step, 0)
-            if extra is not None:
-                more = lax.dynamic_index_in_dim(extra, goal, 0, keepdims=False)
-                block = jnp.concatenate([block, more], axis=0)
-            blocks.append(block)
-        mine = rel_scatter(blocks).astype(BF16)
-        height, width = mine.shape
-        whole = jnp.zeros((replicas, height, width), BF16)
-        for bit in range(0, replicas, 2):
-            same = mine if bit == 0 else swap_xor(mine, bit)
-            for other, part in enumerate((same, swap_core(same))):
-                whole = lax.dynamic_update_index_in_dim(whole, part, replica ^ (bit + other), 0)
-        return whole
-
-    left_rows = both_rows(
-        [jnp.concatenate([state["attn_in"], state["mixed_low"]], axis=1) for state in kept]
-    )
-    grad = own_batch(cotangent[:, 0])
-    grads, grad_attn, grad_lin = [None, None], [None, None], [None, None]
-    smalls, expert_rows = [None, None], [None, None]
-    tie = ()
-    held = []
-
-    def send_first(value):
-        held.append(chip_rows([value])[0])
-        return ()
-
-    def send_both(value):
-        chip = (chip_rows([value])[0], held[0])
-        mine = own_layer(chip)
-        return by_order(mine, all_x(mine)), swap_section(other_layer(chip))
-
-    for layer in (1, 0):
-        late_tie = (x_rows, left_rows) if layer == 1 else ()
-        (grad, grad_attn[layer], grad_lin[layer], smalls[layer], expert_rows[layer], tied, late_tied) = layer_backward(
-            grad, kept[layer], weights[layer], experts_w, common, slots_all[layer], scalars[layer], tie, late_tie,
-            send_first if layer == 1 else send_both,
-        )
-        if layer == 1:
-            x_rows, left_rows = late_tied
-            x_rows = lax.all_gather(x_rows, R_AX, axis=0, axis_index_groups=same_core)
-            left_rows = lax.all_gather(left_rows, R_AX, axis=0, tiled=True)
-            tie = (x_rows, left_rows)
-        else:
-            x_rows, left_rows = tied
-        grads[layer] = grad
-    x_rows = flat_rows(x_rows)
+        if extra is not None:
+            total = total.reshape(folds, -1, total.shape[1])
+            total = jnp.concatenate([total, extra], axis=1).reshape(-1, total.shape[2])
+        mine = lax.psum_scatter(total, F_AX, scatter_dimension=0, tiled=True)
+        whole = jnp.zeros((replicas,) + mine.shape, BF16)
+        for bit, part in enumerate(group_rows(mine)):
+            whole = lax.dynamic_update_index_in_dim(whole, part, replica ^ bit, 0)
+        return whole, tie
+
+    def side_by_side(value):
+        return jnp.concatenate([value[j].astype(F32) for j in range(replicas)], axis=1)
+
+    left_whole = group_rows(left_rows)
     model = tokens.shape[3]
     piece = model // (folds * replicas)
-    count = smalls[0].shape[0]
+    count = expert_count + 1
     tall = -(-count // 16) * 16
-    with_small = []
-    for layer in range(2):
-        value = smalls[layer].reshape(count, folds, replicas, piece)
+
+    def with_small(grad_attn, small):
+        value = small.reshape(count, folds, replicas, piece)
         value = jnp.transpose(value, (0, 2, 1, 3)).reshape(count, model)
-        with_small.append(jnp.concatenate([grad_attn[layer], jnp.pad(value, ((0, tall - count), (0, 0)))], axis=0))
-    right = own_columns(both_rows(with_small))
-    right = right.reshape(replicas, 2, rows + tall, right.shape[2])
-    extra = jnp.sum(right[:, :, rows:].astype(F32), axis=(0, 1)).reshape(tall, folds, piece)
+        return jnp.concatenate([grad_attn, jnp.pad(value, ((0, tall - count), (0, 0)))], axis=0)
+
+    def last_rows(grad_expert):
+        held["rows"] = chip_rows([grad_expert])[0]
+        return left_whole, stacked_parts(second_parts), swap_section(x_give)
+
+    def last_attn(grad_attn, small, sent):
+        held["attn"] = with_small(grad_attn, small)
+        return all_x(x_mine)
+
+    def first_rows(grad_expert):
+        chip = (chip_rows([grad_expert])[0], held["rows"])
+        mine = own_layer(chip)
+        return mine, all_x(mine), swap_section(other_layer(chip))
+
+    def first_attn(grad_attn, small, sent):
+        return both_rows((with_small(grad_attn, small), held["attn"])), sent
+
+    def first_later(sent, crossed):
+        right_out, (mine, mine_x, got) = crossed
+        held["got_x"] = all_x(got)
+        g_own = by_order(mine, mine_x)
+        return g_own, [expert_middle(x_own[i], flat_rows(g_own)[i], *[w[i] for w in mine_w]) for i in range(half)], got, own_columns(right_out)
+
+    grads, grad_lin = [None, None], [None, None]
+    grads[1], grad_lin[1], ((left_whole, second_stack, x_got), x_mine_x, x_got_x), _ = layer_backward(
+        last_grad, kept[1], weights[1], experts_w, common, scalars[1], (),
+        dict(rows=last_rows, attn=last_attn, later=lambda sent, crossed: (sent, crossed, all_x(sent[2])), blocks=last_blocks),
+    )
+    second_sum = lax.psum_scatter(second_stack, F_AX, scatter_dimension=0, tiled=True)
+    outs = [first_value, second_finish([second_sum])]
+    x_own = flat_rows(by_order(x_mine, x_mine_x))
+    x_own = [x_own[i] for i in range(half)]
+    mine_w = [lax.dynamic_slice_in_dim(part[0], core * half, half, 0) for part in (w_gate, w_up, w_down)]
+    grads[0], grad_lin[0], later, _ = layer_backward(
+        grads[1], kept[0], weights[0], experts_w, common, scalars[0], (),
+        dict(rows=first_rows, attn=first_attn, later=first_later),
+    )
+    g_own, middle_own, got, right_out = later
+    left_whole = jnp.concatenate(left_whole, axis=0)
+    lin_rows = both_rows(grad_lin)
+    got_x = held["got_x"]
+    lin_rows, outs = lax.optimization_barrier((lin_rows, outs))
+    right = own_columns(lin_rows)
+    g_got, x_got = by_order(got, got_x), by_order(x_got, x_got_x)
+    right, g_got, x_got = lax.optimization_barrier((right, g_got, x_got))
+    x_got = [flat_rows(x_got)[i] for i in range(half)]
+    g_own, g_got = [[flat_rows(value)[i] for i in range(half)] for value in (g_own, g_got)]
+    middle_got = [expert_middle(x_got[i], g_got[i], *[w[i] for w in mine_w]) for i in range(half)]
+
+    right_out = right_out.reshape(replicas, 2, rows + tall, -1)
+    extra = jnp.sum(right_out[:, :, rows:].astype(F32), axis=(0, 1)).reshape(tall, folds, piece)
     extra = jnp.pad(
-        jnp.transpose(extra, (1, 0, 2)), ((0, 0), (0, 0), (0, right.shape[3] - piece))
+        jnp.transpose(extra, (1, 0, 2)), ((0, 0), (0, 0), (0, right_out.shape[3] - piece))
     ).astype(BF16)
-    out_shard = weight_gradient(
-        left_rows[:, model:], right[:, :, :rows].reshape(-1, right.shape[3]), extra
-    )
-    def side_by_side(value):
-        return jnp.concatenate([value[j].astype(F32) for j in range(replicas)], axis=1)
-
-    small = side_by_side(out_shard[:, gains.shape[2] :, :piece])
-    out_shard = side_by_side(out_shard[:, : gains.shape[2]])
-    right = own_columns(both_rows(grad_lin))
-    shard = weight_gradient(left_rows[:, :model], right.reshape(-1, right.shape[2]), None)
+    right_out = right_out[:, :, :rows].reshape(-1, right_out.shape[3])
+    out_shard, _ = fold_sum(left_whole[:, model:], right_out, extra, ())
+    shard, middle_got = fold_sum(left_whole[:, :model], right.reshape(-1, right.shape[2]), None, middle_got)
+    made = []
+    for i in range(half):
+        inner, gate, up = zip(middle_own[i], middle_got[i])
+        made.append(
+            (
+                (mm_tn(x_own[i], gate[0]) + mm_tn(x_got[i], gate[1])).astype(BF16),
+                (mm_tn(x_own[i], up[0]) + mm_tn(x_got[i], up[1])).astype(BF16),
+                (mm_tn(inner[0], g_own[i]) + mm_tn(inner[1], g_got[i])).astype(BF16),
+            )
+        )
+    small = side_by_side(out_shard[:, depth:, :piece])
+    out_shard = side_by_side(out_shard[:, :depth])
     shard = side_by_side(shard)
-    own_w = jnp.concatenate([w_query[0], w_key[0], w_value[0]], axis=1).astype(F32)
-    gain_one = jnp.sum(shard * own_w, axis=1) / gains[0, 0].astype(F32)
-    mine, got = expert_rows[0]
-    got = by_order(got, all_x(got))
-    batches = [jnp.where(is_first, mine, got), jnp.where(is_first, got, mine)]
-    g_rows = flat_rows(jnp.stack(batches, axis=1))
-    mine_w = [lax.dynamic_slice_in_dim(part[0], core * half, half, 0) for part in (w_gate, w_up, w_down)]
-    made = [
-        expert_grads(x_rows[i], g_rows[i], mine_w[0][i], mine_w[1][i], mine_w[2][i]) for i in range(half)
-    ]
+    gain_one = jnp.sum(shard * joined.astype(F32), axis=1) / gains[0, 0].astype(F32)
     expert_out = []
     for slot in range(3):
         keep = jnp.stack([one[slot] for one in made])
@@ -750,7 +925,6 @@
             [jnp.where(core == 0, keep, got), jnp.where(core == 0, got, keep)], axis=0
         )
         expert_out.append(both.astype(F32)[None])
-
     layer_outputs = both_batches(outs)
     input_grads = both_batches(grads)
     return (

time: 1040 us -> 891 us (0.86)
  waiting for transfers between devices: 507 us -> 331 us
  local copies, waits for them, and re-layouts: 89.1 us -> 103 us
    all_gather x6 -> x3, waiting for transfers between devices: 86.2 us -> 0.02 us  [the longest x1 0.02 us: whole_weights(): full = lax.all_gather(piece, (F_AX, S_AX, R_AX), axis=0, tiled=True)]
    ppermute x24 -> x12, waiting for transfers between devices: 127 us -> 52.2 us  [rel_scatter(): lax.ppermute(parts[k], F_AX, [(i, (i - k) % folds) for i in range(folds)])]
    ppermute x24 -> x12, starting transfers between devices: 77.5 us -> 44.8 us  [rel_scatter(): lax.ppermute(parts[k], F_AX, [(i, (i - k) % folds) for i in range(folds)])]
    ppermute x13 -> x24, waiting for transfers between devices: 99.4 us -> 69.6 us  [swap_xor(): return lax.ppermute(value, R_AX, [(i, i ^ bit) for i in range(replicas)])]
    ppermute x21 -> x24, starting transfers between devices: 45.4 us -> 69.3 us  [rel_gather(): lax.ppermute(value, F_AX, [(i, (i + k) % folds) for i in range(folds)])]
    ppermute x0 -> x3, waiting for transfers between devices: none -> 22.6 us  [send_back(): lax.ppermute(parts[k], F_AX, [(i, (i - k) % folds) for i in range(folds)])]
    ppermute x12 -> x13, waiting for transfers between devices: 53.4 us -> 32 us  [swap_section(): return lax.ppermute(value, S_AX, [(0, 1), (1, 0)])]
    dot_general x5 -> x16, matrix products: 18.6 us -> 34.6 us  [mm_nt(): lax.dot_general(a, b, (((1,), (1,)), ((), ())), preferred_element_type=F32)]
  transfers between devices with their start and end apart: 93 -> 105, of which waited for: 44 -> 43; matrix products, arithmetic and copies ran while one was open for 25% -> 31% of each run, Pallas kernels for 4% -> 4%
where the time goes in v2:
time: 891 us; the launch traced here: 882 us
  waiting for transfers between devices  331 us (37%)
  starting transfers between devices  161 us (18%)
  matrix products  133 us (15%)
  local copies, waits for them, and re-layouts  103 us (12%)
  other arithmetic  83.5 us (9%)
  Pallas kernels  52.6 us (6%)
  between operations  17.9 us (2%)
    ppermute x24, waiting for transfers between devices, rel_gather(): lax.ppermute(value, F_AX, [(i, (i + k) % folds) for i in range(folds)])  131 us
    ppermute x24, waiting for transfers between devices, swap_xor(): return lax.ppermute(value, R_AX, [(i, i ^ bit) for i in range(replicas)])  69.6 us
    ppermute x24, starting transfers between devices, rel_gather(): lax.ppermute(value, F_AX, [(i, (i + k) % folds) for i in range(folds)])  69.3 us
    ppermute x12, waiting for transfers between devices, rel_scatter(): lax.ppermute(parts[k], F_AX, [(i, (i - k) % folds) for i in range(folds)])  52.2 us
    dot_general x10, matrix products, mm_tn(): lax.dot_general(a, b, (((0,), (0,)), ((), ())), preferred_element_type=F32)  46.5 us
    ppermute x12, starting transfers between devices, rel_scatter(): lax.ppermute(parts[k], F_AX, [(i, (i - k) % folds) for i in range(folds)])  44.8 us
    dot_general x16, matrix products, mm_nt(): lax.dot_general(a, b, (((1,), (1,)), ((), ())), preferred_element_type=F32)  34.6 us
    dot_general x8, matrix products, mm(): return jnp.dot(a, b, preferred_element_type=F32)  33.3 us
  transfers between devices with their start and end apart: 105, of which 43 were waited for; matrix products, arithmetic and copies ran while one was open for 31% of the time, Pallas kernels for 4%

profile of v2, /device:TPU:0, one launch (start us, length us, event | category | flops | bytes accessed | tf_op | source)
XLA Modules:
  0.0 881.7 jit_solution(2665459458604365062)
XLA Ops:
  36.3 5.3 collective-permute-done.11
  62.1 5.3 collective-permute-done.7
  67.4 17.6 %collective-permute-done.8 = bf16[384,640]{1,0:T(8,128)(2,1)S(1)} collective-permute-done((bf16[384,640]{1,0:T(8,128)(2,1)S(1)}, bf16[384,640]{1,0:T(8,128)(2,1)S(1)}, u32[]{:S(2)}, u32[]{:S(2)}) %collective-permute-start.8) | collective-permute-done | bytes 491552 | tf_op jit(solution)/shard_map/ppermute | solution.py:333
  103.6 11.7 %collective-permute-start.18 = (bf16[128,512]{0,1:T(8,128)(2,1)S(1)}, bf16[128,512]{0,1:T(8,128)(2,1)S(1)}, u32[]{:S(2)}, u32[]{:S(2)}) collective-permute-start(bf16[128,512]{0,1:T(8,128)(2,1)S(1)} %pad_maximum_fusion.23), channel_id=1, source_target_pairs={{0,12},{4,0},{8,4},{12,8},{1,13},{5,1},{9,5},{13,9},{2,14},{6,2},{... | collective-permute-start | bytes 393224 | tf_op jit(solution)/shard_map/ppermute | solution.py:333
  121.2 13.8 %collective-permute-done.17 = bf16[128,512]{0,1:T(8,128)(2,1)S(1)} collective-permute-done((bf16[128,512]{0,1:T(8,128)(2,1)S(1)}, bf16[128,512]{0,1:T(8,128)(2,1)S(1)}, u32[]{:S(2)}, u32[]{:S(2)}) %collective-permute-start.17) | collective-permute-done | bytes 131104 | tf_op jit(solution)/shard_map/ppermute | solution.py:333
  137.5 6.0 collective-permute-start.27
  151.9 9.7 %collective-permute-done.21.refs_21_ = bf16[384,1536]{1,0:T(8,128)(2,1)} collective-permute-done((bf16[384,1536]{1,0:T(8,128)(2,1)}, bf16[384,1536]{1,0:T(8,128)(2,1)}, u32[]{:S(2)}, u32[]{:S(2)}) %collective-permute-start.21) | collective-permute-done | bytes 1179680 | tf_op jit(solution)/shard_map/ppermute | solution.py:361
  182.1 6.2 collective-permute-done.29
  195.8 11.3 %collective-permute-start.31 = (bf16[128,1536]{1,0:T(8,128)(2,1)S(1)}, bf16[128,1536]{1,0:T(8,128)(2,1)S(1)}, u32[]{:S(2)}, u32[]{:S(2)}) collective-permute-start(bf16[128,1536]{1,0:T(8,128)(2,1)S(1)} %get-tuple-element.166.refs_6_), channel_id=1, source_target_pairs={{0,4},{4,8},{8,12},{12,0},{1,5},{5,9},{9,13},{13,1},{2,6},{6,10},{... | collective-permute-start | bytes 1179656 | tf_op jit(solution)/shard_map/ppermute | solution.py:333
  208.1 14.6 %collective-permute-done.31.refs_7_ = bf16[128,1536]{1,0:T(8,128)(2,1)S(1)} collective-permute-done((bf16[128,1536]{1,0:T(8,128)(2,1)S(1)}, bf16[128,1536]{1,0:T(8,128)(2,1)S(1)}, u32[]{:S(2)}, u32[]{:S(2)}) %collective-permute-start.31) | collective-permute-done | bytes 393248 | tf_op jit(solution)/shard_map/ppermute | solution.py:333
  222.7 5.5 collective-permute-start.33
  228.2 15.7 %collective-permute-done.32.refs_8_ = bf16[128,1536]{1,0:T(8,128)(2,1)S(1)} collective-permute-done((bf16[128,1536]{1,0:T(8,128)(2,1)S(1)}, bf16[128,1536]{1,0:T(8,128)(2,1)S(1)}, u32[]{:S(2)}, u32[]{:S(2)}) %collective-permute-start.32) | collective-permute-done | bytes 393248 | tf_op jit(solution)/shard_map/ppermute | solution.py:333
  249.0 8.0 collective-permute-done.40.refs_23_
  268.6 12.7 %shard_map.212 = (bf16[2,256,1536]{2,1,0:T(8,128)(2,1)}, f32[2,256,768]{2,1,0:T(8,128)}, f32[2,256,768]{2,1,0:T(8,128)}, bf16[2,256,1536]{2,1,0:T(8,128)(2,1)}, ...) custom-call(s32[4]{0:T(128)} %get-tuple-element.479.refs_0_, ...), custom_call_target="tpu_custom_call" | custom-call | flops 3623878656 | bytes 20447232 | tf_op jit(solution)/shard_map/pallas_call | solution.py:273
  290.2 6.1 collective-permute-done.44
  296.3 16.5 %collective-permute-done.43 = bf16[128,1536]{1,0:T(8,128)(2,1)} collective-permute-done((bf16[128,1536]{1,0:T(8,128)(2,1)}, bf16[128,1536]{1,0:T(8,128)(2,1)}, u32[]{:S(2)}, u32[]{:S(2)}) %collective-permute-start.43) | collective-permute-done | bytes 393248 | tf_op jit(solution)/shard_map/ppermute | solution.py:349
  326.1 10.1 %collective-permute-start.47 = (bf16[128,512]{1,0:T(8,128)(2,1)S(1)}, bf16[128,512]{1,0:T(8,128)(2,1)S(1)}, u32[]{:S(2)}, u32[]{:S(2)}) collective-permute-start(bf16[128,512]{1,0:T(8,128)(2,1)S(1)} %pad_maximum_fusion.24), channel_id=1, source_target_pairs={{0,12},{4,0},{8,4},{12,8},{1,13},{5,1},{9,5},{13,9},{2,14},{6,2},{... | collective-permute-start | bytes 393224 | tf_op jit(solution)/shard_map/ppermute | solution.py:333
  340.1 8.3 collective-permute-done.46
  374.2 5.5 collective-permute-done.48.refs_7_
  379.7 14.8 %collective-permute-done.49.refs_8_ = bf16[128,1536]{1,0:T(8,128)(2,1)} collective-permute-done((bf16[128,1536]{1,0:T(8,128)(2,1)}, bf16[128,1536]{1,0:T(8,128)(2,1)}, u32[]{:S(2)}, u32[]{:S(2)}) %collective-permute-start.49) | collective-permute-done | bytes 393248 | tf_op jit(solution)/shard_map/ppermute | solution.py:333
  397.9 12.7 %shard_map.213 = (bf16[2,256,1536]{2,1,0:T(8,128)(2,1)}, f32[2,256,768]{2,1,0:T(8,128)}, f32[2,256,768]{2,1,0:T(8,128)}, bf16[2,256,1536]{2,1,0:T(8,128)(2,1)}, ...) custom-call(s32[4]{0:T(128)} %get-tuple-element.478.refs_0_, ...), custom_call_target="tpu_custom_call" | custom-call | flops 3623878656 | bytes 20447232 | tf_op jit(solution)/shard_map/pallas_call | solution.py:273
  410.6 13.3 %shard_map.214 = (bf16[2,256,1536]{2,1,0:T(8,128)(2,1)}, bf16[128,1664]{1,0:T(8,128)(2,1)}, bf16[128,1664]{1,0:T(8,128)(2,1)}, bf16[128,1664]{1,0:T(8,128)(2,1)}, bf16[128,1664]{1,0:T(8,128)(2,1)}) custom-call(s32[4]{0:T(128)} %get-tuple-element.478.refs_0_, s32[4,2,128]{2,1,0:T(2,128)} %get-tuple-element.190.refs_1_, ...), custom_call_target="tpu_custom_call" | custom-call | flops 3623878656 | bytes 20447232 | tf_op jit(solution)/shard_map/pallas_call | solution.py:292
  423.9 8.0 collective-permute-start.54
  444.3 17.1 %collective-permute-done.53 = bf16[128,1664]{1,0:T(8,128)(2,1)S(1)} collective-permute-done((bf16[128,1664]{1,0:T(8,128)(2,1)}, bf16[128,1664]{1,0:T(8,128)(2,1)S(1)}, u32[]{:S(2)}, u32[]{:S(2)}) %collective-permute-start.53) | collective-permute-done | bytes 426016 | tf_op jit(solution)/shard_map/ppermute | solution.py:341
  466.9 12.2 %collective-permute-done.60 = bf16[1,512,1536]{2,1,0:T(8,128)(2,1)} collective-permute-done((bf16[1,512,1536]{2,1,0:T(8,128)(2,1)S(1)}, bf16[1,512,1536]{2,1,0:T(8,128)(2,1)}, u32[]{:S(2)}, u32[]{:S(2)}) %collective-permute-start.60) | collective-permute-done | bytes 1572896 | tf_op jit(solution)/shard_map/ppermute | solution.py:361
  486.6 4.7 fusion.53
  500.4 9.2 %collective-permute-start.64 = (bf16[128,512]{0,1:T(8,128)(2,1)}, bf16[128,512]{0,1:T(8,128)(2,1)}, u32[]{:S(2)}, u32[]{:S(2)}) collective-permute-start(bf16[128,512]{0,1:T(8,128)(2,1)} %get-tuple-element.446), channel_id=1, source_target_pairs={{0,4},{4,8},{8,12},{12,0},{1,5},{5,9},{9,13},{13,1},{2,6},{6,10},{... | collective-permute-start | bytes 393224 | tf_op jit(solution)/shard_map/ppermute | solution.py:341
  521.7 25.7 %collective-permute-done.65 = bf16[1,512,1536]{2,1,0:T(8,128)(2,1)} collective-permute-done((bf16[1,512,1536]{2,1,0:T(8,128)(2,1)}, bf16[1,512,1536]{2,1,0:T(8,128)(2,1)}, u32[]{:S(2)}, u32[]{:S(2)}) %collective-permute-start.65) | collective-permute-done | bytes 1572896 | tf_op jit(solution)/shard_map/ppermute | solution.py:591
  548.6 6.0 fusion.148
  567.0 14.4 %reduce-scatter.4.cloned.1.call-done = bf16[128,1536]{1,0:T(8,128)(2,1)} async-done(((bf16[512,1536]{1,0:T(8,128)(2,1)}), bf16[128,1536]{1,0:T(8,128)(2,1)}) %reduce-scatter.4.cloned.1.call-update) | async-done | bytes 393232 | tf_op jit(solution)/shard_map/reduce_scatter | solution.py:877
  590.8 6.9 collective-permute-done.66.refs_7_
  597.8 15.6 %collective-permute-done.67.refs_8_ = bf16[128,1536]{1,0:T(8,128)(2,1)S(1)} collective-permute-done((bf16[128,1536]{1,0:T(8,128)(2,1)S(1)}, bf16[128,1536]{1,0:T(8,128)(2,1)S(1)}, u32[]{:S(2)}, u32[]{:S(2)}) %collective-permute-start.67) | collective-permute-done | bytes 393248 | tf_op jit(solution)/shard_map/ppermute | solution.py:333
  614.3 13.9 %shard_map.215 = (bf16[2,256,1536]{2,1,0:T(8,128)(2,1)}, bf16[128,1664]{1,0:T(8,128)(2,1)}, bf16[128,1664]{1,0:T(8,128)(2,1)}, bf16[128,1664]{1,0:T(8,128)(2,1)}, bf16[128,1664]{1,0:T(8,128)(2,1)}) custom-call(s32[4]{0:T(128)} %get-tuple-element.479.refs_0_, s32[4,2,128]{2,1,0:T(2,128)} %get-tuple-element.226.refs_1_, ...), custom_call_target="tpu_custom_call" | custom-call | flops 3623878656 | bytes 20447232 | tf_op jit(solution)/shard_map/pallas_call | solution.py:292
  639.7 7.6 collective-permute-start.71
  650.3 9.2 %collective-permute-done.71 = bf16[128,1664]{1,0:T(8,128)(2,1)S(1)} collective-permute-done((bf16[128,1664]{1,0:T(8,128)(2,1)S(1)}, bf16[128,1664]{1,0:T(8,128)(2,1)S(1)}, u32[]{:S(2)}, u32[]{:S(2)}) %collective-permute-start.71) | collective-permute-done | bytes 426016 | tf_op jit(solution)/shard_map/ppermute | solution.py:341
  659.5 16.9 %collective-permute-done.70 = bf16[128,1664]{1,0:T(8,128)(2,1)S(1)} collective-permute-done((bf16[128,1664]{1,0:T(8,128)(2,1)S(1)}, bf16[128,1664]{1,0:T(8,128)(2,1)S(1)}, u32[]{:S(2)}, u32[]{:S(2)}) %collective-permute-start.70) | collective-permute-done | bytes 426016 | tf_op jit(solution)/shard_map/ppermute | solution.py:341
  698.2 4.7 collective-permute-done.76
  703.1 9.7 %collective-permute-start.79 = (bf16[128,512]{0,1:T(8,128)(2,1)S(1)}, bf16[128,512]{0,1:T(8,128)(2,1)S(1)}, u32[]{:S(2)}, u32[]{:S(2)}) collective-permute-start(bf16[128,512]{0,1:T(8,128)(2,1)S(1)} %get-tuple-element.443), channel_id=1, source_target_pairs={{0,4},{4,8},{8,12},{12,0},{1,5},{5,9},{9,13},{13,1},{2,6},{6,10},{... | collective-permute-start | bytes 393224 | tf_op jit(solution)/shard_map/ppermute | solution.py:341
  719.7 7.0 multiply_convert_fusion.2
  744.0 7.4 fusion.276
  776.1 4.9 collective-permute-done.87
  785.3 6.3 fusion.67
  791.6 6.1 fusion.63
  798.3 5.4 fusion.59
  803.8 8.4 fusion.39
  812.5 5.0 fusion.40
  822.4 8.4 fusion.41
  856.4 6.1 maximum_convert_fusion.2
  (904 shorter events, 386.1 us)
Async XLA Ops:
  7.2 307.5 %all-gather.6.cloned.1.call-start = ((), (), s32[]{:S(2)}) async-start(), calls=%async_computation.3 | async-start | bytes 11759616 | tf_op jit(solution)/shard_map/all_gather | solution.py:708
  9.1 38.6 %collective-permute-start.4 = (bf16[128,1536]{1,0:T(8,128)(2,1)}, bf16[128,1536]{1,0:T(8,128)(2,1)}, u32[]{:S(2)}, u32[]{:S(2)}) collective-permute-start(bf16[128,1536]{1,0:T(8,128)(2,1)} %dynamic-slice_bitcast_fusion.3.refs_6_), channel_id=1, source_target_pairs={{0,4},{4,8},{8,12},{12,0},{1,5},{5,9},{9,13},{13,1},{2,6},{6,10},{... | collective-permute-start | bytes 1179656 | tf_op jit(solution)/shard_map/ppermute | solution.py:333
  12.1 35.6 %collective-permute-start.5 = (bf16[128,1536]{1,0:T(8,128)(2,1)}, bf16[128,1536]{1,0:T(8,128)(2,1)}, u32[]{:S(2)}, u32[]{:S(2)}) collective-permute-start(bf16[128,1536]{1,0:T(8,128)(2,1)} %dynamic-slice_bitcast_fusion.3.refs_6_), channel_id=1, source_target_pairs={{0,8},{4,12},{8,0},{12,4},{1,9},{5,13},{9,1},{13,5},{2,10},{6,14},... | collective-permute-start | bytes 1179656 | tf_op jit(solution)/shard_map/ppermute | solution.py:333
  52.1 32.9 %collective-permute-start.8 = (bf16[384,640]{1,0:T(8,128)(2,1)S(1)}, bf16[384,640]{1,0:T(8,128)(2,1)S(1)}, u32[]{:S(2)}, u32[]{:S(2)}) collective-permute-start(bf16[384,640]{1,0:T(8,128)(2,1)S(1)} %fusion.167), channel_id=1, source_target_pairs={{0,8},{4,12},{8,0},{12,4},{1,9},{5,13},{9,1},{13,5},{2,10},{6,14},... | collective-permute-start | bytes 1474568 | tf_op jit(solution)/shard_map/ppermute | solution.py:333
  55.5 29.5 %collective-permute-start.10 = (bf16[1536,384]{1,0:T(8,128)(2,1)S(1)}, bf16[1536,384]{1,0:T(8,128)(2,1)S(1)}, u32[]{:S(2)}, u32[]{:S(2)}) collective-permute-start(bf16[1536,384]{1,0:T(8,128)(2,1)S(1)} %copy-done.109), channel_id=1, source_target_pairs={{0,16},{16,0},{1,17},{17,1},{2,18},{18,2},{3,19},{19,3},{4,20},{20... | collective-permute-start | bytes 3538952 | tf_op jit(solution)/shard_map/ppermute | solution.py:361
  59.2 25.8 %collective-permute-start.9 = (bf16[384,640]{1,0:T(8,128)(2,1)S(1)}, bf16[384,640]{1,0:T(8,128)(2,1)S(1)}, u32[]{:S(2)}, u32[]{:S(2)}) collective-permute-start(bf16[384,640]{1,0:T(8,128)(2,1)S(1)} %fusion.167), channel_id=1, source_target_pairs={{0,12},{4,0},{8,4},{12,8},{1,13},{5,1},{9,5},{13,9},{2,14},{6,2},{... | collective-permute-start | bytes 1474568 | tf_op jit(solution)/shard_map/ppermute | solution.py:333
  60.5 37.1 %collective-permute-start.15 = (bf16[48,3712]{1,0:T(8,128)(2,1)S(1)}, bf16[48,3712]{1,0:T(8,128)(2,1)S(1)}, u32[]{:S(2)}, u32[]{:S(2)}) collective-permute-start(bf16[48,3712]{1,0:T(8,128)(2,1)S(1)} %get-tuple-element.151), channel_id=1, source_target_pairs={{0,16},{16,0},{1,17},{17,1},{2,18},{18,2},{3,19},{19,3},{4,20},{20... | collective-permute-start | bytes 1069064 | tf_op jit(solution)/shard_map/ppermute | solution.py:361
  98.5 275.7 %all-gather.10.cloned.1.call-start = ((), (), s32[]{:S(2)}) async-start(), calls=%async_computation.8 | async-start | bytes 5898240 | tf_op jit(solution)/shard_map/all_gather | solution.py:758
  100.2 37.3 %collective-permute-start.20 = (bf16[1536,384]{1,0:T(8,128)(2,1)}, bf16[1536,384]{1,0:T(8,128)(2,1)S(1)}, u32[]{:S(2)}, u32[]{:S(2)}) collective-permute-start(bf16[1536,384]{1,0:T(8,128)(2,1)} %get-tuple-element.154), channel_id=1, source_target_pairs={{0,16},{16,0},{1,17},{17,1},{2,18},{18,2},{3,19},{19,3},{4,20},{20... | collective-permute-start | bytes 3538952 | tf_op jit(solution)/shard_map/ppermute | solution.py:361
  101.7 41.8 %collective-permute-start.19 = (bf16[1536,384]{1,0:T(8,128)(2,1)S(1)}, bf16[1536,384]{1,0:T(8,128)(2,1)}, u32[]{:S(2)}, u32[]{:S(2)}) collective-permute-start(bf16[1536,384]{1,0:T(8,128)(2,1)S(1)} %collective-permute-done.10.refs_13_), channel_id=1, source_target_pairs={{0,2},{1,3},{2,0},{3,1},{4,6},{5,7},{6,4},{7,5},{8,10},{9,11},{10,... | collective-permute-start | bytes 3538952 | tf_op jit(solution)/shard_map/ppermute | solution.py:591
  121.2 40.4 %collective-permute-start.21 = (bf16[384,1536]{1,0:T(8,128)(2,1)}, bf16[384,1536]{1,0:T(8,128)(2,1)}, u32[]{:S(2)}, u32[]{:S(2)}) collective-permute-start(bf16[384,1536]{1,0:T(8,128)(2,1)} %dynamic-slice_bitcast_fusion), channel_id=1, source_target_pairs={{0,16},{16,0},{1,17},{17,1},{2,18},{18,2},{3,19},{19,3},{4,20},{20... | collective-permute-start | bytes 3538952 | tf_op jit(solution)/shard_map/ppermute | solution.py:361
  135.0 31.3 %collective-permute-start.25 = (bf16[384,384]{1,0:T(8,128)(2,1)}, bf16[384,384]{1,0:T(8,128)(2,1)}, u32[]{:S(2)}, u32[]{:S(2)}) collective-permute-start(bf16[384,384]{1,0:T(8,128)(2,1)} %broadcast_select_fusion.23), channel_id=1, source_target_pairs={{0,4},{4,8},{8,12},{12,0},{1,5},{5,9},{9,13},{13,1},{2,6},{6,10},{... | collective-permute-start | bytes 884744 | tf_op jit(solution)/shard_map/ppermute | solution.py:333
  135.1 37.0 %collective-permute-start.26 = (bf16[384,384]{1,0:T(8,128)(2,1)}, bf16[384,384]{1,0:T(8,128)(2,1)}, u32[]{:S(2)}, u32[]{:S(2)}) collective-permute-start(bf16[384,384]{1,0:T(8,128)(2,1)} %broadcast_select_fusion.23), channel_id=1, source_target_pairs={{0,8},{4,12},{8,0},{12,4},{1,9},{5,13},{9,1},{13,5},{2,10},{6,14},... | collective-permute-start | bytes 884744 | tf_op jit(solution)/shard_map/ppermute | solution.py:333
  137.5 36.4 %collective-permute-start.27 = (bf16[384,384]{1,0:T(8,128)(2,1)}, bf16[384,384]{1,0:T(8,128)(2,1)}, u32[]{:S(2)}, u32[]{:S(2)}) collective-permute-start(bf16[384,384]{1,0:T(8,128)(2,1)} %broadcast_select_fusion.23), channel_id=1, source_target_pairs={{0,12},{4,0},{8,4},{12,8},{1,13},{5,1},{9,5},{13,9},{2,14},{6,2},{... | collective-permute-start | bytes 884744 | tf_op jit(solution)/shard_map/ppermute | solution.py:333
  192.6 54.8 %collective-permute-start.34 = (bf16[1536,384]{1,0:T(8,128)(2,1)S(1)}, bf16[1536,384]{1,0:T(8,128)(2,1)S(1)}, u32[]{:S(2)}, u32[]{:S(2)}) collective-permute-start(bf16[1536,384]{1,0:T(8,128)(2,1)S(1)} %collective-permute-done.10.refs_13_), channel_id=1, source_target_pairs={{0,1},{1,0},{2,3},{3,2},{4,5},{5,4},{6,7},{7,6},{8,9},{9,8},{10,11... | collective-permute-start | bytes 3538952 | tf_op jit(solution)/shard_map/ppermute | solution.py:366
  193.8 54.2 %collective-permute-start.37 = (bf16[1536,384]{1,0:T(8,128)(2,1)S(1)}, bf16[1536,384]{1,0:T(8,128)(2,1)}, u32[]{:S(2)}, u32[]{:S(2)}) collective-permute-start(bf16[1536,384]{1,0:T(8,128)(2,1)S(1)} %collective-permute-done.20.refs_17_), channel_id=1, source_target_pairs={{0,2},{1,3},{2,0},{3,1},{4,6},{5,7},{6,4},{7,5},{8,10},{9,11},{10,... | collective-permute-start | bytes 3538952 | tf_op jit(solution)/shard_map/ppermute | solution.py:591
  195.3 61.7 %collective-permute-start.40 = (bf16[384,1536]{1,0:T(8,128)(2,1)}, bf16[384,1536]{1,0:T(8,128)(2,1)}, u32[]{:S(2)}, u32[]{:S(2)}) collective-permute-start(bf16[384,1536]{1,0:T(8,128)(2,1)} %collective-permute-done.21.refs_21_), channel_id=1, source_target_pairs={{0,2},{1,3},{2,0},{3,1},{4,6},{5,7},{6,4},{7,5},{8,10},{9,11},{10,... | collective-permute-start | bytes 3538952 | tf_op jit(solution)/shard_map/ppermute | solution.py:591
  195.8 26.9 %collective-permute-start.31 = (bf16[128,1536]{1,0:T(8,128)(2,1)S(1)}, bf16[128,1536]{1,0:T(8,128)(2,1)S(1)}, u32[]{:S(2)}, u32[]{:S(2)}) collective-permute-start(bf16[128,1536]{1,0:T(8,128)(2,1)S(1)} %get-tuple-element.166.refs_6_), channel_id=1, source_target_pairs={{0,4},{4,8},{8,12},{12,0},{1,5},{5,9},{9,13},{13,1},{2,6},{6,10},{... | collective-permute-start | bytes 1179656 | tf_op jit(solution)/shard_map/ppermute | solution.py:333
  207.1 36.8 %collective-permute-start.32 = (bf16[128,1536]{1,0:T(8,128)(2,1)S(1)}, bf16[128,1536]{1,0:T(8,128)(2,1)S(1)}, u32[]{:S(2)}, u32[]{:S(2)}) collective-permute-start(bf16[128,1536]{1,0:T(8,128)(2,1)S(1)} %get-tuple-element.166.refs_6_), channel_id=1, source_target_pairs={{0,8},{4,12},{8,0},{12,4},{1,9},{5,13},{9,1},{13,5},{2,10},{6,14},... | collective-permute-start | bytes 1179656 | tf_op jit(solution)/shard_map/ppermute | solution.py:333
  222.7 24.7 %collective-permute-start.33 = (bf16[128,1536]{1,0:T(8,128)(2,1)S(1)}, bf16[128,1536]{1,0:T(8,128)(2,1)S(1)}, u32[]{:S(2)}, u32[]{:S(2)}) collective-permute-start(bf16[128,1536]{1,0:T(8,128)(2,1)S(1)} %get-tuple-element.166.refs_6_), channel_id=1, source_target_pairs={{0,12},{4,0},{8,4},{12,8},{1,13},{5,1},{9,5},{13,9},{2,14},{6,2},{... | collective-permute-start | bytes 1179656 | tf_op jit(solution)/shard_map/ppermute | solution.py:333
  281.4 92.8 %all-gather.8.cloned.1.call-start = ((), (), s32[]{:S(2)}) async-start(), calls=%async_computation.7 | async-start | bytes 7864320 | tf_op jit(solution)/shard_map/all_gather | solution.py:758
  282.1 299.3 %reduce-scatter.4.cloned.1.call-start = ((), (), s32[]{:S(2)}) async-start(), calls=%async_computation.4 | async-start | bytes 1966080 | tf_op jit(solution)/shard_map/reduce_scatter | solution.py:877
  283.8 29.0 %collective-permute-start.43 = (bf16[128,1536]{1,0:T(8,128)(2,1)}, bf16[128,1536]{1,0:T(8,128)(2,1)}, u32[]{:S(2)}, u32[]{:S(2)}) collective-permute-start(bf16[128,1536]{1,0:T(8,128)(2,1)} %get-tuple-element.176), channel_id=1, source_target_pairs={{0,8},{4,12},{8,0},{12,4},{1,9},{5,13},{9,1},{13,5},{2,10},{6,14},... | collective-permute-start | bytes 1179656 | tf_op jit(solution)/shard_map/ppermute | solution.py:349
  286.1 26.7 %collective-permute-start.42 = (bf16[128,1536]{1,0:T(8,128)(2,1)}, bf16[128,1536]{1,0:T(8,128)(2,1)}, u32[]{:S(2)}, u32[]{:S(2)}) collective-permute-start(bf16[128,1536]{1,0:T(8,128)(2,1)} %get-tuple-element.175), channel_id=1, source_target_pairs={{0,12},{4,0},{8,4},{12,8},{1,13},{5,1},{9,5},{13,9},{2,14},{6,2},{... | collective-permute-start | bytes 1179656 | tf_op jit(solution)/shard_map/ppermute | solution.py:349
  337.8 32.2 %collective-permute-start.59 = (bf16[1,256,1536]{2,1,0:T(8,128)(2,1)}, bf16[1,256,1536]{2,1,0:T(8,128)(2,1)}, u32[]{:S(2)}, u32[]{:S(2)}) collective-permute-start(bf16[1,256,1536]{2,1,0:T(8,128)(2,1)} %constant_dynamic-slice_fusion.8), channel_id=1, source_target_pairs={{0,1},{1,0},{2,3},{3,2},{4,5},{5,4},{6,7},{7,6},{8,9},{9,8},{10,11... | collective-permute-start | bytes 2359304 | tf_op jit(solution)/shard_map/ppermute | solution.py:366
  359.6 34.9 %collective-permute-start.51 = (bf16[128,3072]{1,0:T(8,128)(2,1)}, bf16[128,3072]{1,0:T(8,128)(2,1)}, u32[]{:S(2)}, u32[]{:S(2)}) collective-permute-start(bf16[128,3072]{1,0:T(8,128)(2,1)} %get-tuple-element.404), channel_id=1, source_target_pairs={{0,16},{16,0},{1,17},{17,1},{2,18},{18,2},{3,19},{19,3},{4,20},{20... | collective-permute-start | bytes 2359304 | tf_op jit(solution)/shard_map/ppermute | solution.py:361
  365.4 29.1 %collective-permute-start.49 = (bf16[128,1536]{1,0:T(8,128)(2,1)}, bf16[128,1536]{1,0:T(8,128)(2,1)}, u32[]{:S(2)}, u32[]{:S(2)}) collective-permute-start(bf16[128,1536]{1,0:T(8,128)(2,1)} %multiply_convert_fusion.6.refs_6_), channel_id=1, source_target_pairs={{0,8},{4,12},{8,0},{12,4},{1,9},{5,13},{9,1},{13,5},{2,10},{6,14},... | collective-permute-start | bytes 1179656 | tf_op jit(solution)/shard_map/ppermute | solution.py:333
  366.9 27.6 %collective-permute-start.50 = (bf16[128,1536]{1,0:T(8,128)(2,1)}, bf16[128,1536]{1,0:T(8,128)(2,1)}, u32[]{:S(2)}, u32[]{:S(2)}) collective-permute-start(bf16[128,1536]{1,0:T(8,128)(2,1)} %multiply_convert_fusion.6.refs_6_), channel_id=1, source_target_pairs={{0,12},{4,0},{8,4},{12,8},{1,13},{5,1},{9,5},{13,9},{2,14},{6,2},{... | collective-permute-start | bytes 1179656 | tf_op jit(solution)/shard_map/ppermute | solution.py:333
  396.9 69.2 %collective-permute-start.55 = (bf16[256,3072]{1,0:T(8,128)(2,1)S(1)}, bf16[256,3072]{1,0:T(8,128)(2,1)S(1)}, u32[]{:S(2)}, u32[]{:S(2)}) collective-permute-start(bf16[256,3072]{1,0:T(8,128)(2,1)S(1)} %constant_dynamic-update-slice_fusion.3), channel_id=1, source_target_pairs={{0,1},{1,0},{2,3},{3,2},{4,5},{5,4},{6,7},{7,6},{8,9},{9,8},{10,11... | collective-permute-start | bytes 4718600 | tf_op jit(solution)/shard_map/ppermute | solution.py:366
  397.0 47.2 %collective-permute-start.56 = (bf16[256,3072]{1,0:T(8,128)(2,1)S(1)}, bf16[256,3072]{1,0:T(8,128)(2,1)S(1)}, u32[]{:S(2)}, u32[]{:S(2)}) collective-permute-start(bf16[256,3072]{1,0:T(8,128)(2,1)S(1)} %constant_dynamic-update-slice_fusion.3), channel_id=1, source_target_pairs={{0,2},{1,3},{2,0},{3,1},{4,6},{5,7},{6,4},{7,5},{8,10},{9,11},{10,... | collective-permute-start | bytes 4718600 | tf_op jit(solution)/shard_map/ppermute | solution.py:591
  431.9 29.5 %collective-permute-start.53 = (bf16[128,1664]{1,0:T(8,128)(2,1)}, bf16[128,1664]{1,0:T(8,128)(2,1)S(1)}, u32[]{:S(2)}, u32[]{:S(2)}) collective-permute-start(bf16[128,1664]{1,0:T(8,128)(2,1)} %get-tuple-element.205), channel_id=1, source_target_pairs={{0,8},{4,12},{8,0},{12,4},{1,9},{5,13},{9,1},{13,5},{2,10},{6,14},... | collective-permute-start | bytes 1277960 | tf_op jit(solution)/shard_map/ppermute | solution.py:341
  443.6 35.6 %collective-permute-start.60 = (bf16[1,512,1536]{2,1,0:T(8,128)(2,1)S(1)}, bf16[1,512,1536]{2,1,0:T(8,128)(2,1)}, u32[]{:S(2)}, u32[]{:S(2)}) collective-permute-start(bf16[1,512,1536]{2,1,0:T(8,128)(2,1)S(1)} %get-tuple-element.389), channel_id=1, source_target_pairs={{0,16},{16,0},{1,17},{17,1},{2,18},{18,2},{3,19},{19,3},{4,20},{20... | collective-permute-start | bytes 4718600 | tf_op jit(solution)/shard_map/ppermute | solution.py:361
  444.2 35.0 %collective-permute-start.57 = (bf16[256,3072]{1,0:T(8,128)(2,1)S(1)}, bf16[256,3072]{1,0:T(8,128)(2,1)S(1)}, u32[]{:S(2)}, u32[]{:S(2)}) collective-permute-start(bf16[256,3072]{1,0:T(8,128)(2,1)S(1)} %collective-permute-done.56), channel_id=1, source_target_pairs={{0,1},{1,0},{2,3},{3,2},{4,5},{5,4},{6,7},{7,6},{8,9},{9,8},{10,11... | collective-permute-start | bytes 4718600 | tf_op jit(solution)/shard_map/ppermute | solution.py:366
  462.6 37.1 %collective-permute-start.61 = (bf16[1,512,1536]{2,1,0:T(8,128)(2,1)}, bf16[1,512,1536]{2,1,0:T(8,128)(2,1)}, u32[]{:S(2)}, u32[]{:S(2)}) collective-permute-start(bf16[1,512,1536]{2,1,0:T(8,128)(2,1)} %get-tuple-element.388), channel_id=1, source_target_pairs={{0,2},{1,3},{2,0},{3,1},{4,6},{5,7},{6,4},{7,5},{8,10},{9,11},{10,... | collective-permute-start | bytes 4718600 | tf_op jit(solution)/shard_map/ppermute | solution.py:591
  512.0 35.4 %collective-permute-start.65 = (bf16[1,512,1536]{2,1,0:T(8,128)(2,1)}, bf16[1,512,1536]{2,1,0:T(8,128)(2,1)}, u32[]{:S(2)}, u32[]{:S(2)}) collective-permute-start(bf16[1,512,1536]{2,1,0:T(8,128)(2,1)} %collective-permute-done.60), channel_id=1, source_target_pairs={{0,2},{1,3},{2,0},{3,1},{4,6},{5,7},{6,4},{7,5},{8,10},{9,11},{10,... | collective-permute-start | bytes 4718600 | tf_op jit(solution)/shard_map/ppermute | solution.py:591
  547.4 273.5 %reduce-scatter.8.cloned.1.call-start = ((), (), s32[]{:S(2)}) async-start(), calls=%async_computation.6 | async-start | bytes 1536000 | tf_op jit(solution)/shard_map/reduce_scatter | solution.py:830
  584.2 29.2 %collective-permute-start.67 = (bf16[128,1536]{1,0:T(8,128)(2,1)S(1)}, bf16[128,1536]{1,0:T(8,128)(2,1)S(1)}, u32[]{:S(2)}, u32[]{:S(2)}) collective-permute-start(bf16[128,1536]{1,0:T(8,128)(2,1)S(1)} %get-tuple-element.230.refs_6_), channel_id=1, source_target_pairs={{0,8},{4,12},{8,0},{12,4},{1,9},{5,13},{9,1},{13,5},{2,10},{6,14},... | collective-permute-start | bytes 1179656 | tf_op jit(solution)/shard_map/ppermute | solution.py:333
  585.8 27.6 %collective-permute-start.68 = (bf16[128,1536]{1,0:T(8,128)(2,1)S(1)}, bf16[128,1536]{1,0:T(8,128)(2,1)S(1)}, u32[]{:S(2)}, u32[]{:S(2)}) collective-permute-start(bf16[128,1536]{1,0:T(8,128)(2,1)S(1)} %get-tuple-element.230.refs_6_), channel_id=1, source_target_pairs={{0,12},{4,0},{8,4},{12,8},{1,13},{5,1},{9,5},{13,9},{2,14},{6,2},{... | collective-permute-start | bytes 1179656 | tf_op jit(solution)/shard_map/ppermute | solution.py:333
  636.6 40.1 %collective-permute-start.74 = (bf16[1,512,1536]{2,1,0:T(8,128)(2,1)S(1)}, bf16[1,512,1536]{2,1,0:T(8,128)(2,1)S(1)}, u32[]{:S(2)}, u32[]{:S(2)}) collective-permute-start(bf16[1,512,1536]{2,1,0:T(8,128)(2,1)S(1)} %get-tuple-element.249), channel_id=1, source_target_pairs={{0,2},{1,3},{2,0},{3,1},{4,6},{5,7},{6,4},{7,5},{8,10},{9,11},{10,... | collective-permute-start | bytes 4718600 | tf_op jit(solution)/shard_map/ppermute | solution.py:591
  638.1 38.6 %collective-permute-start.75 = (bf16[1,512,1536]{2,1,0:T(8,128)(2,1)S(1)}, bf16[1,512,1536]{2,1,0:T(8,128)(2,1)}, u32[]{:S(2)}, u32[]{:S(2)}) collective-permute-start(bf16[1,512,1536]{2,1,0:T(8,128)(2,1)S(1)} %get-tuple-element.386), channel_id=1, source_target_pairs={{0,16},{16,0},{1,17},{17,1},{2,18},{18,2},{3,19},{19,3},{4,20},{20... | collective-permute-start | bytes 4718600 | tf_op jit(solution)/shard_map/ppermute | solution.py:361
  647.3 29.2 %collective-permute-start.70 = (bf16[128,1664]{1,0:T(8,128)(2,1)S(1)}, bf16[128,1664]{1,0:T(8,128)(2,1)S(1)}, u32[]{:S(2)}, u32[]{:S(2)}) collective-permute-start(bf16[128,1664]{1,0:T(8,128)(2,1)S(1)} %copy-done.177), channel_id=1, source_target_pairs={{0,8},{4,12},{8,0},{12,4},{1,9},{5,13},{9,1},{13,5},{2,10},{6,14},... | collective-permute-start | bytes 1277960 | tf_op jit(solution)/shard_map/ppermute | solution.py:341
  649.2 27.2 %collective-permute-start.69 = (bf16[128,1664]{1,0:T(8,128)(2,1)S(1)}, bf16[128,1664]{1,0:T(8,128)(2,1)S(1)}, u32[]{:S(2)}, u32[]{:S(2)}) collective-permute-start(bf16[128,1664]{1,0:T(8,128)(2,1)S(1)} %copy-done.176), channel_id=1, source_target_pairs={{0,12},{4,0},{8,4},{12,8},{1,13},{5,1},{9,5},{13,9},{2,14},{6,2},{... | collective-permute-start | bytes 1277960 | tf_op jit(solution)/shard_map/ppermute | solution.py:341
  727.8 54.3 %collective-permute-start.89 = (bf16[1,512,1536]{2,1,0:T(8,128)(2,1)}, bf16[1,512,1536]{2,1,0:T(8,128)(2,1)}, u32[]{:S(2)}, u32[]{:S(2)}) collective-permute-start(bf16[1,512,1536]{2,1,0:T(8,128)(2,1)} %collective-permute-done.75), channel_id=1, source_target_pairs={{0,2},{1,3},{2,0},{3,1},{4,6},{5,7},{6,4},{7,5},{8,10},{9,11},{10,... | collective-permute-start | bytes 4718600 | tf_op jit(solution)/shard_map/ppermute | solution.py:591
  732.1 32.8 %collective-permute-start.83 = (bf16[128,2048]{0,1:T(8,128)(2,1)}, bf16[128,2048]{0,1:T(8,128)(2,1)}, u32[]{:S(2)}, u32[]{:S(2)}) collective-permute-start(bf16[128,2048]{0,1:T(8,128)(2,1)} %get-tuple-element.423), channel_id=1, source_target_pairs={{0,16},{16,0},{1,17},{17,1},{2,18},{18,2},{3,19},{19,3},{4,20},{20... | collective-permute-start | bytes 1572872 | tf_op jit(solution)/shard_map/ppermute | solution.py:361
  737.1 31.5 %collective-permute-start.85 = (bf16[128,1536]{1,0:T(8,128)(2,1)}, bf16[128,1536]{1,0:T(8,128)(2,1)}, u32[]{:S(2)}, u32[]{:S(2)}) collective-permute-start(bf16[128,1536]{1,0:T(8,128)(2,1)} %get-tuple-element.366), channel_id=1, source_target_pairs={{0,16},{16,0},{1,17},{17,1},{2,18},{18,2},{3,19},{19,3},{4,20},{20... | collective-permute-start | bytes 1179656 | tf_op jit(solution)/shard_map/ppermute | solution.py:361
  744.0 110.9 %reduce-scatter.6.cloned.1.call-start = ((), (), s32[]{:S(2)}) async-start(), calls=%async_computation.5 | async-start | bytes 1966080 | tf_op jit(solution)/shard_map/reduce_scatter | solution.py:830
  812.2 26.3 %collective-permute-start.96 = (bf16[1,1536,768]{2,1,0:T(8,128)(2,1)}, bf16[1,1536,768]{2,1,0:T(8,128)(2,1)}, u32[]{:S(2)}, u32[]{:S(2)}) collective-permute-start(bf16[1,1536,768]{2,1,0:T(8,128)(2,1)} %fusion.39), channel_id=1, source_target_pairs={{0,1},{1,0},{2,3},{3,2},{4,5},{5,4},{6,7},{7,6},{8,9},{9,8},{10,11... | collective-permute-start | bytes 7077896 | tf_op jit(solution)/shard_map/ppermute | solution.py:366
  817.5 28.1 %collective-permute-start.97 = (bf16[1,1536,768]{2,1,0:T(8,128)(2,1)S(1)}, bf16[1,1536,768]{2,1,0:T(8,128)(2,1)}, u32[]{:S(2)}, u32[]{:S(2)}) collective-permute-start(bf16[1,1536,768]{2,1,0:T(8,128)(2,1)S(1)} %fusion.40), channel_id=1, source_target_pairs={{0,1},{1,0},{2,3},{3,2},{4,5},{5,4},{6,7},{7,6},{8,9},{9,8},{10,11... | collective-permute-start | bytes 7077896 | tf_op jit(solution)/shard_map/ppermute | solution.py:366
  (261 other events, 4288.7 us)
Sparse Core Ops, SparseCore 0:
  98.6 144.1 all-gather.5
  281.5 37.5 all-gather.9
  321.3 46.3 all-gather.7
  547.6 33.7 reduce-scatter.3
  744.1 28.8 reduce-scatter.7
  821.0 33.8 reduce-scatter.5

commit v3 on v2

--- a/solution.py
+++ b/solution.py
@@ -258,8 +258,9 @@
 
 
 def moe_fwd_call(
-    scalars, tiles, routes_at, router, blocks, own, flat, folds, local, rows, parts, width, ff, capacity, top
+    scalars, tiles, routes_at, router, blocks, own, flat, folds, local, rows, parts, width, ff, capacity, top, tile_at
 ):
+    router, router_at = router
     picked_rows = folds * capacity
     shapes = [
         jax.ShapeDtypeStruct((local, picked_rows, width), BF16),
@@ -273,8 +274,13 @@
     out = pl.pallas_call(
         functools.partial(moe_fwd_kernel, folds, local, parts, capacity, routes_at, top),
         out_shape=shapes,
-        in_specs=[pl.BlockSpec(memory_space=pltpu.SMEM)]
-        + vmem(1 + 2 * folds) + anywhere(3 + len(flat)),
+        in_specs=[
+            pl.BlockSpec(memory_space=pltpu.SMEM),
+            pl.BlockSpec((router.shape[0], LANES), lambda i: (0, router_at)),
+        ]
+        + [pl.BlockSpec((rows, LANES), lambda i: (0, tile_at))] * folds
+        + vmem(folds) + anywhere(3 + len(flat)),
+        grid=(1,),
         out_specs=vmem(len(shapes)),
         scratch_shapes=weight_scratch(own, local, parts),
         cost_estimate=cost(local * picked_rows, width, ff, 3),
@@ -283,7 +289,7 @@
     return out[:7], out[7:]
 
 
-def moe_bwd_call(scalars, kept, blocks, own, flat, folds, local, rows, parts, width, ff, capacity, top):
+def moe_bwd_call(scalars, kept, blocks, own, flat, folds, local, rows, parts, width, ff, capacity, top, tile_at):
     _, gate_pre, up_pre, made, gate_rows, slots, _ = kept
     picked_rows = folds * capacity
     shapes = [jax.ShapeDtypeStruct((local, picked_rows, width), BF16)] + [
@@ -490,7 +496,7 @@
     if "moe" in tie:
         moe_in, experts_w, more = tie["moe"](moe_in, experts_w, more)
     blocks, tied = lax.optimization_barrier((rel_gather(moe_in), more))
-    parts, moe_kept = moe_forward(router, tiles, routes_at, scalars, experts_w, common["size"], blocks)
+    parts, moe_kept = moe_forward(tie["router"], tiles, routes_at, scalars, experts_w, common["size"], blocks)
     finish = lambda got: (residual + add_up(got)).astype(BF16)
     out = finish(send_back(parts)) if "last" not in tie else (parts, finish)
     kept = dict(
@@ -674,7 +680,7 @@
     head_got, last_blocks = lax.optimization_barrier((head_got, rel_gather(last_grad)))
     head_parts, crossed_y[0] = lax.optimization_barrier((rel_gather(head_got), crossed_y[0]))
     head_block = stacked_parts(head_parts)
-    tiles = [part[:rows, lin_width:] for part in head_parts]
+    tiles = head_parts
     crossed_y[1:] = [swap_section(value) for value in pieces[1:]]
     first = fold_id * local
     numbers = first + (jnp.arange(local, dtype=jnp.int32) ^ flip)
@@ -707,6 +713,7 @@
         piece = jnp.where(section == layer, keep, got)
         full = lax.all_gather(piece, (F_AX, S_AX, R_AX), axis=0, tiled=True)
         tail = full[:, split : split + LANES]
+        held["full"] = full
         return tail[:, expert_count : expert_count + 2].T, full[:, :split], full[:, split + LANES :], tail
 
     first_w = (
@@ -714,7 +721,7 @@
     )
     size = dict(
         folds=folds, local=local, rows=rows, parts=2, width=tokens.shape[3], ff=w_gate.shape[3],
-        capacity=capacity, top=top,
+        capacity=capacity, top=top, tile_at=lin_width // LANES,
     )
 
     lengths = own_batch(seq_lengths[:, 0])
@@ -735,10 +742,11 @@
     def first_mixed(tied_lin, tied, attn_in, mixed_low):
         gate_x, up_y = tied
         held["second"] = whole_weights(1, *tied_lin)
-        return (crossed_y[0], up_y, crossed_y[2]), (gate_x,)
+        return (crossed_y[0], up_y), (gate_x,)
 
     def first_moe(moe_in, own, more):
-        same, cross, moe_in = lax.optimization_barrier((*more, moe_in))
+        same, cross = more
+        same, cross, moe_in = lax.optimization_barrier(((*same, crossed_y[2]), cross, moe_in))
         cross = [*cross, swap_xor(same[1], 2), swap_xor(same[2], 2)]
         flat = []
         for one, two in zip(same, cross):
@@ -748,7 +756,7 @@
     held = {}
     first_value, first_kept, experts_w, _ = layer_forward(
         my_tokens, first_w, (w_gate[0], w_up[0], w_down[0]), common, tiles, routes_at, scalars[0],
-        dict(lin=(keep, got), kv=(swap_xor(crossed_y[0], 2), crossed_y[1]), mixed=first_mixed, moe=first_moe),
+        dict(router=(head_block, lin_width // LANES), lin=(keep, got), kv=(swap_xor(crossed_y[0], 2), crossed_y[1]), mixed=first_mixed, moe=first_moe),
         first_lin, first_out,
     )
     head_share, out_share, _ = lax.optimization_barrier(
@@ -772,7 +780,7 @@
         dict(
             mixed=lambda one, two, attn_in, mixed_low: (attn_in, mixed_low),
             moe=lambda moe_in, own, more: (moe_in, own, (left_pair(*more), weights_first)),
-            last=True,
+            last=True, router=(held["full"], split // LANES),
         ),
     )
     left_rows, weights_first = tied
@@ -788,11 +796,7 @@
             keep = lax.dynamic_slice_in_dim(value, (core ^ flip) * half, half, 0)
             give = lax.dynamic_slice_in_dim(value, (1 - (core ^ flip)) * half, half, 0)
             got = swap_core(give)
-            chip.append(
-                jnp.concatenate(
-                    [jnp.where(core == 0, keep, got), jnp.where(core == 0, got, keep)], axis=1
-                )
-            )
+            chip.append(jnp.concatenate([keep, got], axis=1))
         return chip
 
     chips = replicas // 2
@@ -822,12 +826,25 @@
             parts.append(piece if bit == 0 else swap_xor(piece, bit))
         return jnp.stack(parts)
 
-    def fold_sum(left, right, extra, tie):
+    def fold_sum(left, right, extra):
         total = mm_tn(left, right).astype(BF16)
         if extra is not None:
             total = total.reshape(folds, -1, total.shape[1])
             total = jnp.concatenate([total, extra], axis=1).reshape(-1, total.shape[2])
-        mine = lax.psum_scatter(total, F_AX, scatter_dimension=0, tiled=True)
+        return total
+
+    def late_part(total, tie):
+        if tie == ():
+            mine = lax.psum_scatter(total, F_AX, scatter_dimension=0, tiled=True)
+        else:
+            step = total.shape[0] // folds
+            mine = rel_scatter(
+                [
+                    lax.dynamic_slice_in_dim(total, ((fold_id - k) % folds) * step, step, 0)
+                    for k in range(folds)
+                ]
+            ).astype(BF16)
+            mine, tie = lax.optimization_barrier((mine, tie))
         whole = jnp.zeros((replicas,) + mine.shape, BF16)
         for bit, part in enumerate(group_rows(mine)):
             whole = lax.dynamic_update_index_in_dim(whole, part, replica ^ bit, 0)
@@ -849,60 +866,61 @@
 
     def last_rows(grad_expert):
         held["rows"] = chip_rows([grad_expert])[0]
-        return left_whole, stacked_parts(second_parts), swap_section(x_give)
+        return left_whole, stacked_parts(second_parts)
 
     def last_attn(grad_attn, small, sent):
         held["attn"] = with_small(grad_attn, small)
-        return all_x(x_mine)
+        return swap_section(x_give), sent[1]
 
     def first_rows(grad_expert):
         chip = (chip_rows([grad_expert])[0], held["rows"])
         mine = own_layer(chip)
-        return mine, all_x(mine), swap_section(other_layer(chip))
+        return mine, all_x(mine), swap_section(other_layer(chip)), x_own, second_stack
 
     def first_attn(grad_attn, small, sent):
+        *sent, stack = sent
+        held["second_sum"] = lax.psum_scatter(stack, F_AX, scatter_dimension=0, tiled=True)
         return both_rows((with_small(grad_attn, small), held["attn"])), sent
 
     def first_later(sent, crossed):
-        right_out, (mine, mine_x, got) = crossed
-        held["got_x"] = all_x(got)
+        right_out, (mine, mine_x, got, x_own) = crossed
         g_own = by_order(mine, mine_x)
-        return g_own, [expert_middle(x_own[i], flat_rows(g_own)[i], *[w[i] for w in mine_w]) for i in range(half)], got, own_columns(right_out)
+        return x_own, g_own, [expert_middle(x_own[i], flat_rows(g_own)[i], *[w[i] for w in mine_w]) for i in range(half)], got, own_columns(right_out)
 
     grads, grad_lin = [None, None], [None, None]
-    grads[1], grad_lin[1], ((left_whole, second_stack, x_got), x_mine_x, x_got_x), _ = layer_backward(
+    grads[1], grad_lin[1], ((left_whole, _), (x_got, second_stack), x_mine_x), _ = layer_backward(
         last_grad, kept[1], weights[1], experts_w, common, scalars[1], (),
-        dict(rows=last_rows, attn=last_attn, later=lambda sent, crossed: (sent, crossed, all_x(sent[2])), blocks=last_blocks),
-    )
-    second_sum = lax.psum_scatter(second_stack, F_AX, scatter_dimension=0, tiled=True)
-    outs = [first_value, second_finish([second_sum])]
+        dict(rows=last_rows, attn=last_attn, later=lambda sent, crossed: (sent, crossed, all_x(x_mine)), blocks=last_blocks),
+    )
     x_own = flat_rows(by_order(x_mine, x_mine_x))
     x_own = [x_own[i] for i in range(half)]
     mine_w = [lax.dynamic_slice_in_dim(part[0], core * half, half, 0) for part in (w_gate, w_up, w_down)]
-    grads[0], grad_lin[0], later, _ = layer_backward(
-        grads[1], kept[0], weights[0], experts_w, common, scalars[0], (),
+    grads[0], grad_lin[0], later, x_got_x = layer_backward(
+        grads[1], kept[0], weights[0], experts_w, common, scalars[0], all_x(x_got),
         dict(rows=first_rows, attn=first_attn, later=first_later),
     )
-    g_own, middle_own, got, right_out = later
+    x_own, g_own, middle_own, got, right_out = later
     left_whole = jnp.concatenate(left_whole, axis=0)
-    lin_rows = both_rows(grad_lin)
-    got_x = held["got_x"]
-    lin_rows, outs = lax.optimization_barrier((lin_rows, outs))
-    right = own_columns(lin_rows)
-    g_got, x_got = by_order(got, got_x), by_order(x_got, x_got_x)
-    right, g_got, x_got = lax.optimization_barrier((right, g_got, x_got))
-    x_got = [flat_rows(x_got)[i] for i in range(half)]
-    g_own, g_got = [[flat_rows(value)[i] for i in range(half)] for value in (g_own, g_got)]
-    middle_got = [expert_middle(x_got[i], g_got[i], *[w[i] for w in mine_w]) for i in range(half)]
-
     right_out = right_out.reshape(replicas, 2, rows + tall, -1)
     extra = jnp.sum(right_out[:, :, rows:].astype(F32), axis=(0, 1)).reshape(tall, folds, piece)
     extra = jnp.pad(
         jnp.transpose(extra, (1, 0, 2)), ((0, 0), (0, 0), (0, right_out.shape[3] - piece))
     ).astype(BF16)
     right_out = right_out[:, :, :rows].reshape(-1, right_out.shape[3])
-    out_shard, _ = fold_sum(left_whole[:, model:], right_out, extra, ())
-    shard, middle_got = fold_sum(left_whole[:, :model], right.reshape(-1, right.shape[2]), None, middle_got)
+    out_shard, _ = late_part(fold_sum(left_whole[:, model:], right_out, extra), ())
+    lin_rows, second_sum = lax.optimization_barrier((both_rows(grad_lin), held["second_sum"]))
+    right, got = lax.optimization_barrier((own_columns(lin_rows), got))
+    got_x = all_x(got)
+    g_got, x_got = by_order(got, got_x), by_order(x_got, x_got_x)
+    shard = fold_sum(left_whole[:, :model], right.reshape(-1, right.shape[2]), None)
+    shard, (middle_own, x_own, first_value, grads) = lax.optimization_barrier(
+        (shard, (middle_own, x_own, first_value, grads))
+    )
+    x_got = [flat_rows(x_got)[i] for i in range(half)]
+    g_own, g_got = [[flat_rows(value)[i] for i in range(half)] for value in (g_own, g_got)]
+    middle_got = [expert_middle(x_got[i], g_got[i], *[w[i] for w in mine_w]) for i in range(half)]
+
+    shard, middle_got = late_part(shard, middle_got)
     made = []
     for i in range(half):
         inner, gate, up = zip(middle_own[i], middle_got[i])
@@ -913,6 +931,8 @@
                 (mm_tn(inner[0], g_own[i]) + mm_tn(inner[1], g_got[i])).astype(BF16),
             )
         )
+    made, second_sum = lax.optimization_barrier((made, second_sum))
+    outs = [first_value, second_finish([second_sum])]
     small = side_by_side(out_shard[:, depth:, :piece])
     out_shard = side_by_side(out_shard[:, :depth])
     shard = side_by_side(shard)

time: 891 us -> 839 us (0.942)
  matrix products: 133 us -> 115 us
  starting transfers between devices: 161 us -> 151 us
    dot_general x10, matrix products: 46.5 us -> 29.9 us  [mm_tn(): lax.dot_general(a, b, (((0,), (0,)), ((), ())), preferred_element_type=F32)]
    ppermute x12 -> x15, starting transfers between devices: 44.8 us -> 36.7 us  [rel_scatter(): lax.ppermute(parts[k], F_AX, [(i, (i - k) % folds) for i in range(folds)])]
    unnamed x420 -> x432, local copies, waits for them, and re-layouts: 28.3 us -> 29.9 us
    ppermute x12 -> x15, waiting for transfers between devices: 52.2 us -> 53 us  [rel_scatter(): lax.ppermute(parts[k], F_AX, [(i, (i - k) % folds) for i in range(folds)])]
  transfers between devices with their start and end apart: 105 -> 107, of which waited for: 43 -> 44; matrix products, arithmetic and copies ran while one was open for 31% -> 27% of each run, Pallas kernels for 4% -> 6%
where the time goes in v3:
time: 839 us; the launch traced here: 829 us
  waiting for transfers between devices  325 us (39%)
  starting transfers between devices  151 us (18%)
  matrix products  115 us (14%)
  local copies, waits for them, and re-layouts  94.5 us (11%)
  other arithmetic  75 us (9%)
  Pallas kernels  51.4 us (6%)
  between operations  17.8 us (2%)
    ppermute x24, waiting for transfers between devices, rel_gather(): lax.ppermute(value, F_AX, [(i, (i + k) % folds) for i in range(folds)])  131 us
    ppermute x24, starting transfers between devices, rel_gather(): lax.ppermute(value, F_AX, [(i, (i + k) % folds) for i in range(folds)])  66 us
    ppermute x24, waiting for transfers between devices, swap_xor(): return lax.ppermute(value, R_AX, [(i, i ^ bit) for i in range(replicas)])  61.1 us
    ppermute x15, waiting for transfers between devices, rel_scatter(): lax.ppermute(parts[k], F_AX, [(i, (i - k) % folds) for i in range(folds)])  53 us
    dot_general x16, matrix products, mm_nt(): lax.dot_general(a, b, (((1,), (1,)), ((), ())), preferred_element_type=F32)  37.4 us
    ppermute x13, waiting for transfers between devices, swap_section(): return lax.ppermute(value, S_AX, [(0, 1), (1, 0)])  37.1 us
    ppermute x15, starting transfers between devices, rel_scatter(): lax.ppermute(parts[k], F_AX, [(i, (i - k) % folds) for i in range(folds)])  36.7 us
    unnamed x432, local copies, waits for them, and re-layouts  29.9 us
  transfers between devices with their start and end apart: 107, of which 44 were waited for; matrix products, arithmetic and copies ran while one was open for 27% of the time, Pallas kernels for 6%

profile of v3, /device:TPU:0, one launch (start us, length us, event | category | flops | bytes accessed | tf_op | source)
XLA Modules:
  0.0 829.3 jit_solution(1115986616530000430)
XLA Ops:
  29.8 4.6 dynamic-slice_bitcast_fusion.1
  36.0 4.8 collective-permute-done.11
  60.1 6.3 collective-permute-done.7.refs_3_
  66.5 17.5 %collective-permute-done.8.refs_4_ = bf16[384,640]{1,0:T(8,128)(2,1)S(1)} collective-permute-done((bf16[384,640]{1,0:T(8,128)(2,1)S(1)}, bf16[384,640]{1,0:T(8,128)(2,1)S(1)}, u32[]{:S(2)}, u32[]{:S(2)}) %collective-permute-start.8) | collective-permute-done | bytes 491552 | tf_op jit(solution)/shard_map/ppermute | solution.py:339
  88.8 4.3 collective-permute-done.13
  104.0 11.6 %collective-permute-start.18 = (bf16[128,512]{0,1:T(8,128)(2,1)S(1)}, bf16[128,512]{0,1:T(8,128)(2,1)S(1)}, u32[]{:S(2)}, u32[]{:S(2)}) collective-permute-start(bf16[128,512]{0,1:T(8,128)(2,1)S(1)} %pad_maximum_fusion.23), channel_id=1, source_target_pairs={{0,12},{4,0},{8,4},{12,8},{1,13},{5,1},{9,5},{13,9},{2,14},{6,2},{... | collective-permute-start | bytes 393224 | tf_op jit(solution)/shard_map/ppermute | solution.py:339
  122.8 12.8 %collective-permute-done.17 = bf16[128,512]{0,1:T(8,128)(2,1)S(1)} collective-permute-done((bf16[128,512]{0,1:T(8,128)(2,1)S(1)}, bf16[128,512]{0,1:T(8,128)(2,1)S(1)}, u32[]{:S(2)}, u32[]{:S(2)}) %collective-permute-start.17) | collective-permute-done | bytes 131104 | tf_op jit(solution)/shard_map/ppermute | solution.py:339
  157.3 10.7 %collective-permute-done.22 = bf16[128,1536]{0,1:T(8,128)(2,1)S(1)} collective-permute-done((bf16[128,1536]{0,1:T(8,128)(2,1)S(1)}, bf16[128,1536]{0,1:T(8,128)(2,1)S(1)}, u32[]{:S(2)}, u32[]{:S(2)}) %collective-permute-start.22) | collective-permute-done | bytes 393248 | tf_op jit(solution)/shard_map/ppermute | solution.py:597
  186.9 11.6 %collective-permute-start.31 = (bf16[128,1536]{1,0:T(8,128)(2,1)S(1)}, bf16[128,1536]{1,0:T(8,128)(2,1)S(1)}, u32[]{:S(2)}, u32[]{:S(2)}) collective-permute-start(bf16[128,1536]{1,0:T(8,128)(2,1)S(1)} %get-tuple-element.182.refs_6_), channel_id=1, source_target_pairs={{0,4},{4,8},{8,12},{12,0},{1,5},{5,9},{9,13},{13,1},{2,6},{6,10},{... | collective-permute-start | bytes 1179656 | tf_op jit(solution)/shard_map/ppermute | solution.py:339
  202.0 13.8 %collective-permute-done.31.refs_7_ = bf16[128,1536]{1,0:T(8,128)(2,1)S(1)} collective-permute-done((bf16[128,1536]{1,0:T(8,128)(2,1)S(1)}, bf16[128,1536]{1,0:T(8,128)(2,1)S(1)}, u32[]{:S(2)}, u32[]{:S(2)}) %collective-permute-start.31) | collective-permute-done | bytes 393248 | tf_op jit(solution)/shard_map/ppermute | solution.py:339
  217.0 25.4 %collective-permute-done.32.refs_8_ = bf16[128,1536]{1,0:T(8,128)(2,1)S(1)} collective-permute-done((bf16[128,1536]{1,0:T(8,128)(2,1)S(1)}, bf16[128,1536]{1,0:T(8,128)(2,1)S(1)}, u32[]{:S(2)}, u32[]{:S(2)}) %collective-permute-start.32) | collective-permute-done | bytes 393248 | tf_op jit(solution)/shard_map/ppermute | solution.py:339
  244.9 9.5 %collective-permute-done.40.refs_23_ = bf16[384,1536]{1,0:T(8,128)(2,1)} collective-permute-done((bf16[384,1536]{1,0:T(8,128)(2,1)}, bf16[384,1536]{1,0:T(8,128)(2,1)}, u32[]{:S(2)}, u32[]{:S(2)}) %collective-permute-start.40) | collective-permute-done | bytes 1179680 | tf_op jit(solution)/shard_map/ppermute | solution.py:597
  257.8 12.7 %shard_map.212 = (bf16[2,256,1536]{2,1,0:T(8,128)(2,1)}, f32[2,256,768]{2,1,0:T(8,128)}, f32[2,256,768]{2,1,0:T(8,128)}, bf16[2,256,1536]{2,1,0:T(8,128)(2,1)}, ...) custom-call(s32[4]{0:T(128)} %get-tuple-element.517.refs_0_, ...), custom_call_target="tpu_custom_call" | custom-call | flops 3623878656 | bytes 20447232 | tf_op jit(solution)/shard_map/pallas_call | solution.py:274
  271.3 5.5 collective-permute-start.44
  282.2 6.7 collective-permute-done.44
  288.9 16.6 %collective-permute-done.43 = bf16[128,1536]{1,0:T(8,128)(2,1)} collective-permute-done((bf16[128,1536]{1,0:T(8,128)(2,1)}, bf16[128,1536]{1,0:T(8,128)(2,1)}, u32[]{:S(2)}, u32[]{:S(2)}) %collective-permute-start.43) | collective-permute-done | bytes 393248 | tf_op jit(solution)/shard_map/ppermute | solution.py:355
  317.9 9.0 %collective-permute-start.47 = (bf16[128,512]{1,0:T(8,128)(2,1)S(1)}, bf16[128,512]{1,0:T(8,128)(2,1)S(1)}, u32[]{:S(2)}, u32[]{:S(2)}) collective-permute-start(bf16[128,512]{1,0:T(8,128)(2,1)S(1)} %pad_maximum_fusion.24), channel_id=1, source_target_pairs={{0,12},{4,0},{8,4},{12,8},{1,13},{5,1},{9,5},{13,9},{2,14},{6,2},{... | collective-permute-start | bytes 393224 | tf_op jit(solution)/shard_map/ppermute | solution.py:339
  330.8 9.6 %collective-permute-done.46 = bf16[128,512]{1,0:T(8,128)(2,1)S(1)} collective-permute-done((bf16[128,512]{1,0:T(8,128)(2,1)S(1)}, bf16[128,512]{1,0:T(8,128)(2,1)S(1)}, u32[]{:S(2)}, u32[]{:S(2)}) %collective-permute-start.46) | collective-permute-done | bytes 131104 | tf_op jit(solution)/shard_map/ppermute | solution.py:339
  364.2 5.7 collective-permute-done.48.refs_7_
  369.9 14.8 %collective-permute-done.49.refs_8_ = bf16[128,1536]{1,0:T(8,128)(2,1)} collective-permute-done((bf16[128,1536]{1,0:T(8,128)(2,1)S(1)}, bf16[128,1536]{1,0:T(8,128)(2,1)}, u32[]{:S(2)}, u32[]{:S(2)}) %collective-permute-start.49) | collective-permute-done | bytes 393248 | tf_op jit(solution)/shard_map/ppermute | solution.py:339
  387.7 12.7 %shard_map.213 = (bf16[2,256,1536]{2,1,0:T(8,128)(2,1)}, f32[2,256,768]{2,1,0:T(8,128)}, f32[2,256,768]{2,1,0:T(8,128)}, bf16[2,256,1536]{2,1,0:T(8,128)(2,1)}, ...) custom-call(s32[4]{0:T(128)} %get-tuple-element.516.refs_0_, ...), custom_call_target="tpu_custom_call" | custom-call | flops 3623878656 | bytes 20447232 | tf_op jit(solution)/shard_map/pallas_call | solution.py:274
  400.4 13.2 %shard_map.214 = (bf16[2,256,1536]{2,1,0:T(8,128)(2,1)}, bf16[128,1664]{1,0:T(8,128)(2,1)}, bf16[128,1664]{1,0:T(8,128)(2,1)}, bf16[128,1664]{1,0:T(8,128)(2,1)}, bf16[128,1664]{1,0:T(8,128)(2,1)}) custom-call(s32[4]{0:T(128)} %get-tuple-element.516.refs_0_, s32[4,2,128]{2,1,0:T(2,128)} %get-tuple-element.206.refs_1_, ...), custom_call_target="tpu_custom_call" | custom-call | flops 3623878656 | bytes 20447232 | tf_op jit(solution)/shard_map/pallas_call | solution.py:298
  413.6 8.3 %collective-permute-start.54 = (bf16[128,1664]{1,0:T(8,128)(2,1)}, bf16[128,1664]{1,0:T(8,128)(2,1)S(1)}, u32[]{:S(2)}, u32[]{:S(2)}) collective-permute-start(bf16[128,1664]{1,0:T(8,128)(2,1)} %get-tuple-element.222), channel_id=1, source_target_pairs={{0,4},{4,8},{8,12},{12,0},{1,5},{5,9},{9,13},{13,1},{2,6},{6,10},{... | collective-permute-start | bytes 1277960 | tf_op jit(solution)/shard_map/ppermute | solution.py:347
  427.8 5.3 collective-permute-done.54
  433.1 17.8 %collective-permute-done.53 = bf16[128,1664]{1,0:T(8,128)(2,1)S(1)} collective-permute-done((bf16[128,1664]{1,0:T(8,128)(2,1)}, bf16[128,1664]{1,0:T(8,128)(2,1)S(1)}, u32[]{:S(2)}, u32[]{:S(2)}) %collective-permute-start.53) | collective-permute-done | bytes 426016 | tf_op jit(solution)/shard_map/ppermute | solution.py:347
  469.6 4.7 fusion.50
  480.1 12.7 %collective-permute-done.60 = bf16[1,512,1536]{2,1,0:T(8,128)(2,1)} collective-permute-done((bf16[1,512,1536]{2,1,0:T(8,128)(2,1)}, bf16[1,512,1536]{2,1,0:T(8,128)(2,1)}, u32[]{:S(2)}, u32[]{:S(2)}) %collective-permute-start.60) | collective-permute-done | bytes 1572896 | tf_op jit(solution)/shard_map/ppermute | solution.py:367
  493.5 8.4 %collective-permute-start.63 = (bf16[128,512]{0,1:T(8,128)(2,1)}, bf16[128,512]{0,1:T(8,128)(2,1)}, u32[]{:S(2)}, u32[]{:S(2)}) collective-permute-start(bf16[128,512]{0,1:T(8,128)(2,1)} %get-tuple-element.484), channel_id=1, source_target_pairs={{0,4},{4,8},{8,12},{12,0},{1,5},{5,9},{9,13},{13,1},{2,6},{6,10},{... | collective-permute-start | bytes 393224 | tf_op jit(solution)/shard_map/ppermute | solution.py:347
  515.1 5.2 fusion.139
  536.0 14.3 %collective-permute-done.66.refs_8_ = bf16[128,1536]{1,0:T(8,128)(2,1)S(1)} collective-permute-done((bf16[128,1536]{1,0:T(8,128)(2,1)S(1)}, bf16[128,1536]{1,0:T(8,128)(2,1)S(1)}, u32[]{:S(2)}, u32[]{:S(2)}) %collective-permute-start.66) | collective-permute-done | bytes 393248 | tf_op jit(solution)/shard_map/ppermute | solution.py:339
  550.3 11.9 %collective-permute-done.68 = bf16[1,512,1536]{2,1,0:T(8,128)(2,1)S(1)} collective-permute-done((bf16[1,512,1536]{2,1,0:T(8,128)(2,1)}, bf16[1,512,1536]{2,1,0:T(8,128)(2,1)S(1)}, u32[]{:S(2)}, u32[]{:S(2)}) %collective-permute-start.68) | collective-permute-done | bytes 1572896 | tf_op jit(solution)/shard_map/ppermute | solution.py:597
  563.4 12.9 %shard_map.215 = (bf16[2,256,1536]{2,1,0:T(8,128)(2,1)}, bf16[128,1664]{1,0:T(8,128)(2,1)}, bf16[128,1664]{1,0:T(8,128)(2,1)}, bf16[128,1664]{1,0:T(8,128)(2,1)}, bf16[128,1664]{1,0:T(8,128)(2,1)}) custom-call(s32[4]{0:T(128)} %get-tuple-element.517.refs_0_, s32[4,2,128]{2,1,0:T(2,128)} %get-tuple-element.246.refs_1_, ...), custom_call_target="tpu_custom_call" | custom-call | flops 3623878656 | bytes 20447232 | tf_op jit(solution)/shard_map/pallas_call | solution.py:298
  588.4 4.4 fusion.64
  592.8 4.4 fusion.60
  597.2 14.3 %collective-permute-done.70 = bf16[128,1664]{1,0:T(8,128)(2,1)S(1)} collective-permute-done((bf16[128,1664]{1,0:T(8,128)(2,1)}, bf16[128,1664]{1,0:T(8,128)(2,1)S(1)}, u32[]{:S(2)}, u32[]{:S(2)}) %collective-permute-start.70) | collective-permute-done | bytes 426016 | tf_op jit(solution)/shard_map/ppermute | solution.py:347
  611.8 10.5 %collective-permute-done.74 = bf16[1,512,1536]{2,1,0:T(8,128)(2,1)S(1)} collective-permute-done((bf16[1,512,1536]{2,1,0:T(8,128)(2,1)S(1)}, bf16[1,512,1536]{2,1,0:T(8,128)(2,1)S(1)}, u32[]{:S(2)}, u32[]{:S(2)}) %collective-permute-start.74) | collective-permute-done | bytes 1572896 | tf_op jit(solution)/shard_map/ppermute | solution.py:597
  666.3 6.3 multiply_convert_fusion.2
  688.1 10.1 %collective-permute-done.83 = bf16[128,2048]{0,1:T(8,128)(2,1)S(1)} collective-permute-done((bf16[128,2048]{0,1:T(8,128)(2,1)S(1)}, bf16[128,2048]{0,1:T(8,128)(2,1)S(1)}, u32[]{:S(2)}, u32[]{:S(2)}) %collective-permute-start.83) | collective-permute-done | bytes 524320 | tf_op jit(solution)/shard_map/ppermute | solution.py:367
  705.3 12.8 %reduce-scatter.5.cloned.1.call-done = bf16[400,384]{1,0:T(8,128)(2,1)} async-done(((bf16[1600,384]{1,0:T(8,128)(2,1)}), bf16[400,384]{1,0:T(8,128)(2,1)}) %reduce-scatter.5.cloned.1.call-update) | async-done | bytes 307216 | tf_op jit(solution)/shard_map/reduce_scatter | solution.py:838
  732.4 4.8 fusion.253
  752.0 7.5 collective-permute-done.88
  762.0 5.4 collective-permute-done.90
  767.6 7.1 multiply_convert_fusion
  774.7 5.2 add_convert_fusion.2
  789.9 6.2 collective-permute-done.91
  808.9 4.4 maximum_convert_fusion
  813.5 4.4 maximum_convert_fusion.1
  818.2 4.4 maximum_convert_fusion.2
  (911 shorter events, 358.4 us)
Async XLA Ops:
  7.2 300.2 %all-gather.6.cloned.1.call-start = ((), (), s32[]{:S(2)}) async-start(), calls=%async_computation.2 | async-start | bytes 11759616 | tf_op jit(solution)/shard_map/all_gather | solution.py:714
  9.0 37.9 %collective-permute-start.4 = (bf16[128,1536]{1,0:T(8,128)(2,1)}, bf16[128,1536]{1,0:T(8,128)(2,1)}, u32[]{:S(2)}, u32[]{:S(2)}) collective-permute-start(bf16[128,1536]{1,0:T(8,128)(2,1)} %dynamic-slice_bitcast_fusion.3.refs_6_), channel_id=1, source_target_pairs={{0,4},{4,8},{8,12},{12,0},{1,5},{5,9},{9,13},{13,1},{2,6},{6,10},{... | collective-permute-start | bytes 1179656 | tf_op jit(solution)/shard_map/ppermute | solution.py:339
  12.0 34.9 %collective-permute-start.5 = (bf16[128,1536]{1,0:T(8,128)(2,1)}, bf16[128,1536]{1,0:T(8,128)(2,1)}, u32[]{:S(2)}, u32[]{:S(2)}) collective-permute-start(bf16[128,1536]{1,0:T(8,128)(2,1)} %dynamic-slice_bitcast_fusion.3.refs_6_), channel_id=1, source_target_pairs={{0,8},{4,12},{8,0},{12,4},{1,9},{5,13},{9,1},{13,5},{2,10},{6,14},... | collective-permute-start | bytes 1179656 | tf_op jit(solution)/shard_map/ppermute | solution.py:339
  51.2 32.8 %collective-permute-start.8 = (bf16[384,640]{1,0:T(8,128)(2,1)S(1)}, bf16[384,640]{1,0:T(8,128)(2,1)S(1)}, u32[]{:S(2)}, u32[]{:S(2)}) collective-permute-start(bf16[384,640]{1,0:T(8,128)(2,1)S(1)} %fusion.158.refs_2_), channel_id=1, source_target_pairs={{0,8},{4,12},{8,0},{12,4},{1,9},{5,13},{9,1},{13,5},{2,10},{6,14},... | collective-permute-start | bytes 1474568 | tf_op jit(solution)/shard_map/ppermute | solution.py:339
  54.5 29.5 %collective-permute-start.10 = (bf16[1536,384]{1,0:T(8,128)(2,1)}, bf16[1536,384]{1,0:T(8,128)(2,1)S(1)}, u32[]{:S(2)}, u32[]{:S(2)}) collective-permute-start(bf16[1536,384]{1,0:T(8,128)(2,1)} %get-tuple-element.162), channel_id=1, source_target_pairs={{0,16},{16,0},{1,17},{17,1},{2,18},{18,2},{3,19},{19,3},{4,20},{20... | collective-permute-start | bytes 3538952 | tf_op jit(solution)/shard_map/ppermute | solution.py:367
  57.8 26.2 %collective-permute-start.9 = (bf16[384,640]{1,0:T(8,128)(2,1)S(1)}, bf16[384,640]{1,0:T(8,128)(2,1)S(1)}, u32[]{:S(2)}, u32[]{:S(2)}) collective-permute-start(bf16[384,640]{1,0:T(8,128)(2,1)S(1)} %fusion.158.refs_2_), channel_id=1, source_target_pairs={{0,12},{4,0},{8,4},{12,8},{1,13},{5,1},{9,5},{13,9},{2,14},{6,2},{... | collective-permute-start | bytes 1474568 | tf_op jit(solution)/shard_map/ppermute | solution.py:339
  59.2 36.8 %collective-permute-start.15 = (bf16[48,3712]{1,0:T(8,128)(2,1)S(1)}, bf16[48,3712]{1,0:T(8,128)(2,1)S(1)}, u32[]{:S(2)}, u32[]{:S(2)}) collective-permute-start(bf16[48,3712]{1,0:T(8,128)(2,1)S(1)} %get-tuple-element.168), channel_id=1, source_target_pairs={{0,16},{16,0},{1,17},{17,1},{2,18},{18,2},{3,19},{19,3},{4,20},{20... | collective-permute-start | bytes 1069064 | tf_op jit(solution)/shard_map/ppermute | solution.py:367
  96.8 267.4 %all-gather.10.cloned.1.call-start = ((), (), s32[]{:S(2)}) async-start(), calls=%async_computation.6 | async-start | bytes 5898240 | tf_op jit(solution)/shard_map/all_gather | solution.py:766
  98.5 39.4 %collective-permute-start.20 = (bf16[1536,384]{1,0:T(8,128)(2,1)}, bf16[1536,384]{1,0:T(8,128)(2,1)}, u32[]{:S(2)}, u32[]{:S(2)}) collective-permute-start(bf16[1536,384]{1,0:T(8,128)(2,1)} %get-tuple-element.171), channel_id=1, source_target_pairs={{0,16},{16,0},{1,17},{17,1},{2,18},{18,2},{3,19},{19,3},{4,20},{20... | collective-permute-start | bytes 3538952 | tf_op jit(solution)/shard_map/ppermute | solution.py:367
  100.2 41.9 %collective-permute-start.19 = (bf16[1536,384]{1,0:T(8,128)(2,1)S(1)}, bf16[1536,384]{1,0:T(8,128)(2,1)}, u32[]{:S(2)}, u32[]{:S(2)}) collective-permute-start(bf16[1536,384]{1,0:T(8,128)(2,1)S(1)} %collective-permute-done.10.refs_13_), channel_id=1, source_target_pairs={{0,2},{1,3},{2,0},{3,1},{4,6},{5,7},{6,4},{7,5},{8,10},{9,11},{10,... | collective-permute-start | bytes 3538952 | tf_op jit(solution)/shard_map/ppermute | solution.py:597
  121.6 62.5 %collective-permute-start.30 = (bf16[384,1536]{1,0:T(8,128)(2,1)}, bf16[384,1536]{1,0:T(8,128)(2,1)}, u32[]{:S(2)}, u32[]{:S(2)}) collective-permute-start(bf16[384,1536]{1,0:T(8,128)(2,1)} %dynamic-slice_bitcast_fusion), channel_id=1, source_target_pairs={{0,16},{16,0},{1,17},{17,1},{2,18},{18,2},{3,19},{19,3},{4,20},{20... | collective-permute-start | bytes 3538952 | tf_op jit(solution)/shard_map/ppermute | solution.py:367
  135.6 32.5 %collective-permute-start.25 = (bf16[384,384]{1,0:T(8,128)(2,1)}, bf16[384,384]{1,0:T(8,128)(2,1)}, u32[]{:S(2)}, u32[]{:S(2)}) collective-permute-start(bf16[384,384]{1,0:T(8,128)(2,1)} %broadcast_select_fusion.15), channel_id=1, source_target_pairs={{0,8},{4,12},{8,0},{12,4},{1,9},{5,13},{9,1},{13,5},{2,10},{6,14},... | collective-permute-start | bytes 884744 | tf_op jit(solution)/shard_map/ppermute | solution.py:339
  137.9 32.0 %collective-permute-start.26 = (bf16[384,384]{1,0:T(8,128)(2,1)}, bf16[384,384]{1,0:T(8,128)(2,1)}, u32[]{:S(2)}, u32[]{:S(2)}) collective-permute-start(bf16[384,384]{1,0:T(8,128)(2,1)} %broadcast_select_fusion.15), channel_id=1, source_target_pairs={{0,12},{4,0},{8,4},{12,8},{1,13},{5,1},{9,5},{13,9},{2,14},{6,2},{... | collective-permute-start | bytes 884744 | tf_op jit(solution)/shard_map/ppermute | solution.py:339
  184.0 59.2 %collective-permute-start.34 = (bf16[1536,384]{1,0:T(8,128)(2,1)S(1)}, bf16[1536,384]{1,0:T(8,128)(2,1)S(1)}, u32[]{:S(2)}, u32[]{:S(2)}) collective-permute-start(bf16[1536,384]{1,0:T(8,128)(2,1)S(1)} %collective-permute-done.10.refs_13_), channel_id=1, source_target_pairs={{0,1},{1,0},{2,3},{3,2},{4,5},{5,4},{6,7},{7,6},{8,9},{9,8},{10,11... | collective-permute-start | bytes 3538952 | tf_op jit(solution)/shard_map/ppermute | solution.py:372
  184.9 59.9 %collective-permute-start.37 = (bf16[1536,384]{1,0:T(8,128)(2,1)}, bf16[1536,384]{1,0:T(8,128)(2,1)}, u32[]{:S(2)}, u32[]{:S(2)}) collective-permute-start(bf16[1536,384]{1,0:T(8,128)(2,1)} %collective-permute-done.20.refs_17_), channel_id=1, source_target_pairs={{0,2},{1,3},{2,0},{3,1},{4,6},{5,7},{6,4},{7,5},{8,10},{9,11},{10,... | collective-permute-start | bytes 3538952 | tf_op jit(solution)/shard_map/ppermute | solution.py:597
  185.6 68.8 %collective-permute-start.40 = (bf16[384,1536]{1,0:T(8,128)(2,1)}, bf16[384,1536]{1,0:T(8,128)(2,1)}, u32[]{:S(2)}, u32[]{:S(2)}) collective-permute-start(bf16[384,1536]{1,0:T(8,128)(2,1)} %collective-permute-done.30.refs_21_), channel_id=1, source_target_pairs={{0,2},{1,3},{2,0},{3,1},{4,6},{5,7},{6,4},{7,5},{8,10},{9,11},{10,... | collective-permute-start | bytes 3538952 | tf_op jit(solution)/shard_map/ppermute | solution.py:597
  186.9 28.9 %collective-permute-start.31 = (bf16[128,1536]{1,0:T(8,128)(2,1)S(1)}, bf16[128,1536]{1,0:T(8,128)(2,1)S(1)}, u32[]{:S(2)}, u32[]{:S(2)}) collective-permute-start(bf16[128,1536]{1,0:T(8,128)(2,1)S(1)} %get-tuple-element.182.refs_6_), channel_id=1, source_target_pairs={{0,4},{4,8},{8,12},{12,0},{1,5},{5,9},{9,13},{13,1},{2,6},{6,10},{... | collective-permute-start | bytes 1179656 | tf_op jit(solution)/shard_map/ppermute | solution.py:339
  198.5 43.9 %collective-permute-start.32 = (bf16[128,1536]{1,0:T(8,128)(2,1)S(1)}, bf16[128,1536]{1,0:T(8,128)(2,1)S(1)}, u32[]{:S(2)}, u32[]{:S(2)}) collective-permute-start(bf16[128,1536]{1,0:T(8,128)(2,1)S(1)} %get-tuple-element.182.refs_6_), channel_id=1, source_target_pairs={{0,8},{4,12},{8,0},{12,4},{1,9},{5,13},{9,1},{13,5},{2,10},{6,14},... | collective-permute-start | bytes 1179656 | tf_op jit(solution)/shard_map/ppermute | solution.py:339
  215.8 27.4 %collective-permute-start.33 = (bf16[128,1536]{1,0:T(8,128)(2,1)S(1)}, bf16[128,1536]{1,0:T(8,128)(2,1)S(1)}, u32[]{:S(2)}, u32[]{:S(2)}) collective-permute-start(bf16[128,1536]{1,0:T(8,128)(2,1)S(1)} %get-tuple-element.182.refs_6_), channel_id=1, source_target_pairs={{0,12},{4,0},{8,4},{12,8},{1,13},{5,1},{9,5},{13,9},{2,14},{6,2},{... | collective-permute-start | bytes 1179656 | tf_op jit(solution)/shard_map/ppermute | solution.py:339
  270.5 93.6 %all-gather.8.cloned.1.call-start = ((), (), s32[]{:S(2)}) async-start(), calls=%async_computation.5 | async-start | bytes 7864320 | tf_op jit(solution)/shard_map/all_gather | solution.py:766
  271.3 428.0 %reduce-scatter.3.cloned.1.call-start = ((), (), s32[]{:S(2)}) async-start(), calls=%async_computation.3 | async-start | bytes 1966080 | tf_op jit(solution)/shard_map/reduce_scatter | solution.py:882
  276.8 28.7 %collective-permute-start.43 = (bf16[128,1536]{1,0:T(8,128)(2,1)}, bf16[128,1536]{1,0:T(8,128)(2,1)}, u32[]{:S(2)}, u32[]{:S(2)}) collective-permute-start(bf16[128,1536]{1,0:T(8,128)(2,1)} %get-tuple-element.192), channel_id=1, source_target_pairs={{0,8},{4,12},{8,0},{12,4},{1,9},{5,13},{9,1},{13,5},{2,10},{6,14},... | collective-permute-start | bytes 1179656 | tf_op jit(solution)/shard_map/ppermute | solution.py:355
  279.2 26.3 %collective-permute-start.42 = (bf16[128,1536]{1,0:T(8,128)(2,1)}, bf16[128,1536]{1,0:T(8,128)(2,1)}, u32[]{:S(2)}, u32[]{:S(2)}) collective-permute-start(bf16[128,1536]{1,0:T(8,128)(2,1)} %get-tuple-element.191), channel_id=1, source_target_pairs={{0,12},{4,0},{8,4},{12,8},{1,13},{5,1},{9,5},{13,9},{2,14},{6,2},{... | collective-permute-start | bytes 1179656 | tf_op jit(solution)/shard_map/ppermute | solution.py:355
  350.7 34.0 %collective-permute-start.51 = (bf16[128,3072]{1,0:T(8,128)(2,1)}, bf16[128,3072]{1,0:T(8,128)(2,1)}, u32[]{:S(2)}, u32[]{:S(2)}) collective-permute-start(bf16[128,3072]{1,0:T(8,128)(2,1)} %get-tuple-element.444), channel_id=1, source_target_pairs={{0,16},{16,0},{1,17},{17,1},{2,18},{18,2},{3,19},{19,3},{4,20},{20... | collective-permute-start | bytes 2359304 | tf_op jit(solution)/shard_map/ppermute | solution.py:367
  356.2 28.5 %collective-permute-start.49 = (bf16[128,1536]{1,0:T(8,128)(2,1)S(1)}, bf16[128,1536]{1,0:T(8,128)(2,1)}, u32[]{:S(2)}, u32[]{:S(2)}) collective-permute-start(bf16[128,1536]{1,0:T(8,128)(2,1)S(1)} %multiply_convert_fusion.4.refs_6_), channel_id=1, source_target_pairs={{0,8},{4,12},{8,0},{12,4},{1,9},{5,13},{9,1},{13,5},{2,10},{6,14},... | collective-permute-start | bytes 1179656 | tf_op jit(solution)/shard_map/ppermute | solution.py:339
  356.4 28.3 %collective-permute-start.50 = (bf16[128,1536]{1,0:T(8,128)(2,1)S(1)}, bf16[128,1536]{1,0:T(8,128)(2,1)}, u32[]{:S(2)}, u32[]{:S(2)}) collective-permute-start(bf16[128,1536]{1,0:T(8,128)(2,1)S(1)} %multiply_convert_fusion.4.refs_6_), channel_id=1, source_target_pairs={{0,12},{4,0},{8,4},{12,8},{1,13},{5,1},{9,5},{13,9},{2,14},{6,2},{... | collective-permute-start | bytes 1179656 | tf_op jit(solution)/shard_map/ppermute | solution.py:339
  387.1 71.7 %collective-permute-start.55 = (bf16[256,3072]{1,0:T(8,128)(2,1)S(1)}, bf16[256,3072]{1,0:T(8,128)(2,1)S(1)}, u32[]{:S(2)}, u32[]{:S(2)}) collective-permute-start(bf16[256,3072]{1,0:T(8,128)(2,1)S(1)} %constant_dynamic-update-slice_fusion.3), channel_id=1, source_target_pairs={{0,1},{1,0},{2,3},{3,2},{4,5},{5,4},{6,7},{7,6},{8,9},{9,8},{10,11... | collective-permute-start | bytes 4718600 | tf_op jit(solution)/shard_map/ppermute | solution.py:372
  387.2 39.5 %collective-permute-start.56 = (bf16[256,3072]{1,0:T(8,128)(2,1)S(1)}, bf16[256,3072]{1,0:T(8,128)(2,1)}, u32[]{:S(2)}, u32[]{:S(2)}) collective-permute-start(bf16[256,3072]{1,0:T(8,128)(2,1)S(1)} %constant_dynamic-update-slice_fusion.3), channel_id=1, source_target_pairs={{0,2},{1,3},{2,0},{3,1},{4,6},{5,7},{6,4},{7,5},{8,10},{9,11},{10,... | collective-permute-start | bytes 4718600 | tf_op jit(solution)/shard_map/ppermute | solution.py:597
  421.9 29.0 %collective-permute-start.53 = (bf16[128,1664]{1,0:T(8,128)(2,1)}, bf16[128,1664]{1,0:T(8,128)(2,1)S(1)}, u32[]{:S(2)}, u32[]{:S(2)}) collective-permute-start(bf16[128,1664]{1,0:T(8,128)(2,1)} %get-tuple-element.221), channel_id=1, source_target_pairs={{0,8},{4,12},{8,0},{12,4},{1,9},{5,13},{9,1},{13,5},{2,10},{6,14},... | collective-permute-start | bytes 1277960 | tf_op jit(solution)/shard_map/ppermute | solution.py:347
  422.8 29.5 %collective-permute-start.52 = (bf16[128,1664]{1,0:T(8,128)(2,1)}, bf16[128,1664]{1,0:T(8,128)(2,1)S(1)}, u32[]{:S(2)}, u32[]{:S(2)}) collective-permute-start(bf16[128,1664]{1,0:T(8,128)(2,1)} %get-tuple-element.220), channel_id=1, source_target_pairs={{0,12},{4,0},{8,4},{12,8},{1,13},{5,1},{9,5},{13,9},{2,14},{6,2},{... | collective-permute-start | bytes 1277960 | tf_op jit(solution)/shard_map/ppermute | solution.py:347
  426.7 33.8 %collective-permute-start.57 = (bf16[256,3072]{1,0:T(8,128)(2,1)}, bf16[256,3072]{1,0:T(8,128)(2,1)S(1)}, u32[]{:S(2)}, u32[]{:S(2)}) collective-permute-start(bf16[256,3072]{1,0:T(8,128)(2,1)} %collective-permute-done.56), channel_id=1, source_target_pairs={{0,1},{1,0},{2,3},{3,2},{4,5},{5,4},{6,7},{7,6},{8,9},{9,8},{10,11... | collective-permute-start | bytes 4718600 | tf_op jit(solution)/shard_map/ppermute | solution.py:372
  452.3 131.4 %collective-permute-start.73 = (bf16[1,256,1536]{2,1,0:T(8,128)(2,1)}, bf16[1,256,1536]{2,1,0:T(8,128)(2,1)}, u32[]{:S(2)}, u32[]{:S(2)}) collective-permute-start(bf16[1,256,1536]{2,1,0:T(8,128)(2,1)} %get-tuple-element.439), channel_id=1, source_target_pairs={{0,1},{1,0},{2,3},{3,2},{4,5},{5,4},{6,7},{7,6},{8,9},{9,8},{10,11... | collective-permute-start | bytes 2359304 | tf_op jit(solution)/shard_map/ppermute | solution.py:372
  456.1 36.6 %collective-permute-start.60 = (bf16[1,512,1536]{2,1,0:T(8,128)(2,1)}, bf16[1,512,1536]{2,1,0:T(8,128)(2,1)}, u32[]{:S(2)}, u32[]{:S(2)}) collective-permute-start(bf16[1,512,1536]{2,1,0:T(8,128)(2,1)} %get-tuple-element.426), channel_id=1, source_target_pairs={{0,16},{16,0},{1,17},{17,1},{2,18},{18,2},{3,19},{19,3},{4,20},{20... | collective-permute-start | bytes 4718600 | tf_op jit(solution)/shard_map/ppermute | solution.py:367
  456.6 58.3 %collective-permute-start.64 = (bf16[1,512,1536]{2,1,0:T(8,128)(2,1)}, bf16[1,512,1536]{2,1,0:T(8,128)(2,1)}, u32[]{:S(2)}, u32[]{:S(2)}) collective-permute-start(bf16[1,512,1536]{2,1,0:T(8,128)(2,1)} %get-tuple-element.425), channel_id=1, source_target_pairs={{0,2},{1,3},{2,0},{3,1},{4,6},{5,7},{6,4},{7,5},{8,10},{9,11},{10,... | collective-permute-start | bytes 4718600 | tf_op jit(solution)/shard_map/ppermute | solution.py:597
  523.8 26.5 %collective-permute-start.66 = (bf16[128,1536]{1,0:T(8,128)(2,1)S(1)}, bf16[128,1536]{1,0:T(8,128)(2,1)S(1)}, u32[]{:S(2)}, u32[]{:S(2)}) collective-permute-start(bf16[128,1536]{1,0:T(8,128)(2,1)S(1)} %fusion.143.refs_6_), channel_id=1, source_target_pairs={{0,8},{4,12},{8,0},{12,4},{1,9},{5,13},{9,1},{13,5},{2,10},{6,14},... | collective-permute-start | bytes 1179656 | tf_op jit(solution)/shard_map/ppermute | solution.py:339
  523.8 26.5 %collective-permute-start.67 = (bf16[128,1536]{1,0:T(8,128)(2,1)S(1)}, bf16[128,1536]{1,0:T(8,128)(2,1)S(1)}, u32[]{:S(2)}, u32[]{:S(2)}) collective-permute-start(bf16[128,1536]{1,0:T(8,128)(2,1)S(1)} %fusion.143.refs_6_), channel_id=1, source_target_pairs={{0,12},{4,0},{8,4},{12,8},{1,13},{5,1},{9,5},{13,9},{2,14},{6,2},{... | collective-permute-start | bytes 1179656 | tf_op jit(solution)/shard_map/ppermute | solution.py:339
  526.3 36.0 %collective-permute-start.68 = (bf16[1,512,1536]{2,1,0:T(8,128)(2,1)}, bf16[1,512,1536]{2,1,0:T(8,128)(2,1)S(1)}, u32[]{:S(2)}, u32[]{:S(2)}) collective-permute-start(bf16[1,512,1536]{2,1,0:T(8,128)(2,1)} %collective-permute-done.60), channel_id=1, source_target_pairs={{0,2},{1,3},{2,0},{3,1},{4,6},{5,7},{6,4},{7,5},{8,10},{9,11},{10,... | collective-permute-start | bytes 4718600 | tf_op jit(solution)/shard_map/ppermute | solution.py:597
  579.5 32.1 %collective-permute-start.70 = (bf16[128,1664]{1,0:T(8,128)(2,1)}, bf16[128,1664]{1,0:T(8,128)(2,1)S(1)}, u32[]{:S(2)}, u32[]{:S(2)}) collective-permute-start(bf16[128,1664]{1,0:T(8,128)(2,1)} %get-tuple-element.257), channel_id=1, source_target_pairs={{0,8},{4,12},{8,0},{12,4},{1,9},{5,13},{9,1},{13,5},{2,10},{6,14},... | collective-permute-start | bytes 1277960 | tf_op jit(solution)/shard_map/ppermute | solution.py:347
  581.7 29.8 %collective-permute-start.69 = (bf16[128,1664]{1,0:T(8,128)(2,1)}, bf16[128,1664]{1,0:T(8,128)(2,1)S(1)}, u32[]{:S(2)}, u32[]{:S(2)}) collective-permute-start(bf16[128,1664]{1,0:T(8,128)(2,1)} %get-tuple-element.256), channel_id=1, source_target_pairs={{0,12},{4,0},{8,4},{12,8},{1,13},{5,1},{9,5},{13,9},{2,14},{6,2},{... | collective-permute-start | bytes 1277960 | tf_op jit(solution)/shard_map/ppermute | solution.py:347
  586.1 36.2 %collective-permute-start.74 = (bf16[1,512,1536]{2,1,0:T(8,128)(2,1)S(1)}, bf16[1,512,1536]{2,1,0:T(8,128)(2,1)S(1)}, u32[]{:S(2)}, u32[]{:S(2)}) collective-permute-start(bf16[1,512,1536]{2,1,0:T(8,128)(2,1)S(1)} %get-tuple-element.274), channel_id=1, source_target_pairs={{0,2},{1,3},{2,0},{3,1},{4,6},{5,7},{6,4},{7,5},{8,10},{9,11},{10,... | collective-permute-start | bytes 4718600 | tf_op jit(solution)/shard_map/ppermute | solution.py:597
  587.8 35.8 %collective-permute-start.75 = (bf16[1,512,1536]{2,1,0:T(8,128)(2,1)S(1)}, bf16[1,512,1536]{2,1,0:T(8,128)(2,1)S(1)}, u32[]{:S(2)}, u32[]{:S(2)}) collective-permute-start(bf16[1,512,1536]{2,1,0:T(8,128)(2,1)S(1)} %get-tuple-element.423), channel_id=1, source_target_pairs={{0,16},{16,0},{1,17},{17,1},{2,18},{18,2},{3,19},{19,3},{4,20},{20... | collective-permute-start | bytes 4718600 | tf_op jit(solution)/shard_map/ppermute | solution.py:367
  642.4 75.7 %reduce-scatter.5.cloned.1.call-start = ((), (), s32[]{:S(2)}) async-start(), calls=%async_computation.4 | async-start | bytes 1536000 | tf_op jit(solution)/shard_map/reduce_scatter | solution.py:838
  718.2 24.6 %collective-permute-start.96 = (bf16[400,384]{1,0:T(8,128)(2,1)}, bf16[400,384]{1,0:T(8,128)(2,1)S(1)}, u32[]{:S(2)}, u32[]{:S(2)}) collective-permute-start(bf16[400,384]{1,0:T(8,128)(2,1)} %reduce-scatter.5.cloned.1.call-done), channel_id=1, source_target_pairs={{0,1},{1,0},{2,3},{3,2},{4,5},{5,4},{6,7},{7,6},{8,9},{9,8},{10,11... | collective-permute-start | bytes 921608 | tf_op jit(solution)/shard_map/ppermute | solution.py:372
  718.2 28.1 %collective-permute-start.97 = (bf16[400,384]{1,0:T(8,128)(2,1)}, bf16[400,384]{1,0:T(8,128)(2,1)S(1)}, u32[]{:S(2)}, u32[]{:S(2)}) collective-permute-start(bf16[400,384]{1,0:T(8,128)(2,1)} %reduce-scatter.5.cloned.1.call-done), channel_id=1, source_target_pairs={{0,2},{1,3},{2,0},{3,1},{4,6},{5,7},{6,4},{7,5},{8,10},{9,11},{10,... | collective-permute-start | bytes 921608 | tf_op jit(solution)/shard_map/ppermute | solution.py:597
  729.6 22.4 %collective-permute-start.89 = (bf16[384,512]{1,0:T(8,128)(2,1)S(1)}, bf16[384,512]{1,0:T(8,128)(2,1)S(1)}, u32[]{:S(2)}, u32[]{:S(2)}) collective-permute-start(bf16[384,512]{1,0:T(8,128)(2,1)S(1)} %get-tuple-element.434), channel_id=1, source_target_pairs={{0,4},{4,8},{8,12},{12,0},{1,5},{5,9},{9,13},{13,1},{2,6},{6,10},{... | collective-permute-start | bytes 1179656 | tf_op jit(solution)/shard_map/ppermute | solution.py:347
  729.7 29.8 %collective-permute-start.88 = (bf16[384,512]{1,0:T(8,128)(2,1)S(1)}, bf16[384,512]{1,0:T(8,128)(2,1)S(1)}, u32[]{:S(2)}, u32[]{:S(2)}) collective-permute-start(bf16[384,512]{1,0:T(8,128)(2,1)S(1)} %get-tuple-element.435), channel_id=1, source_target_pairs={{0,8},{4,12},{8,0},{12,4},{1,9},{5,13},{9,1},{13,5},{2,10},{6,14},... | collective-permute-start | bytes 1179656 | tf_op jit(solution)/shard_map/ppermute | solution.py:347
  731.4 36.0 %collective-permute-start.90 = (bf16[1,512,1536]{2,1,0:T(8,128)(2,1)S(1)}, bf16[1,512,1536]{2,1,0:T(8,128)(2,1)S(1)}, u32[]{:S(2)}, u32[]{:S(2)}) collective-permute-start(bf16[1,512,1536]{2,1,0:T(8,128)(2,1)S(1)} %copy-done.103), channel_id=1, source_target_pairs={{0,2},{1,3},{2,0},{3,1},{4,6},{5,7},{6,4},{7,5},{8,10},{9,11},{10,... | collective-permute-start | bytes 4718600 | tf_op jit(solution)/shard_map/ppermute | solution.py:597
  789.8 23.4 %collective-permute-start.100 = (bf16[1,1536,768]{2,1,0:T(8,128)(2,1)S(1)}, bf16[1,1536,768]{2,1,0:T(8,128)(2,1)S(1)}, u32[]{:S(2)}, u32[]{:S(2)}) collective-permute-start(bf16[1,1536,768]{2,1,0:T(8,128)(2,1)S(1)} %bitcast.614), channel_id=1, source_target_pairs={{0,1},{1,0},{2,3},{3,2},{4,5},{5,4},{6,7},{7,6},{8,9},{9,8},{10,11... | collective-permute-start | bytes 7077896 | tf_op jit(solution)/shard_map/ppermute | solution.py:372
  (269 other events, 3423.4 us)
Sparse Core Ops, SparseCore 0:
  96.9 147.5 all-gather.5
  270.6 41.4 all-gather.9
  314.2 46.3 all-gather.7
  642.6 42.7 reduce-scatter.2
  687.6 30.5 reduce-scatter.4

commit v4 on v3

--- a/solution.py
+++ b/solution.py
@@ -835,7 +835,7 @@
 
     def late_part(total, tie):
         if tie == ():
-            mine = lax.psum_scatter(total, F_AX, scatter_dimension=0, tiled=True)
+            return lax.psum_scatter(total, F_AX, scatter_dimension=0, tiled=True)
         else:
             step = total.shape[0] // folds
             mine = rel_scatter(
@@ -844,11 +844,13 @@
                     for k in range(folds)
                 ]
             ).astype(BF16)
-            mine, tie = lax.optimization_barrier((mine, tie))
+        return lax.optimization_barrier((mine, tie))
+
+    def spread_rows(mine):
         whole = jnp.zeros((replicas,) + mine.shape, BF16)
         for bit, part in enumerate(group_rows(mine)):
             whole = lax.dynamic_update_index_in_dim(whole, part, replica ^ bit, 0)
-        return whole, tie
+        return whole
 
     def side_by_side(value):
         return jnp.concatenate([value[j].astype(F32) for j in range(replicas)], axis=1)
@@ -868,9 +870,21 @@
         held["rows"] = chip_rows([grad_expert])[0]
         return left_whole, stacked_parts(second_parts)
 
+    def two(value):
+        middle_row = value.shape[1] // 2
+        return value[:, :middle_row], value[:, middle_row:]
+
+    def joined_rows(one, other):
+        return [jnp.concatenate(pair, axis=1) for pair in zip(one, other)]
+
     def last_attn(grad_attn, small, sent):
         held["attn"] = with_small(grad_attn, small)
-        return swap_section(x_give), sent[1]
+        give_one, give_two = two(x_give)
+        return swap_section(give_one), give_two, sent[1]
+
+    def last_later(sent, crossed):
+        got_one, give_two, stack = crossed
+        return sent[0], stack, got_one, swap_section(give_two), all_x(got_one), all_x(x_mine)
 
     def first_rows(grad_expert):
         chip = (chip_rows([grad_expert])[0], held["rows"])
@@ -888,18 +902,20 @@
         return x_own, g_own, [expert_middle(x_own[i], flat_rows(g_own)[i], *[w[i] for w in mine_w]) for i in range(half)], got, own_columns(right_out)
 
     grads, grad_lin = [None, None], [None, None]
-    grads[1], grad_lin[1], ((left_whole, _), (x_got, second_stack), x_mine_x), _ = layer_backward(
+    grads[1], grad_lin[1], (left_whole, second_stack, x_got, x_got_two, x_got_x, x_mine_x), _ = layer_backward(
         last_grad, kept[1], weights[1], experts_w, common, scalars[1], (),
-        dict(rows=last_rows, attn=last_attn, later=lambda sent, crossed: (sent, crossed, all_x(x_mine)), blocks=last_blocks),
+        dict(rows=last_rows, attn=last_attn, later=last_later, blocks=last_blocks),
     )
     x_own = flat_rows(by_order(x_mine, x_mine_x))
     x_own = [x_own[i] for i in range(half)]
     mine_w = [lax.dynamic_slice_in_dim(part[0], core * half, half, 0) for part in (w_gate, w_up, w_down)]
-    grads[0], grad_lin[0], later, x_got_x = layer_backward(
-        grads[1], kept[0], weights[0], experts_w, common, scalars[0], all_x(x_got),
+    grads[0], grad_lin[0], later, x_got_two_x = layer_backward(
+        grads[1], kept[0], weights[0], experts_w, common, scalars[0], all_x(x_got_two),
         dict(rows=first_rows, attn=first_attn, later=first_later),
     )
     x_own, g_own, middle_own, got, right_out = later
+    (x_got,) = joined_rows([x_got], [x_got_two])
+    x_got_x = joined_rows(x_got_x, x_got_two_x)
     left_whole = jnp.concatenate(left_whole, axis=0)
     right_out = right_out.reshape(replicas, 2, rows + tall, -1)
     extra = jnp.sum(right_out[:, :, rows:].astype(F32), axis=(0, 1)).reshape(tall, folds, piece)
@@ -907,7 +923,7 @@
         jnp.transpose(extra, (1, 0, 2)), ((0, 0), (0, 0), (0, right_out.shape[3] - piece))
     ).astype(BF16)
     right_out = right_out[:, :, :rows].reshape(-1, right_out.shape[3])
-    out_shard, _ = late_part(fold_sum(left_whole[:, model:], right_out, extra), ())
+    out_shard = late_part(fold_sum(left_whole[:, model:], right_out, extra), ())
     lin_rows, second_sum = lax.optimization_barrier((both_rows(grad_lin), held["second_sum"]))
     right, got = lax.optimization_barrier((own_columns(lin_rows), got))
     got_x = all_x(got)
@@ -920,7 +936,8 @@
     g_own, g_got = [[flat_rows(value)[i] for i in range(half)] for value in (g_own, g_got)]
     middle_got = [expert_middle(x_got[i], g_got[i], *[w[i] for w in mine_w]) for i in range(half)]
 
-    shard, middle_got = late_part(shard, middle_got)
+    shard, (middle_got, out_shard) = late_part(shard, (middle_got, out_shard))
+    shard, out_shard = spread_rows(shard), spread_rows(out_shard)
     made = []
     for i in range(half):
         inner, gate, up = zip(middle_own[i], middle_got[i])

time: 839 us -> 835 us (level)
  local copies, waits for them, and re-layouts: 94.5 us -> 85.5 us
    ppermute x24 -> x25, waiting for transfers between devices: 61.1 us -> 86.6 us  [swap_xor(): return lax.ppermute(value, R_AX, [(i, i ^ bit) for i in range(replicas)])]
    reduce_scatter x1, waiting for transfers between devices: 12.8 us -> 0.01 us  [late_part(): return lax.psum_scatter(total, F_AX, scatter_dimension=0, tiled=True)]
    ppermute x15, waiting for transfers between devices: 53 us -> 40.5 us  [rel_scatter(): lax.ppermute(parts[k], F_AX, [(i, (i - k) % folds) for i in range(folds)])]
    ppermute x13 -> x14, waiting for transfers between devices: 37.1 us -> 28.9 us  [swap_section(): return lax.ppermute(value, S_AX, [(0, 1), (1, 0)])]
    unnamed x432 -> x456, local copies, waits for them, and re-layouts: 29.9 us -> 28.3 us
    ppermute x24 -> x25, starting transfers between devices: 22.3 us -> 20.8 us  [swap_xor(): return lax.ppermute(value, R_AX, [(i, i ^ bit) for i in range(replicas)])]
  transfers between devices with their start and end apart: 107 -> 109, of which waited for: 44 -> 44; matrix products, arithmetic and copies ran while one was open for 27% -> 29% of each run, Pallas kernels for 6% -> 6%
where the time goes in v4:
time: 835 us; the launch traced here: 826 us
  waiting for transfers between devices  323 us (39%)
  starting transfers between devices  146 us (17%)
  matrix products  122 us (15%)
  local copies, waits for them, and re-layouts  85.5 us (10%)
  other arithmetic  79.6 us (10%)
  Pallas kernels  51.5 us (6%)
  between operations  18 us (2%)
    ppermute x24, waiting for transfers between devices, rel_gather(): lax.ppermute(value, F_AX, [(i, (i + k) % folds) for i in range(folds)])  138 us
    ppermute x25, waiting for transfers between devices, swap_xor(): return lax.ppermute(value, R_AX, [(i, i ^ bit) for i in range(replicas)])  86.6 us
    ppermute x24, starting transfers between devices, rel_gather(): lax.ppermute(value, F_AX, [(i, (i + k) % folds) for i in range(folds)])  64.7 us
    ppermute x15, waiting for transfers between devices, rel_scatter(): lax.ppermute(parts[k], F_AX, [(i, (i - k) % folds) for i in range(folds)])  40.5 us
    dot_general x16, matrix products, mm_nt(): lax.dot_general(a, b, (((1,), (1,)), ((), ())), preferred_element_type=F32)  37.3 us
    dot_general x10, matrix products, mm_tn(): lax.dot_general(a, b, (((0,), (0,)), ((), ())), preferred_element_type=F32)  34.8 us
    ppermute x15, starting transfers between devices, rel_scatter(): lax.ppermute(parts[k], F_AX, [(i, (i - k) % folds) for i in range(folds)])  33.1 us
    ppermute x14, waiting for transfers between devices, swap_section(): return lax.ppermute(value, S_AX, [(0, 1), (1, 0)])  28.9 us
  transfers between devices with their start and end apart: 109, of which 44 were waited for; matrix products, arithmetic and copies ran while one was open for 29% of the time, Pallas kernels for 6%

profile of v4, /device:TPU:0, one launch (start us, length us, event | category | flops | bytes accessed | tf_op | source)
XLA Modules:
  0.0 826.0 jit_solution(8913141413617830839)
XLA Ops:
  29.9 4.6 dynamic-slice_bitcast_fusion.1
  36.0 4.8 collective-permute-done.11
  60.1 6.4 collective-permute-done.7.refs_3_
  66.5 17.5 %collective-permute-done.8.refs_4_ = bf16[384,640]{1,0:T(8,128)(2,1)S(1)} collective-permute-done((bf16[384,640]{1,0:T(8,128)(2,1)S(1)}, bf16[384,640]{1,0:T(8,128)(2,1)S(1)}, u32[]{:S(2)}, u32[]{:S(2)}) %collective-permute-start.8) | collective-permute-done | bytes 491552 | tf_op jit(solution)/shard_map/ppermute | solution.py:339
  88.8 4.3 collective-permute-done.13
  104.0 11.6 %collective-permute-start.18 = (bf16[128,512]{0,1:T(8,128)(2,1)S(1)}, bf16[128,512]{0,1:T(8,128)(2,1)S(1)}, u32[]{:S(2)}, u32[]{:S(2)}) collective-permute-start(bf16[128,512]{0,1:T(8,128)(2,1)S(1)} %pad_maximum_fusion.23), channel_id=1, source_target_pairs={{0,12},{4,0},{8,4},{12,8},{1,13},{5,1},{9,5},{13,9},{2,14},{6,2},{... | collective-permute-start | bytes 393224 | tf_op jit(solution)/shard_map/ppermute | solution.py:339
  122.8 12.8 %collective-permute-done.17 = bf16[128,512]{0,1:T(8,128)(2,1)S(1)} collective-permute-done((bf16[128,512]{0,1:T(8,128)(2,1)S(1)}, bf16[128,512]{0,1:T(8,128)(2,1)S(1)}, u32[]{:S(2)}, u32[]{:S(2)}) %collective-permute-start.17) | collective-permute-done | bytes 131104 | tf_op jit(solution)/shard_map/ppermute | solution.py:339
  157.2 10.8 %collective-permute-done.22 = bf16[128,1536]{0,1:T(8,128)(2,1)S(1)} collective-permute-done((bf16[128,1536]{0,1:T(8,128)(2,1)S(1)}, bf16[128,1536]{0,1:T(8,128)(2,1)S(1)}, u32[]{:S(2)}, u32[]{:S(2)}) %collective-permute-start.22) | collective-permute-done | bytes 393248 | tf_op jit(solution)/shard_map/ppermute | solution.py:597
  186.9 11.8 %collective-permute-start.31 = (bf16[128,1536]{1,0:T(8,128)(2,1)S(1)}, bf16[128,1536]{1,0:T(8,128)(2,1)S(1)}, u32[]{:S(2)}, u32[]{:S(2)}) collective-permute-start(bf16[128,1536]{1,0:T(8,128)(2,1)S(1)} %get-tuple-element.186.refs_6_), channel_id=1, source_target_pairs={{0,4},{4,8},{8,12},{12,0},{1,5},{5,9},{9,13},{13,1},{2,6},{6,10},{... | collective-permute-start | bytes 1179656 | tf_op jit(solution)/shard_map/ppermute | solution.py:339
  202.1 13.8 %collective-permute-done.31.refs_7_ = bf16[128,1536]{1,0:T(8,128)(2,1)S(1)} collective-permute-done((bf16[128,1536]{1,0:T(8,128)(2,1)S(1)}, bf16[128,1536]{1,0:T(8,128)(2,1)S(1)}, u32[]{:S(2)}, u32[]{:S(2)}) %collective-permute-start.31) | collective-permute-done | bytes 393248 | tf_op jit(solution)/shard_map/ppermute | solution.py:339
  217.1 25.4 %collective-permute-done.32.refs_8_ = bf16[128,1536]{1,0:T(8,128)(2,1)S(1)} collective-permute-done((bf16[128,1536]{1,0:T(8,128)(2,1)S(1)}, bf16[128,1536]{1,0:T(8,128)(2,1)S(1)}, u32[]{:S(2)}, u32[]{:S(2)}) %collective-permute-start.32) | collective-permute-done | bytes 393248 | tf_op jit(solution)/shard_map/ppermute | solution.py:339
  245.2 9.2 %collective-permute-done.40.refs_23_ = bf16[384,1536]{1,0:T(8,128)(2,1)} collective-permute-done((bf16[384,1536]{1,0:T(8,128)(2,1)}, bf16[384,1536]{1,0:T(8,128)(2,1)}, u32[]{:S(2)}, u32[]{:S(2)}) %collective-permute-start.40) | collective-permute-done | bytes 1179680 | tf_op jit(solution)/shard_map/ppermute | solution.py:597
  257.7 12.6 %shard_map.212 = (bf16[2,256,1536]{2,1,0:T(8,128)(2,1)}, f32[2,256,768]{2,1,0:T(8,128)}, f32[2,256,768]{2,1,0:T(8,128)}, bf16[2,256,1536]{2,1,0:T(8,128)(2,1)}, ...) custom-call(s32[4]{0:T(128)} %get-tuple-element.527.refs_0_, ...), custom_call_target="tpu_custom_call" | custom-call | flops 3623878656 | bytes 20447232 | tf_op jit(solution)/shard_map/pallas_call | solution.py:274
  271.3 5.5 collective-permute-start.44
  282.0 6.9 collective-permute-done.44
  288.9 16.6 %collective-permute-done.43 = bf16[128,1536]{1,0:T(8,128)(2,1)} collective-permute-done((bf16[128,1536]{1,0:T(8,128)(2,1)}, bf16[128,1536]{1,0:T(8,128)(2,1)}, u32[]{:S(2)}, u32[]{:S(2)}) %collective-permute-start.43) | collective-permute-done | bytes 393248 | tf_op jit(solution)/shard_map/ppermute | solution.py:355
  317.8 9.0 %collective-permute-start.47 = (bf16[128,512]{1,0:T(8,128)(2,1)S(1)}, bf16[128,512]{1,0:T(8,128)(2,1)S(1)}, u32[]{:S(2)}, u32[]{:S(2)}) collective-permute-start(bf16[128,512]{1,0:T(8,128)(2,1)S(1)} %pad_maximum_fusion.24), channel_id=1, source_target_pairs={{0,12},{4,0},{8,4},{12,8},{1,13},{5,1},{9,5},{13,9},{2,14},{6,2},{... | collective-permute-start | bytes 393224 | tf_op jit(solution)/shard_map/ppermute | solution.py:339
  330.7 9.6 %collective-permute-done.46 = bf16[128,512]{1,0:T(8,128)(2,1)S(1)} collective-permute-done((bf16[128,512]{1,0:T(8,128)(2,1)S(1)}, bf16[128,512]{1,0:T(8,128)(2,1)S(1)}, u32[]{:S(2)}, u32[]{:S(2)}) %collective-permute-start.46) | collective-permute-done | bytes 131104 | tf_op jit(solution)/shard_map/ppermute | solution.py:339
  364.4 5.4 collective-permute-done.48.refs_7_
  369.8 14.9 %collective-permute-done.49.refs_8_ = bf16[128,1536]{1,0:T(8,128)(2,1)} collective-permute-done((bf16[128,1536]{1,0:T(8,128)(2,1)S(1)}, bf16[128,1536]{1,0:T(8,128)(2,1)}, u32[]{:S(2)}, u32[]{:S(2)}) %collective-permute-start.49) | collective-permute-done | bytes 393248 | tf_op jit(solution)/shard_map/ppermute | solution.py:339
  384.7 12.8 %shard_map.213 = (bf16[2,256,1536]{2,1,0:T(8,128)(2,1)}, f32[2,256,768]{2,1,0:T(8,128)}, f32[2,256,768]{2,1,0:T(8,128)}, bf16[2,256,1536]{2,1,0:T(8,128)(2,1)}, ...) custom-call(s32[4]{0:T(128)} %get-tuple-element.526.refs_0_, ...), custom_call_target="tpu_custom_call" | custom-call | flops 3623878656 | bytes 20447232 | tf_op jit(solution)/shard_map/pallas_call | solution.py:274
  397.4 13.1 %shard_map.214 = (bf16[2,256,1536]{2,1,0:T(8,128)(2,1)}, bf16[128,1664]{1,0:T(8,128)(2,1)}, bf16[128,1664]{1,0:T(8,128)(2,1)}, bf16[128,1664]{1,0:T(8,128)(2,1)}, bf16[128,1664]{1,0:T(8,128)(2,1)}) custom-call(s32[4]{0:T(128)} %get-tuple-element.526.refs_0_, s32[4,2,128]{2,1,0:T(2,128)} %get-tuple-element.210.refs_1_, ...), custom_call_target="tpu_custom_call" | custom-call | flops 3623878656 | bytes 20447232 | tf_op jit(solution)/shard_map/pallas_call | solution.py:298
  410.6 8.3 %collective-permute-start.54 = (bf16[128,1664]{1,0:T(8,128)(2,1)}, bf16[128,1664]{1,0:T(8,128)(2,1)S(1)}, u32[]{:S(2)}, u32[]{:S(2)}) collective-permute-start(bf16[128,1664]{1,0:T(8,128)(2,1)} %get-tuple-element.226), channel_id=1, source_target_pairs={{0,4},{4,8},{8,12},{12,0},{1,5},{5,9},{9,13},{13,1},{2,6},{6,10},{... | collective-permute-start | bytes 1277960 | tf_op jit(solution)/shard_map/ppermute | solution.py:347
  431.4 15.2 %collective-permute-done.53 = bf16[128,1664]{1,0:T(8,128)(2,1)S(1)} collective-permute-done((bf16[128,1664]{1,0:T(8,128)(2,1)}, bf16[128,1664]{1,0:T(8,128)(2,1)S(1)}, u32[]{:S(2)}, u32[]{:S(2)}) %collective-permute-start.53) | collective-permute-done | bytes 426016 | tf_op jit(solution)/shard_map/ppermute | solution.py:347
  446.6 11.3 %collective-permute-done.56 = bf16[256,3072]{1,0:T(8,128)(2,1)S(1)} collective-permute-done((bf16[256,3072]{1,0:T(8,128)(2,1)S(1)}, bf16[256,3072]{1,0:T(8,128)(2,1)S(1)}, u32[]{:S(2)}, u32[]{:S(2)}) %collective-permute-start.56) | collective-permute-done | bytes 1572896 | tf_op jit(solution)/shard_map/ppermute | solution.py:597
  477.0 4.8 fusion.50
  504.7 6.1 collective-permute-done.64
  510.8 6.6 collective-permute-done.65
  517.6 5.2 fusion.141
  530.1 7.2 collective-permute-done.67.refs_7_
  537.3 15.1 %collective-permute-done.68.refs_8_ = bf16[128,1536]{1,0:T(8,128)(2,1)S(1)} collective-permute-done((bf16[128,1536]{1,0:T(8,128)(2,1)S(1)}, bf16[128,1536]{1,0:T(8,128)(2,1)S(1)}, u32[]{:S(2)}, u32[]{:S(2)}) %collective-permute-start.68) | collective-permute-done | bytes 393248 | tf_op jit(solution)/shard_map/ppermute | solution.py:339
  553.6 13.0 %shard_map.215 = (bf16[2,256,1536]{2,1,0:T(8,128)(2,1)}, bf16[128,1664]{1,0:T(8,128)(2,1)}, bf16[128,1664]{1,0:T(8,128)(2,1)}, bf16[128,1664]{1,0:T(8,128)(2,1)}, bf16[128,1664]{1,0:T(8,128)(2,1)}) custom-call(s32[4]{0:T(128)} %get-tuple-element.527.refs_0_, s32[4,2,128]{2,1,0:T(2,128)} %get-tuple-element.251.refs_1_, ...), custom_call_target="tpu_custom_call" | custom-call | flops 3623878656 | bytes 20447232 | tf_op jit(solution)/shard_map/pallas_call | solution.py:298
  570.8 8.0 collective-permute-start.73
  596.1 10.8 %collective-permute-done.72 = bf16[128,1664]{1,0:T(8,128)(2,1)S(1)} collective-permute-done((bf16[128,1664]{1,0:T(8,128)(2,1)}, bf16[128,1664]{1,0:T(8,128)(2,1)S(1)}, u32[]{:S(2)}, u32[]{:S(2)}) %collective-permute-start.72) | collective-permute-done | bytes 426016 | tf_op jit(solution)/shard_map/ppermute | solution.py:347
  607.1 13.7 %collective-permute-done.76 = bf16[1,512,1536]{2,1,0:T(8,128)(2,1)S(1)} collective-permute-done((bf16[1,512,1536]{2,1,0:T(8,128)(2,1)S(1)}, bf16[1,512,1536]{2,1,0:T(8,128)(2,1)S(1)}, u32[]{:S(2)}, u32[]{:S(2)}) %collective-permute-start.76) | collective-permute-done | bytes 1572896 | tf_op jit(solution)/shard_map/ppermute | solution.py:597
  663.9 6.2 multiply_convert_fusion.2
  698.2 4.8 collective-permute-done.88
  703.0 5.4 collective-permute-done.87
  719.8 4.4 fusion.256
  724.2 4.4 fusion.257
  734.6 4.5 collective-permute-done.94
  744.7 10.3 %collective-permute-done.92 = bf16[1,512,1536]{2,1,0:T(8,128)(2,1)S(1)} collective-permute-done((bf16[1,512,1536]{2,1,0:T(8,128)(2,1)S(1)}, bf16[1,512,1536]{2,1,0:T(8,128)(2,1)S(1)}, u32[]{:S(2)}, u32[]{:S(2)}) %collective-permute-start.92) | collective-permute-done | bytes 1572896 | tf_op jit(solution)/shard_map/ppermute | solution.py:597
  756.9 7.0 multiply_convert_fusion
  766.3 6.8 add_convert_fusion.2
  781.4 9.3 %collective-permute-done.93 = bf16[128,1536]{1,0:T(8,128)(2,1)S(1)} collective-permute-done((bf16[128,1536]{1,0:T(8,128)(2,1)S(1)}, bf16[128,1536]{1,0:T(8,128)(2,1)S(1)}, u32[]{:S(2)}, u32[]{:S(2)}) %collective-permute-start.93) | collective-permute-done | bytes 393248 | tf_op jit(solution)/shard_map/ppermute | solution.py:367
  805.3 4.4 maximum_convert_fusion
  810.0 4.4 maximum_convert_fusion.1
  814.6 4.4 maximum_convert_fusion.2
  (942 shorter events, 367.2 us)
Async XLA Ops:
  7.2 300.1 %all-gather.6.cloned.1.call-start = ((), (), s32[]{:S(2)}) async-start(), calls=%async_computation.2 | async-start | bytes 11759616 | tf_op jit(solution)/shard_map/all_gather | solution.py:714
  9.0 37.9 %collective-permute-start.4 = (bf16[128,1536]{1,0:T(8,128)(2,1)}, bf16[128,1536]{1,0:T(8,128)(2,1)}, u32[]{:S(2)}, u32[]{:S(2)}) collective-permute-start(bf16[128,1536]{1,0:T(8,128)(2,1)} %dynamic-slice_bitcast_fusion.3.refs_6_), channel_id=1, source_target_pairs={{0,4},{4,8},{8,12},{12,0},{1,5},{5,9},{9,13},{13,1},{2,6},{6,10},{... | collective-permute-start | bytes 1179656 | tf_op jit(solution)/shard_map/ppermute | solution.py:339
  12.0 34.9 %collective-permute-start.5 = (bf16[128,1536]{1,0:T(8,128)(2,1)}, bf16[128,1536]{1,0:T(8,128)(2,1)}, u32[]{:S(2)}, u32[]{:S(2)}) collective-permute-start(bf16[128,1536]{1,0:T(8,128)(2,1)} %dynamic-slice_bitcast_fusion.3.refs_6_), channel_id=1, source_target_pairs={{0,8},{4,12},{8,0},{12,4},{1,9},{5,13},{9,1},{13,5},{2,10},{6,14},... | collective-permute-start | bytes 1179656 | tf_op jit(solution)/shard_map/ppermute | solution.py:339
  51.2 32.8 %collective-permute-start.8 = (bf16[384,640]{1,0:T(8,128)(2,1)S(1)}, bf16[384,640]{1,0:T(8,128)(2,1)S(1)}, u32[]{:S(2)}, u32[]{:S(2)}) collective-permute-start(bf16[384,640]{1,0:T(8,128)(2,1)S(1)} %fusion.160.refs_2_), channel_id=1, source_target_pairs={{0,8},{4,12},{8,0},{12,4},{1,9},{5,13},{9,1},{13,5},{2,10},{6,14},... | collective-permute-start | bytes 1474568 | tf_op jit(solution)/shard_map/ppermute | solution.py:339
  54.5 29.5 %collective-permute-start.10 = (bf16[1536,384]{1,0:T(8,128)(2,1)}, bf16[1536,384]{1,0:T(8,128)(2,1)S(1)}, u32[]{:S(2)}, u32[]{:S(2)}) collective-permute-start(bf16[1536,384]{1,0:T(8,128)(2,1)} %get-tuple-element.166), channel_id=1, source_target_pairs={{0,16},{16,0},{1,17},{17,1},{2,18},{18,2},{3,19},{19,3},{4,20},{20... | collective-permute-start | bytes 3538952 | tf_op jit(solution)/shard_map/ppermute | solution.py:367
  57.8 26.2 %collective-permute-start.9 = (bf16[384,640]{1,0:T(8,128)(2,1)S(1)}, bf16[384,640]{1,0:T(8,128)(2,1)S(1)}, u32[]{:S(2)}, u32[]{:S(2)}) collective-permute-start(bf16[384,640]{1,0:T(8,128)(2,1)S(1)} %fusion.160.refs_2_), channel_id=1, source_target_pairs={{0,12},{4,0},{8,4},{12,8},{1,13},{5,1},{9,5},{13,9},{2,14},{6,2},{... | collective-permute-start | bytes 1474568 | tf_op jit(solution)/shard_map/ppermute | solution.py:339
  59.2 36.8 %collective-permute-start.15 = (bf16[48,3712]{1,0:T(8,128)(2,1)S(1)}, bf16[48,3712]{1,0:T(8,128)(2,1)S(1)}, u32[]{:S(2)}, u32[]{:S(2)}) collective-permute-start(bf16[48,3712]{1,0:T(8,128)(2,1)S(1)} %get-tuple-element.172), channel_id=1, source_target_pairs={{0,16},{16,0},{1,17},{17,1},{2,18},{18,2},{3,19},{19,3},{4,20},{20... | collective-permute-start | bytes 1069064 | tf_op jit(solution)/shard_map/ppermute | solution.py:367
  96.8 267.5 %all-gather.10.cloned.1.call-start = ((), (), s32[]{:S(2)}) async-start(), calls=%async_computation.6 | async-start | bytes 5898240 | tf_op jit(solution)/shard_map/all_gather | solution.py:766
  98.5 39.4 %collective-permute-start.20 = (bf16[1536,384]{1,0:T(8,128)(2,1)}, bf16[1536,384]{1,0:T(8,128)(2,1)}, u32[]{:S(2)}, u32[]{:S(2)}) collective-permute-start(bf16[1536,384]{1,0:T(8,128)(2,1)} %get-tuple-element.175), channel_id=1, source_target_pairs={{0,16},{16,0},{1,17},{17,1},{2,18},{18,2},{3,19},{19,3},{4,20},{20... | collective-permute-start | bytes 3538952 | tf_op jit(solution)/shard_map/ppermute | solution.py:367
  100.2 41.8 %collective-permute-start.19 = (bf16[1536,384]{1,0:T(8,128)(2,1)S(1)}, bf16[1536,384]{1,0:T(8,128)(2,1)}, u32[]{:S(2)}, u32[]{:S(2)}) collective-permute-start(bf16[1536,384]{1,0:T(8,128)(2,1)S(1)} %collective-permute-done.10.refs_13_), channel_id=1, source_target_pairs={{0,2},{1,3},{2,0},{3,1},{4,6},{5,7},{6,4},{7,5},{8,10},{9,11},{10,... | collective-permute-start | bytes 3538952 | tf_op jit(solution)/shard_map/ppermute | solution.py:597
  121.5 62.5 %collective-permute-start.30 = (bf16[384,1536]{1,0:T(8,128)(2,1)}, bf16[384,1536]{1,0:T(8,128)(2,1)}, u32[]{:S(2)}, u32[]{:S(2)}) collective-permute-start(bf16[384,1536]{1,0:T(8,128)(2,1)} %dynamic-slice_bitcast_fusion), channel_id=1, source_target_pairs={{0,16},{16,0},{1,17},{17,1},{2,18},{18,2},{3,19},{19,3},{4,20},{20... | collective-permute-start | bytes 3538952 | tf_op jit(solution)/shard_map/ppermute | solution.py:367
  135.6 32.4 %collective-permute-start.25 = (bf16[384,384]{1,0:T(8,128)(2,1)}, bf16[384,384]{1,0:T(8,128)(2,1)}, u32[]{:S(2)}, u32[]{:S(2)}) collective-permute-start(bf16[384,384]{1,0:T(8,128)(2,1)} %broadcast_select_fusion.15), channel_id=1, source_target_pairs={{0,8},{4,12},{8,0},{12,4},{1,9},{5,13},{9,1},{13,5},{2,10},{6,14},... | collective-permute-start | bytes 884744 | tf_op jit(solution)/shard_map/ppermute | solution.py:339
  137.9 31.9 %collective-permute-start.26 = (bf16[384,384]{1,0:T(8,128)(2,1)}, bf16[384,384]{1,0:T(8,128)(2,1)}, u32[]{:S(2)}, u32[]{:S(2)}) collective-permute-start(bf16[384,384]{1,0:T(8,128)(2,1)} %broadcast_select_fusion.15), channel_id=1, source_target_pairs={{0,12},{4,0},{8,4},{12,8},{1,13},{5,1},{9,5},{13,9},{2,14},{6,2},{... | collective-permute-start | bytes 884744 | tf_op jit(solution)/shard_map/ppermute | solution.py:339
  184.0 59.5 %collective-permute-start.34 = (bf16[1536,384]{1,0:T(8,128)(2,1)S(1)}, bf16[1536,384]{1,0:T(8,128)(2,1)S(1)}, u32[]{:S(2)}, u32[]{:S(2)}) collective-permute-start(bf16[1536,384]{1,0:T(8,128)(2,1)S(1)} %collective-permute-done.10.refs_13_), channel_id=1, source_target_pairs={{0,1},{1,0},{2,3},{3,2},{4,5},{5,4},{6,7},{7,6},{8,9},{9,8},{10,11... | collective-permute-start | bytes 3538952 | tf_op jit(solution)/shard_map/ppermute | solution.py:372
  184.8 60.2 %collective-permute-start.37 = (bf16[1536,384]{1,0:T(8,128)(2,1)}, bf16[1536,384]{1,0:T(8,128)(2,1)}, u32[]{:S(2)}, u32[]{:S(2)}) collective-permute-start(bf16[1536,384]{1,0:T(8,128)(2,1)} %collective-permute-done.20.refs_17_), channel_id=1, source_target_pairs={{0,2},{1,3},{2,0},{3,1},{4,6},{5,7},{6,4},{7,5},{8,10},{9,11},{10,... | collective-permute-start | bytes 3538952 | tf_op jit(solution)/shard_map/ppermute | solution.py:597
  185.6 68.8 %collective-permute-start.40 = (bf16[384,1536]{1,0:T(8,128)(2,1)}, bf16[384,1536]{1,0:T(8,128)(2,1)}, u32[]{:S(2)}, u32[]{:S(2)}) collective-permute-start(bf16[384,1536]{1,0:T(8,128)(2,1)} %collective-permute-done.30.refs_21_), channel_id=1, source_target_pairs={{0,2},{1,3},{2,0},{3,1},{4,6},{5,7},{6,4},{7,5},{8,10},{9,11},{10,... | collective-permute-start | bytes 3538952 | tf_op jit(solution)/shard_map/ppermute | solution.py:597
  186.9 29.1 %collective-permute-start.31 = (bf16[128,1536]{1,0:T(8,128)(2,1)S(1)}, bf16[128,1536]{1,0:T(8,128)(2,1)S(1)}, u32[]{:S(2)}, u32[]{:S(2)}) collective-permute-start(bf16[128,1536]{1,0:T(8,128)(2,1)S(1)} %get-tuple-element.186.refs_6_), channel_id=1, source_target_pairs={{0,4},{4,8},{8,12},{12,0},{1,5},{5,9},{9,13},{13,1},{2,6},{6,10},{... | collective-permute-start | bytes 1179656 | tf_op jit(solution)/shard_map/ppermute | solution.py:339
  198.6 43.9 %collective-permute-start.32 = (bf16[128,1536]{1,0:T(8,128)(2,1)S(1)}, bf16[128,1536]{1,0:T(8,128)(2,1)S(1)}, u32[]{:S(2)}, u32[]{:S(2)}) collective-permute-start(bf16[128,1536]{1,0:T(8,128)(2,1)S(1)} %get-tuple-element.186.refs_6_), channel_id=1, source_target_pairs={{0,8},{4,12},{8,0},{12,4},{1,9},{5,13},{9,1},{13,5},{2,10},{6,14},... | collective-permute-start | bytes 1179656 | tf_op jit(solution)/shard_map/ppermute | solution.py:339
  215.9 27.6 %collective-permute-start.33 = (bf16[128,1536]{1,0:T(8,128)(2,1)S(1)}, bf16[128,1536]{1,0:T(8,128)(2,1)S(1)}, u32[]{:S(2)}, u32[]{:S(2)}) collective-permute-start(bf16[128,1536]{1,0:T(8,128)(2,1)S(1)} %get-tuple-element.186.refs_6_), channel_id=1, source_target_pairs={{0,12},{4,0},{8,4},{12,8},{1,13},{5,1},{9,5},{13,9},{2,14},{6,2},{... | collective-permute-start | bytes 1179656 | tf_op jit(solution)/shard_map/ppermute | solution.py:339
  270.5 93.9 %all-gather.8.cloned.1.call-start = ((), (), s32[]{:S(2)}) async-start(), calls=%async_computation.5 | async-start | bytes 7864320 | tf_op jit(solution)/shard_map/all_gather | solution.py:766
  271.2 421.8 %reduce-scatter.3.cloned.1.call-start = ((), (), s32[]{:S(2)}) async-start(), calls=%async_computation.3 | async-start | bytes 1966080 | tf_op jit(solution)/shard_map/reduce_scatter | solution.py:896
  276.8 28.7 %collective-permute-start.43 = (bf16[128,1536]{1,0:T(8,128)(2,1)}, bf16[128,1536]{1,0:T(8,128)(2,1)}, u32[]{:S(2)}, u32[]{:S(2)}) collective-permute-start(bf16[128,1536]{1,0:T(8,128)(2,1)} %get-tuple-element.196), channel_id=1, source_target_pairs={{0,8},{4,12},{8,0},{12,4},{1,9},{5,13},{9,1},{13,5},{2,10},{6,14},... | collective-permute-start | bytes 1179656 | tf_op jit(solution)/shard_map/ppermute | solution.py:355
  279.2 26.3 %collective-permute-start.42 = (bf16[128,1536]{1,0:T(8,128)(2,1)}, bf16[128,1536]{1,0:T(8,128)(2,1)}, u32[]{:S(2)}, u32[]{:S(2)}) collective-permute-start(bf16[128,1536]{1,0:T(8,128)(2,1)} %get-tuple-element.195), channel_id=1, source_target_pairs={{0,12},{4,0},{8,4},{12,8},{1,13},{5,1},{9,5},{13,9},{2,14},{6,2},{... | collective-permute-start | bytes 1179656 | tf_op jit(solution)/shard_map/ppermute | solution.py:355
  350.6 34.0 %collective-permute-start.51 = (bf16[128,3072]{1,0:T(8,128)(2,1)}, bf16[128,3072]{1,0:T(8,128)(2,1)}, u32[]{:S(2)}, u32[]{:S(2)}) collective-permute-start(bf16[128,3072]{1,0:T(8,128)(2,1)} %get-tuple-element.454), channel_id=1, source_target_pairs={{0,16},{16,0},{1,17},{17,1},{2,18},{18,2},{3,19},{19,3},{4,20},{20... | collective-permute-start | bytes 2359304 | tf_op jit(solution)/shard_map/ppermute | solution.py:367
  356.1 28.6 %collective-permute-start.49 = (bf16[128,1536]{1,0:T(8,128)(2,1)S(1)}, bf16[128,1536]{1,0:T(8,128)(2,1)}, u32[]{:S(2)}, u32[]{:S(2)}) collective-permute-start(bf16[128,1536]{1,0:T(8,128)(2,1)S(1)} %multiply_convert_fusion.4.refs_6_), channel_id=1, source_target_pairs={{0,8},{4,12},{8,0},{12,4},{1,9},{5,13},{9,1},{13,5},{2,10},{6,14},... | collective-permute-start | bytes 1179656 | tf_op jit(solution)/shard_map/ppermute | solution.py:339
  356.3 28.4 %collective-permute-start.50 = (bf16[128,1536]{1,0:T(8,128)(2,1)S(1)}, bf16[128,1536]{1,0:T(8,128)(2,1)}, u32[]{:S(2)}, u32[]{:S(2)}) collective-permute-start(bf16[128,1536]{1,0:T(8,128)(2,1)S(1)} %multiply_convert_fusion.4.refs_6_), channel_id=1, source_target_pairs={{0,12},{4,0},{8,4},{12,8},{1,13},{5,1},{9,5},{13,9},{2,14},{6,2},{... | collective-permute-start | bytes 1179656 | tf_op jit(solution)/shard_map/ppermute | solution.py:339
  364.3 94.9 %collective-permute-start.59 = (bf16[1,256,1536]{2,1,0:T(8,128)(2,1)}, bf16[1,256,1536]{2,1,0:T(8,128)(2,1)}, u32[]{:S(2)}, u32[]{:S(2)}) collective-permute-start(bf16[1,256,1536]{2,1,0:T(8,128)(2,1)} %get-tuple-element.453), channel_id=1, source_target_pairs={{0,1},{1,0},{2,3},{3,2},{4,5},{5,4},{6,7},{7,6},{8,9},{9,8},{10,11... | collective-permute-start | bytes 2359304 | tf_op jit(solution)/shard_map/ppermute | solution.py:372
  418.9 27.8 %collective-permute-start.53 = (bf16[128,1664]{1,0:T(8,128)(2,1)}, bf16[128,1664]{1,0:T(8,128)(2,1)S(1)}, u32[]{:S(2)}, u32[]{:S(2)}) collective-permute-start(bf16[128,1664]{1,0:T(8,128)(2,1)} %get-tuple-element.225), channel_id=1, source_target_pairs={{0,8},{4,12},{8,0},{12,4},{1,9},{5,13},{9,1},{13,5},{2,10},{6,14},... | collective-permute-start | bytes 1277960 | tf_op jit(solution)/shard_map/ppermute | solution.py:347
  419.6 38.3 %collective-permute-start.52 = (bf16[128,1664]{1,0:T(8,128)(2,1)}, bf16[128,1664]{1,0:T(8,128)(2,1)S(1)}, u32[]{:S(2)}, u32[]{:S(2)}) collective-permute-start(bf16[128,1664]{1,0:T(8,128)(2,1)} %get-tuple-element.224), channel_id=1, source_target_pairs={{0,12},{4,0},{8,4},{12,8},{1,13},{5,1},{9,5},{13,9},{2,14},{6,2},{... | collective-permute-start | bytes 1277960 | tf_op jit(solution)/shard_map/ppermute | solution.py:347
  422.7 35.2 %collective-permute-start.56 = (bf16[256,3072]{1,0:T(8,128)(2,1)S(1)}, bf16[256,3072]{1,0:T(8,128)(2,1)S(1)}, u32[]{:S(2)}, u32[]{:S(2)}) collective-permute-start(bf16[256,3072]{1,0:T(8,128)(2,1)S(1)} %constant_dynamic-update-slice_fusion.3), channel_id=1, source_target_pairs={{0,2},{1,3},{2,0},{3,1},{4,6},{5,7},{6,4},{7,5},{8,10},{9,11},{10,... | collective-permute-start | bytes 4718600 | tf_op jit(solution)/shard_map/ppermute | solution.py:597
  430.2 29.1 %collective-permute-start.58 = (bf16[1,256,1536]{2,1,0:T(8,128)(2,1)S(1)}, bf16[1,256,1536]{2,1,0:T(8,128)(2,1)S(1)}, u32[]{:S(2)}, u32[]{:S(2)}) collective-permute-start(bf16[1,256,1536]{2,1,0:T(8,128)(2,1)S(1)} %get-tuple-element.451), channel_id=1, source_target_pairs={{0,1},{1,0},{2,3},{3,2},{4,5},{5,4},{6,7},{7,6},{8,9},{9,8},{10,11... | collective-permute-start | bytes 2359304 | tf_op jit(solution)/shard_map/ppermute | solution.py:372
  463.4 25.5 %collective-permute-start.60 = (bf16[1,256,1536]{2,1,0:T(8,128)(2,1)}, bf16[1,256,1536]{2,1,0:T(8,128)(2,1)}, u32[]{:S(2)}, u32[]{:S(2)}) collective-permute-start(bf16[1,256,1536]{2,1,0:T(8,128)(2,1)} %get-tuple-element.449), channel_id=1, source_target_pairs={{0,16},{16,0},{1,17},{17,1},{2,18},{18,2},{3,19},{19,3},{4,20},{20... | collective-permute-start | bytes 2359304 | tf_op jit(solution)/shard_map/ppermute | solution.py:367
  463.9 40.7 %collective-permute-start.66 = (bf16[1,512,1536]{2,1,0:T(8,128)(2,1)}, bf16[1,512,1536]{2,1,0:T(8,128)(2,1)}, u32[]{:S(2)}, u32[]{:S(2)}) collective-permute-start(bf16[1,512,1536]{2,1,0:T(8,128)(2,1)} %get-tuple-element.433), channel_id=1, source_target_pairs={{0,2},{1,3},{2,0},{3,1},{4,6},{5,7},{6,4},{7,5},{8,10},{9,11},{10,... | collective-permute-start | bytes 4718600 | tf_op jit(solution)/shard_map/ppermute | solution.py:597
  502.4 80.6 %collective-permute-start.75 = (bf16[1,256,1536]{2,1,0:T(8,128)(2,1)}, bf16[1,256,1536]{2,1,0:T(8,128)(2,1)}, u32[]{:S(2)}, u32[]{:S(2)}) collective-permute-start(bf16[1,256,1536]{2,1,0:T(8,128)(2,1)} %get-tuple-element.447), channel_id=1, source_target_pairs={{0,1},{1,0},{2,3},{3,2},{4,5},{5,4},{6,7},{7,6},{8,9},{9,8},{10,11... | collective-permute-start | bytes 2359304 | tf_op jit(solution)/shard_map/ppermute | solution.py:372
  523.4 29.0 %collective-permute-start.68 = (bf16[128,1536]{1,0:T(8,128)(2,1)S(1)}, bf16[128,1536]{1,0:T(8,128)(2,1)S(1)}, u32[]{:S(2)}, u32[]{:S(2)}) collective-permute-start(bf16[128,1536]{1,0:T(8,128)(2,1)S(1)} %fusion.145.refs_6_), channel_id=1, source_target_pairs={{0,8},{4,12},{8,0},{12,4},{1,9},{5,13},{9,1},{13,5},{2,10},{6,14},... | collective-permute-start | bytes 1179656 | tf_op jit(solution)/shard_map/ppermute | solution.py:339
  525.6 26.8 %collective-permute-start.69 = (bf16[128,1536]{1,0:T(8,128)(2,1)S(1)}, bf16[128,1536]{1,0:T(8,128)(2,1)S(1)}, u32[]{:S(2)}, u32[]{:S(2)}) collective-permute-start(bf16[128,1536]{1,0:T(8,128)(2,1)S(1)} %fusion.145.refs_6_), channel_id=1, source_target_pairs={{0,12},{4,0},{8,4},{12,8},{1,13},{5,1},{9,5},{13,9},{2,14},{6,2},{... | collective-permute-start | bytes 1179656 | tf_op jit(solution)/shard_map/ppermute | solution.py:339
  578.8 28.1 %collective-permute-start.72 = (bf16[128,1664]{1,0:T(8,128)(2,1)}, bf16[128,1664]{1,0:T(8,128)(2,1)S(1)}, u32[]{:S(2)}, u32[]{:S(2)}) collective-permute-start(bf16[128,1664]{1,0:T(8,128)(2,1)} %get-tuple-element.262), channel_id=1, source_target_pairs={{0,8},{4,12},{8,0},{12,4},{1,9},{5,13},{9,1},{13,5},{2,10},{6,14},... | collective-permute-start | bytes 1277960 | tf_op jit(solution)/shard_map/ppermute | solution.py:347
  579.2 27.7 %collective-permute-start.71 = (bf16[128,1664]{1,0:T(8,128)(2,1)}, bf16[128,1664]{1,0:T(8,128)(2,1)S(1)}, u32[]{:S(2)}, u32[]{:S(2)}) collective-permute-start(bf16[128,1664]{1,0:T(8,128)(2,1)} %get-tuple-element.261), channel_id=1, source_target_pairs={{0,12},{4,0},{8,4},{12,8},{1,13},{5,1},{9,5},{13,9},{2,14},{6,2},{... | collective-permute-start | bytes 1277960 | tf_op jit(solution)/shard_map/ppermute | solution.py:347
  585.4 35.4 %collective-permute-start.76 = (bf16[1,512,1536]{2,1,0:T(8,128)(2,1)S(1)}, bf16[1,512,1536]{2,1,0:T(8,128)(2,1)S(1)}, u32[]{:S(2)}, u32[]{:S(2)}) collective-permute-start(bf16[1,512,1536]{2,1,0:T(8,128)(2,1)S(1)} %get-tuple-element.279), channel_id=1, source_target_pairs={{0,2},{1,3},{2,0},{3,1},{4,6},{5,7},{6,4},{7,5},{8,10},{9,11},{10,... | collective-permute-start | bytes 4718600 | tf_op jit(solution)/shard_map/ppermute | solution.py:597
  585.9 35.1 %collective-permute-start.77 = (bf16[1,512,1536]{2,1,0:T(8,128)(2,1)S(1)}, bf16[1,512,1536]{2,1,0:T(8,128)(2,1)S(1)}, u32[]{:S(2)}, u32[]{:S(2)}) collective-permute-start(bf16[1,512,1536]{2,1,0:T(8,128)(2,1)S(1)} %get-tuple-element.431), channel_id=1, source_target_pairs={{0,16},{16,0},{1,17},{17,1},{2,18},{18,2},{3,19},{19,3},{4,20},{20... | collective-permute-start | bytes 4718600 | tf_op jit(solution)/shard_map/ppermute | solution.py:367
  641.2 122.7 %reduce-scatter.5.cloned.1.call-start = ((), (), s32[]{:S(2)}) async-start(), calls=%async_computation.4 | async-start | bytes 1536000 | tf_op jit(solution)/shard_map/reduce_scatter | solution.py:838
  714.1 26.1 %collective-permute-start.91 = (bf16[384,512]{1,0:T(8,128)(2,1)S(1)}, bf16[384,512]{1,0:T(8,128)(2,1)S(1)}, u32[]{:S(2)}, u32[]{:S(2)}) collective-permute-start(bf16[384,512]{1,0:T(8,128)(2,1)S(1)} %get-tuple-element.442), channel_id=1, source_target_pairs={{0,4},{4,8},{8,12},{12,0},{1,5},{5,9},{9,13},{13,1},{2,6},{6,10},{... | collective-permute-start | bytes 1179656 | tf_op jit(solution)/shard_map/ppermute | solution.py:347
  716.7 27.8 %collective-permute-start.90 = (bf16[384,512]{1,0:T(8,128)(2,1)S(1)}, bf16[384,512]{1,0:T(8,128)(2,1)S(1)}, u32[]{:S(2)}, u32[]{:S(2)}) collective-permute-start(bf16[384,512]{1,0:T(8,128)(2,1)S(1)} %get-tuple-element.443), channel_id=1, source_target_pairs={{0,8},{4,12},{8,0},{12,4},{1,9},{5,13},{9,1},{13,5},{2,10},{6,14},... | collective-permute-start | bytes 1179656 | tf_op jit(solution)/shard_map/ppermute | solution.py:347
  716.7 27.8 %collective-permute-start.89 = (bf16[384,512]{1,0:T(8,128)(2,1)S(1)}, bf16[384,512]{1,0:T(8,128)(2,1)S(1)}, u32[]{:S(2)}, u32[]{:S(2)}) collective-permute-start(bf16[384,512]{1,0:T(8,128)(2,1)S(1)} %get-tuple-element.441), channel_id=1, source_target_pairs={{0,12},{4,0},{8,4},{12,8},{1,13},{5,1},{9,5},{13,9},{2,14},{6,2},{... | collective-permute-start | bytes 1179656 | tf_op jit(solution)/shard_map/ppermute | solution.py:347
  719.2 35.9 %collective-permute-start.92 = (bf16[1,512,1536]{2,1,0:T(8,128)(2,1)S(1)}, bf16[1,512,1536]{2,1,0:T(8,128)(2,1)S(1)}, u32[]{:S(2)}, u32[]{:S(2)}) collective-permute-start(bf16[1,512,1536]{2,1,0:T(8,128)(2,1)S(1)} %copy-done.108), channel_id=1, source_target_pairs={{0,2},{1,3},{2,0},{3,1},{4,6},{5,7},{6,4},{7,5},{8,10},{9,11},{10,... | collective-permute-start | bytes 4718600 | tf_op jit(solution)/shard_map/ppermute | solution.py:597
  764.9 25.9 %collective-permute-start.95 = (bf16[384,512]{1,0:T(8,128)(2,1)S(1)}, bf16[384,512]{1,0:T(8,128)(2,1)S(1)}, u32[]{:S(2)}, u32[]{:S(2)}) collective-permute-start(bf16[384,512]{1,0:T(8,128)(2,1)S(1)} %add_convert_fusion.5), channel_id=1, source_target_pairs={{0,1},{1,0},{2,3},{3,2},{4,5},{5,4},{6,7},{7,6},{8,9},{9,8},{10,11... | collective-permute-start | bytes 1179656 | tf_op jit(solution)/shard_map/ppermute | solution.py:372
  765.0 26.4 %collective-permute-start.96 = (bf16[384,512]{1,0:T(8,128)(2,1)S(1)}, bf16[384,512]{1,0:T(8,128)(2,1)S(1)}, u32[]{:S(2)}, u32[]{:S(2)}) collective-permute-start(bf16[384,512]{1,0:T(8,128)(2,1)S(1)} %add_convert_fusion.5), channel_id=1, source_target_pairs={{0,2},{1,3},{2,0},{3,1},{4,6},{5,7},{6,4},{7,5},{8,10},{9,11},{10,... | collective-permute-start | bytes 1179656 | tf_op jit(solution)/shard_map/ppermute | solution.py:597
  780.8 28.8 %collective-permute-start.102 = (bf16[1,1536,768]{2,1,0:T(8,128)(2,1)S(1)}, bf16[1,1536,768]{2,1,0:T(8,128)(2,1)S(1)}, u32[]{:S(2)}, u32[]{:S(2)}) collective-permute-start(bf16[1,1536,768]{2,1,0:T(8,128)(2,1)S(1)} %bitcast.619), channel_id=1, source_target_pairs={{0,1},{1,0},{2,3},{3,2},{4,5},{5,4},{6,7},{7,6},{8,9},{9,8},{10,11... | collective-permute-start | bytes 7077896 | tf_op jit(solution)/shard_map/ppermute | solution.py:372
  (283 other events, 3569.6 us)
Sparse Core Ops, SparseCore 0:
  96.9 147.5 all-gather.5
  270.5 41.4 all-gather.9
  314.2 46.3 all-gather.7
  641.3 42.1 reduce-scatter.2
  685.7 30.9 reduce-scatter.4

commit v5 on v4

--- a/solution.py
+++ b/solution.py
@@ -929,8 +929,8 @@
     got_x = all_x(got)
     g_got, x_got = by_order(got, got_x), by_order(x_got, x_got_x)
     shard = fold_sum(left_whole[:, :model], right.reshape(-1, right.shape[2]), None)
-    shard, (middle_own, x_own, first_value, grads) = lax.optimization_barrier(
-        (shard, (middle_own, x_own, first_value, grads))
+    shard, (middle_own, x_own, first_value, grads, second_sum) = lax.optimization_barrier(
+        (shard, (middle_own, x_own, first_value, grads, second_sum))
     )
     x_got = [flat_rows(x_got)[i] for i in range(half)]
     g_own, g_got = [[flat_rows(value)[i] for i in range(half)] for value in (g_own, g_got)]
@@ -948,7 +948,6 @@
                 (mm_tn(inner[0], g_own[i]) + mm_tn(inner[1], g_got[i])).astype(BF16),
             )
         )
-    made, second_sum = lax.optimization_barrier((made, second_sum))
     outs = [first_value, second_finish([second_sum])]
     small = side_by_side(out_shard[:, depth:, :piece])
     out_shard = side_by_side(out_shard[:, :depth])

time: 835 us -> 826 us (0.989)
    ppermute x14, waiting for transfers between devices: 28.9 us -> 15 us  [swap_section(): return lax.ppermute(value, S_AX, [(0, 1), (1, 0)])]
    ppermute x15, waiting for transfers between devices: 40.5 us -> 51.6 us  [rel_scatter(): lax.ppermute(parts[k], F_AX, [(i, (i - k) % folds) for i in range(folds)])]
where the time goes in v5:
time: 826 us; the launch traced here: 817 us
  waiting for transfers between devices  315 us (38%)
  starting transfers between devices  146 us (18%)
  matrix products  120 us (15%)
  local copies, waits for them, and re-layouts  85.8 us (10%)
  other arithmetic  79.8 us (10%)
  Pallas kernels  51.5 us (6%)
  between operations  17.9 us (2%)
    ppermute x24, waiting for transfers between devices, rel_gather(): lax.ppermute(value, F_AX, [(i, (i + k) % folds) for i in range(folds)])  138 us
    ppermute x25, waiting for transfers between devices, swap_xor(): return lax.ppermute(value, R_AX, [(i, i ^ bit) for i in range(replicas)])  80.7 us
    ppermute x24, starting transfers between devices, rel_gather(): lax.ppermute(value, F_AX, [(i, (i + k) % folds) for i in range(folds)])  63.9 us
    ppermute x15, waiting for transfers between devices, rel_scatter(): lax.ppermute(parts[k], F_AX, [(i, (i - k) % folds) for i in range(folds)])  51.6 us
    dot_general x16, matrix products, mm_nt(): lax.dot_general(a, b, (((1,), (1,)), ((), ())), preferred_element_type=F32)  37.4 us
    dot_general x10, matrix products, mm_tn(): lax.dot_general(a, b, (((0,), (0,)), ((), ())), preferred_element_type=F32)  33.3 us
    ppermute x15, starting transfers between devices, rel_scatter(): lax.ppermute(parts[k], F_AX, [(i, (i - k) % folds) for i in range(folds)])  32 us
    dot_general x8, matrix products, mm(): return jnp.dot(a, b, preferred_element_type=F32)  28.8 us
  transfers between devices with their start and end apart: 109, of which 44 were waited for; matrix products, arithmetic and copies ran while one was open for 29% of the time, Pallas kernels for 6%

profile of v5, /device:TPU:0, one launch (start us, length us, event | category | flops | bytes accessed | tf_op | source)
XLA Modules:
  0.0 816.6 jit_solution(10438735409828646806)
XLA Ops:
  29.9 4.6 dynamic-slice_bitcast_fusion.1
  36.0 4.8 collective-permute-done.11
  60.1 6.4 collective-permute-done.7.refs_3_
  66.5 17.5 %collective-permute-done.8.refs_4_ = bf16[384,640]{1,0:T(8,128)(2,1)S(1)} collective-permute-done((bf16[384,640]{1,0:T(8,128)(2,1)S(1)}, bf16[384,640]{1,0:T(8,128)(2,1)S(1)}, u32[]{:S(2)}, u32[]{:S(2)}) %collective-permute-start.8) | collective-permute-done | bytes 491552 | tf_op jit(solution)/shard_map/ppermute | solution.py:339
  88.8 4.3 collective-permute-done.13
  104.0 11.6 %collective-permute-start.18 = (bf16[128,512]{0,1:T(8,128)(2,1)S(1)}, bf16[128,512]{0,1:T(8,128)(2,1)S(1)}, u32[]{:S(2)}, u32[]{:S(2)}) collective-permute-start(bf16[128,512]{0,1:T(8,128)(2,1)S(1)} %pad_maximum_fusion.23), channel_id=1, source_target_pairs={{0,12},{4,0},{8,4},{12,8},{1,13},{5,1},{9,5},{13,9},{2,14},{6,2},{... | collective-permute-start | bytes 393224 | tf_op jit(solution)/shard_map/ppermute | solution.py:339
  122.8 12.8 %collective-permute-done.17 = bf16[128,512]{0,1:T(8,128)(2,1)S(1)} collective-permute-done((bf16[128,512]{0,1:T(8,128)(2,1)S(1)}, bf16[128,512]{0,1:T(8,128)(2,1)S(1)}, u32[]{:S(2)}, u32[]{:S(2)}) %collective-permute-start.17) | collective-permute-done | bytes 131104 | tf_op jit(solution)/shard_map/ppermute | solution.py:339
  157.3 10.8 %collective-permute-done.22 = bf16[128,1536]{0,1:T(8,128)(2,1)S(1)} collective-permute-done((bf16[128,1536]{0,1:T(8,128)(2,1)S(1)}, bf16[128,1536]{0,1:T(8,128)(2,1)S(1)}, u32[]{:S(2)}, u32[]{:S(2)}) %collective-permute-start.22) | collective-permute-done | bytes 393248 | tf_op jit(solution)/shard_map/ppermute | solution.py:597
  187.5 11.0 %collective-permute-start.31 = (bf16[128,1536]{1,0:T(8,128)(2,1)S(1)}, bf16[128,1536]{1,0:T(8,128)(2,1)S(1)}, u32[]{:S(2)}, u32[]{:S(2)}) collective-permute-start(bf16[128,1536]{1,0:T(8,128)(2,1)S(1)} %get-tuple-element.183.refs_6_), channel_id=1, source_target_pairs={{0,4},{4,8},{8,12},{12,0},{1,5},{5,9},{9,13},{13,1},{2,6},{6,10},{... | collective-permute-start | bytes 1179656 | tf_op jit(solution)/shard_map/ppermute | solution.py:339
  202.0 13.8 %collective-permute-done.31.refs_7_ = bf16[128,1536]{1,0:T(8,128)(2,1)S(1)} collective-permute-done((bf16[128,1536]{1,0:T(8,128)(2,1)S(1)}, bf16[128,1536]{1,0:T(8,128)(2,1)S(1)}, u32[]{:S(2)}, u32[]{:S(2)}) %collective-permute-start.31) | collective-permute-done | bytes 393248 | tf_op jit(solution)/shard_map/ppermute | solution.py:339
  217.1 25.3 %collective-permute-done.32.refs_8_ = bf16[128,1536]{1,0:T(8,128)(2,1)S(1)} collective-permute-done((bf16[128,1536]{1,0:T(8,128)(2,1)S(1)}, bf16[128,1536]{1,0:T(8,128)(2,1)S(1)}, u32[]{:S(2)}, u32[]{:S(2)}) %collective-permute-start.32) | collective-permute-done | bytes 393248 | tf_op jit(solution)/shard_map/ppermute | solution.py:339
  244.9 9.6 %collective-permute-done.40.refs_23_ = bf16[384,1536]{1,0:T(8,128)(2,1)} collective-permute-done((bf16[384,1536]{1,0:T(8,128)(2,1)}, bf16[384,1536]{1,0:T(8,128)(2,1)}, u32[]{:S(2)}, u32[]{:S(2)}) %collective-permute-start.40) | collective-permute-done | bytes 1179680 | tf_op jit(solution)/shard_map/ppermute | solution.py:597
  257.8 12.6 %shard_map.212 = (bf16[2,256,1536]{2,1,0:T(8,128)(2,1)}, f32[2,256,768]{2,1,0:T(8,128)}, f32[2,256,768]{2,1,0:T(8,128)}, bf16[2,256,1536]{2,1,0:T(8,128)(2,1)}, ...) custom-call(s32[4]{0:T(128)} %get-tuple-element.521.refs_0_, ...), custom_call_target="tpu_custom_call" | custom-call | flops 3623878656 | bytes 20447232 | tf_op jit(solution)/shard_map/pallas_call | solution.py:274
  271.3 5.5 collective-permute-start.44
  282.2 6.7 collective-permute-done.44
  288.9 16.6 %collective-permute-done.43 = bf16[128,1536]{1,0:T(8,128)(2,1)} collective-permute-done((bf16[128,1536]{1,0:T(8,128)(2,1)}, bf16[128,1536]{1,0:T(8,128)(2,1)}, u32[]{:S(2)}, u32[]{:S(2)}) %collective-permute-start.43) | collective-permute-done | bytes 393248 | tf_op jit(solution)/shard_map/ppermute | solution.py:355
  317.8 9.0 %collective-permute-start.47 = (bf16[128,512]{1,0:T(8,128)(2,1)S(1)}, bf16[128,512]{1,0:T(8,128)(2,1)S(1)}, u32[]{:S(2)}, u32[]{:S(2)}) collective-permute-start(bf16[128,512]{1,0:T(8,128)(2,1)S(1)} %pad_maximum_fusion.24), channel_id=1, source_target_pairs={{0,12},{4,0},{8,4},{12,8},{1,13},{5,1},{9,5},{13,9},{2,14},{6,2},{... | collective-permute-start | bytes 393224 | tf_op jit(solution)/shard_map/ppermute | solution.py:339
  330.7 9.6 %collective-permute-done.46 = bf16[128,512]{1,0:T(8,128)(2,1)S(1)} collective-permute-done((bf16[128,512]{1,0:T(8,128)(2,1)S(1)}, bf16[128,512]{1,0:T(8,128)(2,1)S(1)}, u32[]{:S(2)}, u32[]{:S(2)}) %collective-permute-start.46) | collective-permute-done | bytes 131104 | tf_op jit(solution)/shard_map/ppermute | solution.py:339
  364.1 5.7 collective-permute-done.48.refs_7_
  369.8 14.8 %collective-permute-done.49.refs_8_ = bf16[128,1536]{1,0:T(8,128)(2,1)} collective-permute-done((bf16[128,1536]{1,0:T(8,128)(2,1)S(1)}, bf16[128,1536]{1,0:T(8,128)(2,1)}, u32[]{:S(2)}, u32[]{:S(2)}) %collective-permute-start.49) | collective-permute-done | bytes 393248 | tf_op jit(solution)/shard_map/ppermute | solution.py:339
  384.6 12.8 %shard_map.213 = (bf16[2,256,1536]{2,1,0:T(8,128)(2,1)}, f32[2,256,768]{2,1,0:T(8,128)}, f32[2,256,768]{2,1,0:T(8,128)}, bf16[2,256,1536]{2,1,0:T(8,128)(2,1)}, ...) custom-call(s32[4]{0:T(128)} %get-tuple-element.520.refs_0_, ...), custom_call_target="tpu_custom_call" | custom-call | flops 3623878656 | bytes 20447232 | tf_op jit(solution)/shard_map/pallas_call | solution.py:274
  397.4 13.2 %shard_map.214 = (bf16[2,256,1536]{2,1,0:T(8,128)(2,1)}, bf16[128,1664]{1,0:T(8,128)(2,1)}, bf16[128,1664]{1,0:T(8,128)(2,1)}, bf16[128,1664]{1,0:T(8,128)(2,1)}, bf16[128,1664]{1,0:T(8,128)(2,1)}) custom-call(s32[4]{0:T(128)} %get-tuple-element.520.refs_0_, s32[4,2,128]{2,1,0:T(2,128)} %get-tuple-element.207.refs_1_, ...), custom_call_target="tpu_custom_call" | custom-call | flops 3623878656 | bytes 20447232 | tf_op jit(solution)/shard_map/pallas_call | solution.py:298
  410.6 8.3 %collective-permute-start.54 = (bf16[128,1664]{1,0:T(8,128)(2,1)}, bf16[128,1664]{1,0:T(8,128)(2,1)S(1)}, u32[]{:S(2)}, u32[]{:S(2)}) collective-permute-start(bf16[128,1664]{1,0:T(8,128)(2,1)} %get-tuple-element.223), channel_id=1, source_target_pairs={{0,4},{4,8},{8,12},{12,0},{1,5},{5,9},{9,13},{13,1},{2,6},{6,10},{... | collective-permute-start | bytes 1277960 | tf_op jit(solution)/shard_map/ppermute | solution.py:347
  431.4 15.2 %collective-permute-done.53 = bf16[128,1664]{1,0:T(8,128)(2,1)S(1)} collective-permute-done((bf16[128,1664]{1,0:T(8,128)(2,1)}, bf16[128,1664]{1,0:T(8,128)(2,1)S(1)}, u32[]{:S(2)}, u32[]{:S(2)}) %collective-permute-start.53) | collective-permute-done | bytes 426016 | tf_op jit(solution)/shard_map/ppermute | solution.py:347
  446.6 11.3 %collective-permute-done.56 = bf16[256,3072]{1,0:T(8,128)(2,1)S(1)} collective-permute-done((bf16[256,3072]{1,0:T(8,128)(2,1)S(1)}, bf16[256,3072]{1,0:T(8,128)(2,1)S(1)}, u32[]{:S(2)}, u32[]{:S(2)}) %collective-permute-start.56) | collective-permute-done | bytes 1572896 | tf_op jit(solution)/shard_map/ppermute | solution.py:597
  477.0 4.8 fusion.53
  504.8 6.0 collective-permute-done.64
  510.8 6.6 collective-permute-done.65
  517.6 5.2 fusion.144
  530.2 7.2 collective-permute-done.67.refs_7_
  537.4 15.1 %collective-permute-done.68.refs_8_ = bf16[128,1536]{1,0:T(8,128)(2,1)S(1)} collective-permute-done((bf16[128,1536]{1,0:T(8,128)(2,1)S(1)}, bf16[128,1536]{1,0:T(8,128)(2,1)S(1)}, u32[]{:S(2)}, u32[]{:S(2)}) %collective-permute-start.68) | collective-permute-done | bytes 393248 | tf_op jit(solution)/shard_map/ppermute | solution.py:339
  553.7 13.0 %shard_map.215 = (bf16[2,256,1536]{2,1,0:T(8,128)(2,1)}, bf16[128,1664]{1,0:T(8,128)(2,1)}, bf16[128,1664]{1,0:T(8,128)(2,1)}, bf16[128,1664]{1,0:T(8,128)(2,1)}, bf16[128,1664]{1,0:T(8,128)(2,1)}) custom-call(s32[4]{0:T(128)} %get-tuple-element.521.refs_0_, s32[4,2,128]{2,1,0:T(2,128)} %get-tuple-element.248.refs_1_, ...), custom_call_target="tpu_custom_call" | custom-call | flops 3623878656 | bytes 20447232 | tf_op jit(solution)/shard_map/pallas_call | solution.py:298
  570.8 8.0 collective-permute-start.73
  591.5 4.3 fusion.63
  595.9 11.0 %collective-permute-done.72 = bf16[128,1664]{1,0:T(8,128)(2,1)S(1)} collective-permute-done((bf16[128,1664]{1,0:T(8,128)(2,1)}, bf16[128,1664]{1,0:T(8,128)(2,1)S(1)}, u32[]{:S(2)}, u32[]{:S(2)}) %collective-permute-start.72) | collective-permute-done | bytes 426016 | tf_op jit(solution)/shard_map/ppermute | solution.py:347
  607.2 13.4 %collective-permute-done.76 = bf16[1,512,1536]{2,1,0:T(8,128)(2,1)S(1)} collective-permute-done((bf16[1,512,1536]{2,1,0:T(8,128)(2,1)S(1)}, bf16[1,512,1536]{2,1,0:T(8,128)(2,1)S(1)}, u32[]{:S(2)}, u32[]{:S(2)}) %collective-permute-start.76) | collective-permute-done | bytes 1572896 | tf_op jit(solution)/shard_map/ppermute | solution.py:597
  663.7 6.2 multiply_convert_fusion.2
  698.0 4.8 collective-permute-done.88
  702.8 5.3 collective-permute-done.87
  720.3 4.8 fusion.259
  725.1 4.4 fusion.260
  737.9 8.1 collective-permute-done.92
  745.9 6.9 collective-permute-done.91
  756.4 7.2 multiply_convert_fusion
  766.0 5.2 fusion.39
  796.1 4.4 maximum_convert_fusion
  800.8 4.4 maximum_convert_fusion.1
  805.4 4.4 maximum_convert_fusion.2
  (942 shorter events, 364.5 us)
Async XLA Ops:
  7.2 300.1 %all-gather.6.cloned.1.call-start = ((), (), s32[]{:S(2)}) async-start(), calls=%async_computation.2 | async-start | bytes 11759616 | tf_op jit(solution)/shard_map/all_gather | solution.py:714
  9.0 37.9 %collective-permute-start.4 = (bf16[128,1536]{1,0:T(8,128)(2,1)}, bf16[128,1536]{1,0:T(8,128)(2,1)}, u32[]{:S(2)}, u32[]{:S(2)}) collective-permute-start(bf16[128,1536]{1,0:T(8,128)(2,1)} %dynamic-slice_bitcast_fusion.3.refs_6_), channel_id=1, source_target_pairs={{0,4},{4,8},{8,12},{12,0},{1,5},{5,9},{9,13},{13,1},{2,6},{6,10},{... | collective-permute-start | bytes 1179656 | tf_op jit(solution)/shard_map/ppermute | solution.py:339
  12.0 34.9 %collective-permute-start.5 = (bf16[128,1536]{1,0:T(8,128)(2,1)}, bf16[128,1536]{1,0:T(8,128)(2,1)}, u32[]{:S(2)}, u32[]{:S(2)}) collective-permute-start(bf16[128,1536]{1,0:T(8,128)(2,1)} %dynamic-slice_bitcast_fusion.3.refs_6_), channel_id=1, source_target_pairs={{0,8},{4,12},{8,0},{12,4},{1,9},{5,13},{9,1},{13,5},{2,10},{6,14},... | collective-permute-start | bytes 1179656 | tf_op jit(solution)/shard_map/ppermute | solution.py:339
  51.2 32.8 %collective-permute-start.8 = (bf16[384,640]{1,0:T(8,128)(2,1)S(1)}, bf16[384,640]{1,0:T(8,128)(2,1)S(1)}, u32[]{:S(2)}, u32[]{:S(2)}) collective-permute-start(bf16[384,640]{1,0:T(8,128)(2,1)S(1)} %fusion.163.refs_2_), channel_id=1, source_target_pairs={{0,8},{4,12},{8,0},{12,4},{1,9},{5,13},{9,1},{13,5},{2,10},{6,14},... | collective-permute-start | bytes 1474568 | tf_op jit(solution)/shard_map/ppermute | solution.py:339
  54.5 29.5 %collective-permute-start.10 = (bf16[1536,384]{1,0:T(8,128)(2,1)}, bf16[1536,384]{1,0:T(8,128)(2,1)S(1)}, u32[]{:S(2)}, u32[]{:S(2)}) collective-permute-start(bf16[1536,384]{1,0:T(8,128)(2,1)} %get-tuple-element.163), channel_id=1, source_target_pairs={{0,16},{16,0},{1,17},{17,1},{2,18},{18,2},{3,19},{19,3},{4,20},{20... | collective-permute-start | bytes 3538952 | tf_op jit(solution)/shard_map/ppermute | solution.py:367
  57.8 26.2 %collective-permute-start.9 = (bf16[384,640]{1,0:T(8,128)(2,1)S(1)}, bf16[384,640]{1,0:T(8,128)(2,1)S(1)}, u32[]{:S(2)}, u32[]{:S(2)}) collective-permute-start(bf16[384,640]{1,0:T(8,128)(2,1)S(1)} %fusion.163.refs_2_), channel_id=1, source_target_pairs={{0,12},{4,0},{8,4},{12,8},{1,13},{5,1},{9,5},{13,9},{2,14},{6,2},{... | collective-permute-start | bytes 1474568 | tf_op jit(solution)/shard_map/ppermute | solution.py:339
  59.2 36.8 %collective-permute-start.15 = (bf16[48,3712]{1,0:T(8,128)(2,1)S(1)}, bf16[48,3712]{1,0:T(8,128)(2,1)S(1)}, u32[]{:S(2)}, u32[]{:S(2)}) collective-permute-start(bf16[48,3712]{1,0:T(8,128)(2,1)S(1)} %get-tuple-element.169), channel_id=1, source_target_pairs={{0,16},{16,0},{1,17},{17,1},{2,18},{18,2},{3,19},{19,3},{4,20},{20... | collective-permute-start | bytes 1069064 | tf_op jit(solution)/shard_map/ppermute | solution.py:367
  96.8 267.3 %all-gather.10.cloned.1.call-start = ((), (), s32[]{:S(2)}) async-start(), calls=%async_computation.6 | async-start | bytes 5898240 | tf_op jit(solution)/shard_map/all_gather | solution.py:766
  98.5 39.4 %collective-permute-start.20 = (bf16[1536,384]{1,0:T(8,128)(2,1)}, bf16[1536,384]{1,0:T(8,128)(2,1)}, u32[]{:S(2)}, u32[]{:S(2)}) collective-permute-start(bf16[1536,384]{1,0:T(8,128)(2,1)} %get-tuple-element.172), channel_id=1, source_target_pairs={{0,16},{16,0},{1,17},{17,1},{2,18},{18,2},{3,19},{19,3},{4,20},{20... | collective-permute-start | bytes 3538952 | tf_op jit(solution)/shard_map/ppermute | solution.py:367
  100.2 41.9 %collective-permute-start.19 = (bf16[1536,384]{1,0:T(8,128)(2,1)S(1)}, bf16[1536,384]{1,0:T(8,128)(2,1)}, u32[]{:S(2)}, u32[]{:S(2)}) collective-permute-start(bf16[1536,384]{1,0:T(8,128)(2,1)S(1)} %collective-permute-done.10.refs_13_), channel_id=1, source_target_pairs={{0,2},{1,3},{2,0},{3,1},{4,6},{5,7},{6,4},{7,5},{8,10},{9,11},{10,... | collective-permute-start | bytes 3538952 | tf_op jit(solution)/shard_map/ppermute | solution.py:597
  121.5 62.5 %collective-permute-start.30 = (bf16[384,1536]{1,0:T(8,128)(2,1)}, bf16[384,1536]{1,0:T(8,128)(2,1)}, u32[]{:S(2)}, u32[]{:S(2)}) collective-permute-start(bf16[384,1536]{1,0:T(8,128)(2,1)} %dynamic-slice_bitcast_fusion), channel_id=1, source_target_pairs={{0,16},{16,0},{1,17},{17,1},{2,18},{18,2},{3,19},{19,3},{4,20},{20... | collective-permute-start | bytes 3538952 | tf_op jit(solution)/shard_map/ppermute | solution.py:367
  135.6 32.4 %collective-permute-start.25 = (bf16[384,384]{1,0:T(8,128)(2,1)}, bf16[384,384]{1,0:T(8,128)(2,1)}, u32[]{:S(2)}, u32[]{:S(2)}) collective-permute-start(bf16[384,384]{1,0:T(8,128)(2,1)} %broadcast_select_fusion.15), channel_id=1, source_target_pairs={{0,8},{4,12},{8,0},{12,4},{1,9},{5,13},{9,1},{13,5},{2,10},{6,14},... | collective-permute-start | bytes 884744 | tf_op jit(solution)/shard_map/ppermute | solution.py:339
  137.9 32.0 %collective-permute-start.26 = (bf16[384,384]{1,0:T(8,128)(2,1)}, bf16[384,384]{1,0:T(8,128)(2,1)}, u32[]{:S(2)}, u32[]{:S(2)}) collective-permute-start(bf16[384,384]{1,0:T(8,128)(2,1)} %broadcast_select_fusion.15), channel_id=1, source_target_pairs={{0,12},{4,0},{8,4},{12,8},{1,13},{5,1},{9,5},{13,9},{2,14},{6,2},{... | collective-permute-start | bytes 884744 | tf_op jit(solution)/shard_map/ppermute | solution.py:339
  184.0 59.2 %collective-permute-start.34 = (bf16[1536,384]{1,0:T(8,128)(2,1)S(1)}, bf16[1536,384]{1,0:T(8,128)(2,1)S(1)}, u32[]{:S(2)}, u32[]{:S(2)}) collective-permute-start(bf16[1536,384]{1,0:T(8,128)(2,1)S(1)} %collective-permute-done.10.refs_13_), channel_id=1, source_target_pairs={{0,1},{1,0},{2,3},{3,2},{4,5},{5,4},{6,7},{7,6},{8,9},{9,8},{10,11... | collective-permute-start | bytes 3538952 | tf_op jit(solution)/shard_map/ppermute | solution.py:372
  185.5 59.3 %collective-permute-start.37 = (bf16[1536,384]{1,0:T(8,128)(2,1)}, bf16[1536,384]{1,0:T(8,128)(2,1)}, u32[]{:S(2)}, u32[]{:S(2)}) collective-permute-start(bf16[1536,384]{1,0:T(8,128)(2,1)} %collective-permute-done.20.refs_17_), channel_id=1, source_target_pairs={{0,2},{1,3},{2,0},{3,1},{4,6},{5,7},{6,4},{7,5},{8,10},{9,11},{10,... | collective-permute-start | bytes 3538952 | tf_op jit(solution)/shard_map/ppermute | solution.py:597
  185.7 68.7 %collective-permute-start.40 = (bf16[384,1536]{1,0:T(8,128)(2,1)}, bf16[384,1536]{1,0:T(8,128)(2,1)}, u32[]{:S(2)}, u32[]{:S(2)}) collective-permute-start(bf16[384,1536]{1,0:T(8,128)(2,1)} %collective-permute-done.30.refs_21_), channel_id=1, source_target_pairs={{0,2},{1,3},{2,0},{3,1},{4,6},{5,7},{6,4},{7,5},{8,10},{9,11},{10,... | collective-permute-start | bytes 3538952 | tf_op jit(solution)/shard_map/ppermute | solution.py:597
  187.5 28.3 %collective-permute-start.31 = (bf16[128,1536]{1,0:T(8,128)(2,1)S(1)}, bf16[128,1536]{1,0:T(8,128)(2,1)S(1)}, u32[]{:S(2)}, u32[]{:S(2)}) collective-permute-start(bf16[128,1536]{1,0:T(8,128)(2,1)S(1)} %get-tuple-element.183.refs_6_), channel_id=1, source_target_pairs={{0,4},{4,8},{8,12},{12,0},{1,5},{5,9},{9,13},{13,1},{2,6},{6,10},{... | collective-permute-start | bytes 1179656 | tf_op jit(solution)/shard_map/ppermute | solution.py:339
  198.5 43.9 %collective-permute-start.32 = (bf16[128,1536]{1,0:T(8,128)(2,1)S(1)}, bf16[128,1536]{1,0:T(8,128)(2,1)S(1)}, u32[]{:S(2)}, u32[]{:S(2)}) collective-permute-start(bf16[128,1536]{1,0:T(8,128)(2,1)S(1)} %get-tuple-element.183.refs_6_), channel_id=1, source_target_pairs={{0,8},{4,12},{8,0},{12,4},{1,9},{5,13},{9,1},{13,5},{2,10},{6,14},... | collective-permute-start | bytes 1179656 | tf_op jit(solution)/shard_map/ppermute | solution.py:339
  215.8 27.4 %collective-permute-start.33 = (bf16[128,1536]{1,0:T(8,128)(2,1)S(1)}, bf16[128,1536]{1,0:T(8,128)(2,1)S(1)}, u32[]{:S(2)}, u32[]{:S(2)}) collective-permute-start(bf16[128,1536]{1,0:T(8,128)(2,1)S(1)} %get-tuple-element.183.refs_6_), channel_id=1, source_target_pairs={{0,12},{4,0},{8,4},{12,8},{1,13},{5,1},{9,5},{13,9},{2,14},{6,2},{... | collective-permute-start | bytes 1179656 | tf_op jit(solution)/shard_map/ppermute | solution.py:339
  270.5 93.6 %all-gather.8.cloned.1.call-start = ((), (), s32[]{:S(2)}) async-start(), calls=%async_computation.5 | async-start | bytes 7864320 | tf_op jit(solution)/shard_map/all_gather | solution.py:766
  271.3 421.5 %reduce-scatter.3.cloned.1.call-start = ((), (), s32[]{:S(2)}) async-start(), calls=%async_computation.3 | async-start | bytes 1966080 | tf_op jit(solution)/shard_map/reduce_scatter | solution.py:896
  276.8 28.7 %collective-permute-start.43 = (bf16[128,1536]{1,0:T(8,128)(2,1)}, bf16[128,1536]{1,0:T(8,128)(2,1)}, u32[]{:S(2)}, u32[]{:S(2)}) collective-permute-start(bf16[128,1536]{1,0:T(8,128)(2,1)} %get-tuple-element.193), channel_id=1, source_target_pairs={{0,8},{4,12},{8,0},{12,4},{1,9},{5,13},{9,1},{13,5},{2,10},{6,14},... | collective-permute-start | bytes 1179656 | tf_op jit(solution)/shard_map/ppermute | solution.py:355
  279.2 26.3 %collective-permute-start.42 = (bf16[128,1536]{1,0:T(8,128)(2,1)}, bf16[128,1536]{1,0:T(8,128)(2,1)}, u32[]{:S(2)}, u32[]{:S(2)}) collective-permute-start(bf16[128,1536]{1,0:T(8,128)(2,1)} %get-tuple-element.192), channel_id=1, source_target_pairs={{0,12},{4,0},{8,4},{12,8},{1,13},{5,1},{9,5},{13,9},{2,14},{6,2},{... | collective-permute-start | bytes 1179656 | tf_op jit(solution)/shard_map/ppermute | solution.py:355
  350.6 34.0 %collective-permute-start.51 = (bf16[128,3072]{1,0:T(8,128)(2,1)}, bf16[128,3072]{1,0:T(8,128)(2,1)}, u32[]{:S(2)}, u32[]{:S(2)}) collective-permute-start(bf16[128,3072]{1,0:T(8,128)(2,1)} %get-tuple-element.448), channel_id=1, source_target_pairs={{0,16},{16,0},{1,17},{17,1},{2,18},{18,2},{3,19},{19,3},{4,20},{20... | collective-permute-start | bytes 2359304 | tf_op jit(solution)/shard_map/ppermute | solution.py:367
  356.1 28.5 %collective-permute-start.49 = (bf16[128,1536]{1,0:T(8,128)(2,1)S(1)}, bf16[128,1536]{1,0:T(8,128)(2,1)}, u32[]{:S(2)}, u32[]{:S(2)}) collective-permute-start(bf16[128,1536]{1,0:T(8,128)(2,1)S(1)} %multiply_convert_fusion.4.refs_6_), channel_id=1, source_target_pairs={{0,8},{4,12},{8,0},{12,4},{1,9},{5,13},{9,1},{13,5},{2,10},{6,14},... | collective-permute-start | bytes 1179656 | tf_op jit(solution)/shard_map/ppermute | solution.py:339
  356.2 28.4 %collective-permute-start.50 = (bf16[128,1536]{1,0:T(8,128)(2,1)S(1)}, bf16[128,1536]{1,0:T(8,128)(2,1)}, u32[]{:S(2)}, u32[]{:S(2)}) collective-permute-start(bf16[128,1536]{1,0:T(8,128)(2,1)S(1)} %multiply_convert_fusion.4.refs_6_), channel_id=1, source_target_pairs={{0,12},{4,0},{8,4},{12,8},{1,13},{5,1},{9,5},{13,9},{2,14},{6,2},{... | collective-permute-start | bytes 1179656 | tf_op jit(solution)/shard_map/ppermute | solution.py:339
  364.1 95.1 %collective-permute-start.59 = (bf16[1,256,1536]{2,1,0:T(8,128)(2,1)}, bf16[1,256,1536]{2,1,0:T(8,128)(2,1)}, u32[]{:S(2)}, u32[]{:S(2)}) collective-permute-start(bf16[1,256,1536]{2,1,0:T(8,128)(2,1)} %get-tuple-element.447), channel_id=1, source_target_pairs={{0,1},{1,0},{2,3},{3,2},{4,5},{5,4},{6,7},{7,6},{8,9},{9,8},{10,11... | collective-permute-start | bytes 2359304 | tf_op jit(solution)/shard_map/ppermute | solution.py:372
  418.9 27.7 %collective-permute-start.53 = (bf16[128,1664]{1,0:T(8,128)(2,1)}, bf16[128,1664]{1,0:T(8,128)(2,1)S(1)}, u32[]{:S(2)}, u32[]{:S(2)}) collective-permute-start(bf16[128,1664]{1,0:T(8,128)(2,1)} %get-tuple-element.222), channel_id=1, source_target_pairs={{0,8},{4,12},{8,0},{12,4},{1,9},{5,13},{9,1},{13,5},{2,10},{6,14},... | collective-permute-start | bytes 1277960 | tf_op jit(solution)/shard_map/ppermute | solution.py:347
  419.6 38.3 %collective-permute-start.52 = (bf16[128,1664]{1,0:T(8,128)(2,1)}, bf16[128,1664]{1,0:T(8,128)(2,1)S(1)}, u32[]{:S(2)}, u32[]{:S(2)}) collective-permute-start(bf16[128,1664]{1,0:T(8,128)(2,1)} %get-tuple-element.221), channel_id=1, source_target_pairs={{0,12},{4,0},{8,4},{12,8},{1,13},{5,1},{9,5},{13,9},{2,14},{6,2},{... | collective-permute-start | bytes 1277960 | tf_op jit(solution)/shard_map/ppermute | solution.py:347
  422.7 35.2 %collective-permute-start.56 = (bf16[256,3072]{1,0:T(8,128)(2,1)S(1)}, bf16[256,3072]{1,0:T(8,128)(2,1)S(1)}, u32[]{:S(2)}, u32[]{:S(2)}) collective-permute-start(bf16[256,3072]{1,0:T(8,128)(2,1)S(1)} %constant_dynamic-update-slice_fusion.3), channel_id=1, source_target_pairs={{0,2},{1,3},{2,0},{3,1},{4,6},{5,7},{6,4},{7,5},{8,10},{9,11},{10,... | collective-permute-start | bytes 4718600 | tf_op jit(solution)/shard_map/ppermute | solution.py:597
  430.1 29.1 %collective-permute-start.58 = (bf16[1,256,1536]{2,1,0:T(8,128)(2,1)S(1)}, bf16[1,256,1536]{2,1,0:T(8,128)(2,1)S(1)}, u32[]{:S(2)}, u32[]{:S(2)}) collective-permute-start(bf16[1,256,1536]{2,1,0:T(8,128)(2,1)S(1)} %get-tuple-element.445), channel_id=1, source_target_pairs={{0,1},{1,0},{2,3},{3,2},{4,5},{5,4},{6,7},{7,6},{8,9},{9,8},{10,11... | collective-permute-start | bytes 2359304 | tf_op jit(solution)/shard_map/ppermute | solution.py:372
  463.4 25.5 %collective-permute-start.60 = (bf16[1,256,1536]{2,1,0:T(8,128)(2,1)}, bf16[1,256,1536]{2,1,0:T(8,128)(2,1)}, u32[]{:S(2)}, u32[]{:S(2)}) collective-permute-start(bf16[1,256,1536]{2,1,0:T(8,128)(2,1)} %get-tuple-element.443), channel_id=1, source_target_pairs={{0,16},{16,0},{1,17},{17,1},{2,18},{18,2},{3,19},{19,3},{4,20},{20... | collective-permute-start | bytes 2359304 | tf_op jit(solution)/shard_map/ppermute | solution.py:367
  464.0 40.9 %collective-permute-start.66 = (bf16[1,512,1536]{2,1,0:T(8,128)(2,1)}, bf16[1,512,1536]{2,1,0:T(8,128)(2,1)}, u32[]{:S(2)}, u32[]{:S(2)}) collective-permute-start(bf16[1,512,1536]{2,1,0:T(8,128)(2,1)} %get-tuple-element.427), channel_id=1, source_target_pairs={{0,2},{1,3},{2,0},{3,1},{4,6},{5,7},{6,4},{7,5},{8,10},{9,11},{10,... | collective-permute-start | bytes 4718600 | tf_op jit(solution)/shard_map/ppermute | solution.py:597
  493.3 24.1 %collective-permute-start.65 = (bf16[1,256,1536]{2,1,0:T(8,128)(2,1)}, bf16[1,256,1536]{2,1,0:T(8,128)(2,1)}, u32[]{:S(2)}, u32[]{:S(2)}) collective-permute-start(bf16[1,256,1536]{2,1,0:T(8,128)(2,1)} %collective-permute-done.60), channel_id=1, source_target_pairs={{0,2},{1,3},{2,0},{3,1},{4,6},{5,7},{6,4},{7,5},{8,10},{9,11},{10,... | collective-permute-start | bytes 2359304 | tf_op jit(solution)/shard_map/ppermute | solution.py:597
  502.4 80.3 %collective-permute-start.75 = (bf16[1,256,1536]{2,1,0:T(8,128)(2,1)}, bf16[1,256,1536]{2,1,0:T(8,128)(2,1)}, u32[]{:S(2)}, u32[]{:S(2)}) collective-permute-start(bf16[1,256,1536]{2,1,0:T(8,128)(2,1)} %get-tuple-element.441), channel_id=1, source_target_pairs={{0,1},{1,0},{2,3},{3,2},{4,5},{5,4},{6,7},{7,6},{8,9},{9,8},{10,11... | collective-permute-start | bytes 2359304 | tf_op jit(solution)/shard_map/ppermute | solution.py:372
  523.4 29.0 %collective-permute-start.68 = (bf16[128,1536]{1,0:T(8,128)(2,1)S(1)}, bf16[128,1536]{1,0:T(8,128)(2,1)S(1)}, u32[]{:S(2)}, u32[]{:S(2)}) collective-permute-start(bf16[128,1536]{1,0:T(8,128)(2,1)S(1)} %fusion.148.refs_6_), channel_id=1, source_target_pairs={{0,8},{4,12},{8,0},{12,4},{1,9},{5,13},{9,1},{13,5},{2,10},{6,14},... | collective-permute-start | bytes 1179656 | tf_op jit(solution)/shard_map/ppermute | solution.py:339
  525.7 26.8 %collective-permute-start.69 = (bf16[128,1536]{1,0:T(8,128)(2,1)S(1)}, bf16[128,1536]{1,0:T(8,128)(2,1)S(1)}, u32[]{:S(2)}, u32[]{:S(2)}) collective-permute-start(bf16[128,1536]{1,0:T(8,128)(2,1)S(1)} %fusion.148.refs_6_), channel_id=1, source_target_pairs={{0,12},{4,0},{8,4},{12,8},{1,13},{5,1},{9,5},{13,9},{2,14},{6,2},{... | collective-permute-start | bytes 1179656 | tf_op jit(solution)/shard_map/ppermute | solution.py:339
  527.3 25.2 %collective-permute-start.70 = (bf16[1,256,1536]{2,1,0:T(8,128)(2,1)}, bf16[1,256,1536]{2,1,0:T(8,128)(2,1)S(1)}, u32[]{:S(2)}, u32[]{:S(2)}) collective-permute-start(bf16[1,256,1536]{2,1,0:T(8,128)(2,1)} %collective-permute-done.64), channel_id=1, source_target_pairs={{0,2},{1,3},{2,0},{3,1},{4,6},{5,7},{6,4},{7,5},{8,10},{9,11},{10,... | collective-permute-start | bytes 2359304 | tf_op jit(solution)/shard_map/ppermute | solution.py:597
  570.8 25.1 %collective-permute-start.73 = (bf16[128,1664]{1,0:T(8,128)(2,1)}, bf16[128,1664]{1,0:T(8,128)(2,1)S(1)}, u32[]{:S(2)}, u32[]{:S(2)}) collective-permute-start(bf16[128,1664]{1,0:T(8,128)(2,1)} %get-tuple-element.260), channel_id=1, source_target_pairs={{0,4},{4,8},{8,12},{12,0},{1,5},{5,9},{9,13},{13,1},{2,6},{6,10},{... | collective-permute-start | bytes 1277960 | tf_op jit(solution)/shard_map/ppermute | solution.py:347
  578.8 28.1 %collective-permute-start.72 = (bf16[128,1664]{1,0:T(8,128)(2,1)}, bf16[128,1664]{1,0:T(8,128)(2,1)S(1)}, u32[]{:S(2)}, u32[]{:S(2)}) collective-permute-start(bf16[128,1664]{1,0:T(8,128)(2,1)} %get-tuple-element.259), channel_id=1, source_target_pairs={{0,8},{4,12},{8,0},{12,4},{1,9},{5,13},{9,1},{13,5},{2,10},{6,14},... | collective-permute-start | bytes 1277960 | tf_op jit(solution)/shard_map/ppermute | solution.py:347
  579.3 27.7 %collective-permute-start.71 = (bf16[128,1664]{1,0:T(8,128)(2,1)}, bf16[128,1664]{1,0:T(8,128)(2,1)S(1)}, u32[]{:S(2)}, u32[]{:S(2)}) collective-permute-start(bf16[128,1664]{1,0:T(8,128)(2,1)} %get-tuple-element.258), channel_id=1, source_target_pairs={{0,12},{4,0},{8,4},{12,8},{1,13},{5,1},{9,5},{13,9},{2,14},{6,2},{... | collective-permute-start | bytes 1277960 | tf_op jit(solution)/shard_map/ppermute | solution.py:347
  585.2 35.4 %collective-permute-start.76 = (bf16[1,512,1536]{2,1,0:T(8,128)(2,1)S(1)}, bf16[1,512,1536]{2,1,0:T(8,128)(2,1)S(1)}, u32[]{:S(2)}, u32[]{:S(2)}) collective-permute-start(bf16[1,512,1536]{2,1,0:T(8,128)(2,1)S(1)} %get-tuple-element.276), channel_id=1, source_target_pairs={{0,2},{1,3},{2,0},{3,1},{4,6},{5,7},{6,4},{7,5},{8,10},{9,11},{10,... | collective-permute-start | bytes 4718600 | tf_op jit(solution)/shard_map/ppermute | solution.py:597
  585.7 35.1 %collective-permute-start.77 = (bf16[1,512,1536]{2,1,0:T(8,128)(2,1)S(1)}, bf16[1,512,1536]{2,1,0:T(8,128)(2,1)S(1)}, u32[]{:S(2)}, u32[]{:S(2)}) collective-permute-start(bf16[1,512,1536]{2,1,0:T(8,128)(2,1)S(1)} %get-tuple-element.425), channel_id=1, source_target_pairs={{0,16},{16,0},{1,17},{17,1},{2,18},{18,2},{3,19},{19,3},{4,20},{20... | collective-permute-start | bytes 4718600 | tf_op jit(solution)/shard_map/ppermute | solution.py:367
  641.0 122.6 %reduce-scatter.5.cloned.1.call-start = ((), (), s32[]{:S(2)}) async-start(), calls=%async_computation.4 | async-start | bytes 1536000 | tf_op jit(solution)/shard_map/reduce_scatter | solution.py:838
  718.7 27.3 %collective-permute-start.92 = (bf16[384,512]{1,0:T(8,128)(2,1)S(1)}, bf16[384,512]{1,0:T(8,128)(2,1)S(1)}, u32[]{:S(2)}, u32[]{:S(2)}) collective-permute-start(bf16[384,512]{1,0:T(8,128)(2,1)S(1)} %get-tuple-element.437), channel_id=1, source_target_pairs={{0,8},{4,12},{8,0},{12,4},{1,9},{5,13},{9,1},{13,5},{2,10},{6,14},... | collective-permute-start | bytes 1179656 | tf_op jit(solution)/shard_map/ppermute | solution.py:347
  718.7 35.8 %collective-permute-start.94 = (bf16[1,512,1536]{2,1,0:T(8,128)(2,1)S(1)}, bf16[1,512,1536]{2,1,0:T(8,128)(2,1)S(1)}, u32[]{:S(2)}, u32[]{:S(2)}) collective-permute-start(bf16[1,512,1536]{2,1,0:T(8,128)(2,1)S(1)} %copy-done.108), channel_id=1, source_target_pairs={{0,2},{1,3},{2,0},{3,1},{4,6},{5,7},{6,4},{7,5},{8,10},{9,11},{10,... | collective-permute-start | bytes 4718600 | tf_op jit(solution)/shard_map/ppermute | solution.py:597
  771.3 24.5 %collective-permute-start.101 = (bf16[1,1536,768]{2,1,0:T(8,128)(2,1)S(1)}, bf16[1,1536,768]{2,1,0:T(8,128)(2,1)S(1)}, u32[]{:S(2)}, u32[]{:S(2)}) collective-permute-start(bf16[1,1536,768]{2,1,0:T(8,128)(2,1)S(1)} %fusion.39), channel_id=1, source_target_pairs={{0,1},{1,0},{2,3},{3,2},{4,5},{5,4},{6,7},{7,6},{8,9},{9,8},{10,11... | collective-permute-start | bytes 7077896 | tf_op jit(solution)/shard_map/ppermute | solution.py:372
  778.4 26.8 %collective-permute-start.103 = (bf16[1,768,1536]{2,1,0:T(8,128)(2,1)S(1)}, bf16[1,768,1536]{2,1,0:T(8,128)(2,1)S(1)}, u32[]{:S(2)}, u32[]{:S(2)}) collective-permute-start(bf16[1,768,1536]{2,1,0:T(8,128)(2,1)S(1)} %fusion.41), channel_id=1, source_target_pairs={{0,1},{1,0},{2,3},{3,2},{4,5},{5,4},{6,7},{7,6},{8,9},{9,8},{10,11... | collective-permute-start | bytes 7077896 | tf_op jit(solution)/shard_map/ppermute | solution.py:372
  (283 other events, 3536.0 us)
Sparse Core Ops, SparseCore 0:
  96.9 147.4 all-gather.5
  270.6 41.4 all-gather.9
  314.2 46.3 all-gather.7
  641.1 42.1 reduce-scatter.2
  685.5 30.9 reduce-scatter.4

commit v6 on v5

--- a/solution.py
+++ b/solution.py
@@ -955,12 +955,11 @@
     gain_one = jnp.sum(shard * joined.astype(F32), axis=1) / gains[0, 0].astype(F32)
     expert_out = []
     for slot in range(3):
-        keep = jnp.stack([one[slot] for one in made])
+        keep = made[0][slot]
         got = swap_core(keep)
-        both = jnp.concatenate(
-            [jnp.where(core == 0, keep, got), jnp.where(core == 0, got, keep)], axis=0
-        )
-        expert_out.append(both.astype(F32)[None])
+        both = jnp.broadcast_to(keep.astype(F32)[None], (2,) + keep.shape)
+        both = lax.dynamic_update_index_in_dim(both, got.astype(F32), 1 - core, 0)
+        expert_out.append(both[None])
     layer_outputs = both_batches(outs)
     input_grads = both_batches(grads)
     return (

time: 826 us -> 830 us (level)
  local copies, waits for them, and re-layouts: 85.8 us -> 94.9 us
    convert_element_type x3 -> x0, other arithmetic: 13.1 us -> none  [body(): expert_out.append(both.astype(F32)[None])]
    unnamed x456 -> x454, local copies, waits for them, and re-layouts: 28.6 us -> 31.8 us
  transfers between devices with their start and end apart: 109 -> 109, of which waited for: 44 -> 45; matrix products, arithmetic and copies ran while one was open for 29% -> 29% of each run, Pallas kernels for 6% -> 6%
where the time goes in v6:
time: 830 us; the launch traced here: 821 us
  waiting for transfers between devices  314 us (38%)
  starting transfers between devices  147 us (18%)
  matrix products  124 us (15%)
  local copies, waits for them, and re-layouts  94.9 us (11%)
  other arithmetic  71.6 us (9%)
  Pallas kernels  51.5 us (6%)
  between operations  17.9 us (2%)
    ppermute x24, waiting for transfers between devices, rel_gather(): lax.ppermute(value, F_AX, [(i, (i + k) % folds) for i in range(folds)])  138 us
    ppermute x25, waiting for transfers between devices, swap_xor(): return lax.ppermute(value, R_AX, [(i, i ^ bit) for i in range(replicas)])  78.6 us
    ppermute x24, starting transfers between devices, rel_gather(): lax.ppermute(value, F_AX, [(i, (i + k) % folds) for i in range(folds)])  63.9 us
    ppermute x15, waiting for transfers between devices, rel_scatter(): lax.ppermute(parts[k], F_AX, [(i, (i - k) % folds) for i in range(folds)])  53.1 us
    dot_general x16, matrix products, mm_nt(): lax.dot_general(a, b, (((1,), (1,)), ((), ())), preferred_element_type=F32)  37.5 us
    dot_general x10, matrix products, mm_tn(): lax.dot_general(a, b, (((0,), (0,)), ((), ())), preferred_element_type=F32)  34.3 us
    ppermute x15, starting transfers between devices, rel_scatter(): lax.ppermute(parts[k], F_AX, [(i, (i - k) % folds) for i in range(folds)])  32.9 us
    unnamed x454, local copies, waits for them, and re-layouts  31.8 us
  transfers between devices with their start and end apart: 109, of which 45 were waited for; matrix products, arithmetic and copies ran while one was open for 29% of the time, Pallas kernels for 6%

profile of v6, /device:TPU:0, one launch (start us, length us, event | category | flops | bytes accessed | tf_op | source)
XLA Modules:
  0.0 820.8 jit_solution(2141512835531205096)
XLA Ops:
  30.0 4.6 dynamic-slice_bitcast_fusion.1
  36.2 4.8 collective-permute-done.11
  60.2 6.3 collective-permute-done.7.refs_3_
  66.6 17.5 %collective-permute-done.8.refs_4_ = bf16[384,640]{1,0:T(8,128)(2,1)S(1)} collective-permute-done((bf16[384,640]{1,0:T(8,128)(2,1)S(1)}, bf16[384,640]{1,0:T(8,128)(2,1)S(1)}, u32[]{:S(2)}, u32[]{:S(2)}) %collective-permute-start.8) | collective-permute-done | bytes 491552 | tf_op jit(solution)/shard_map/ppermute | solution.py:339
  88.7 4.3 collective-permute-done.13
  103.8 11.6 %collective-permute-start.18 = (bf16[128,512]{0,1:T(8,128)(2,1)S(1)}, bf16[128,512]{0,1:T(8,128)(2,1)S(1)}, u32[]{:S(2)}, u32[]{:S(2)}) collective-permute-start(bf16[128,512]{0,1:T(8,128)(2,1)S(1)} %pad_maximum_fusion.23), channel_id=1, source_target_pairs={{0,12},{4,0},{8,4},{12,8},{1,13},{5,1},{9,5},{13,9},{2,14},{6,2},{... | collective-permute-start | bytes 393224 | tf_op jit(solution)/shard_map/ppermute | solution.py:339
  117.0 4.4 collective-permute-done.18
  122.5 12.7 %collective-permute-done.17 = bf16[128,512]{0,1:T(8,128)(2,1)S(1)} collective-permute-done((bf16[128,512]{0,1:T(8,128)(2,1)S(1)}, bf16[128,512]{0,1:T(8,128)(2,1)S(1)}, u32[]{:S(2)}, u32[]{:S(2)}) %collective-permute-start.17) | collective-permute-done | bytes 131104 | tf_op jit(solution)/shard_map/ppermute | solution.py:339
  157.1 10.7 %collective-permute-done.22 = bf16[128,1536]{0,1:T(8,128)(2,1)S(1)} collective-permute-done((bf16[128,1536]{0,1:T(8,128)(2,1)S(1)}, bf16[128,1536]{0,1:T(8,128)(2,1)S(1)}, u32[]{:S(2)}, u32[]{:S(2)}) %collective-permute-start.22) | collective-permute-done | bytes 393248 | tf_op jit(solution)/shard_map/ppermute | solution.py:597
  187.5 10.8 %collective-permute-start.31 = (bf16[128,1536]{1,0:T(8,128)(2,1)S(1)}, bf16[128,1536]{1,0:T(8,128)(2,1)S(1)}, u32[]{:S(2)}, u32[]{:S(2)}) collective-permute-start(bf16[128,1536]{1,0:T(8,128)(2,1)S(1)} %get-tuple-element.183.refs_6_), channel_id=1, source_target_pairs={{0,4},{4,8},{8,12},{12,0},{1,5},{5,9},{9,13},{13,1},{2,6},{6,10},{... | collective-permute-start | bytes 1179656 | tf_op jit(solution)/shard_map/ppermute | solution.py:339
  201.8 13.7 %collective-permute-done.31.refs_7_ = bf16[128,1536]{1,0:T(8,128)(2,1)S(1)} collective-permute-done((bf16[128,1536]{1,0:T(8,128)(2,1)S(1)}, bf16[128,1536]{1,0:T(8,128)(2,1)S(1)}, u32[]{:S(2)}, u32[]{:S(2)}) %collective-permute-start.31) | collective-permute-done | bytes 393248 | tf_op jit(solution)/shard_map/ppermute | solution.py:339
  216.9 25.3 %collective-permute-done.32.refs_8_ = bf16[128,1536]{1,0:T(8,128)(2,1)S(1)} collective-permute-done((bf16[128,1536]{1,0:T(8,128)(2,1)S(1)}, bf16[128,1536]{1,0:T(8,128)(2,1)S(1)}, u32[]{:S(2)}, u32[]{:S(2)}) %collective-permute-start.32) | collective-permute-done | bytes 393248 | tf_op jit(solution)/shard_map/ppermute | solution.py:339
  244.6 9.7 %collective-permute-done.40.refs_23_ = bf16[384,1536]{1,0:T(8,128)(2,1)} collective-permute-done((bf16[384,1536]{1,0:T(8,128)(2,1)}, bf16[384,1536]{1,0:T(8,128)(2,1)}, u32[]{:S(2)}, u32[]{:S(2)}) %collective-permute-start.40) | collective-permute-done | bytes 1179680 | tf_op jit(solution)/shard_map/ppermute | solution.py:597
  257.6 12.7 %shard_map.212 = (bf16[2,256,1536]{2,1,0:T(8,128)(2,1)}, f32[2,256,768]{2,1,0:T(8,128)}, f32[2,256,768]{2,1,0:T(8,128)}, bf16[2,256,1536]{2,1,0:T(8,128)(2,1)}, ...) custom-call(s32[4]{0:T(128)} %get-tuple-element.515.refs_0_, ...), custom_call_target="tpu_custom_call" | custom-call | flops 3623878656 | bytes 20447232 | tf_op jit(solution)/shard_map/pallas_call | solution.py:274
  271.2 5.5 collective-permute-start.44
  282.1 6.7 collective-permute-done.44
  288.8 16.6 %collective-permute-done.43 = bf16[128,1536]{1,0:T(8,128)(2,1)} collective-permute-done((bf16[128,1536]{1,0:T(8,128)(2,1)}, bf16[128,1536]{1,0:T(8,128)(2,1)}, u32[]{:S(2)}, u32[]{:S(2)}) %collective-permute-start.43) | collective-permute-done | bytes 393248 | tf_op jit(solution)/shard_map/ppermute | solution.py:355
  317.7 9.0 %collective-permute-start.47 = (bf16[128,512]{1,0:T(8,128)(2,1)S(1)}, bf16[128,512]{1,0:T(8,128)(2,1)S(1)}, u32[]{:S(2)}, u32[]{:S(2)}) collective-permute-start(bf16[128,512]{1,0:T(8,128)(2,1)S(1)} %pad_maximum_fusion.24), channel_id=1, source_target_pairs={{0,12},{4,0},{8,4},{12,8},{1,13},{5,1},{9,5},{13,9},{2,14},{6,2},{... | collective-permute-start | bytes 393224 | tf_op jit(solution)/shard_map/ppermute | solution.py:339
  330.6 9.5 %collective-permute-done.46 = bf16[128,512]{1,0:T(8,128)(2,1)S(1)} collective-permute-done((bf16[128,512]{1,0:T(8,128)(2,1)S(1)}, bf16[128,512]{1,0:T(8,128)(2,1)S(1)}, u32[]{:S(2)}, u32[]{:S(2)}) %collective-permute-start.46) | collective-permute-done | bytes 131104 | tf_op jit(solution)/shard_map/ppermute | solution.py:339
  364.6 5.6 collective-permute-done.48.refs_7_
  370.2 14.7 %collective-permute-done.49.refs_8_ = bf16[128,1536]{1,0:T(8,128)(2,1)} collective-permute-done((bf16[128,1536]{1,0:T(8,128)(2,1)S(1)}, bf16[128,1536]{1,0:T(8,128)(2,1)}, u32[]{:S(2)}, u32[]{:S(2)}) %collective-permute-start.49) | collective-permute-done | bytes 393248 | tf_op jit(solution)/shard_map/ppermute | solution.py:339
  385.0 12.7 %shard_map.213 = (bf16[2,256,1536]{2,1,0:T(8,128)(2,1)}, f32[2,256,768]{2,1,0:T(8,128)}, f32[2,256,768]{2,1,0:T(8,128)}, bf16[2,256,1536]{2,1,0:T(8,128)(2,1)}, ...) custom-call(s32[4]{0:T(128)} %get-tuple-element.514.refs_0_, ...), custom_call_target="tpu_custom_call" | custom-call | flops 3623878656 | bytes 20447232 | tf_op jit(solution)/shard_map/pallas_call | solution.py:274
  397.7 13.2 %shard_map.214 = (bf16[2,256,1536]{2,1,0:T(8,128)(2,1)}, bf16[128,1664]{1,0:T(8,128)(2,1)}, bf16[128,1664]{1,0:T(8,128)(2,1)}, bf16[128,1664]{1,0:T(8,128)(2,1)}, bf16[128,1664]{1,0:T(8,128)(2,1)}) custom-call(s32[4]{0:T(128)} %get-tuple-element.514.refs_0_, s32[4,2,128]{2,1,0:T(2,128)} %get-tuple-element.207.refs_1_, ...), custom_call_target="tpu_custom_call" | custom-call | flops 3623878656 | bytes 20447232 | tf_op jit(solution)/shard_map/pallas_call | solution.py:298
  411.0 8.2 %collective-permute-start.54 = (bf16[128,1664]{1,0:T(8,128)(2,1)}, bf16[128,1664]{1,0:T(8,128)(2,1)S(1)}, u32[]{:S(2)}, u32[]{:S(2)}) collective-permute-start(bf16[128,1664]{1,0:T(8,128)(2,1)} %get-tuple-element.223), channel_id=1, source_target_pairs={{0,4},{4,8},{8,12},{12,0},{1,5},{5,9},{9,13},{13,1},{2,6},{6,10},{... | collective-permute-start | bytes 1277960 | tf_op jit(solution)/shard_map/ppermute | solution.py:347
  425.1 5.4 collective-permute-done.54
  431.8 15.1 %collective-permute-done.53 = bf16[128,1664]{1,0:T(8,128)(2,1)S(1)} collective-permute-done((bf16[128,1664]{1,0:T(8,128)(2,1)}, bf16[128,1664]{1,0:T(8,128)(2,1)S(1)}, u32[]{:S(2)}, u32[]{:S(2)}) %collective-permute-start.53) | collective-permute-done | bytes 426016 | tf_op jit(solution)/shard_map/ppermute | solution.py:347
  447.0 11.3 %collective-permute-done.56 = bf16[256,3072]{1,0:T(8,128)(2,1)S(1)} collective-permute-done((bf16[256,3072]{1,0:T(8,128)(2,1)S(1)}, bf16[256,3072]{1,0:T(8,128)(2,1)S(1)}, u32[]{:S(2)}, u32[]{:S(2)}) %collective-permute-start.56) | collective-permute-done | bytes 1572896 | tf_op jit(solution)/shard_map/ppermute | solution.py:597
  478.5 4.8 fusion.50
  506.0 6.0 collective-permute-done.64
  512.0 5.9 collective-permute-done.65
  518.2 5.2 fusion.141
  530.7 7.2 collective-permute-done.67.refs_7_
  537.9 15.1 %collective-permute-done.68.refs_8_ = bf16[128,1536]{1,0:T(8,128)(2,1)S(1)} collective-permute-done((bf16[128,1536]{1,0:T(8,128)(2,1)S(1)}, bf16[128,1536]{1,0:T(8,128)(2,1)S(1)}, u32[]{:S(2)}, u32[]{:S(2)}) %collective-permute-start.68) | collective-permute-done | bytes 393248 | tf_op jit(solution)/shard_map/ppermute | solution.py:339
  554.2 12.9 %shard_map.215 = (bf16[2,256,1536]{2,1,0:T(8,128)(2,1)}, bf16[128,1664]{1,0:T(8,128)(2,1)}, bf16[128,1664]{1,0:T(8,128)(2,1)}, bf16[128,1664]{1,0:T(8,128)(2,1)}, bf16[128,1664]{1,0:T(8,128)(2,1)}) custom-call(s32[4]{0:T(128)} %get-tuple-element.515.refs_0_, s32[4,2,128]{2,1,0:T(2,128)} %get-tuple-element.248.refs_1_, ...), custom_call_target="tpu_custom_call" | custom-call | flops 3623878656 | bytes 20447232 | tf_op jit(solution)/shard_map/pallas_call | solution.py:298
  571.3 8.0 collective-permute-start.73
  587.8 4.4 fusion.64
  592.2 4.3 fusion.60
  596.6 10.8 %collective-permute-done.72 = bf16[128,1664]{1,0:T(8,128)(2,1)S(1)} collective-permute-done((bf16[128,1664]{1,0:T(8,128)(2,1)}, bf16[128,1664]{1,0:T(8,128)(2,1)S(1)}, u32[]{:S(2)}, u32[]{:S(2)}) %collective-permute-start.72) | collective-permute-done | bytes 426016 | tf_op jit(solution)/shard_map/ppermute | solution.py:347
  607.7 13.6 %collective-permute-done.76 = bf16[1,512,1536]{2,1,0:T(8,128)(2,1)S(1)} collective-permute-done((bf16[1,512,1536]{2,1,0:T(8,128)(2,1)S(1)}, bf16[1,512,1536]{2,1,0:T(8,128)(2,1)S(1)}, u32[]{:S(2)}, u32[]{:S(2)}) %collective-permute-start.76) | collective-permute-done | bytes 1572896 | tf_op jit(solution)/shard_map/ppermute | solution.py:597
  666.3 6.2 multiply_convert_fusion.2
  705.4 5.1 collective-permute-done.87
  722.3 4.8 fusion.256
  727.1 4.4 fusion.257
  740.5 7.9 collective-permute-done.92
  748.4 7.2 collective-permute-done.91
  758.9 7.2 multiply_convert_fusion
  768.6 5.2 add_convert_fusion.2
  803.4 4.6 broadcast_in_dim.311
  (940 shorter events, 369.2 us)
Async XLA Ops:
  7.2 299.9 %all-gather.6.cloned.1.call-start = ((), (), s32[]{:S(2)}) async-start(), calls=%async_computation.2 | async-start | bytes 11759616 | tf_op jit(solution)/shard_map/all_gather | solution.py:714
  9.0 38.0 %collective-permute-start.4 = (bf16[128,1536]{1,0:T(8,128)(2,1)}, bf16[128,1536]{1,0:T(8,128)(2,1)}, u32[]{:S(2)}, u32[]{:S(2)}) collective-permute-start(bf16[128,1536]{1,0:T(8,128)(2,1)} %dynamic-slice_bitcast_fusion.3.refs_6_), channel_id=1, source_target_pairs={{0,4},{4,8},{8,12},{12,0},{1,5},{5,9},{9,13},{13,1},{2,6},{6,10},{... | collective-permute-start | bytes 1179656 | tf_op jit(solution)/shard_map/ppermute | solution.py:339
  12.0 35.0 %collective-permute-start.5 = (bf16[128,1536]{1,0:T(8,128)(2,1)}, bf16[128,1536]{1,0:T(8,128)(2,1)}, u32[]{:S(2)}, u32[]{:S(2)}) collective-permute-start(bf16[128,1536]{1,0:T(8,128)(2,1)} %dynamic-slice_bitcast_fusion.3.refs_6_), channel_id=1, source_target_pairs={{0,8},{4,12},{8,0},{12,4},{1,9},{5,13},{9,1},{13,5},{2,10},{6,14},... | collective-permute-start | bytes 1179656 | tf_op jit(solution)/shard_map/ppermute | solution.py:339
  51.3 32.8 %collective-permute-start.8 = (bf16[384,640]{1,0:T(8,128)(2,1)S(1)}, bf16[384,640]{1,0:T(8,128)(2,1)S(1)}, u32[]{:S(2)}, u32[]{:S(2)}) collective-permute-start(bf16[384,640]{1,0:T(8,128)(2,1)S(1)} %fusion.160.refs_2_), channel_id=1, source_target_pairs={{0,8},{4,12},{8,0},{12,4},{1,9},{5,13},{9,1},{13,5},{2,10},{6,14},... | collective-permute-start | bytes 1474568 | tf_op jit(solution)/shard_map/ppermute | solution.py:339
  54.6 29.5 %collective-permute-start.10 = (bf16[1536,384]{1,0:T(8,128)(2,1)S(1)}, bf16[1536,384]{1,0:T(8,128)(2,1)S(1)}, u32[]{:S(2)}, u32[]{:S(2)}) collective-permute-start(bf16[1536,384]{1,0:T(8,128)(2,1)S(1)} %copy-done.122), channel_id=1, source_target_pairs={{0,16},{16,0},{1,17},{17,1},{2,18},{18,2},{3,19},{19,3},{4,20},{20... | collective-permute-start | bytes 3538952 | tf_op jit(solution)/shard_map/ppermute | solution.py:367
  57.9 26.2 %collective-permute-start.9 = (bf16[384,640]{1,0:T(8,128)(2,1)S(1)}, bf16[384,640]{1,0:T(8,128)(2,1)S(1)}, u32[]{:S(2)}, u32[]{:S(2)}) collective-permute-start(bf16[384,640]{1,0:T(8,128)(2,1)S(1)} %fusion.160.refs_2_), channel_id=1, source_target_pairs={{0,12},{4,0},{8,4},{12,8},{1,13},{5,1},{9,5},{13,9},{2,14},{6,2},{... | collective-permute-start | bytes 1474568 | tf_op jit(solution)/shard_map/ppermute | solution.py:339
  59.3 36.6 %collective-permute-start.15 = (bf16[48,3712]{1,0:T(8,128)(2,1)S(1)}, bf16[48,3712]{1,0:T(8,128)(2,1)S(1)}, u32[]{:S(2)}, u32[]{:S(2)}) collective-permute-start(bf16[48,3712]{1,0:T(8,128)(2,1)S(1)} %get-tuple-element.169), channel_id=1, source_target_pairs={{0,16},{16,0},{1,17},{17,1},{2,18},{18,2},{3,19},{19,3},{4,20},{20... | collective-permute-start | bytes 1069064 | tf_op jit(solution)/shard_map/ppermute | solution.py:367
  96.6 267.9 %all-gather.10.cloned.1.call-start = ((), (), s32[]{:S(2)}) async-start(), calls=%async_computation.6 | async-start | bytes 5898240 | tf_op jit(solution)/shard_map/all_gather | solution.py:766
  98.4 39.3 %collective-permute-start.20 = (bf16[1536,384]{1,0:T(8,128)(2,1)}, bf16[1536,384]{1,0:T(8,128)(2,1)}, u32[]{:S(2)}, u32[]{:S(2)}) collective-permute-start(bf16[1536,384]{1,0:T(8,128)(2,1)} %get-tuple-element.172), channel_id=1, source_target_pairs={{0,16},{16,0},{1,17},{17,1},{2,18},{18,2},{3,19},{19,3},{4,20},{20... | collective-permute-start | bytes 3538952 | tf_op jit(solution)/shard_map/ppermute | solution.py:367
  100.1 41.9 %collective-permute-start.19 = (bf16[1536,384]{1,0:T(8,128)(2,1)S(1)}, bf16[1536,384]{1,0:T(8,128)(2,1)}, u32[]{:S(2)}, u32[]{:S(2)}) collective-permute-start(bf16[1536,384]{1,0:T(8,128)(2,1)S(1)} %collective-permute-done.10.refs_13_), channel_id=1, source_target_pairs={{0,2},{1,3},{2,0},{3,1},{4,6},{5,7},{6,4},{7,5},{8,10},{9,11},{10,... | collective-permute-start | bytes 3538952 | tf_op jit(solution)/shard_map/ppermute | solution.py:597
  121.4 62.6 %collective-permute-start.30 = (bf16[384,1536]{1,0:T(8,128)(2,1)}, bf16[384,1536]{1,0:T(8,128)(2,1)}, u32[]{:S(2)}, u32[]{:S(2)}) collective-permute-start(bf16[384,1536]{1,0:T(8,128)(2,1)} %dynamic-slice_bitcast_fusion), channel_id=1, source_target_pairs={{0,16},{16,0},{1,17},{17,1},{2,18},{18,2},{3,19},{19,3},{4,20},{20... | collective-permute-start | bytes 3538952 | tf_op jit(solution)/shard_map/ppermute | solution.py:367
  135.2 32.7 %collective-permute-start.25 = (bf16[384,384]{1,0:T(8,128)(2,1)}, bf16[384,384]{1,0:T(8,128)(2,1)}, u32[]{:S(2)}, u32[]{:S(2)}) collective-permute-start(bf16[384,384]{1,0:T(8,128)(2,1)} %broadcast_select_fusion.15), channel_id=1, source_target_pairs={{0,8},{4,12},{8,0},{12,4},{1,9},{5,13},{9,1},{13,5},{2,10},{6,14},... | collective-permute-start | bytes 884744 | tf_op jit(solution)/shard_map/ppermute | solution.py:339
  137.7 32.0 %collective-permute-start.26 = (bf16[384,384]{1,0:T(8,128)(2,1)}, bf16[384,384]{1,0:T(8,128)(2,1)}, u32[]{:S(2)}, u32[]{:S(2)}) collective-permute-start(bf16[384,384]{1,0:T(8,128)(2,1)} %broadcast_select_fusion.15), channel_id=1, source_target_pairs={{0,12},{4,0},{8,4},{12,8},{1,13},{5,1},{9,5},{13,9},{2,14},{6,2},{... | collective-permute-start | bytes 884744 | tf_op jit(solution)/shard_map/ppermute | solution.py:339
  183.9 59.0 %collective-permute-start.34 = (bf16[1536,384]{1,0:T(8,128)(2,1)S(1)}, bf16[1536,384]{1,0:T(8,128)(2,1)S(1)}, u32[]{:S(2)}, u32[]{:S(2)}) collective-permute-start(bf16[1536,384]{1,0:T(8,128)(2,1)S(1)} %collective-permute-done.10.refs_13_), channel_id=1, source_target_pairs={{0,1},{1,0},{2,3},{3,2},{4,5},{5,4},{6,7},{7,6},{8,9},{9,8},{10,11... | collective-permute-start | bytes 3538952 | tf_op jit(solution)/shard_map/ppermute | solution.py:372
  185.4 59.1 %collective-permute-start.37 = (bf16[1536,384]{1,0:T(8,128)(2,1)}, bf16[1536,384]{1,0:T(8,128)(2,1)}, u32[]{:S(2)}, u32[]{:S(2)}) collective-permute-start(bf16[1536,384]{1,0:T(8,128)(2,1)} %collective-permute-done.20.refs_17_), channel_id=1, source_target_pairs={{0,2},{1,3},{2,0},{3,1},{4,6},{5,7},{6,4},{7,5},{8,10},{9,11},{10,... | collective-permute-start | bytes 3538952 | tf_op jit(solution)/shard_map/ppermute | solution.py:597
  185.6 68.7 %collective-permute-start.40 = (bf16[384,1536]{1,0:T(8,128)(2,1)}, bf16[384,1536]{1,0:T(8,128)(2,1)}, u32[]{:S(2)}, u32[]{:S(2)}) collective-permute-start(bf16[384,1536]{1,0:T(8,128)(2,1)} %collective-permute-done.30.refs_21_), channel_id=1, source_target_pairs={{0,2},{1,3},{2,0},{3,1},{4,6},{5,7},{6,4},{7,5},{8,10},{9,11},{10,... | collective-permute-start | bytes 3538952 | tf_op jit(solution)/shard_map/ppermute | solution.py:597
  187.5 28.0 %collective-permute-start.31 = (bf16[128,1536]{1,0:T(8,128)(2,1)S(1)}, bf16[128,1536]{1,0:T(8,128)(2,1)S(1)}, u32[]{:S(2)}, u32[]{:S(2)}) collective-permute-start(bf16[128,1536]{1,0:T(8,128)(2,1)S(1)} %get-tuple-element.183.refs_6_), channel_id=1, source_target_pairs={{0,4},{4,8},{8,12},{12,0},{1,5},{5,9},{9,13},{13,1},{2,6},{6,10},{... | collective-permute-start | bytes 1179656 | tf_op jit(solution)/shard_map/ppermute | solution.py:339
  198.2 43.9 %collective-permute-start.32 = (bf16[128,1536]{1,0:T(8,128)(2,1)S(1)}, bf16[128,1536]{1,0:T(8,128)(2,1)S(1)}, u32[]{:S(2)}, u32[]{:S(2)}) collective-permute-start(bf16[128,1536]{1,0:T(8,128)(2,1)S(1)} %get-tuple-element.183.refs_6_), channel_id=1, source_target_pairs={{0,8},{4,12},{8,0},{12,4},{1,9},{5,13},{9,1},{13,5},{2,10},{6,14},... | collective-permute-start | bytes 1179656 | tf_op jit(solution)/shard_map/ppermute | solution.py:339
  215.4 27.5 %collective-permute-start.33 = (bf16[128,1536]{1,0:T(8,128)(2,1)S(1)}, bf16[128,1536]{1,0:T(8,128)(2,1)S(1)}, u32[]{:S(2)}, u32[]{:S(2)}) collective-permute-start(bf16[128,1536]{1,0:T(8,128)(2,1)S(1)} %get-tuple-element.183.refs_6_), channel_id=1, source_target_pairs={{0,12},{4,0},{8,4},{12,8},{1,13},{5,1},{9,5},{13,9},{2,14},{6,2},{... | collective-permute-start | bytes 1179656 | tf_op jit(solution)/shard_map/ppermute | solution.py:339
  270.4 94.1 %all-gather.8.cloned.1.call-start = ((), (), s32[]{:S(2)}) async-start(), calls=%async_computation.5 | async-start | bytes 7864320 | tf_op jit(solution)/shard_map/all_gather | solution.py:766
  271.2 424.3 %reduce-scatter.3.cloned.1.call-start = ((), (), s32[]{:S(2)}) async-start(), calls=%async_computation.3 | async-start | bytes 1966080 | tf_op jit(solution)/shard_map/reduce_scatter | solution.py:896
  276.7 28.7 %collective-permute-start.43 = (bf16[128,1536]{1,0:T(8,128)(2,1)}, bf16[128,1536]{1,0:T(8,128)(2,1)}, u32[]{:S(2)}, u32[]{:S(2)}) collective-permute-start(bf16[128,1536]{1,0:T(8,128)(2,1)} %get-tuple-element.193), channel_id=1, source_target_pairs={{0,8},{4,12},{8,0},{12,4},{1,9},{5,13},{9,1},{13,5},{2,10},{6,14},... | collective-permute-start | bytes 1179656 | tf_op jit(solution)/shard_map/ppermute | solution.py:355
  279.1 26.3 %collective-permute-start.42 = (bf16[128,1536]{1,0:T(8,128)(2,1)}, bf16[128,1536]{1,0:T(8,128)(2,1)}, u32[]{:S(2)}, u32[]{:S(2)}) collective-permute-start(bf16[128,1536]{1,0:T(8,128)(2,1)} %get-tuple-element.192), channel_id=1, source_target_pairs={{0,12},{4,0},{8,4},{12,8},{1,13},{5,1},{9,5},{13,9},{2,14},{6,2},{... | collective-permute-start | bytes 1179656 | tf_op jit(solution)/shard_map/ppermute | solution.py:355
  351.2 33.7 %collective-permute-start.51 = (bf16[128,3072]{1,0:T(8,128)(2,1)}, bf16[128,3072]{1,0:T(8,128)(2,1)}, u32[]{:S(2)}, u32[]{:S(2)}) collective-permute-start(bf16[128,3072]{1,0:T(8,128)(2,1)} %get-tuple-element.442), channel_id=1, source_target_pairs={{0,16},{16,0},{1,17},{17,1},{2,18},{18,2},{3,19},{19,3},{4,20},{20... | collective-permute-start | bytes 2359304 | tf_op jit(solution)/shard_map/ppermute | solution.py:367
  356.5 28.5 %collective-permute-start.49 = (bf16[128,1536]{1,0:T(8,128)(2,1)S(1)}, bf16[128,1536]{1,0:T(8,128)(2,1)}, u32[]{:S(2)}, u32[]{:S(2)}) collective-permute-start(bf16[128,1536]{1,0:T(8,128)(2,1)S(1)} %multiply_convert_fusion.4.refs_6_), channel_id=1, source_target_pairs={{0,8},{4,12},{8,0},{12,4},{1,9},{5,13},{9,1},{13,5},{2,10},{6,14},... | collective-permute-start | bytes 1179656 | tf_op jit(solution)/shard_map/ppermute | solution.py:339
  356.6 28.3 %collective-permute-start.50 = (bf16[128,1536]{1,0:T(8,128)(2,1)S(1)}, bf16[128,1536]{1,0:T(8,128)(2,1)}, u32[]{:S(2)}, u32[]{:S(2)}) collective-permute-start(bf16[128,1536]{1,0:T(8,128)(2,1)S(1)} %multiply_convert_fusion.4.refs_6_), channel_id=1, source_target_pairs={{0,12},{4,0},{8,4},{12,8},{1,13},{5,1},{9,5},{13,9},{2,14},{6,2},{... | collective-permute-start | bytes 1179656 | tf_op jit(solution)/shard_map/ppermute | solution.py:339
  364.6 95.0 %collective-permute-start.59 = (bf16[1,256,1536]{2,1,0:T(8,128)(2,1)}, bf16[1,256,1536]{2,1,0:T(8,128)(2,1)}, u32[]{:S(2)}, u32[]{:S(2)}) collective-permute-start(bf16[1,256,1536]{2,1,0:T(8,128)(2,1)} %get-tuple-element.441), channel_id=1, source_target_pairs={{0,1},{1,0},{2,3},{3,2},{4,5},{5,4},{6,7},{7,6},{8,9},{9,8},{10,11... | collective-permute-start | bytes 2359304 | tf_op jit(solution)/shard_map/ppermute | solution.py:372
  419.2 27.7 %collective-permute-start.53 = (bf16[128,1664]{1,0:T(8,128)(2,1)}, bf16[128,1664]{1,0:T(8,128)(2,1)S(1)}, u32[]{:S(2)}, u32[]{:S(2)}) collective-permute-start(bf16[128,1664]{1,0:T(8,128)(2,1)} %get-tuple-element.222), channel_id=1, source_target_pairs={{0,8},{4,12},{8,0},{12,4},{1,9},{5,13},{9,1},{13,5},{2,10},{6,14},... | collective-permute-start | bytes 1277960 | tf_op jit(solution)/shard_map/ppermute | solution.py:347
  420.0 38.2 %collective-permute-start.52 = (bf16[128,1664]{1,0:T(8,128)(2,1)}, bf16[128,1664]{1,0:T(8,128)(2,1)S(1)}, u32[]{:S(2)}, u32[]{:S(2)}) collective-permute-start(bf16[128,1664]{1,0:T(8,128)(2,1)} %get-tuple-element.221), channel_id=1, source_target_pairs={{0,12},{4,0},{8,4},{12,8},{1,13},{5,1},{9,5},{13,9},{2,14},{6,2},{... | collective-permute-start | bytes 1277960 | tf_op jit(solution)/shard_map/ppermute | solution.py:347
  423.1 35.2 %collective-permute-start.56 = (bf16[256,3072]{1,0:T(8,128)(2,1)S(1)}, bf16[256,3072]{1,0:T(8,128)(2,1)S(1)}, u32[]{:S(2)}, u32[]{:S(2)}) collective-permute-start(bf16[256,3072]{1,0:T(8,128)(2,1)S(1)} %constant_dynamic-update-slice_fusion.3), channel_id=1, source_target_pairs={{0,2},{1,3},{2,0},{3,1},{4,6},{5,7},{6,4},{7,5},{8,10},{9,11},{10,... | collective-permute-start | bytes 4718600 | tf_op jit(solution)/shard_map/ppermute | solution.py:597
  430.5 29.0 %collective-permute-start.58 = (bf16[1,256,1536]{2,1,0:T(8,128)(2,1)S(1)}, bf16[1,256,1536]{2,1,0:T(8,128)(2,1)S(1)}, u32[]{:S(2)}, u32[]{:S(2)}) collective-permute-start(bf16[1,256,1536]{2,1,0:T(8,128)(2,1)S(1)} %get-tuple-element.439), channel_id=1, source_target_pairs={{0,1},{1,0},{2,3},{3,2},{4,5},{5,4},{6,7},{7,6},{8,9},{9,8},{10,11... | collective-permute-start | bytes 2359304 | tf_op jit(solution)/shard_map/ppermute | solution.py:372
  463.7 26.4 %collective-permute-start.60 = (bf16[1,256,1536]{2,1,0:T(8,128)(2,1)}, bf16[1,256,1536]{2,1,0:T(8,128)(2,1)}, u32[]{:S(2)}, u32[]{:S(2)}) collective-permute-start(bf16[1,256,1536]{2,1,0:T(8,128)(2,1)} %get-tuple-element.437), channel_id=1, source_target_pairs={{0,16},{16,0},{1,17},{17,1},{2,18},{18,2},{3,19},{19,3},{4,20},{20... | collective-permute-start | bytes 2359304 | tf_op jit(solution)/shard_map/ppermute | solution.py:367
  464.5 41.5 %collective-permute-start.66 = (bf16[1,512,1536]{2,1,0:T(8,128)(2,1)}, bf16[1,512,1536]{2,1,0:T(8,128)(2,1)}, u32[]{:S(2)}, u32[]{:S(2)}) collective-permute-start(bf16[1,512,1536]{2,1,0:T(8,128)(2,1)} %get-tuple-element.421), channel_id=1, source_target_pairs={{0,2},{1,3},{2,0},{3,1},{4,6},{5,7},{6,4},{7,5},{8,10},{9,11},{10,... | collective-permute-start | bytes 4718600 | tf_op jit(solution)/shard_map/ppermute | solution.py:597
  494.5 23.5 %collective-permute-start.65 = (bf16[1,256,1536]{2,1,0:T(8,128)(2,1)}, bf16[1,256,1536]{2,1,0:T(8,128)(2,1)}, u32[]{:S(2)}, u32[]{:S(2)}) collective-permute-start(bf16[1,256,1536]{2,1,0:T(8,128)(2,1)} %collective-permute-done.60), channel_id=1, source_target_pairs={{0,2},{1,3},{2,0},{3,1},{4,6},{5,7},{6,4},{7,5},{8,10},{9,11},{10,... | collective-permute-start | bytes 2359304 | tf_op jit(solution)/shard_map/ppermute | solution.py:597
  503.6 79.8 %collective-permute-start.75 = (bf16[1,256,1536]{2,1,0:T(8,128)(2,1)}, bf16[1,256,1536]{2,1,0:T(8,128)(2,1)}, u32[]{:S(2)}, u32[]{:S(2)}) collective-permute-start(bf16[1,256,1536]{2,1,0:T(8,128)(2,1)} %get-tuple-element.435), channel_id=1, source_target_pairs={{0,1},{1,0},{2,3},{3,2},{4,5},{5,4},{6,7},{7,6},{8,9},{9,8},{10,11... | collective-permute-start | bytes 2359304 | tf_op jit(solution)/shard_map/ppermute | solution.py:372
  524.0 29.0 %collective-permute-start.68 = (bf16[128,1536]{1,0:T(8,128)(2,1)S(1)}, bf16[128,1536]{1,0:T(8,128)(2,1)S(1)}, u32[]{:S(2)}, u32[]{:S(2)}) collective-permute-start(bf16[128,1536]{1,0:T(8,128)(2,1)S(1)} %fusion.145.refs_6_), channel_id=1, source_target_pairs={{0,8},{4,12},{8,0},{12,4},{1,9},{5,13},{9,1},{13,5},{2,10},{6,14},... | collective-permute-start | bytes 1179656 | tf_op jit(solution)/shard_map/ppermute | solution.py:339
  526.2 26.8 %collective-permute-start.69 = (bf16[128,1536]{1,0:T(8,128)(2,1)S(1)}, bf16[128,1536]{1,0:T(8,128)(2,1)S(1)}, u32[]{:S(2)}, u32[]{:S(2)}) collective-permute-start(bf16[128,1536]{1,0:T(8,128)(2,1)S(1)} %fusion.145.refs_6_), channel_id=1, source_target_pairs={{0,12},{4,0},{8,4},{12,8},{1,13},{5,1},{9,5},{13,9},{2,14},{6,2},{... | collective-permute-start | bytes 1179656 | tf_op jit(solution)/shard_map/ppermute | solution.py:339
  527.8 25.2 %collective-permute-start.70 = (bf16[1,256,1536]{2,1,0:T(8,128)(2,1)}, bf16[1,256,1536]{2,1,0:T(8,128)(2,1)S(1)}, u32[]{:S(2)}, u32[]{:S(2)}) collective-permute-start(bf16[1,256,1536]{2,1,0:T(8,128)(2,1)} %collective-permute-done.64), channel_id=1, source_target_pairs={{0,2},{1,3},{2,0},{3,1},{4,6},{5,7},{6,4},{7,5},{8,10},{9,11},{10,... | collective-permute-start | bytes 2359304 | tf_op jit(solution)/shard_map/ppermute | solution.py:597
  571.3 25.3 %collective-permute-start.73 = (bf16[128,1664]{1,0:T(8,128)(2,1)}, bf16[128,1664]{1,0:T(8,128)(2,1)S(1)}, u32[]{:S(2)}, u32[]{:S(2)}) collective-permute-start(bf16[128,1664]{1,0:T(8,128)(2,1)} %get-tuple-element.260), channel_id=1, source_target_pairs={{0,4},{4,8},{8,12},{12,0},{1,5},{5,9},{9,13},{13,1},{2,6},{6,10},{... | collective-permute-start | bytes 1277960 | tf_op jit(solution)/shard_map/ppermute | solution.py:347
  579.3 28.2 %collective-permute-start.72 = (bf16[128,1664]{1,0:T(8,128)(2,1)}, bf16[128,1664]{1,0:T(8,128)(2,1)S(1)}, u32[]{:S(2)}, u32[]{:S(2)}) collective-permute-start(bf16[128,1664]{1,0:T(8,128)(2,1)} %get-tuple-element.259), channel_id=1, source_target_pairs={{0,8},{4,12},{8,0},{12,4},{1,9},{5,13},{9,1},{13,5},{2,10},{6,14},... | collective-permute-start | bytes 1277960 | tf_op jit(solution)/shard_map/ppermute | solution.py:347
  579.7 27.7 %collective-permute-start.71 = (bf16[128,1664]{1,0:T(8,128)(2,1)}, bf16[128,1664]{1,0:T(8,128)(2,1)S(1)}, u32[]{:S(2)}, u32[]{:S(2)}) collective-permute-start(bf16[128,1664]{1,0:T(8,128)(2,1)} %get-tuple-element.258), channel_id=1, source_target_pairs={{0,12},{4,0},{8,4},{12,8},{1,13},{5,1},{9,5},{13,9},{2,14},{6,2},{... | collective-permute-start | bytes 1277960 | tf_op jit(solution)/shard_map/ppermute | solution.py:347
  585.8 35.5 %collective-permute-start.76 = (bf16[1,512,1536]{2,1,0:T(8,128)(2,1)S(1)}, bf16[1,512,1536]{2,1,0:T(8,128)(2,1)S(1)}, u32[]{:S(2)}, u32[]{:S(2)}) collective-permute-start(bf16[1,512,1536]{2,1,0:T(8,128)(2,1)S(1)} %get-tuple-element.276), channel_id=1, source_target_pairs={{0,2},{1,3},{2,0},{3,1},{4,6},{5,7},{6,4},{7,5},{8,10},{9,11},{10,... | collective-permute-start | bytes 4718600 | tf_op jit(solution)/shard_map/ppermute | solution.py:597
  586.4 35.2 %collective-permute-start.77 = (bf16[1,512,1536]{2,1,0:T(8,128)(2,1)S(1)}, bf16[1,512,1536]{2,1,0:T(8,128)(2,1)S(1)}, u32[]{:S(2)}, u32[]{:S(2)}) collective-permute-start(bf16[1,512,1536]{2,1,0:T(8,128)(2,1)S(1)} %get-tuple-element.419), channel_id=1, source_target_pairs={{0,16},{16,0},{1,17},{17,1},{2,18},{18,2},{3,19},{19,3},{4,20},{20... | collective-permute-start | bytes 4718600 | tf_op jit(solution)/shard_map/ppermute | solution.py:367
  643.3 122.8 %reduce-scatter.5.cloned.1.call-start = ((), (), s32[]{:S(2)}) async-start(), calls=%async_computation.4 | async-start | bytes 1536000 | tf_op jit(solution)/shard_map/reduce_scatter | solution.py:838
  716.3 22.2 %collective-permute-start.89 = (bf16[128,1536]{1,0:T(8,128)(2,1)S(1)}, bf16[128,1536]{1,0:T(8,128)(2,1)S(1)}, u32[]{:S(2)}, u32[]{:S(2)}) collective-permute-start(bf16[128,1536]{1,0:T(8,128)(2,1)S(1)} %get-tuple-element.402), channel_id=1, source_target_pairs={{0,16},{16,0},{1,17},{17,1},{2,18},{18,2},{3,19},{19,3},{4,20},{20... | collective-permute-start | bytes 1179656 | tf_op jit(solution)/shard_map/ppermute | solution.py:367
  721.4 27.0 %collective-permute-start.92 = (bf16[384,512]{1,0:T(8,128)(2,1)S(1)}, bf16[384,512]{1,0:T(8,128)(2,1)S(1)}, u32[]{:S(2)}, u32[]{:S(2)}) collective-permute-start(bf16[384,512]{1,0:T(8,128)(2,1)S(1)} %get-tuple-element.431), channel_id=1, source_target_pairs={{0,8},{4,12},{8,0},{12,4},{1,9},{5,13},{9,1},{13,5},{2,10},{6,14},... | collective-permute-start | bytes 1179656 | tf_op jit(solution)/shard_map/ppermute | solution.py:347
  721.4 35.7 %collective-permute-start.94 = (bf16[1,512,1536]{2,1,0:T(8,128)(2,1)S(1)}, bf16[1,512,1536]{2,1,0:T(8,128)(2,1)S(1)}, u32[]{:S(2)}, u32[]{:S(2)}) collective-permute-start(bf16[1,512,1536]{2,1,0:T(8,128)(2,1)S(1)} %copy-done.108), channel_id=1, source_target_pairs={{0,2},{1,3},{2,0},{3,1},{4,6},{5,7},{6,4},{7,5},{8,10},{9,11},{10,... | collective-permute-start | bytes 4718600 | tf_op jit(solution)/shard_map/ppermute | solution.py:597
  773.8 24.3 %collective-permute-start.101 = (bf16[1536,768]{1,0:T(8,128)(2,1)S(1)}, bf16[1536,768]{1,0:T(8,128)(2,1)S(1)}, u32[]{:S(2)}, u32[]{:S(2)}) collective-permute-start(bf16[1536,768]{1,0:T(8,128)(2,1)S(1)} %add_convert_fusion.2), channel_id=1, source_target_pairs={{0,1},{1,0},{2,3},{3,2},{4,5},{5,4},{6,7},{7,6},{8,9},{9,8},{10,11... | collective-permute-start | bytes 7077896 | tf_op jit(solution)/shard_map/ppermute | solution.py:372
  (282 other events, 3634.0 us)
Sparse Core Ops, SparseCore 0:
  96.8 147.3 all-gather.5
  270.6 41.3 all-gather.9
  314.1 46.3 all-gather.7
  643.4 42.4 reduce-scatter.2
  688.1 30.9 reduce-scatter.4

commit v7 on v5

--- a/solution.py
+++ b/solution.py
@@ -691,13 +691,14 @@
     first_tail = head_block[:, lin_width:]
     out_block = of_first(column_share(w_out[0]))
     head_block, out_block = lax.optimization_barrier((head_block, out_block))
-    out_block = stacked_rows(out_block)
+    out_parts = rel_gather(out_block)
     group_in = attention_in(token_group.astype(F32), first_tail[:, expert_count])[2]
     first_lin = share_back(
         mm(group_in, head_block[:, :lin_width]).astype(BF16).reshape(replicas, rows, lin_width)
     )
 
     def first_out(mixed_low):
+        out_block = held["out_block"]
         group = jnp.concatenate(group_rows(mixed_low), axis=0)
         made = mm(group, out_block).astype(BF16)
         return share_back(made.reshape(replicas, rows, -1))
@@ -740,7 +741,8 @@
     )
 
     def first_mixed(tied_lin, tied, attn_in, mixed_low):
-        gate_x, up_y = tied
+        gate_x, up_y, parts = tied
+        held["out_block"] = stacked_parts(parts)
         held["second"] = whole_weights(1, *tied_lin)
         return (crossed_y[0], up_y), (gate_x,)
 
@@ -756,11 +758,11 @@
     held = {}
     first_value, first_kept, experts_w, _ = layer_forward(
         my_tokens, first_w, (w_gate[0], w_up[0], w_down[0]), common, tiles, routes_at, scalars[0],
-        dict(router=(head_block, lin_width // LANES), lin=(keep, got), kv=(swap_xor(crossed_y[0], 2), crossed_y[1]), mixed=first_mixed, moe=first_moe),
+        dict(router=(head_block, lin_width // LANES), lin=(keep, got), kv=(swap_xor(crossed_y[0], 2), crossed_y[1], out_parts), mixed=first_mixed, moe=first_moe),
         first_lin, first_out,
     )
     head_share, out_share, _ = lax.optimization_barrier(
-        (head_block[:, :lin_width], out_block, first_kept["moe"][1])
+        (head_block[:, :lin_width], held["out_block"], first_kept["moe"][1])
     )
     weights_first = (
         first_w[0], lax.all_gather(head_share, R_AX, axis=0), lax.all_gather(out_share, R_AX, axis=0), first_tail

time: 826 us -> 833 us (level)
  waiting for transfers between devices: 315 us -> 338 us
  starting transfers between devices: 146 us -> 135 us
    ppermute x24, waiting for transfers between devices: 138 us -> 150 us  [rel_gather(): lax.ppermute(value, F_AX, [(i, (i + k) % folds) for i in range(folds)])]
    ppermute x25, waiting for transfers between devices: 80.7 us -> 91.5 us  [swap_xor(): return lax.ppermute(value, R_AX, [(i, i ^ bit) for i in range(replicas)])]
    unnamed x456 -> x470, local copies, waits for them, and re-layouts: 28.6 us -> 28.2 us
  transfers between devices with their start and end apart: 109 -> 109, of which waited for: 44 -> 47; matrix products, arithmetic and copies ran while one was open for 29% -> 29% of each run, Pallas kernels for 6% -> 6%
where the time goes in v7:
time: 833 us; the launch traced here: 824 us
  waiting for transfers between devices  338 us (41%)
  starting transfers between devices  135 us (16%)
  matrix products  121 us (15%)
  local copies, waits for them, and re-layouts  80.8 us (10%)
  other arithmetic  79.7 us (10%)
  Pallas kernels  51.5 us (6%)
  between operations  17.9 us (2%)
    ppermute x24, waiting for transfers between devices, rel_gather(): lax.ppermute(value, F_AX, [(i, (i + k) % folds) for i in range(folds)])  150 us
    ppermute x25, waiting for transfers between devices, swap_xor(): return lax.ppermute(value, R_AX, [(i, i ^ bit) for i in range(replicas)])  91.5 us
    ppermute x24, starting transfers between devices, rel_gather(): lax.ppermute(value, F_AX, [(i, (i + k) % folds) for i in range(folds)])  60.2 us
    ppermute x15, waiting for transfers between devices, rel_scatter(): lax.ppermute(parts[k], F_AX, [(i, (i - k) % folds) for i in range(folds)])  53.9 us
    dot_general x16, matrix products, mm_nt(): lax.dot_general(a, b, (((1,), (1,)), ((), ())), preferred_element_type=F32)  37.4 us
    ppermute x15, starting transfers between devices, rel_scatter(): lax.ppermute(parts[k], F_AX, [(i, (i - k) % folds) for i in range(folds)])  34.4 us
    dot_general x10, matrix products, mm_tn(): lax.dot_general(a, b, (((0,), (0,)), ((), ())), preferred_element_type=F32)  33.3 us
    dot_general x8, matrix products, mm(): return jnp.dot(a, b, preferred_element_type=F32)  28.8 us
  transfers between devices with their start and end apart: 109, of which 47 were waited for; matrix products, arithmetic and copies ran while one was open for 29% of the time, Pallas kernels for 6%

profile of v7, /device:TPU:0, one launch (start us, length us, event | category | flops | bytes accessed | tf_op | source)
XLA Modules:
  0.0 823.5 jit_solution(7518665261114240998)
XLA Ops:
  29.8 4.6 dynamic-slice_bitcast_fusion.1
  36.0 4.8 collective-permute-done.11
  60.1 6.4 collective-permute-done.7.refs_3_
  66.5 17.5 %collective-permute-done.8.refs_4_ = bf16[384,640]{1,0:T(8,128)(2,1)S(1)} collective-permute-done((bf16[384,640]{1,0:T(8,128)(2,1)S(1)}, bf16[384,640]{1,0:T(8,128)(2,1)S(1)}, u32[]{:S(2)}, u32[]{:S(2)}) %collective-permute-start.8) | collective-permute-done | bytes 491552 | tf_op jit(solution)/shard_map/ppermute | solution.py:339
  102.4 11.6 %collective-permute-start.18 = (bf16[128,512]{0,1:T(8,128)(2,1)S(1)}, bf16[128,512]{0,1:T(8,128)(2,1)S(1)}, u32[]{:S(2)}, u32[]{:S(2)}) collective-permute-start(bf16[128,512]{0,1:T(8,128)(2,1)S(1)} %pad_maximum_fusion.23), channel_id=1, source_target_pairs={{0,12},{4,0},{8,4},{12,8},{1,13},{5,1},{9,5},{13,9},{2,14},{6,2},{... | collective-permute-start | bytes 393224 | tf_op jit(solution)/shard_map/ppermute | solution.py:339
  115.5 4.6 collective-permute-done.18
  120.1 12.2 %collective-permute-start.21 = (bf16[384,384]{1,0:T(8,128)(2,1)S(1)}, bf16[384,384]{1,0:T(8,128)(2,1)S(1)}, u32[]{:S(2)}, u32[]{:S(2)}) collective-permute-start(bf16[384,384]{1,0:T(8,128)(2,1)S(1)} %copy-done.122), channel_id=1, source_target_pairs={{0,4},{4,8},{8,12},{12,0},{1,5},{5,9},{9,13},{13,1},{2,6},{6,10},{... | collective-permute-start | bytes 884744 | tf_op jit(solution)/shard_map/ppermute | solution.py:339
  132.3 14.2 %collective-permute-done.17 = bf16[128,512]{0,1:T(8,128)(2,1)S(1)} collective-permute-done((bf16[128,512]{0,1:T(8,128)(2,1)S(1)}, bf16[128,512]{0,1:T(8,128)(2,1)S(1)}, u32[]{:S(2)}, u32[]{:S(2)}) %collective-permute-start.17) | collective-permute-done | bytes 131104 | tf_op jit(solution)/shard_map/ppermute | solution.py:339
  148.6 14.0 %collective-permute-done.22 = bf16[384,384]{1,0:T(8,128)(2,1)S(1)} collective-permute-done((bf16[384,384]{1,0:T(8,128)(2,1)S(1)}, bf16[384,384]{1,0:T(8,128)(2,1)S(1)}, u32[]{:S(2)}, u32[]{:S(2)}) %collective-permute-start.22) | collective-permute-done | bytes 294944 | tf_op jit(solution)/shard_map/ppermute | solution.py:339
  162.6 5.9 collective-permute-done.23
  169.4 4.5 fusion.254
  180.2 12.8 %collective-permute-done.25 = bf16[128,1536]{0,1:T(8,128)(2,1)S(1)} collective-permute-done((bf16[128,1536]{0,1:T(8,128)(2,1)S(1)}, bf16[128,1536]{0,1:T(8,128)(2,1)S(1)}, u32[]{:S(2)}, u32[]{:S(2)}) %collective-permute-start.25) | collective-permute-done | bytes 393248 | tf_op jit(solution)/shard_map/ppermute | solution.py:597
  201.1 6.2 collective-permute-done.28
  217.1 16.0 %collective-permute-done.31.refs_7_ = bf16[128,1536]{1,0:T(8,128)(2,1)S(1)} collective-permute-done((bf16[128,1536]{1,0:T(8,128)(2,1)S(1)}, bf16[128,1536]{1,0:T(8,128)(2,1)S(1)}, u32[]{:S(2)}, u32[]{:S(2)}) %collective-permute-start.31) | collective-permute-done | bytes 393248 | tf_op jit(solution)/shard_map/ppermute | solution.py:339
  233.4 13.6 %collective-permute-done.32.refs_8_ = bf16[128,1536]{1,0:T(8,128)(2,1)S(1)} collective-permute-done((bf16[128,1536]{1,0:T(8,128)(2,1)S(1)}, bf16[128,1536]{1,0:T(8,128)(2,1)S(1)}, u32[]{:S(2)}, u32[]{:S(2)}) %collective-permute-start.32) | collective-permute-done | bytes 393248 | tf_op jit(solution)/shard_map/ppermute | solution.py:339
  250.7 14.4 %collective-permute-done.40.refs_23_ = bf16[384,1536]{1,0:T(8,128)(2,1)} collective-permute-done((bf16[384,1536]{1,0:T(8,128)(2,1)}, bf16[384,1536]{1,0:T(8,128)(2,1)}, u32[]{:S(2)}, u32[]{:S(2)}) %collective-permute-start.40) | collective-permute-done | bytes 1179680 | tf_op jit(solution)/shard_map/ppermute | solution.py:597
  268.4 12.7 %shard_map.212 = (bf16[2,256,1536]{2,1,0:T(8,128)(2,1)}, f32[2,256,768]{2,1,0:T(8,128)}, f32[2,256,768]{2,1,0:T(8,128)}, bf16[2,256,1536]{2,1,0:T(8,128)(2,1)}, ...) custom-call(s32[4]{0:T(128)} %get-tuple-element.529.refs_0_, ...), custom_call_target="tpu_custom_call" | custom-call | flops 3623878656 | bytes 20447232 | tf_op jit(solution)/shard_map/pallas_call | solution.py:274
  291.2 5.0 collective-permute-done.44
  296.2 16.3 %collective-permute-done.43 = bf16[128,1536]{1,0:T(8,128)(2,1)} collective-permute-done((bf16[128,1536]{1,0:T(8,128)(2,1)}, bf16[128,1536]{1,0:T(8,128)(2,1)}, u32[]{:S(2)}, u32[]{:S(2)}) %collective-permute-start.43) | collective-permute-done | bytes 393248 | tf_op jit(solution)/shard_map/ppermute | solution.py:355
  324.8 10.8 %collective-permute-start.47 = (bf16[128,512]{1,0:T(8,128)(2,1)S(1)}, bf16[128,512]{1,0:T(8,128)(2,1)S(1)}, u32[]{:S(2)}, u32[]{:S(2)}) collective-permute-start(bf16[128,512]{1,0:T(8,128)(2,1)S(1)} %pad_maximum_fusion.24), channel_id=1, source_target_pairs={{0,12},{4,0},{8,4},{12,8},{1,13},{5,1},{9,5},{13,9},{2,14},{6,2},{... | collective-permute-start | bytes 393224 | tf_op jit(solution)/shard_map/ppermute | solution.py:339
  339.5 7.7 collective-permute-done.46
  375.1 15.5 %collective-permute-done.49.refs_8_ = bf16[128,1536]{1,0:T(8,128)(2,1)} collective-permute-done((bf16[128,1536]{1,0:T(8,128)(2,1)S(1)}, bf16[128,1536]{1,0:T(8,128)(2,1)}, u32[]{:S(2)}, u32[]{:S(2)}) %collective-permute-start.49) | collective-permute-done | bytes 393248 | tf_op jit(solution)/shard_map/ppermute | solution.py:339
  390.6 12.7 %shard_map.213 = (bf16[2,256,1536]{2,1,0:T(8,128)(2,1)}, f32[2,256,768]{2,1,0:T(8,128)}, f32[2,256,768]{2,1,0:T(8,128)}, bf16[2,256,1536]{2,1,0:T(8,128)(2,1)}, ...) custom-call(s32[4]{0:T(128)} %get-tuple-element.528.refs_0_, ...), custom_call_target="tpu_custom_call" | custom-call | flops 3623878656 | bytes 20447232 | tf_op jit(solution)/shard_map/pallas_call | solution.py:274
  403.4 13.2 %shard_map.214 = (bf16[2,256,1536]{2,1,0:T(8,128)(2,1)}, bf16[128,1664]{1,0:T(8,128)(2,1)}, bf16[128,1664]{1,0:T(8,128)(2,1)}, bf16[128,1664]{1,0:T(8,128)(2,1)}, bf16[128,1664]{1,0:T(8,128)(2,1)}) custom-call(s32[4]{0:T(128)} %get-tuple-element.528.refs_0_, s32[4,2,128]{2,1,0:T(2,128)} %get-tuple-element.215.refs_1_, ...), custom_call_target="tpu_custom_call" | custom-call | flops 3623878656 | bytes 20447232 | tf_op jit(solution)/shard_map/pallas_call | solution.py:298
  416.5 8.3 %collective-permute-start.54 = (bf16[128,1664]{1,0:T(8,128)(2,1)}, bf16[128,1664]{1,0:T(8,128)(2,1)S(1)}, u32[]{:S(2)}, u32[]{:S(2)}) collective-permute-start(bf16[128,1664]{1,0:T(8,128)(2,1)} %get-tuple-element.231), channel_id=1, source_target_pairs={{0,4},{4,8},{8,12},{12,0},{1,5},{5,9},{9,13},{13,1},{2,6},{6,10},{... | collective-permute-start | bytes 1277960 | tf_op jit(solution)/shard_map/ppermute | solution.py:347
  432.2 4.9 collective-permute-done.54
  438.4 14.6 %collective-permute-done.53 = bf16[128,1664]{1,0:T(8,128)(2,1)S(1)} collective-permute-done((bf16[128,1664]{1,0:T(8,128)(2,1)}, bf16[128,1664]{1,0:T(8,128)(2,1)S(1)}, u32[]{:S(2)}, u32[]{:S(2)}) %collective-permute-start.53) | collective-permute-done | bytes 426016 | tf_op jit(solution)/shard_map/ppermute | solution.py:347
  453.0 10.9 %collective-permute-done.56 = bf16[256,3072]{1,0:T(8,128)(2,1)S(1)} collective-permute-done((bf16[256,3072]{1,0:T(8,128)(2,1)S(1)}, bf16[256,3072]{1,0:T(8,128)(2,1)S(1)}, u32[]{:S(2)}, u32[]{:S(2)}) %collective-permute-start.56) | collective-permute-done | bytes 1572896 | tf_op jit(solution)/shard_map/ppermute | solution.py:597
  484.0 4.7 fusion.53
  511.7 6.0 collective-permute-done.64
  517.7 6.8 collective-permute-done.65
  524.7 5.2 fusion.144
  537.1 7.4 collective-permute-done.67.refs_7_
  544.5 15.1 %collective-permute-done.68.refs_8_ = bf16[128,1536]{1,0:T(8,128)(2,1)S(1)} collective-permute-done((bf16[128,1536]{1,0:T(8,128)(2,1)S(1)}, bf16[128,1536]{1,0:T(8,128)(2,1)S(1)}, u32[]{:S(2)}, u32[]{:S(2)}) %collective-permute-start.68) | collective-permute-done | bytes 393248 | tf_op jit(solution)/shard_map/ppermute | solution.py:339
  560.8 12.9 %shard_map.215 = (bf16[2,256,1536]{2,1,0:T(8,128)(2,1)}, bf16[128,1664]{1,0:T(8,128)(2,1)}, bf16[128,1664]{1,0:T(8,128)(2,1)}, bf16[128,1664]{1,0:T(8,128)(2,1)}, bf16[128,1664]{1,0:T(8,128)(2,1)}) custom-call(s32[4]{0:T(128)} %get-tuple-element.529.refs_0_, s32[4,2,128]{2,1,0:T(2,128)} %get-tuple-element.256.refs_1_, ...), custom_call_target="tpu_custom_call" | custom-call | flops 3623878656 | bytes 20447232 | tf_op jit(solution)/shard_map/pallas_call | solution.py:298
  577.9 7.9 collective-permute-start.73
  601.7 12.3 %collective-permute-done.72 = bf16[128,1664]{1,0:T(8,128)(2,1)S(1)} collective-permute-done((bf16[128,1664]{1,0:T(8,128)(2,1)}, bf16[128,1664]{1,0:T(8,128)(2,1)S(1)}, u32[]{:S(2)}, u32[]{:S(2)}) %collective-permute-start.72) | collective-permute-done | bytes 426016 | tf_op jit(solution)/shard_map/ppermute | solution.py:347
  614.3 13.4 %collective-permute-done.76 = bf16[1,512,1536]{2,1,0:T(8,128)(2,1)S(1)} collective-permute-done((bf16[1,512,1536]{2,1,0:T(8,128)(2,1)S(1)}, bf16[1,512,1536]{2,1,0:T(8,128)(2,1)S(1)}, u32[]{:S(2)}, u32[]{:S(2)}) %collective-permute-start.76) | collective-permute-done | bytes 1572896 | tf_op jit(solution)/shard_map/ppermute | solution.py:597
  669.8 6.2 multiply_convert_fusion.2
  704.1 4.8 collective-permute-done.88
  708.9 5.4 collective-permute-done.87
  726.1 4.8 fusion.259
  730.9 4.4 fusion.260
  745.0 7.5 collective-permute-done.92
  752.4 7.2 collective-permute-done.91
  763.3 7.2 multiply_convert_fusion
  773.0 5.2 fusion.39
  803.1 4.4 maximum_convert_fusion
  (956 shorter events, 361.2 us)
Async XLA Ops:
  7.2 307.1 %all-gather.6.cloned.1.call-start = ((), (), s32[]{:S(2)}) async-start(), calls=%async_computation.2 | async-start | bytes 11759616 | tf_op jit(solution)/shard_map/all_gather | solution.py:715
  9.0 37.9 %collective-permute-start.4 = (bf16[128,1536]{1,0:T(8,128)(2,1)}, bf16[128,1536]{1,0:T(8,128)(2,1)}, u32[]{:S(2)}, u32[]{:S(2)}) collective-permute-start(bf16[128,1536]{1,0:T(8,128)(2,1)} %dynamic-slice_bitcast_fusion.3.refs_6_), channel_id=1, source_target_pairs={{0,4},{4,8},{8,12},{12,0},{1,5},{5,9},{9,13},{13,1},{2,6},{6,10},{... | collective-permute-start | bytes 1179656 | tf_op jit(solution)/shard_map/ppermute | solution.py:339
  12.0 34.9 %collective-permute-start.5 = (bf16[128,1536]{1,0:T(8,128)(2,1)}, bf16[128,1536]{1,0:T(8,128)(2,1)}, u32[]{:S(2)}, u32[]{:S(2)}) collective-permute-start(bf16[128,1536]{1,0:T(8,128)(2,1)} %dynamic-slice_bitcast_fusion.3.refs_6_), channel_id=1, source_target_pairs={{0,8},{4,12},{8,0},{12,4},{1,9},{5,13},{9,1},{13,5},{2,10},{6,14},... | collective-permute-start | bytes 1179656 | tf_op jit(solution)/shard_map/ppermute | solution.py:339
  51.2 32.8 %collective-permute-start.8 = (bf16[384,640]{1,0:T(8,128)(2,1)S(1)}, bf16[384,640]{1,0:T(8,128)(2,1)S(1)}, u32[]{:S(2)}, u32[]{:S(2)}) collective-permute-start(bf16[384,640]{1,0:T(8,128)(2,1)S(1)} %fusion.163.refs_2_), channel_id=1, source_target_pairs={{0,8},{4,12},{8,0},{12,4},{1,9},{5,13},{9,1},{13,5},{2,10},{6,14},... | collective-permute-start | bytes 1474568 | tf_op jit(solution)/shard_map/ppermute | solution.py:339
  54.5 29.5 %collective-permute-start.10 = (bf16[1536,384]{1,0:T(8,128)(2,1)}, bf16[1536,384]{1,0:T(8,128)(2,1)S(1)}, u32[]{:S(2)}, u32[]{:S(2)}) collective-permute-start(bf16[1536,384]{1,0:T(8,128)(2,1)} %get-tuple-element.167), channel_id=1, source_target_pairs={{0,16},{16,0},{1,17},{17,1},{2,18},{18,2},{3,19},{19,3},{4,20},{20... | collective-permute-start | bytes 3538952 | tf_op jit(solution)/shard_map/ppermute | solution.py:367
  57.8 26.2 %collective-permute-start.9 = (bf16[384,640]{1,0:T(8,128)(2,1)S(1)}, bf16[384,640]{1,0:T(8,128)(2,1)S(1)}, u32[]{:S(2)}, u32[]{:S(2)}) collective-permute-start(bf16[384,640]{1,0:T(8,128)(2,1)S(1)} %fusion.163.refs_2_), channel_id=1, source_target_pairs={{0,12},{4,0},{8,4},{12,8},{1,13},{5,1},{9,5},{13,9},{2,14},{6,2},{... | collective-permute-start | bytes 1474568 | tf_op jit(solution)/shard_map/ppermute | solution.py:339
  59.1 36.8 %collective-permute-start.15 = (bf16[48,3712]{1,0:T(8,128)(2,1)S(1)}, bf16[48,3712]{1,0:T(8,128)(2,1)S(1)}, u32[]{:S(2)}, u32[]{:S(2)}) collective-permute-start(bf16[48,3712]{1,0:T(8,128)(2,1)S(1)} %get-tuple-element.173), channel_id=1, source_target_pairs={{0,16},{16,0},{1,17},{17,1},{2,18},{18,2},{3,19},{19,3},{4,20},{20... | collective-permute-start | bytes 1069064 | tf_op jit(solution)/shard_map/ppermute | solution.py:367
  96.7 274.1 %all-gather.10.cloned.1.call-start = ((), (), s32[]{:S(2)}) async-start(), calls=%async_computation.6 | async-start | bytes 5898240 | tf_op jit(solution)/shard_map/all_gather | solution.py:768
  97.6 50.5 %collective-permute-start.20 = (bf16[1536,384]{1,0:T(8,128)(2,1)}, bf16[1536,384]{1,0:T(8,128)(2,1)}, u32[]{:S(2)}, u32[]{:S(2)}) collective-permute-start(bf16[1536,384]{1,0:T(8,128)(2,1)} %get-tuple-element.176), channel_id=1, source_target_pairs={{0,16},{16,0},{1,17},{17,1},{2,18},{18,2},{3,19},{19,3},{4,20},{20... | collective-permute-start | bytes 3538952 | tf_op jit(solution)/shard_map/ppermute | solution.py:367
  99.4 69.1 %collective-permute-start.19 = (bf16[1536,384]{1,0:T(8,128)(2,1)S(1)}, bf16[1536,384]{1,0:T(8,128)(2,1)}, u32[]{:S(2)}, u32[]{:S(2)}) collective-permute-start(bf16[1536,384]{1,0:T(8,128)(2,1)S(1)} %collective-permute-done.10.refs_13_), channel_id=1, source_target_pairs={{0,2},{1,3},{2,0},{3,1},{4,6},{5,7},{6,4},{7,5},{8,10},{9,11},{10,... | collective-permute-start | bytes 3538952 | tf_op jit(solution)/shard_map/ppermute | solution.py:597
  113.9 32.5 %collective-permute-start.17 = (bf16[128,512]{0,1:T(8,128)(2,1)S(1)}, bf16[128,512]{0,1:T(8,128)(2,1)S(1)}, u32[]{:S(2)}, u32[]{:S(2)}) collective-permute-start(bf16[128,512]{0,1:T(8,128)(2,1)S(1)} %pad_maximum_fusion.23), channel_id=1, source_target_pairs={{0,8},{4,12},{8,0},{12,4},{1,9},{5,13},{9,1},{13,5},{2,10},{6,14},... | collective-permute-start | bytes 393224 | tf_op jit(solution)/shard_map/ppermute | solution.py:339
  114.7 31.8 %collective-permute-start.16 = (bf16[128,512]{0,1:T(8,128)(2,1)S(1)}, bf16[128,512]{0,1:T(8,128)(2,1)S(1)}, u32[]{:S(2)}, u32[]{:S(2)}) collective-permute-start(bf16[128,512]{0,1:T(8,128)(2,1)S(1)} %pad_maximum_fusion.23), channel_id=1, source_target_pairs={{0,4},{4,8},{8,12},{12,0},{1,5},{5,9},{9,13},{13,1},{2,6},{6,10},{... | collective-permute-start | bytes 393224 | tf_op jit(solution)/shard_map/ppermute | solution.py:339
  120.1 28.4 %collective-permute-start.21 = (bf16[384,384]{1,0:T(8,128)(2,1)S(1)}, bf16[384,384]{1,0:T(8,128)(2,1)S(1)}, u32[]{:S(2)}, u32[]{:S(2)}) collective-permute-start(bf16[384,384]{1,0:T(8,128)(2,1)S(1)} %copy-done.122), channel_id=1, source_target_pairs={{0,4},{4,8},{8,12},{12,0},{1,5},{5,9},{9,13},{13,1},{2,6},{6,10},{... | collective-permute-start | bytes 884744 | tf_op jit(solution)/shard_map/ppermute | solution.py:339
  148.1 62.9 %collective-permute-start.30 = (bf16[384,1536]{1,0:T(8,128)(2,1)}, bf16[384,1536]{1,0:T(8,128)(2,1)}, u32[]{:S(2)}, u32[]{:S(2)}) collective-permute-start(bf16[384,1536]{1,0:T(8,128)(2,1)} %dynamic-slice_bitcast_fusion), channel_id=1, source_target_pairs={{0,16},{16,0},{1,17},{17,1},{2,18},{18,2},{3,19},{19,3},{4,20},{20... | collective-permute-start | bytes 3538952 | tf_op jit(solution)/shard_map/ppermute | solution.py:367
  211.0 38.1 %collective-permute-start.34 = (bf16[1536,384]{1,0:T(8,128)(2,1)S(1)}, bf16[1536,384]{1,0:T(8,128)(2,1)S(1)}, u32[]{:S(2)}, u32[]{:S(2)}) collective-permute-start(bf16[1536,384]{1,0:T(8,128)(2,1)S(1)} %collective-permute-done.10.refs_13_), channel_id=1, source_target_pairs={{0,1},{1,0},{2,3},{3,2},{4,5},{5,4},{6,7},{7,6},{8,9},{9,8},{10,11... | collective-permute-start | bytes 3538952 | tf_op jit(solution)/shard_map/ppermute | solution.py:372
  211.6 39.0 %collective-permute-start.37 = (bf16[1536,384]{1,0:T(8,128)(2,1)}, bf16[1536,384]{1,0:T(8,128)(2,1)}, u32[]{:S(2)}, u32[]{:S(2)}) collective-permute-start(bf16[1536,384]{1,0:T(8,128)(2,1)} %collective-permute-done.20.refs_17_), channel_id=1, source_target_pairs={{0,2},{1,3},{2,0},{3,1},{4,6},{5,7},{6,4},{7,5},{8,10},{9,11},{10,... | collective-permute-start | bytes 3538952 | tf_op jit(solution)/shard_map/ppermute | solution.py:597
  211.6 53.5 %collective-permute-start.40 = (bf16[384,1536]{1,0:T(8,128)(2,1)}, bf16[384,1536]{1,0:T(8,128)(2,1)}, u32[]{:S(2)}, u32[]{:S(2)}) collective-permute-start(bf16[384,1536]{1,0:T(8,128)(2,1)} %collective-permute-done.30.refs_21_), channel_id=1, source_target_pairs={{0,2},{1,3},{2,0},{3,1},{4,6},{5,7},{6,4},{7,5},{8,10},{9,11},{10,... | collective-permute-start | bytes 3538952 | tf_op jit(solution)/shard_map/ppermute | solution.py:597
  217.1 29.9 %collective-permute-start.32 = (bf16[128,1536]{1,0:T(8,128)(2,1)S(1)}, bf16[128,1536]{1,0:T(8,128)(2,1)S(1)}, u32[]{:S(2)}, u32[]{:S(2)}) collective-permute-start(bf16[128,1536]{1,0:T(8,128)(2,1)S(1)} %get-tuple-element.191.refs_6_), channel_id=1, source_target_pairs={{0,8},{4,12},{8,0},{12,4},{1,9},{5,13},{9,1},{13,5},{2,10},{6,14},... | collective-permute-start | bytes 1179656 | tf_op jit(solution)/shard_map/ppermute | solution.py:339
  281.2 89.7 %all-gather.8.cloned.1.call-start = ((), (), s32[]{:S(2)}) async-start(), calls=%async_computation.5 | async-start | bytes 7864320 | tf_op jit(solution)/shard_map/all_gather | solution.py:768
  282.0 416.9 %reduce-scatter.3.cloned.1.call-start = ((), (), s32[]{:S(2)}) async-start(), calls=%async_computation.3 | async-start | bytes 1966080 | tf_op jit(solution)/shard_map/reduce_scatter | solution.py:898
  285.6 26.9 %collective-permute-start.43 = (bf16[128,1536]{1,0:T(8,128)(2,1)}, bf16[128,1536]{1,0:T(8,128)(2,1)}, u32[]{:S(2)}, u32[]{:S(2)}) collective-permute-start(bf16[128,1536]{1,0:T(8,128)(2,1)} %get-tuple-element.201), channel_id=1, source_target_pairs={{0,8},{4,12},{8,0},{12,4},{1,9},{5,13},{9,1},{13,5},{2,10},{6,14},... | collective-permute-start | bytes 1179656 | tf_op jit(solution)/shard_map/ppermute | solution.py:355
  285.6 26.9 %collective-permute-start.42 = (bf16[128,1536]{1,0:T(8,128)(2,1)}, bf16[128,1536]{1,0:T(8,128)(2,1)}, u32[]{:S(2)}, u32[]{:S(2)}) collective-permute-start(bf16[128,1536]{1,0:T(8,128)(2,1)} %get-tuple-element.200), channel_id=1, source_target_pairs={{0,12},{4,0},{8,4},{12,8},{1,13},{5,1},{9,5},{13,9},{2,14},{6,2},{... | collective-permute-start | bytes 1179656 | tf_op jit(solution)/shard_map/ppermute | solution.py:355
  357.5 33.1 %collective-permute-start.51 = (bf16[128,3072]{1,0:T(8,128)(2,1)}, bf16[128,3072]{1,0:T(8,128)(2,1)}, u32[]{:S(2)}, u32[]{:S(2)}) collective-permute-start(bf16[128,3072]{1,0:T(8,128)(2,1)} %get-tuple-element.456), channel_id=1, source_target_pairs={{0,16},{16,0},{1,17},{17,1},{2,18},{18,2},{3,19},{19,3},{4,20},{20... | collective-permute-start | bytes 2359304 | tf_op jit(solution)/shard_map/ppermute | solution.py:367
  361.5 29.1 %collective-permute-start.49 = (bf16[128,1536]{1,0:T(8,128)(2,1)S(1)}, bf16[128,1536]{1,0:T(8,128)(2,1)}, u32[]{:S(2)}, u32[]{:S(2)}) collective-permute-start(bf16[128,1536]{1,0:T(8,128)(2,1)S(1)} %multiply_convert_fusion.4.refs_6_), channel_id=1, source_target_pairs={{0,8},{4,12},{8,0},{12,4},{1,9},{5,13},{9,1},{13,5},{2,10},{6,14},... | collective-permute-start | bytes 1179656 | tf_op jit(solution)/shard_map/ppermute | solution.py:339
  363.8 26.8 %collective-permute-start.50 = (bf16[128,1536]{1,0:T(8,128)(2,1)S(1)}, bf16[128,1536]{1,0:T(8,128)(2,1)}, u32[]{:S(2)}, u32[]{:S(2)}) collective-permute-start(bf16[128,1536]{1,0:T(8,128)(2,1)S(1)} %multiply_convert_fusion.4.refs_6_), channel_id=1, source_target_pairs={{0,12},{4,0},{8,4},{12,8},{1,13},{5,1},{9,5},{13,9},{2,14},{6,2},{... | collective-permute-start | bytes 1179656 | tf_op jit(solution)/shard_map/ppermute | solution.py:339
  370.9 94.4 %collective-permute-start.59 = (bf16[1,256,1536]{2,1,0:T(8,128)(2,1)}, bf16[1,256,1536]{2,1,0:T(8,128)(2,1)}, u32[]{:S(2)}, u32[]{:S(2)}) collective-permute-start(bf16[1,256,1536]{2,1,0:T(8,128)(2,1)} %get-tuple-element.455), channel_id=1, source_target_pairs={{0,1},{1,0},{2,3},{3,2},{4,5},{5,4},{6,7},{7,6},{8,9},{9,8},{10,11... | collective-permute-start | bytes 2359304 | tf_op jit(solution)/shard_map/ppermute | solution.py:372
  424.8 28.1 %collective-permute-start.53 = (bf16[128,1664]{1,0:T(8,128)(2,1)}, bf16[128,1664]{1,0:T(8,128)(2,1)S(1)}, u32[]{:S(2)}, u32[]{:S(2)}) collective-permute-start(bf16[128,1664]{1,0:T(8,128)(2,1)} %get-tuple-element.230), channel_id=1, source_target_pairs={{0,8},{4,12},{8,0},{12,4},{1,9},{5,13},{9,1},{13,5},{2,10},{6,14},... | collective-permute-start | bytes 1277960 | tf_op jit(solution)/shard_map/ppermute | solution.py:347
  426.6 37.3 %collective-permute-start.52 = (bf16[128,1664]{1,0:T(8,128)(2,1)}, bf16[128,1664]{1,0:T(8,128)(2,1)S(1)}, u32[]{:S(2)}, u32[]{:S(2)}) collective-permute-start(bf16[128,1664]{1,0:T(8,128)(2,1)} %get-tuple-element.229), channel_id=1, source_target_pairs={{0,12},{4,0},{8,4},{12,8},{1,13},{5,1},{9,5},{13,9},{2,14},{6,2},{... | collective-permute-start | bytes 1277960 | tf_op jit(solution)/shard_map/ppermute | solution.py:347
  428.6 35.2 %collective-permute-start.56 = (bf16[256,3072]{1,0:T(8,128)(2,1)S(1)}, bf16[256,3072]{1,0:T(8,128)(2,1)S(1)}, u32[]{:S(2)}, u32[]{:S(2)}) collective-permute-start(bf16[256,3072]{1,0:T(8,128)(2,1)S(1)} %constant_dynamic-update-slice_fusion.3), channel_id=1, source_target_pairs={{0,2},{1,3},{2,0},{3,1},{4,6},{5,7},{6,4},{7,5},{8,10},{9,11},{10,... | collective-permute-start | bytes 4718600 | tf_op jit(solution)/shard_map/ppermute | solution.py:597
  437.1 28.1 %collective-permute-start.58 = (bf16[1,256,1536]{2,1,0:T(8,128)(2,1)S(1)}, bf16[1,256,1536]{2,1,0:T(8,128)(2,1)S(1)}, u32[]{:S(2)}, u32[]{:S(2)}) collective-permute-start(bf16[1,256,1536]{2,1,0:T(8,128)(2,1)S(1)} %get-tuple-element.453), channel_id=1, source_target_pairs={{0,1},{1,0},{2,3},{3,2},{4,5},{5,4},{6,7},{7,6},{8,9},{9,8},{10,11... | collective-permute-start | bytes 2359304 | tf_op jit(solution)/shard_map/ppermute | solution.py:372
  469.3 26.4 %collective-permute-start.60 = (bf16[1,256,1536]{2,1,0:T(8,128)(2,1)}, bf16[1,256,1536]{2,1,0:T(8,128)(2,1)}, u32[]{:S(2)}, u32[]{:S(2)}) collective-permute-start(bf16[1,256,1536]{2,1,0:T(8,128)(2,1)} %get-tuple-element.451), channel_id=1, source_target_pairs={{0,16},{16,0},{1,17},{17,1},{2,18},{18,2},{3,19},{19,3},{4,20},{20... | collective-permute-start | bytes 2359304 | tf_op jit(solution)/shard_map/ppermute | solution.py:367
  471.0 40.7 %collective-permute-start.66 = (bf16[1,512,1536]{2,1,0:T(8,128)(2,1)}, bf16[1,512,1536]{2,1,0:T(8,128)(2,1)}, u32[]{:S(2)}, u32[]{:S(2)}) collective-permute-start(bf16[1,512,1536]{2,1,0:T(8,128)(2,1)} %get-tuple-element.435), channel_id=1, source_target_pairs={{0,2},{1,3},{2,0},{3,1},{4,6},{5,7},{6,4},{7,5},{8,10},{9,11},{10,... | collective-permute-start | bytes 4718600 | tf_op jit(solution)/shard_map/ppermute | solution.py:597
  499.1 25.4 %collective-permute-start.65 = (bf16[1,256,1536]{2,1,0:T(8,128)(2,1)}, bf16[1,256,1536]{2,1,0:T(8,128)(2,1)}, u32[]{:S(2)}, u32[]{:S(2)}) collective-permute-start(bf16[1,256,1536]{2,1,0:T(8,128)(2,1)} %collective-permute-done.60), channel_id=1, source_target_pairs={{0,2},{1,3},{2,0},{3,1},{4,6},{5,7},{6,4},{7,5},{8,10},{9,11},{10,... | collective-permute-start | bytes 2359304 | tf_op jit(solution)/shard_map/ppermute | solution.py:597
  509.3 80.5 %collective-permute-start.75 = (bf16[1,256,1536]{2,1,0:T(8,128)(2,1)}, bf16[1,256,1536]{2,1,0:T(8,128)(2,1)}, u32[]{:S(2)}, u32[]{:S(2)}) collective-permute-start(bf16[1,256,1536]{2,1,0:T(8,128)(2,1)} %get-tuple-element.449), channel_id=1, source_target_pairs={{0,1},{1,0},{2,3},{3,2},{4,5},{5,4},{6,7},{7,6},{8,9},{9,8},{10,11... | collective-permute-start | bytes 2359304 | tf_op jit(solution)/shard_map/ppermute | solution.py:372
  530.5 29.0 %collective-permute-start.68 = (bf16[128,1536]{1,0:T(8,128)(2,1)S(1)}, bf16[128,1536]{1,0:T(8,128)(2,1)S(1)}, u32[]{:S(2)}, u32[]{:S(2)}) collective-permute-start(bf16[128,1536]{1,0:T(8,128)(2,1)S(1)} %fusion.148.refs_6_), channel_id=1, source_target_pairs={{0,8},{4,12},{8,0},{12,4},{1,9},{5,13},{9,1},{13,5},{2,10},{6,14},... | collective-permute-start | bytes 1179656 | tf_op jit(solution)/shard_map/ppermute | solution.py:339
  532.8 26.8 %collective-permute-start.69 = (bf16[128,1536]{1,0:T(8,128)(2,1)S(1)}, bf16[128,1536]{1,0:T(8,128)(2,1)S(1)}, u32[]{:S(2)}, u32[]{:S(2)}) collective-permute-start(bf16[128,1536]{1,0:T(8,128)(2,1)S(1)} %fusion.148.refs_6_), channel_id=1, source_target_pairs={{0,12},{4,0},{8,4},{12,8},{1,13},{5,1},{9,5},{13,9},{2,14},{6,2},{... | collective-permute-start | bytes 1179656 | tf_op jit(solution)/shard_map/ppermute | solution.py:339
  534.3 25.2 %collective-permute-start.70 = (bf16[1,256,1536]{2,1,0:T(8,128)(2,1)}, bf16[1,256,1536]{2,1,0:T(8,128)(2,1)S(1)}, u32[]{:S(2)}, u32[]{:S(2)}) collective-permute-start(bf16[1,256,1536]{2,1,0:T(8,128)(2,1)} %collective-permute-done.64), channel_id=1, source_target_pairs={{0,2},{1,3},{2,0},{3,1},{4,6},{5,7},{6,4},{7,5},{8,10},{9,11},{10,... | collective-permute-start | bytes 2359304 | tf_op jit(solution)/shard_map/ppermute | solution.py:597
  577.9 23.8 %collective-permute-start.73 = (bf16[128,1664]{1,0:T(8,128)(2,1)}, bf16[128,1664]{1,0:T(8,128)(2,1)S(1)}, u32[]{:S(2)}, u32[]{:S(2)}) collective-permute-start(bf16[128,1664]{1,0:T(8,128)(2,1)} %get-tuple-element.268), channel_id=1, source_target_pairs={{0,4},{4,8},{8,12},{12,0},{1,5},{5,9},{9,13},{13,1},{2,6},{6,10},{... | collective-permute-start | bytes 1277960 | tf_op jit(solution)/shard_map/ppermute | solution.py:347
  585.9 28.2 %collective-permute-start.72 = (bf16[128,1664]{1,0:T(8,128)(2,1)}, bf16[128,1664]{1,0:T(8,128)(2,1)S(1)}, u32[]{:S(2)}, u32[]{:S(2)}) collective-permute-start(bf16[128,1664]{1,0:T(8,128)(2,1)} %get-tuple-element.267), channel_id=1, source_target_pairs={{0,8},{4,12},{8,0},{12,4},{1,9},{5,13},{9,1},{13,5},{2,10},{6,14},... | collective-permute-start | bytes 1277960 | tf_op jit(solution)/shard_map/ppermute | solution.py:347
  586.4 27.7 %collective-permute-start.71 = (bf16[128,1664]{1,0:T(8,128)(2,1)}, bf16[128,1664]{1,0:T(8,128)(2,1)S(1)}, u32[]{:S(2)}, u32[]{:S(2)}) collective-permute-start(bf16[128,1664]{1,0:T(8,128)(2,1)} %get-tuple-element.266), channel_id=1, source_target_pairs={{0,12},{4,0},{8,4},{12,8},{1,13},{5,1},{9,5},{13,9},{2,14},{6,2},{... | collective-permute-start | bytes 1277960 | tf_op jit(solution)/shard_map/ppermute | solution.py:347
  592.2 35.4 %collective-permute-start.76 = (bf16[1,512,1536]{2,1,0:T(8,128)(2,1)S(1)}, bf16[1,512,1536]{2,1,0:T(8,128)(2,1)S(1)}, u32[]{:S(2)}, u32[]{:S(2)}) collective-permute-start(bf16[1,512,1536]{2,1,0:T(8,128)(2,1)S(1)} %get-tuple-element.284), channel_id=1, source_target_pairs={{0,2},{1,3},{2,0},{3,1},{4,6},{5,7},{6,4},{7,5},{8,10},{9,11},{10,... | collective-permute-start | bytes 4718600 | tf_op jit(solution)/shard_map/ppermute | solution.py:597
  592.6 35.2 %collective-permute-start.77 = (bf16[1,512,1536]{2,1,0:T(8,128)(2,1)S(1)}, bf16[1,512,1536]{2,1,0:T(8,128)(2,1)S(1)}, u32[]{:S(2)}, u32[]{:S(2)}) collective-permute-start(bf16[1,512,1536]{2,1,0:T(8,128)(2,1)S(1)} %get-tuple-element.433), channel_id=1, source_target_pairs={{0,16},{16,0},{1,17},{17,1},{2,18},{18,2},{3,19},{19,3},{4,20},{20... | collective-permute-start | bytes 4718600 | tf_op jit(solution)/shard_map/ppermute | solution.py:367
  646.9 123.6 %reduce-scatter.5.cloned.1.call-start = ((), (), s32[]{:S(2)}) async-start(), calls=%async_computation.4 | async-start | bytes 1536000 | tf_op jit(solution)/shard_map/reduce_scatter | solution.py:840
  720.0 22.9 %collective-permute-start.89 = (bf16[128,1536]{1,0:T(8,128)(2,1)S(1)}, bf16[128,1536]{1,0:T(8,128)(2,1)S(1)}, u32[]{:S(2)}, u32[]{:S(2)}) collective-permute-start(bf16[128,1536]{1,0:T(8,128)(2,1)S(1)} %get-tuple-element.410), channel_id=1, source_target_pairs={{0,16},{16,0},{1,17},{17,1},{2,18},{18,2},{3,19},{19,3},{4,20},{20... | collective-permute-start | bytes 1179656 | tf_op jit(solution)/shard_map/ppermute | solution.py:367
  723.8 28.6 %collective-permute-start.92 = (bf16[384,512]{1,0:T(8,128)(2,1)S(1)}, bf16[384,512]{1,0:T(8,128)(2,1)S(1)}, u32[]{:S(2)}, u32[]{:S(2)}) collective-permute-start(bf16[384,512]{1,0:T(8,128)(2,1)S(1)} %get-tuple-element.445), channel_id=1, source_target_pairs={{0,8},{4,12},{8,0},{12,4},{1,9},{5,13},{9,1},{13,5},{2,10},{6,14},... | collective-permute-start | bytes 1179656 | tf_op jit(solution)/shard_map/ppermute | solution.py:347
  726.0 35.5 %collective-permute-start.94 = (bf16[1,512,1536]{2,1,0:T(8,128)(2,1)S(1)}, bf16[1,512,1536]{2,1,0:T(8,128)(2,1)S(1)}, u32[]{:S(2)}, u32[]{:S(2)}) collective-permute-start(bf16[1,512,1536]{2,1,0:T(8,128)(2,1)S(1)} %copy-done.108), channel_id=1, source_target_pairs={{0,2},{1,3},{2,0},{3,1},{4,6},{5,7},{6,4},{7,5},{8,10},{9,11},{10,... | collective-permute-start | bytes 4718600 | tf_op jit(solution)/shard_map/ppermute | solution.py:597
  778.2 24.5 %collective-permute-start.101 = (bf16[1,1536,768]{2,1,0:T(8,128)(2,1)S(1)}, bf16[1,1536,768]{2,1,0:T(8,128)(2,1)S(1)}, u32[]{:S(2)}, u32[]{:S(2)}) collective-permute-start(bf16[1,1536,768]{2,1,0:T(8,128)(2,1)S(1)} %fusion.39), channel_id=1, source_target_pairs={{0,1},{1,0},{2,3},{3,2},{4,5},{5,4},{6,7},{7,6},{8,9},{9,8},{10,11... | collective-permute-start | bytes 7077896 | tf_op jit(solution)/shard_map/ppermute | solution.py:372
  785.3 26.8 %collective-permute-start.103 = (bf16[1,768,1536]{2,1,0:T(8,128)(2,1)S(1)}, bf16[1,768,1536]{2,1,0:T(8,128)(2,1)S(1)}, u32[]{:S(2)}, u32[]{:S(2)}) collective-permute-start(bf16[1,768,1536]{2,1,0:T(8,128)(2,1)S(1)} %fusion.41), channel_id=1, source_target_pairs={{0,1},{1,0},{2,3},{3,2},{4,5},{5,4},{6,7},{7,6},{8,9},{9,8},{10,11... | collective-permute-start | bytes 7077896 | tf_op jit(solution)/shard_map/ppermute | solution.py:372
  (290 other events, 3531.5 us)
Sparse Core Ops, SparseCore 0:
  96.9 126.4 all-gather.5
  281.3 36.9 all-gather.9
  320.5 46.3 all-gather.7
  647.0 43.2 reduce-scatter.2
  692.5 30.5 reduce-scatter.4
